TPU v7x, 32 devices: a whole 2x2x4 slice. The times are simulated.
32 devices in a mesh: slab: 8 (over y, x, core), orb: 4 (over z).
Axes of the slice: x: 2, y: 2, z: 4, core: 2. Of those that a mesh axis runs over, the one named last changes fastest.
Arguments:
- orbitals: float32 [4, 32, 256, 512], P('orb', 'slab'), may hold values from -6 to 6
- potential: float32 [32, 256, 512], P('slab'), may hold values from -1 to 1
- coeffs: float32 [3], replicated, may hold values from 0.4 to 1.2
Outputs:
- density: float32 [32, 256, 512], P('slab', 'orb')
All inputs are finite; a program needn't handle non-finite values.
Results may differ from a plain program's by a relative error of at most 0.00002.
Values sent between devices are 32-bit elements; how exact they have to be, the bound alone decides.
No kernel may reach another device: no remote copies, remote signals or barrier semaphores. Data moves between devices by JAX's collectives and lax.ppermute only.
A program may use at most 128 MiB of HBM per device.

v0:
```python
import jax
import jax.numpy as jnp
from jax import lax
from jax.sharding import PartitionSpec as P


def extended_2(x, sides, width):
    for axis, dim in sides:
        count, length = (lax.axis_size(axis), x.shape[dim])
        up = [(i, (i + 1) % count) for i in range(count)]
        down = [(j, i) for i, j in up]
        last = lax.slice_in_dim(x, length - width, length, axis=dim)
        leading = lax.slice_in_dim(x, 0, width, axis=dim)
        before = lax.ppermute(last, axis, up)
        after = lax.ppermute(leading, axis, down)
        x = jnp.concatenate([before, x, after], axis=dim)
    return x


def scaled_ext(extended, potential):
    center = extended[2:-2]
    zterm = (
        -2.5 * center
        + 4.0 / 3.0 * (extended[1:-3] + extended[3:-1])
        - 1.0 / 12.0 * (extended[:-4] + extended[4:])
    )
    total = zterm
    for axis in (1, 2):
        near = jnp.roll(center, 1, axis) + jnp.roll(center, -1, axis)
        far = jnp.roll(center, 2, axis) + jnp.roll(center, -2, axis)
        total = total + (-2.5 * center + 4.0 / 3.0 * near - 1.0 / 12.0 * far)
    return (-0.5 * total + potential * center - 4.0 * center) / 5.0


def extend(field):
    return extended_2(field, (("slab", 0),), 2)


def shards(orbitals, potential, coeffs):
    psi = orbitals[0]
    first = scaled_ext(extend(psi), potential)
    second = 2.0 * scaled_ext(extend(first), potential) - psi
    filtered = coeffs[0] * psi + coeffs[1] * first + coeffs[2] * second
    count = lax.axis_size("orb") * orbitals.shape[0]
    term = filtered * filtered / count
    return lax.psum_scatter(term, "orb", scatter_dimension=1, tiled=True)


def solution(mesh):
    return jax.shard_map(
        shards,
        mesh=mesh,
        in_specs=(P("orb", "slab", None, None), P("slab", None, None), P()),
        out_specs=P("slab", "orb", None),
        check_vma=False,
    )
```

profile of v0, /device:TPU:0, one launch (start us, length us, event | category | flops | bytes accessed | tf_op | source)
XLA Modules:
  0.0 136.2 jit_solution(4283276691926660273)
XLA Ops:
  6.5 0.0 copy-start
  6.5 0.0 reduce-scatter.2.cloned.1.call-start
  6.5 1.9 %slice_bitcast_fusion.1 = (f32[2,256,512]{2,1,0:T(8,128)S(1)}, f32[2,256,512]{2,1,0:T(8,128)S(1)}) fusion(f32[1,4,256,512]{3,2,1,0:T(8,128)} %param.3), kind=kLoop, calls=%fused_computation.70 | loop fusion | bytes 4194304 | tf_op jit(solution)/shard_map/slice | solution.py:12
  8.4 0.5 collective-permute-start
  8.9 2.9 %collective-permute-start.1 = (f32[2,256,512]{2,1,0:T(8,128)S(1)}, f32[2,256,512]{2,1,0:T(8,128)S(1)}, u32[]{:S(2)}, u32[]{:S(2)}) collective-permute-start(f32[2,256,512]{2,1,0:T(8,128)S(1)} %get-tuple-element.26), channel_id=1, source_target_pairs={{4,0},{8,4},{12,8},{16,12},{20,16},{24,20},{28,24},{0,28},{5,1},{9... | collective-permute-start | bytes 3145736 | tf_op jit(solution)/shard_map/ppermute | solution.py:15
  11.9 0.0 copy-done
  11.9 0.2 fusion.61
  12.1 0.5 fusion.60
  12.6 0.0 copy-start.4
  12.6 0.5 fusion.58
  13.1 0.2 copy-done.4
  13.2 0.6 fusion.65
  14.5 1.1 fusion.63
  15.6 2.7 %fusion.64 = (f32[4,256,510]{2,1,0:T(8,128)}, f32[4,256,510]{2,1,0:T(8,128)}) fusion(f32[4,256,512]{2,1,0:T(8,128)S(1)} %bitcast.15), kind=kLoop, calls=%fused_computation.87 | loop fusion | bytes 8355840 | tf_op jit(solution)/shard_map/jit(_roll_static)/slice | solution.py:30
  18.3 0.0 copy-start.1
  18.3 2.8 %fusion.62 = (f32[4,256,511]{2,1,0:T(8,128)}, f32[4,256,511]{2,1,0:T(8,128)}) fusion(f32[4,256,512]{2,1,0:T(8,128)S(1)} %bitcast.16), kind=kLoop, calls=%fused_computation.85 | loop fusion | bytes 8372224 | tf_op jit(solution)/shard_map/jit(_roll_static)/slice | solution.py:29
  21.1 11.7 %collective-permute-done = f32[2,256,512]{2,1,0:T(8,128)S(1)} collective-permute-done((f32[2,256,512]{2,1,0:T(8,128)S(1)}, f32[2,256,512]{2,1,0:T(8,128)S(1)}, u32[]{:S(2)}, u32[]{:S(2)}) %collective-permute-start) | collective-permute-done | bytes 1048608 | tf_op jit(solution)/shard_map/ppermute | solution.py:14
  32.8 0.0 copy-start.2
  32.8 1.5 %collective-permute-done.1 = f32[2,256,512]{2,1,0:T(8,128)S(1)} collective-permute-done((f32[2,256,512]{2,1,0:T(8,128)S(1)}, f32[2,256,512]{2,1,0:T(8,128)S(1)}, u32[]{:S(2)}, u32[]{:S(2)}) %collective-permute-start.1) | collective-permute-done | bytes 1048608 | tf_op jit(solution)/shard_map/ppermute | solution.py:15
  34.4 0.0 copy-start.3
  34.4 0.0 copy-done.2
  34.4 1.0 copy-done.3
  35.3 0.0 copy-done.1
  35.3 8.6 %broadcast_multiply_fusion = (f32[4,256,512]{2,1,0:T(8,128)S(1)}, f32[4,256,512]{2,1,0:T(8,128)}) fusion(f32[4,256,512]{2,1,0:T(8,128)S(1)} %bitcast.17, f32[4,256,512]{2,1,0:T(8,128)S(1)} %copy-done.1, f32[4,256,2]{2,1,0:T(8,128)} %get-tuple-element.40, f32[4,256,510]{2,1,0:T(8,128)} %get-tuple-element.42, f32[4,256,510]{2,1,0:T(8,128)} %get-tuple-element.41, ...), kind=kLoop, calls=%fused_computation.68 | loop fusion | flops 20447232 | bytes 27262976 | tf_op jit(solution)/shard_map/div | solution.py:32
  44.0 1.2 fusion.53
  45.1 0.2 fusion.48
  45.3 0.5 fusion.52
  45.8 0.5 fusion.50
  46.3 1.8 %collective-permute-start.2 = (f32[2,256,512]{2,1,0:T(8,128)S(1)}, f32[2,256,512]{2,1,0:T(8,128)}, u32[]{:S(2)}, u32[]{:S(2)}) collective-permute-start(f32[2,256,512]{2,1,0:T(8,128)S(1)} %get-tuple-element.7), channel_id=1, source_target_pairs={{0,4},{4,8},{8,12},{12,16},{16,20},{20,24},{24,28},{28,0},{1,5},{5... | collective-permute-start | bytes 3145736 | tf_op jit(solution)/shard_map/ppermute | solution.py:14
  48.1 1.1 collective-permute-start.3
  49.2 1.1 fusion.55
  50.3 2.8 %fusion.54 = (f32[4,256,511]{2,1,0:T(8,128)}, f32[4,256,511]{2,1,0:T(8,128)}) fusion(f32[4,256,512]{2,1,0:T(8,128)S(1)} %get-tuple-element.5), kind=kLoop, calls=%fused_computation.77 | loop fusion | bytes 8372224 | tf_op jit(solution)/shard_map/jit(_roll_static)/slice | solution.py:29
  53.1 2.7 %fusion.56 = (f32[4,256,510]{2,1,0:T(8,128)}, f32[4,256,510]{2,1,0:T(8,128)}) fusion(f32[4,256,512]{2,1,0:T(8,128)S(1)} %get-tuple-element.5), kind=kLoop, calls=%fused_computation.79 | loop fusion | bytes 8355840 | tf_op jit(solution)/shard_map/jit(_roll_static)/slice | solution.py:30
  55.8 15.8 %collective-permute-done.2 = f32[2,256,512]{2,1,0:T(8,128)} collective-permute-done((f32[2,256,512]{2,1,0:T(8,128)S(1)}, f32[2,256,512]{2,1,0:T(8,128)}, u32[]{:S(2)}, u32[]{:S(2)}) %collective-permute-start.2) | collective-permute-done | bytes 1048608 | tf_op jit(solution)/shard_map/ppermute | solution.py:14
  71.6 0.0 collective-permute-done.3
  71.6 11.1 %fusion.46 = f32[4,256,512]{2,1,0:T(8,128)} fusion(f32[4,256,512]{2,1,0:T(8,128)} %get-tuple-element.6, f32[4,256,512]{2,1,0:T(8,128)} %param.4, f32[4,256,512]{2,1,0:T(8,128)S(1)} %get-tuple-element.5, f32[4,256,2]{2,1,0:T(8,128)} %get-tuple-element.22, f32[4,256,510]{2,1,0:T(8,128)} %get-tuple-element.24, f32[4,256,510]{2,1,0:T(8,128)} %get-tuple-element.23, ...), kind=kLoop, calls=%fused_computation.67 | loop fusion | flops 24641536 | bytes 29360140 | tf_op jit(solution)/shard_map/div | solution.py:45
  82.8 0.0 reduce-scatter.2.cloned.1.call-update
  82.8 46.5 %reduce-scatter.2.cloned.1.call-done = f32[4,64,512]{2,1,0:T(8,128)} async-done(((f32[4,256,512]{2,1,0:T(8,128)}), f32[4,64,512]{2,1,0:T(8,128)}) %reduce-scatter.2.cloned.1.call-update) | async-done | bytes 524304 | tf_op jit(solution)/shard_map/reduce_scatter | solution.py:46
  (4 shorter events, 0.1 us)
Async XLA Ops:
  6.5 5.3 %copy-start = (f32[1,4,256,512]{3,2,1,0:T(8,128)S(1)}, f32[1,4,256,512]{3,2,1,0:T(8,128)}, u32[]{:S(2)}) copy-start(f32[1,4,256,512]{3,2,1,0:T(8,128)} %param.3) | copy-start | bytes 6291460
  6.5 122.8 %reduce-scatter.2.cloned.1.call-start = ((), (), s32[]{:S(2)}) async-start(), calls=%async_computation.1 | async-start | bytes 2621440 | tf_op jit(solution)/shard_map/reduce_scatter | solution.py:46
  8.4 24.4 %collective-permute-start = (f32[2,256,512]{2,1,0:T(8,128)S(1)}, f32[2,256,512]{2,1,0:T(8,128)S(1)}, u32[]{:S(2)}, u32[]{:S(2)}) collective-permute-start(f32[2,256,512]{2,1,0:T(8,128)S(1)} %get-tuple-element.25), channel_id=1, source_target_pairs={{0,4},{4,8},{8,12},{12,16},{16,20},{20,24},{24,28},{28,0},{1,5},{5... | collective-permute-start | bytes 3145736 | tf_op jit(solution)/shard_map/ppermute | solution.py:14
  8.9 25.5 %collective-permute-start.1 = (f32[2,256,512]{2,1,0:T(8,128)S(1)}, f32[2,256,512]{2,1,0:T(8,128)S(1)}, u32[]{:S(2)}, u32[]{:S(2)}) collective-permute-start(f32[2,256,512]{2,1,0:T(8,128)S(1)} %get-tuple-element.26), channel_id=1, source_target_pairs={{4,0},{8,4},{12,8},{16,12},{20,16},{24,20},{28,24},{0,28},{5,1},{9... | collective-permute-start | bytes 3145736 | tf_op jit(solution)/shard_map/ppermute | solution.py:15
  12.6 0.7 copy-start.4
  18.3 17.0 %copy-start.1 = (f32[4,256,512]{2,1,0:T(8,128)S(1)}, f32[4,256,512]{2,1,0:T(8,128)}, u32[]{:S(2)}) copy-start(f32[4,256,512]{2,1,0:T(8,128)} %param.4) | copy-start | bytes 6291460
  32.8 1.5 %copy-start.2 = (f32[2,256,512]{2,1,0:T(8,128)}, f32[2,256,512]{2,1,0:T(8,128)S(1)}, u32[]{:S(2)}) copy-start(f32[2,256,512]{2,1,0:T(8,128)S(1)} %collective-permute-done) | copy-start | bytes 3145732
  34.4 1.0 copy-start.3
  46.3 25.4 %collective-permute-start.2 = (f32[2,256,512]{2,1,0:T(8,128)S(1)}, f32[2,256,512]{2,1,0:T(8,128)}, u32[]{:S(2)}, u32[]{:S(2)}) collective-permute-start(f32[2,256,512]{2,1,0:T(8,128)S(1)} %get-tuple-element.7), channel_id=1, source_target_pairs={{0,4},{4,8},{8,12},{12,16},{16,20},{20,24},{24,28},{28,0},{1,5},{5... | collective-permute-start | bytes 3145736 | tf_op jit(solution)/shard_map/ppermute | solution.py:14
  48.1 23.6 %collective-permute-start.3 = (f32[2,256,512]{2,1,0:T(8,128)S(1)}, f32[2,256,512]{2,1,0:T(8,128)}, u32[]{:S(2)}, u32[]{:S(2)}) collective-permute-start(f32[2,256,512]{2,1,0:T(8,128)S(1)} %get-tuple-element.8), channel_id=1, source_target_pairs={{4,0},{8,4},{12,8},{16,12},{20,16},{24,20},{28,24},{0,28},{5,1},{9... | collective-permute-start | bytes 3145736 | tf_op jit(solution)/shard_map/ppermute | solution.py:15
Sparse Core Ops, SparseCore 0:
  82.9 46.3 reduce-scatter.1
where the time goes:
time: 136 us
  waiting for transfers between devices  75.6 us (56%)
  local copies, waits for them, and re-layouts  20.4 us (15%)
  other arithmetic  19.7 us (14%)
  between operations  14.1 us (10%)
  starting transfers between devices  6.38 us (5%)
    reduce_scatter x1, waiting for transfers between devices, shards(): return lax.psum_scatter(term, 'orb', scatter_dimension=1, tiled=True)  46.5 us
    ppermute x2, waiting for transfers between devices, extended_2(): before = lax.ppermute(last, axis, up)  27.5 us
    div x1, other arithmetic, shards(): term = filtered * filtered / count  11.1 us
    slice x8, local copies, waits for them, and re-layouts, scaled_ext(): far = jnp.roll(center, 2, axis) + jnp.roll(center, -2, axis)  8.68 us
    div x1, other arithmetic, scaled_ext(): return (-0.5 * total + potential * center - 4.0 * center) / 5.0  8.59 us
    slice x8, local copies, waits for them, and re-layouts, scaled_ext(): near = jnp.roll(center, 1, axis) + jnp.roll(center, -1, axis)  7.91 us
    ppermute x2, starting transfers between devices, extended_2(): after = lax.ppermute(leading, axis, down)  4.05 us
  transfers between devices with their start and end apart: 5, of which 4 were waited for; matrix products, arithmetic and copies ran while one was open for 11% of the time, Pallas kernels for 0%

commit v1 on v0

v1 whole, which is shorter than its diff:
```python
import functools

import jax
import jax.numpy as jnp
from jax import lax
from jax.experimental import pallas as pl
from jax.experimental.pallas import tpu as pltpu
from jax.sharding import PartitionSpec as P

NEAR = -2.0 / 15.0
FAR = 1.0 / 120.0
BLOCK = 16


def own(q, odd):
    return jnp.where(odd == 1, 3 - q, q)


def parity():
    return lax.rem(lax.axis_index("slab"), 2)


def with_halo(ref, plane, start, count):
    rows = ref.shape[-2]
    before = pl.multiple_of(lax.rem(start + rows - 8, rows), 8)
    after = pl.multiple_of(lax.rem(start + count, rows), 8)
    return jnp.concatenate(
        [
            ref[plane, pl.ds(before, 8), :],
            ref[plane, pl.ds(start, count), :],
            ref[plane, pl.ds(after, 8), :],
        ],
        axis=0,
    )


def in_plane(ext):
    count, lanes = ext.shape[0] - 16, ext.shape[1]
    mid = ext[8 : 8 + count]
    near = ext[7 : 7 + count] + ext[9 : 9 + count]
    near = near + (pltpu.roll(mid, 1, 1) + pltpu.roll(mid, lanes - 1, 1))
    far = ext[6 : 6 + count] + ext[10 : 10 + count]
    far = far + (pltpu.roll(mid, 2, 1) + pltpu.roll(mid, lanes - 2, 1))
    return mid, near, far


def apply_s(ext, pot, near_z, far_z):
    mid, near, far = in_plane(ext)
    return mid, (
        mid * (0.2 * pot - 0.05) + NEAR * (near + near_z) + FAR * (far + far_z)
    )


def blocks(rows, body):
    def step(i, carry):
        body(pl.multiple_of(i * BLOCK, BLOCK))
        return carry

    lax.fori_loop(0, rows // BLOCK, step, 0)


def start_kernel(psi, pot, g):
    odd = parity()

    def body(r):
        here = pl.ds(r, BLOCK)
        at = [own(q, odd) for q in range(4)]
        e0, e1 = with_halo(psi, at[0], r, BLOCK), with_halo(psi, at[1], r, BLOCK)
        p2, p3 = psi[at[2], here, :], psi[at[3], here, :]
        g[0, here, :] = apply_s(e0, pot[at[0], here, :], e1[8:-8], p2)[1]
        g[1, here, :] = apply_s(e1, pot[at[1], here, :], e0[8:-8] + p2, p3)[1]

    blocks(psi.shape[1], body)


def inner_kernel(c, psi, pot, psi_in, pot_in, g, t, h):
    odd = parity()
    at = [own(q, odd) for q in range(4)]
    base, one, two = c[0] - c[2], c[1], 2.0 * c[2]

    def first(r):
        here = pl.ds(r, BLOCK)
        e2, e3 = with_halo(psi, at[2], r, BLOCK), with_halo(psi, at[3], r, BLOCK)
        p0, p1 = psi[at[0], here, :], psi[at[1], here, :]
        p4, p5 = psi_in[at[0], here, :], psi_in[at[1], here, :]
        t[0, here, :] = apply_s(e2, pot[at[2], here, :], p1 + e3[8:-8], p0 + p4)[1]
        t[1, here, :] = apply_s(e3, pot[at[3], here, :], e2[8:-8] + p4, p1 + p5)[1]

    def second(r):
        here = pl.ds(r, BLOCK)
        e4 = with_halo(psi_in, at[0], r, BLOCK)
        e5 = with_halo(psi_in, at[1], r, BLOCK)
        p2, p3 = psi[at[2], here, :], psi[at[3], here, :]
        p6, p7 = psi_in[at[2], here, :], psi_in[at[3], here, :]
        t4 = apply_s(e4, pot_in[odd, here, :], p3 + e5[8:-8], p2 + p6)[1]
        t5 = apply_s(e5, pot_in[1 - odd, here, :], e4[8:-8] + p6, p3 + p7)[1]
        g0, g1 = g[0, here, :], g[1, here, :]
        e2, e3 = with_halo(t, 0, r, BLOCK), with_halo(t, 1, r, BLOCK)
        t2, s2 = apply_s(e2, pot[at[2], here, :], g1 + e3[8:-8], g0 + t4)
        t3, s3 = apply_s(e3, pot[at[3], here, :], e2[8:-8] + t4, g1 + t5)
        h[0, here, :] = base * p2 + one * t2 + two * s2
        h[1, here, :] = base * p3 + one * t3 + two * s3

    blocks(psi.shape[1], first)
    blocks(psi.shape[1], second)


def halo_terms(halo, band, odd):
    near, far = halo[1 - odd, band], halo[odd, band]
    return NEAR * near + FAR * far, FAR * near


def face_kernel(chunk, halo, g, f):
    odd = parity()
    lo, hi = chunk
    for band in range(halo.shape[1]):
        d0, d1 = halo_terms(halo, band, odd)
        f[0, band] = g[0, band, lo:hi, :] + d0
        f[1, band] = g[1, band, lo:hi, :] + d1


def square(x, bands):
    return x * x * (1.0 / bands)


def back_kernel(chunk, c, halo, h, keep, send):
    odd = parity()
    lo, hi = chunk
    two = 2.0 * c[2]
    me = lax.axis_index("orb")
    bands = halo.shape[1]

    def part(band, out, slot):
        d0, d1 = halo_terms(halo, band, odd)
        v2 = h[0, band, lo:hi, :] + two * (NEAR * d1 + FAR * d0)
        v3 = h[1, band, lo:hi, :] + (two * FAR) * d1
        out[slot, 0] = square(v2, bands)
        out[slot, 1] = square(v3, bands)

    part(me ^ 1, send, 0)
    part(me ^ 2, send, 1)
    part(me, keep, 0)
    part(me ^ 3, keep, 1)


def front_kernel(chunks, c, psi, pot, t, *rest):
    fs, h, scratch = rest[:-2], rest[-2], rest[-1]
    odd = parity()
    at = [own(q, odd) for q in range(2)]
    base, one, two = c[0] - c[2], c[1], 2.0 * c[2]
    rows = psi.shape[1]
    for (lo, hi), f in zip(chunks, fs):
        bands = f.shape[1]
        for band in range(bands):
            first_row = band * (rows // bands)
            for q in range(2):
                scratch[q, first_row + lo : first_row + hi, :] = f[q, band]

    def body(r):
        here = pl.ds(r, BLOCK)
        e0, e1 = with_halo(scratch, 0, r, BLOCK), with_halo(scratch, 1, r, BLOCK)
        t2, t3 = t[0, here, :], t[1, here, :]
        f0, s0 = apply_s(e0, pot[at[0], here, :], e1[8:-8], t2)
        f1, s1 = apply_s(e1, pot[at[1], here, :], e0[8:-8] + t2, t3)
        h[0, here, :] = base * psi[at[0], here, :] + one * f0 + two * s0
        h[1, here, :] = base * psi[at[1], here, :] + one * f1 + two * s1

    blocks(rows, body)


def last_kernel(chunk, c, halo, h, keep, send):
    lo, hi = chunk
    two = 2.0 * c[2]
    me = lax.axis_index("orb")
    bands = halo.shape[1]

    def part(band, out, slot):
        near, far = halo[0, band], halo[1, band]
        v0 = h[0, band, lo:hi, :] + two * (NEAR * near + FAR * far)
        v1 = h[1, band, lo:hi, :] + (two * FAR) * near
        out[slot, 0] = square(v0, bands)
        out[slot, 1] = square(v1, bands)

    part(me ^ 1, send, 0)
    part(me ^ 2, send, 1)
    part(me, keep, 0)
    part(me ^ 3, keep, 1)


def join_kernel(places, *refs):
    out = refs[-1]
    odd = parity()
    for i, (q, (lo, hi)) in enumerate(places):
        keep, came, far = refs[3 * i : 3 * i + 3]
        for j in range(2):
            out[own(q + j, odd), lo:hi, :] = keep[0, j] + came[0, j] + far[j]


def call(kernel, out, args, scalars=0, scratch=(), flops=0):
    vmem = pl.BlockSpec(memory_space=pltpu.VMEM)
    smem = pl.BlockSpec(memory_space=pltpu.SMEM)
    many = isinstance(out, list)
    shapes = [jax.ShapeDtypeStruct(s, jnp.float32) for s in (out if many else [out])]
    total = sum(4 * int(x.size) for x in list(args) + shapes)
    result = pl.pallas_call(
        kernel,
        out_shape=shapes,
        in_specs=[smem] * scalars + [vmem] * (len(args) - scalars),
        out_specs=[vmem] * len(shapes),
        scratch_shapes=list(scratch),
        compiler_params=pltpu.CompilerParams(vmem_limit_bytes=40 * 2**20),
        cost_estimate=pl.CostEstimate(
            flops=flops, bytes_accessed=total, transcendentals=0
        ),
    )(*args)
    return result if many else result[0]


def shards(orbitals, potential, coeffs):
    psi = orbitals[0]
    slabs, bands = lax.axis_size("slab"), lax.axis_size("orb")
    planes, rows, lanes = psi.shape
    wide = rows // bands
    odd = parity()
    me = lax.axis_index("orb")
    chunks = [(0, wide // 2), (wide // 2, wide)]
    face = [(s, s - 1 if s % 2 == 0 else s + 1) for s in range(slabs)]
    face = [(s, d % slabs) for s, d in face]
    partner = [(s, s ^ 1) for s in range(slabs)]

    banded = psi.reshape(planes, bands, wide, lanes)
    halos = []
    for lo, hi in chunks:
        piece = lax.dynamic_slice(
            banded[:, :, lo:hi], (2 * odd, 0, 0, 0), (2, bands, hi - lo, lanes)
        )
        halos.append(lax.ppermute(piece, "slab", face))
    psi_in = lax.ppermute(psi, "slab", partner)
    pot_in = lax.ppermute(
        lax.dynamic_slice(potential, (2 - 2 * odd, 0, 0), (2, rows, lanes)),
        "slab",
        partner,
    )

    plane2 = (2, rows, lanes)
    cells = 2 * rows * lanes
    g = call(start_kernel, plane2, (psi, potential), flops=24 * cells)
    t, h_back = call(
        inner_kernel,
        [plane2, plane2],
        (coeffs, psi, potential, psi_in, pot_in, g),
        scalars=1,
        flops=80 * cells,
    )
    as_bands = lambda x: x.reshape(x.shape[0], bands, wide, lanes)

    def reduced(keep, send):
        near = [(i, i ^ 1) for i in range(bands)]
        far = [(i, i ^ 3) for i in range(bands)]
        came = lax.ppermute(send, "orb", near)
        return keep, came, lax.ppermute(keep[1] + came[1], "orb", far)

    places, pieces, fs, faces = [], [], [], []
    for chunk, halo in zip(chunks, halos):
        shape = halo.shape
        f = call(functools.partial(face_kernel, chunk), shape, (halo, as_bands(g)))
        fs.append(f)
        faces.append(lax.ppermute(f, "slab", face))
        pair = (2, 2) + shape[2:]
        keep, send = call(
            functools.partial(back_kernel, chunk),
            [pair, pair],
            (coeffs, halo, as_bands(h_back)),
            scalars=1,
        )
        places.append((2, chunk))
        pieces += reduced(keep, send)

    h_front = call(
        functools.partial(front_kernel, chunks),
        plane2,
        (coeffs, psi, potential, t, *fs),
        scalars=1,
        scratch=[pltpu.VMEM(plane2, jnp.float32)],
        flops=40 * cells,
    )
    for chunk, halo in zip(chunks, faces):
        pair = (2, 2) + halo.shape[2:]
        keep, send = call(
            functools.partial(last_kernel, chunk),
            [pair, pair],
            (coeffs, halo, as_bands(h_front)),
            scalars=1,
        )
        places.append((0, chunk))
        pieces += reduced(keep, send)
    return call(
        functools.partial(join_kernel, places), (planes, wide, lanes), pieces
    )


def solution(mesh):
    return jax.shard_map(
        shards,
        mesh=mesh,
        in_specs=(P("orb", "slab", None, None), P("slab", None, None), P()),
        out_specs=P("slab", "orb", None),
        check_vma=False,
    )
```

time: 136 us -> 90 us (0.66)
  waiting for transfers between devices: 75.6 us -> 29.8 us
  starting transfers between devices: 6.38 us -> 39.7 us
  other arithmetic: 19.7 us -> 0.08 us
  local copies, waits for them, and re-layouts: 20.4 us -> 2.74 us
  Pallas kernels: 0 us -> 17.4 us
  between operations: 14.1 us -> 0.12 us
    reduce_scatter x1 -> x0, waiting for transfers between devices: 46.5 us -> none  [shards(): return lax.psum_scatter(term, 'orb', scatter_dimension=1, tiled=True)]
    ppermute x4 -> x14, starting transfers between devices: 6.38 us -> 39.7 us  [the longest x4 23.4 us: reduced(): return (keep, came, lax.ppermute(keep[1] + came[1], 'orb', far))]
    div x2 -> x0, other arithmetic: 19.7 us -> none  [the longest x1 11.1 us: shards(): term = filtered * filtered / count]
    slice x19 -> x1, local copies, waits for them, and re-layouts: 19.2 us -> 0.2 us  [shards(): banded[:, :, lo:hi]]
    pallas_call x0 -> x10, Pallas kernels: none -> 17.4 us  [call(): pl.pallas_call(kernel, out_shape=shapes, in_specs=[smem] * scalars + [vme...]
    dynamic_slice x0 -> x3, local copies, waits for them, and re-layouts: none -> 2.53 us  [the longest x1 2.45 us: shards(): lax.dynamic_slice(potential, (2 - 2 * odd, 0, 0), (2, rows, lanes))]
    ppermute x4 -> x14, waiting for transfers between devices: 29.1 us -> 29.8 us  [the longest x2 18 us: shards(): halos.append(lax.ppermute(piece, 'slab', face))]
  transfers between devices with their start and end apart: 5 -> 14, of which waited for: 4 -> 7; matrix products, arithmetic and copies ran while one was open for 11% -> 3% of each run, Pallas kernels for 0% -> 18%
where the time goes in v1:
time: 90 us; the launch traced here: 89.9 us
  starting transfers between devices  39.7 us (44%)
  waiting for transfers between devices  29.8 us (33%)
  Pallas kernels  17.4 us (19%)
  local copies, waits for them, and re-layouts  2.74 us (3%)
    ppermute x4, starting transfers between devices, reduced(): return (keep, came, lax.ppermute(keep[1] + came[1], 'orb', far))  23.4 us
    ppermute x2, waiting for transfers between devices, shards(): halos.append(lax.ppermute(piece, 'slab', face))  18 us
    pallas_call x10, Pallas kernels, call(): pl.pallas_call(kernel, out_shape=shapes, in_specs=[smem] * scalars + [vme...  17.4 us
    ppermute x4, starting transfers between devices, reduced(): came = lax.ppermute(send, 'orb', near)  6.37 us
    ppermute x2, starting transfers between devices, shards(): faces.append(lax.ppermute(f, 'slab', face))  5.74 us
    ppermute x2, waiting for transfers between devices, shards(): faces.append(lax.ppermute(f, 'slab', face))  5.29 us
    ppermute x2, starting transfers between devices, shards(): halos.append(lax.ppermute(piece, 'slab', face))  3.67 us
    ppermute x4, waiting for transfers between devices, reduced(): came = lax.ppermute(send, 'orb', near)  3.59 us
  transfers between devices with their start and end apart: 14, of which 7 were waited for; matrix products, arithmetic and copies ran while one was open for 3% of the time, Pallas kernels for 18%

profile of v1, /device:TPU:0, one launch (start us, length us, event | category | flops | bytes accessed | tf_op | source)
XLA Modules:
  0.0 89.9 jit_solution(9852689341171185295)
XLA Ops:
  0.0 0.0 copy-start
  0.0 0.5 collective-permute-start.1
  0.5 2.4 %constant_dynamic-slice_fusion.1 = f32[2,256,512]{2,1,0:T(8,128)} fusion(f32[4,256,512]{2,1,0:T(8,128)} %pot.5, s32[]{:T(128)S(6)} %select_n.8), kind=kLoop, calls=%fused_computation.9 | loop fusion | bytes 2097156 | tf_op jit(solution)/shard_map/dynamic_slice | solution.py:240
  2.9 0.0 collective-permute-start.2
  2.9 0.0 copy-done
  2.9 0.2 fusion.4
  3.1 0.0 copy-start.1
  3.2 3.6 %collective-permute-start.5 = (f32[2,4,32,512]{3,2,1,0:T(8,128)S(1)}, f32[2,4,32,512]{3,2,1,0:T(8,128)S(1)}, u32[]{:S(2)}, u32[]{:S(2)}) collective-permute-start(f32[2,4,32,512]{3,2,1,0:T(8,128)S(1)} %constant_dynamic-slice_fusion), channel_id=1, source_target_pairs={{0,28},{4,8},{8,4},{12,16},{16,12},{20,24},{24,20},{28,0},{1,29},{... | collective-permute-start | bytes 1572872 | tf_op jit(solution)/shard_map/ppermute | solution.py:237
  6.8 0.1 collective-permute-start
  6.9 0.0 copy-done.1
  6.9 2.5 %shard_map.37.g = f32[2,256,512]{2,1,0:T(8,128)S(1)} custom-call(f32[4,256,512]{2,1,0:T(8,128)S(1)} %bitcast.15, f32[4,256,512]{2,1,0:T(8,128)S(1)} %copy-done.1), custom_call_target="tpu_custom_call" | custom-call | flops 6291456 | bytes 5242880 | tf_op jit(solution)/shard_map/pallas_call | solution.py:205
  9.4 9.7 %collective-permute-done.5.halo = f32[2,4,32,512]{3,2,1,0:T(8,128)S(1)} collective-permute-done((f32[2,4,32,512]{3,2,1,0:T(8,128)S(1)}, f32[2,4,32,512]{3,2,1,0:T(8,128)S(1)}, u32[]{:S(2)}, u32[]{:S(2)}) %collective-permute-start.5) | collective-permute-done | bytes 524320 | tf_op jit(solution)/shard_map/ppermute | solution.py:237
  19.1 0.0 copy-start.2
  19.1 0.1 shard_map.42.rest_1_
  19.2 2.9 %collective-permute-start.11 = (f32[2,4,32,512]{3,2,1,0:T(8,128)S(1)}, f32[2,4,32,512]{3,2,1,0:T(8,128)S(1)}, u32[]{:S(2)}, u32[]{:S(2)}) collective-permute-start(f32[2,4,32,512]{3,2,1,0:T(8,128)S(1)} %shard_map.42.rest_1_), channel_id=1, source_target_pairs={{0,28},{4,8},{8,4},{12,16},{16,12},{20,24},{24,20},{28,0},{1,29},{... | collective-permute-start | bytes 1572872 | tf_op jit(solution)/shard_map/ppermute | solution.py:268
  22.1 8.3 %collective-permute-done.halo = f32[2,4,32,512]{3,2,1,0:T(8,128)S(1)} collective-permute-done((f32[2,4,32,512]{3,2,1,0:T(8,128)S(1)}, f32[2,4,32,512]{3,2,1,0:T(8,128)S(1)}, u32[]{:S(2)}, u32[]{:S(2)}) %collective-permute-start) | collective-permute-done | bytes 524320 | tf_op jit(solution)/shard_map/ppermute | solution.py:237
  30.4 0.1 shard_map.41.rest_0_
  30.4 2.9 %collective-permute-start.8 = (f32[2,4,32,512]{3,2,1,0:T(8,128)S(1)}, f32[2,4,32,512]{3,2,1,0:T(8,128)S(1)}, u32[]{:S(2)}, u32[]{:S(2)}) collective-permute-start(f32[2,4,32,512]{3,2,1,0:T(8,128)S(1)} %shard_map.41.rest_0_), channel_id=1, source_target_pairs={{0,28},{4,8},{8,4},{12,16},{16,12},{20,24},{24,20},{28,0},{1,29},{... | collective-permute-start | bytes 1572872 | tf_op jit(solution)/shard_map/ppermute | solution.py:268
  33.3 0.0 collective-permute-done.2.pot_in
  33.3 0.0 collective-permute-done.1.psi_in
  33.3 0.0 copy-done.2
  33.3 8.1 %shard_map.38 = (f32[2,256,512]{2,1,0:T(8,128)S(1)}, f32[2,256,512]{2,1,0:T(8,128)S(1)}) custom-call(f32[3]{0:T(128)S(1)} %copy-done.2, f32[4,256,512]{2,1,0:T(8,128)S(1)} %bitcast.16, f32[4,256,512]{2,1,0:T(8,128)S(1)} %copy-done.1, f32[4,256,512]{2,1,0:T(8,128)} %collective-permute-done.1.psi_in, f32[2,256,512]{2,1,0:T(8,128)S(1)} %collective-permute-done.2.pot_in, ...), custom_call_target="tpu_custom_call" | custom-call | flops 20971520 | bytes 10485772 | tf_op jit(solution)/shard_map/pallas_call | solution.py:205
  41.4 3.2 %shard_map.43 = f32[2,256,512]{2,1,0:T(8,128)S(1)} custom-call(f32[3]{0:T(128)S(1)} %copy-done.2, f32[4,256,512]{2,1,0:T(8,128)S(1)} %bitcast.17, f32[4,256,512]{2,1,0:T(8,128)S(1)} %copy-done.1, f32[2,256,512]{2,1,0:T(8,128)S(1)} %get-tuple-element.20.t, f32[2,4,32,512]{3,2,1,0:T(8,128)S(1)} %shard_map.41.rest_0_, f32[2,4,32,512]{3,2,1,0:T(8,128)S(1)} %shard_map.42.rest_1_), custom_call_target="tpu_custom_call" | custom-call | flops 10485760 | bytes 7340044 | tf_op jit(solution)/shard_map/pallas_call | solution.py:205
  44.6 0.0 collective-permute-done.11.halo
  44.6 0.7 shard_map.45
  45.2 1.6 %collective-permute-start.12 = (f32[2,2,32,512]{3,2,1,0:T(8,128)S(1)}, f32[2,2,32,512]{3,2,1,0:T(8,128)S(1)}, u32[]{:S(2)}, u32[]{:S(2)}) collective-permute-start(f32[2,2,32,512]{3,2,1,0:T(8,128)S(1)} %get-tuple-element.24), channel_id=1, source_target_pairs={{0,1},{1,0},{2,3},{3,2},{4,5},{5,4},{6,7},{7,6},{8,9},{9,8},{10,11... | collective-permute-start | bytes 786440 | tf_op jit(solution)/shard_map/ppermute | solution.py:260
  46.9 5.3 %collective-permute-done.8.halo = f32[2,4,32,512]{3,2,1,0:T(8,128)S(1)} collective-permute-done((f32[2,4,32,512]{3,2,1,0:T(8,128)S(1)}, f32[2,4,32,512]{3,2,1,0:T(8,128)S(1)}, u32[]{:S(2)}, u32[]{:S(2)}) %collective-permute-start.8) | collective-permute-done | bytes 524320 | tf_op jit(solution)/shard_map/ppermute | solution.py:268
  52.2 0.6 shard_map.44
  52.8 2.6 %collective-permute-start.9 = (f32[2,2,32,512]{3,2,1,0:T(8,128)S(1)}, f32[2,2,32,512]{3,2,1,0:T(8,128)S(1)}, u32[]{:S(2)}, u32[]{:S(2)}) collective-permute-start(f32[2,2,32,512]{3,2,1,0:T(8,128)S(1)} %get-tuple-element.22), channel_id=1, source_target_pairs={{0,1},{1,0},{2,3},{3,2},{4,5},{5,4},{6,7},{7,6},{8,9},{9,8},{10,11... | collective-permute-start | bytes 786440 | tf_op jit(solution)/shard_map/ppermute | solution.py:260
  55.4 0.7 shard_map.40
  56.1 0.1 collective-permute-start.6
  56.2 0.7 shard_map.39
  56.9 2.1 %collective-permute-start.3 = (f32[2,2,32,512]{3,2,1,0:T(8,128)S(1)}, f32[2,2,32,512]{3,2,1,0:T(8,128)S(1)}, u32[]{:S(2)}, u32[]{:S(2)}) collective-permute-start(f32[2,2,32,512]{3,2,1,0:T(8,128)S(1)} %get-tuple-element.17), channel_id=1, source_target_pairs={{0,1},{1,0},{2,3},{3,2},{4,5},{5,4},{6,7},{7,6},{8,9},{9,8},{10,11... | collective-permute-start | bytes 786440 | tf_op jit(solution)/shard_map/ppermute | solution.py:260
  59.0 0.0 collective-permute-done.12.refs_10_
  59.0 2.5 %collective-permute-start.13 = (f32[2,32,512]{2,1,0:T(8,128)S(1)}, f32[2,32,512]{2,1,0:T(8,128)S(1)}, u32[]{:S(2)}, u32[]{:S(2)}) collective-permute-start(f32[2,32,512]{2,1,0:T(8,128)S(1)} %fusion), channel_id=1, source_target_pairs={{0,3},{1,2},{2,1},{3,0},{4,7},{5,6},{6,5},{7,4},{8,11},{9,10},{10,... | collective-permute-start | bytes 393224 | tf_op jit(solution)/shard_map/ppermute | solution.py:261
  61.5 1.1 %collective-permute-done.9.refs_7_ = f32[2,2,32,512]{3,2,1,0:T(8,128)S(1)} collective-permute-done((f32[2,2,32,512]{3,2,1,0:T(8,128)S(1)}, f32[2,2,32,512]{3,2,1,0:T(8,128)S(1)}, u32[]{:S(2)}, u32[]{:S(2)}) %collective-permute-start.9) | collective-permute-done | bytes 262176 | tf_op jit(solution)/shard_map/ppermute | solution.py:260
  62.6 4.1 %collective-permute-start.10 = (f32[2,32,512]{2,1,0:T(8,128)S(1)}, f32[2,32,512]{2,1,0:T(8,128)S(1)}, u32[]{:S(2)}, u32[]{:S(2)}) collective-permute-start(f32[2,32,512]{2,1,0:T(8,128)S(1)} %fusion.1), channel_id=1, source_target_pairs={{0,3},{1,2},{2,1},{3,0},{4,7},{5,6},{6,5},{7,4},{8,11},{9,10},{10,... | collective-permute-start | bytes 393224 | tf_op jit(solution)/shard_map/ppermute | solution.py:261
  66.8 1.5 %collective-permute-done.6.refs_4_ = f32[2,2,32,512]{3,2,1,0:T(8,128)S(1)} collective-permute-done((f32[2,2,32,512]{3,2,1,0:T(8,128)S(1)}, f32[2,2,32,512]{3,2,1,0:T(8,128)S(1)}, u32[]{:S(2)}, u32[]{:S(2)}) %collective-permute-start.6) | collective-permute-done | bytes 262176 | tf_op jit(solution)/shard_map/ppermute | solution.py:260
  68.2 4.1 %collective-permute-start.7 = (f32[2,32,512]{2,1,0:T(8,128)S(1)}, f32[2,32,512]{2,1,0:T(8,128)S(1)}, u32[]{:S(2)}, u32[]{:S(2)}) collective-permute-start(f32[2,32,512]{2,1,0:T(8,128)S(1)} %fusion.2), channel_id=1, source_target_pairs={{0,3},{1,2},{2,1},{3,0},{4,7},{5,6},{6,5},{7,4},{8,11},{9,10},{10,... | collective-permute-start | bytes 393224 | tf_op jit(solution)/shard_map/ppermute | solution.py:261
  72.4 1.0 %collective-permute-done.3.refs_1_ = f32[2,2,32,512]{3,2,1,0:T(8,128)S(1)} collective-permute-done((f32[2,2,32,512]{3,2,1,0:T(8,128)S(1)}, f32[2,2,32,512]{3,2,1,0:T(8,128)S(1)}, u32[]{:S(2)}, u32[]{:S(2)}) %collective-permute-start.3) | collective-permute-done | bytes 262176 | tf_op jit(solution)/shard_map/ppermute | solution.py:260
  73.4 12.6 %collective-permute-start.4 = (f32[2,32,512]{2,1,0:T(8,128)S(1)}, f32[2,32,512]{2,1,0:T(8,128)S(1)}, u32[]{:S(2)}, u32[]{:S(2)}) collective-permute-start(f32[2,32,512]{2,1,0:T(8,128)S(1)} %fusion.3), channel_id=1, source_target_pairs={{0,3},{1,2},{2,1},{3,0},{4,7},{5,6},{6,5},{7,4},{8,11},{9,10},{10,... | collective-permute-start | bytes 393224 | tf_op jit(solution)/shard_map/ppermute | solution.py:261
  86.1 0.0 collective-permute-done.13.refs_11_
  86.1 0.0 collective-permute-done.10.refs_8_
  86.1 0.0 collective-permute-done.7.refs_5_
  86.1 2.9 %collective-permute-done.4.refs_2_ = f32[2,32,512]{2,1,0:T(8,128)S(1)} collective-permute-done((f32[2,32,512]{2,1,0:T(8,128)S(1)}, f32[2,32,512]{2,1,0:T(8,128)S(1)}, u32[]{:S(2)}, u32[]{:S(2)}) %collective-permute-start.4) | collective-permute-done | bytes 131104 | tf_op jit(solution)/shard_map/ppermute | solution.py:261
  89.0 0.9 shard_map.46
  (6 shorter events, 0.2 us)
Async XLA Ops:
  0.0 2.9 %copy-start = (f32[1,4,256,512]{3,2,1,0:T(8,128)S(1)}, f32[1,4,256,512]{3,2,1,0:T(8,128)}, u32[]{:S(2)}) copy-start(f32[1,4,256,512]{3,2,1,0:T(8,128)} %param.3) | copy-start | bytes 6291460
  0.0 33.3 %collective-permute-start.1 = (f32[4,256,512]{2,1,0:T(8,128)}, f32[4,256,512]{2,1,0:T(8,128)}, u32[]{:S(2)}, u32[]{:S(2)}) collective-permute-start(f32[4,256,512]{2,1,0:T(8,128)} %bitcast.13), channel_id=1, source_target_pairs={{0,4},{4,0},{8,12},{12,8},{16,20},{20,16},{24,28},{28,24},{1,5},{5... | collective-permute-start | bytes 6291464 | tf_op jit(solution)/shard_map/ppermute | solution.py:238
  2.9 30.4 %collective-permute-start.2 = (f32[2,256,512]{2,1,0:T(8,128)}, f32[2,256,512]{2,1,0:T(8,128)S(1)}, u32[]{:S(2)}, u32[]{:S(2)}) collective-permute-start(f32[2,256,512]{2,1,0:T(8,128)} %constant_dynamic-slice_fusion.1), channel_id=1, source_target_pairs={{0,4},{4,0},{8,12},{12,8},{16,20},{20,16},{24,28},{28,24},{1,5},{5... | collective-permute-start | bytes 3145736 | tf_op jit(solution)/shard_map/ppermute | solution.py:239
  3.1 3.8 %copy-start.1 = (f32[4,256,512]{2,1,0:T(8,128)S(1)}, f32[4,256,512]{2,1,0:T(8,128)}, u32[]{:S(2)}) copy-start(f32[4,256,512]{2,1,0:T(8,128)} %pot.5) | copy-start | bytes 6291460
  3.2 15.9 %collective-permute-start.5 = (f32[2,4,32,512]{3,2,1,0:T(8,128)S(1)}, f32[2,4,32,512]{3,2,1,0:T(8,128)S(1)}, u32[]{:S(2)}, u32[]{:S(2)}) collective-permute-start(f32[2,4,32,512]{3,2,1,0:T(8,128)S(1)} %constant_dynamic-slice_fusion), channel_id=1, source_target_pairs={{0,28},{4,8},{8,4},{12,16},{16,12},{20,24},{24,20},{28,0},{1,29},{... | collective-permute-start | bytes 1572872 | tf_op jit(solution)/shard_map/ppermute | solution.py:237
  6.8 23.5 %collective-permute-start = (f32[2,4,32,512]{3,2,1,0:T(8,128)S(1)}, f32[2,4,32,512]{3,2,1,0:T(8,128)S(1)}, u32[]{:S(2)}, u32[]{:S(2)}) collective-permute-start(f32[2,4,32,512]{3,2,1,0:T(8,128)S(1)} %constant_dynamic-slice_fusion.2), channel_id=1, source_target_pairs={{0,28},{4,8},{8,4},{12,16},{16,12},{20,24},{24,20},{28,0},{1,29},{... | collective-permute-start | bytes 1572872 | tf_op jit(solution)/shard_map/ppermute | solution.py:237
  19.1 14.2 %copy-start.2 = (f32[3]{0:T(128)S(1)}, f32[3]{0:T(128)}, u32[]{:S(2)}) copy-start(f32[3]{0:T(128)} %c.11) | copy-start | bytes 40
  19.2 25.3 %collective-permute-start.11 = (f32[2,4,32,512]{3,2,1,0:T(8,128)S(1)}, f32[2,4,32,512]{3,2,1,0:T(8,128)S(1)}, u32[]{:S(2)}, u32[]{:S(2)}) collective-permute-start(f32[2,4,32,512]{3,2,1,0:T(8,128)S(1)} %shard_map.42.rest_1_), channel_id=1, source_target_pairs={{0,28},{4,8},{8,4},{12,16},{16,12},{20,24},{24,20},{28,0},{1,29},{... | collective-permute-start | bytes 1572872 | tf_op jit(solution)/shard_map/ppermute | solution.py:268
  30.4 21.7 %collective-permute-start.8 = (f32[2,4,32,512]{3,2,1,0:T(8,128)S(1)}, f32[2,4,32,512]{3,2,1,0:T(8,128)S(1)}, u32[]{:S(2)}, u32[]{:S(2)}) collective-permute-start(f32[2,4,32,512]{3,2,1,0:T(8,128)S(1)} %shard_map.41.rest_0_), channel_id=1, source_target_pairs={{0,28},{4,8},{8,4},{12,16},{16,12},{20,24},{24,20},{28,0},{1,29},{... | collective-permute-start | bytes 1572872 | tf_op jit(solution)/shard_map/ppermute | solution.py:268
  45.2 13.7 %collective-permute-start.12 = (f32[2,2,32,512]{3,2,1,0:T(8,128)S(1)}, f32[2,2,32,512]{3,2,1,0:T(8,128)S(1)}, u32[]{:S(2)}, u32[]{:S(2)}) collective-permute-start(f32[2,2,32,512]{3,2,1,0:T(8,128)S(1)} %get-tuple-element.24), channel_id=1, source_target_pairs={{0,1},{1,0},{2,3},{3,2},{4,5},{5,4},{6,7},{7,6},{8,9},{9,8},{10,11... | collective-permute-start | bytes 786440 | tf_op jit(solution)/shard_map/ppermute | solution.py:260
  52.8 9.8 %collective-permute-start.9 = (f32[2,2,32,512]{3,2,1,0:T(8,128)S(1)}, f32[2,2,32,512]{3,2,1,0:T(8,128)S(1)}, u32[]{:S(2)}, u32[]{:S(2)}) collective-permute-start(f32[2,2,32,512]{3,2,1,0:T(8,128)S(1)} %get-tuple-element.22), channel_id=1, source_target_pairs={{0,1},{1,0},{2,3},{3,2},{4,5},{5,4},{6,7},{7,6},{8,9},{9,8},{10,11... | collective-permute-start | bytes 786440 | tf_op jit(solution)/shard_map/ppermute | solution.py:260
  56.1 12.1 %collective-permute-start.6 = (f32[2,2,32,512]{3,2,1,0:T(8,128)S(1)}, f32[2,2,32,512]{3,2,1,0:T(8,128)S(1)}, u32[]{:S(2)}, u32[]{:S(2)}) collective-permute-start(f32[2,2,32,512]{3,2,1,0:T(8,128)S(1)} %get-tuple-element.19), channel_id=1, source_target_pairs={{0,1},{1,0},{2,3},{3,2},{4,5},{5,4},{6,7},{7,6},{8,9},{9,8},{10,11... | collective-permute-start | bytes 786440 | tf_op jit(solution)/shard_map/ppermute | solution.py:260
  56.9 16.5 %collective-permute-start.3 = (f32[2,2,32,512]{3,2,1,0:T(8,128)S(1)}, f32[2,2,32,512]{3,2,1,0:T(8,128)S(1)}, u32[]{:S(2)}, u32[]{:S(2)}) collective-permute-start(f32[2,2,32,512]{3,2,1,0:T(8,128)S(1)} %get-tuple-element.17), channel_id=1, source_target_pairs={{0,1},{1,0},{2,3},{3,2},{4,5},{5,4},{6,7},{7,6},{8,9},{9,8},{10,11... | collective-permute-start | bytes 786440 | tf_op jit(solution)/shard_map/ppermute | solution.py:260
  59.0 27.1 %collective-permute-start.13 = (f32[2,32,512]{2,1,0:T(8,128)S(1)}, f32[2,32,512]{2,1,0:T(8,128)S(1)}, u32[]{:S(2)}, u32[]{:S(2)}) collective-permute-start(f32[2,32,512]{2,1,0:T(8,128)S(1)} %fusion), channel_id=1, source_target_pairs={{0,3},{1,2},{2,1},{3,0},{4,7},{5,6},{6,5},{7,4},{8,11},{9,10},{10,... | collective-permute-start | bytes 393224 | tf_op jit(solution)/shard_map/ppermute | solution.py:261
  62.6 23.4 %collective-permute-start.10 = (f32[2,32,512]{2,1,0:T(8,128)S(1)}, f32[2,32,512]{2,1,0:T(8,128)S(1)}, u32[]{:S(2)}, u32[]{:S(2)}) collective-permute-start(f32[2,32,512]{2,1,0:T(8,128)S(1)} %fusion.1), channel_id=1, source_target_pairs={{0,3},{1,2},{2,1},{3,0},{4,7},{5,6},{6,5},{7,4},{8,11},{9,10},{10,... | collective-permute-start | bytes 393224 | tf_op jit(solution)/shard_map/ppermute | solution.py:261
  68.2 17.8 %collective-permute-start.7 = (f32[2,32,512]{2,1,0:T(8,128)S(1)}, f32[2,32,512]{2,1,0:T(8,128)S(1)}, u32[]{:S(2)}, u32[]{:S(2)}) collective-permute-start(f32[2,32,512]{2,1,0:T(8,128)S(1)} %fusion.2), channel_id=1, source_target_pairs={{0,3},{1,2},{2,1},{3,0},{4,7},{5,6},{6,5},{7,4},{8,11},{9,10},{10,... | collective-permute-start | bytes 393224 | tf_op jit(solution)/shard_map/ppermute | solution.py:261
  73.4 15.6 %collective-permute-start.4 = (f32[2,32,512]{2,1,0:T(8,128)S(1)}, f32[2,32,512]{2,1,0:T(8,128)S(1)}, u32[]{:S(2)}, u32[]{:S(2)}) collective-permute-start(f32[2,32,512]{2,1,0:T(8,128)S(1)} %fusion.3), channel_id=1, source_target_pairs={{0,3},{1,2},{2,1},{3,0},{4,7},{5,6},{6,5},{7,4},{8,11},{9,10},{10,... | collective-permute-start | bytes 393224 | tf_op jit(solution)/shard_map/ppermute | solution.py:261

commit v2 on v1

--- a/solution.py
+++ b/solution.py
@@ -59,6 +59,14 @@
     lax.fori_loop(0, rows // BLOCK, step, 0)
 
 
+def pack_kernel(chunk, psi, out):
+    odd = parity()
+    lo, hi = chunk
+    for q in range(out.shape[0]):
+        for band in range(out.shape[1]):
+            out[q, band] = psi[2 * odd + q, band, lo:hi, :]
+
+
 def start_kernel(psi, pot, g):
     odd = parity()
 
@@ -92,8 +100,8 @@
         e5 = with_halo(psi_in, at[1], r, BLOCK)
         p2, p3 = psi[at[2], here, :], psi[at[3], here, :]
         p6, p7 = psi_in[at[2], here, :], psi_in[at[3], here, :]
-        t4 = apply_s(e4, pot_in[odd, here, :], p3 + e5[8:-8], p2 + p6)[1]
-        t5 = apply_s(e5, pot_in[1 - odd, here, :], e4[8:-8] + p6, p3 + p7)[1]
+        t4 = apply_s(e4, pot_in[at[0], here, :], p3 + e5[8:-8], p2 + p6)[1]
+        t5 = apply_s(e5, pot_in[at[1], here, :], e4[8:-8] + p6, p3 + p7)[1]
         g0, g1 = g[0, here, :], g[1, here, :]
         e2, e3 = with_halo(t, 0, r, BLOCK), with_halo(t, 1, r, BLOCK)
         t2, s2 = apply_s(e2, pot[at[2], here, :], g1 + e3[8:-8], g0 + t4)
@@ -105,18 +113,19 @@
     blocks(psi.shape[1], second)
 
 
-def halo_terms(halo, band, odd):
-    near, far = halo[1 - odd, band], halo[odd, band]
+def halo_terms(halo, band, odd, rows=slice(None)):
+    near, far = halo[1 - odd, band, rows, :], halo[odd, band, rows, :]
     return NEAR * near + FAR * far, FAR * near
 
 
-def face_kernel(chunk, halo, g, f):
-    odd = parity()
-    lo, hi = chunk
-    for band in range(halo.shape[1]):
-        d0, d1 = halo_terms(halo, band, odd)
-        f[0, band] = g[0, band, lo:hi, :] + d0
-        f[1, band] = g[1, band, lo:hi, :] + d1
+def face_kernel(chunk, parts, halo, g, *fs):
+    odd = parity()
+    for (lo, hi), f in zip(parts, fs):
+        in_halo = slice(lo - chunk[0], hi - chunk[0])
+        for band in range(halo.shape[1]):
+            d0, d1 = halo_terms(halo, band, odd, in_halo)
+            f[0, band] = g[0, band, lo:hi, :] + d0
+            f[1, band] = g[1, band, lo:hi, :] + d1
 
 
 def square(x, bands):
@@ -187,33 +196,55 @@
     part(me ^ 3, keep, 1)
 
 
+def add_kernel(keep, came, out):
+    out[...] = keep[1] + came[1]
+
+
+def sum_kernel(keep, came, far, out):
+    out[...] = keep[0] + came[0] + far[...]
+
+
 def join_kernel(places, *refs):
     out = refs[-1]
     odd = parity()
-    for i, (q, (lo, hi)) in enumerate(places):
-        keep, came, far = refs[3 * i : 3 * i + 3]
+    for (q, (lo, hi)), ref in zip(places[:-1], refs):
         for j in range(2):
-            out[own(q + j, odd), lo:hi, :] = keep[0, j] + came[0, j] + far[j]
-
-
-def call(kernel, out, args, scalars=0, scratch=(), flops=0):
-    vmem = pl.BlockSpec(memory_space=pltpu.VMEM)
-    smem = pl.BlockSpec(memory_space=pltpu.SMEM)
-    many = isinstance(out, list)
-    shapes = [jax.ShapeDtypeStruct(s, jnp.float32) for s in (out if many else [out])]
-    total = sum(4 * int(x.size) for x in list(args) + shapes)
-    result = pl.pallas_call(
-        kernel,
-        out_shape=shapes,
-        in_specs=[smem] * scalars + [vmem] * (len(args) - scalars),
-        out_specs=[vmem] * len(shapes),
-        scratch_shapes=list(scratch),
-        compiler_params=pltpu.CompilerParams(vmem_limit_bytes=40 * 2**20),
-        cost_estimate=pl.CostEstimate(
-            flops=flops, bytes_accessed=total, transcendentals=0
-        ),
-    )(*args)
-    return result if many else result[0]
+            out[own(q + j, odd), lo:hi, :] = ref[j]
+    (q, (lo, hi)), (keep, came, far) = places[-1], refs[-4:-1]
+    for j in range(2):
+        out[own(q + j, odd), lo:hi, :] = keep[0, j] + came[0, j] + far[j]
+
+
+class Line:
+    def __init__(self):
+        self.last = []
+
+    def __call__(self, kernel, out, args, scalars=0, scratch=(), flops=0):
+        vmem = pl.BlockSpec(memory_space=pltpu.VMEM)
+        smem = pl.BlockSpec(memory_space=pltpu.SMEM)
+        many = isinstance(out, list)
+        shapes = [jax.ShapeDtypeStruct(s, jnp.float32) for s in (out if many else [out])]
+        total = sum(4 * int(x.size) for x in list(args) + shapes)
+        first, last = len(args), self.last
+
+        def body(*refs):
+            kernel(*refs[:first], *refs[first + len(last) :])
+
+        result = pl.pallas_call(
+            body,
+            out_shape=shapes,
+            in_specs=[smem] * scalars
+            + [vmem] * (first - scalars)
+            + [pl.BlockSpec(memory_space=pl.ANY)] * len(last),
+            out_specs=[vmem] * len(shapes),
+            scratch_shapes=list(scratch),
+            compiler_params=pltpu.CompilerParams(vmem_limit_bytes=40 * 2**20),
+            cost_estimate=pl.CostEstimate(
+                flops=flops, bytes_accessed=total, transcendentals=0
+            ),
+        )(*args, *last)
+        self.last = [result[0]]
+        return result if many else result[0]
 
 
 def shards(orbitals, potential, coeffs):
@@ -221,29 +252,55 @@
     slabs, bands = lax.axis_size("slab"), lax.axis_size("orb")
     planes, rows, lanes = psi.shape
     wide = rows // bands
-    odd = parity()
-    me = lax.axis_index("orb")
-    chunks = [(0, wide // 2), (wide // 2, wide)]
-    face = [(s, s - 1 if s % 2 == 0 else s + 1) for s in range(slabs)]
-    face = [(s, d % slabs) for s, d in face]
+    half, part = wide // 2, wide // 4
+    chunks = [(0, half), (half, wide)]
+    cuts = [(0, half), (half, wide - part), (wide - part, wide)]
+    face = [(s, (s - 1 if s % 2 == 0 else s + 1) % slabs) for s in range(slabs)]
     partner = [(s, s ^ 1) for s in range(slabs)]
-
-    banded = psi.reshape(planes, bands, wide, lanes)
+    near = [(i, i ^ 1) for i in range(bands)]
+    far = [(i, i ^ 3) for i in range(bands)]
+    plane2 = (2, rows, lanes)
+    cells = 2 * rows * lanes
+    call = Line()
+
+    def as_bands(x):
+        return x.reshape(x.shape[0], bands, wide, lanes)
+
+    def slab_shape(chunk):
+        return (2, bands, chunk[1] - chunk[0], lanes)
+
+    def pair_shape(chunk):
+        return (2, 2, chunk[1] - chunk[0], lanes)
+
+    def add_far(keep, came):
+        total = call(add_kernel, keep.shape[1:], (keep, came))
+        return keep, came, lax.ppermute(total, "orb", far)
+
+    def face_of(chunk, halo, inside):
+        f = call(
+            functools.partial(face_kernel, chunk, inside),
+            [slab_shape(cut) for cut in inside],
+            (halo, as_bands(g)),
+        )
+        return f, [lax.ppermute(x, "slab", face) for x in f]
+
+    def squares(kernel, chunk, halo, h):
+        keep, send = call(
+            functools.partial(kernel, chunk),
+            [pair_shape(chunk)] * 2,
+            (coeffs, halo, as_bands(h)),
+            scalars=1,
+        )
+        return keep, lax.ppermute(send, "orb", near)
+
+    psi_in = lax.ppermute(psi, "slab", partner)
+    pot_in = lax.ppermute(potential, "slab", partner)
     halos = []
-    for lo, hi in chunks:
-        piece = lax.dynamic_slice(
-            banded[:, :, lo:hi], (2 * odd, 0, 0, 0), (2, bands, hi - lo, lanes)
+    for chunk in chunks:
+        piece = call(
+            functools.partial(pack_kernel, chunk), slab_shape(chunk), (as_bands(psi),)
         )
         halos.append(lax.ppermute(piece, "slab", face))
-    psi_in = lax.ppermute(psi, "slab", partner)
-    pot_in = lax.ppermute(
-        lax.dynamic_slice(potential, (2 - 2 * odd, 0, 0), (2, rows, lanes)),
-        "slab",
-        partner,
-    )
-
-    plane2 = (2, rows, lanes)
-    cells = 2 * rows * lanes
     g = call(start_kernel, plane2, (psi, potential), flops=24 * cells)
     t, h_back = call(
         inner_kernel,
@@ -252,50 +309,40 @@
         scalars=1,
         flops=80 * cells,
     )
-    as_bands = lambda x: x.reshape(x.shape[0], bands, wide, lanes)
-
-    def reduced(keep, send):
-        near = [(i, i ^ 1) for i in range(bands)]
-        far = [(i, i ^ 3) for i in range(bands)]
-        came = lax.ppermute(send, "orb", near)
-        return keep, came, lax.ppermute(keep[1] + came[1], "orb", far)
-
-    places, pieces, fs, faces = [], [], [], []
-    for chunk, halo in zip(chunks, halos):
-        shape = halo.shape
-        f = call(functools.partial(face_kernel, chunk), shape, (halo, as_bands(g)))
-        fs.append(f)
-        faces.append(lax.ppermute(f, "slab", face))
-        pair = (2, 2) + shape[2:]
-        keep, send = call(
-            functools.partial(back_kernel, chunk),
-            [pair, pair],
-            (coeffs, halo, as_bands(h_back)),
-            scalars=1,
-        )
-        places.append((2, chunk))
-        pieces += reduced(keep, send)
-
+
+    def summed(keep, came, from_far):
+        return call(sum_kernel, from_far.shape, (keep, came, from_far))
+
+    cut_a, cut_b, cut_c = cuts
+    f0, (face_a,) = face_of(chunks[0], halos[0], [cut_a])
+    back0 = squares(back_kernel, chunks[0], halos[0], h_back)
+    back0 = add_far(*back0)
+    f1, (face_b, face_c) = face_of(chunks[1], halos[1], [cut_b, cut_c])
+    back1 = squares(back_kernel, chunks[1], halos[1], h_back)
     h_front = call(
-        functools.partial(front_kernel, chunks),
+        functools.partial(front_kernel, cuts),
         plane2,
-        (coeffs, psi, potential, t, *fs),
+        (coeffs, psi, potential, t, *f0, *f1),
         scalars=1,
         scratch=[pltpu.VMEM(plane2, jnp.float32)],
         flops=40 * cells,
     )
-    for chunk, halo in zip(chunks, faces):
-        pair = (2, 2) + halo.shape[2:]
-        keep, send = call(
-            functools.partial(last_kernel, chunk),
-            [pair, pair],
-            (coeffs, halo, as_bands(h_front)),
-            scalars=1,
-        )
-        places.append((0, chunk))
-        pieces += reduced(keep, send)
+    back0 = summed(*back0)
+    back1 = add_far(*back1)
+    front_a = squares(last_kernel, cut_a, face_a, h_front)
+    front_b = squares(last_kernel, cut_b, face_b, h_front)
+    back1 = summed(*back1)
+    front_a = add_far(*front_a)
+    front_c = squares(last_kernel, cut_c, face_c, h_front)
+    front_b = add_far(*front_b)
+    front_a = summed(*front_a)
+    front_c = add_far(*front_c)
+    front_b = summed(*front_b)
+    places = [(2, chunk) for chunk in chunks] + [(0, cut) for cut in cuts]
     return call(
-        functools.partial(join_kernel, places), (planes, wide, lanes), pieces
+        functools.partial(join_kernel, places),
+        (planes, wide, lanes),
+        (back0, back1, front_a, front_b, *front_c),
     )
 
 

time: 90 us -> 71.9 us (0.80)
  starting transfers between devices: 39.7 us -> 25.7 us
  waiting for transfers between devices: 29.8 us -> 26.4 us
  local copies, waits for them, and re-layouts: 2.74 us -> 1.61 us
    ppermute x11 -> x14, starting transfers between devices: 35.6 us -> 21.6 us  [the longest x5 9.09 us: add_far(): return (keep, came, lax.ppermute(total, 'orb', far))]
    ppermute x2, waiting for transfers between devices: 18 us -> 5.59 us  [shards(): halos.append(lax.ppermute(piece, 'slab', face))]
    ppermute x11 -> x14, waiting for transfers between devices: 11.8 us -> 20.8 us  [the longest x5 15.7 us: add_far(): return (keep, came, lax.ppermute(total, 'orb', far))]
    dynamic_slice x3 -> x0, local copies, waits for them, and re-layouts: 2.53 us -> none  [the longest x1 2.45 us: shards(): lax.dynamic_slice(potential, (2 - 2 * odd, 0, 0), (2, rows, lanes))]
    unnamed x6 -> x8, local copies, waits for them, and re-layouts: 0.01 us -> 1.61 us
    pallas_call x10 -> x22, Pallas kernels: 17.4 us -> 17.1 us  [__call__(): pl.pallas_call(body, out_shape=shapes, in_specs=[smem] * scalars + [vmem]...]
  transfers between devices with their start and end apart: 14 -> 17, of which waited for: 7 -> 8; matrix products, arithmetic and copies ran while one was open for 3% -> 0% of each run, Pallas kernels for 18% -> 23%
where the time goes in v2:
time: 71.9 us; the launch traced here: 71 us
  waiting for transfers between devices  26.4 us (37%)
  starting transfers between devices  25.7 us (36%)
  Pallas kernels  17.1 us (24%)
  local copies, waits for them, and re-layouts  1.61 us (2%)
    pallas_call x22, Pallas kernels, __call__(): pl.pallas_call(body, out_shape=shapes, in_specs=[smem] * scalars + [vmem]...  17.1 us
    ppermute x5, waiting for transfers between devices, add_far(): return (keep, came, lax.ppermute(total, 'orb', far))  15.7 us
    ppermute x5, starting transfers between devices, add_far(): return (keep, came, lax.ppermute(total, 'orb', far))  9.09 us
    ppermute x3, starting transfers between devices, face_of(): return (f, [lax.ppermute(x, 'slab', face) for x in f])  7.23 us
    ppermute x2, waiting for transfers between devices, shards(): halos.append(lax.ppermute(piece, 'slab', face))  5.59 us
    ppermute x5, starting transfers between devices, squares(): return (keep, lax.ppermute(send, 'orb', near))  5.25 us
    ppermute x5, waiting for transfers between devices, squares(): return (keep, lax.ppermute(send, 'orb', near))  5.13 us
    ppermute x2, starting transfers between devices, shards(): halos.append(lax.ppermute(piece, 'slab', face))  3.66 us
  transfers between devices with their start and end apart: 17, of which 8 were waited for; matrix products, arithmetic and copies ran while one was open for 0% of the time, Pallas kernels for 23%

profile of v2, /device:TPU:0, one launch (start us, length us, event | category | flops | bytes accessed | tf_op | source)
XLA Modules:
  0.0 71.0 jit_solution(16886044940289502684)
XLA Ops:
  0.0 0.5 collective-permute-start.1
  0.5 0.1 collective-permute-start.2
  0.5 1.6 %copy-done = f32[1,4,256,512]{3,2,1,0:T(8,128)S(1)} copy-done((f32[1,4,256,512]{3,2,1,0:T(8,128)S(1)}, f32[1,4,256,512]{3,2,1,0:T(8,128)}, u32[]{:S(2)}) %copy-start) | copy-done | bytes 2097176
  2.1 0.0 copy-start.2
  2.2 3.6 %collective-permute-start = (f32[2,4,32,512]{3,2,1,0:T(8,128)S(1)}, f32[2,4,32,512]{3,2,1,0:T(8,128)S(1)}, u32[]{:S(2)}, u32[]{:S(2)}) collective-permute-start(f32[2,4,32,512]{3,2,1,0:T(8,128)S(1)} %shard_map.37.refs_1_), channel_id=1, source_target_pairs={{0,28},{4,8},{8,4},{12,16},{16,12},{20,24},{24,20},{28,0},{1,29},{... | collective-permute-start | bytes 1572872 | tf_op jit(solution)/shard_map/ppermute | solution.py:303
  5.8 0.0 copy-start.3
  5.8 0.1 collective-permute-start.5
  5.9 2.5 %shard_map.39.refs_5_.refs_6_ = f32[2,256,512]{2,1,0:T(8,128)S(1)} custom-call(f32[4,256,512]{2,1,0:T(8,128)S(1)} %bitcast.8, f32[4,256,512]{2,1,0:T(8,128)S(1)} %copy-done.2, f32[2,4,32,512]{3,2,1,0:T(8,128)S(1)} %shard_map.38.refs_2_), custom_call_target="tpu_custom_call" | custom-call | flops 6291456 | bytes 5242880 | tf_op jit(solution)/shard_map/pallas_call | solution.py:233
  8.4 0.0 collective-permute-done.1.refs_3_
  8.4 0.0 collective-permute-done.2.refs_4_
  8.4 7.0 %shard_map.40 = (f32[2,256,512]{2,1,0:T(8,128)S(1)}, f32[2,256,512]{2,1,0:T(8,128)S(1)}) custom-call(f32[3]{0:T(128)S(1)} %copy-done.3, f32[4,256,512]{2,1,0:T(8,128)S(1)} %bitcast.9, f32[4,256,512]{2,1,0:T(8,128)S(1)} %copy-done.2, f32[4,256,512]{2,1,0:T(8,128)S(1)} %collective-permute-done.1.refs_3_, f32[4,256,512]{2,1,0:T(8,128)S(1)} %collective-permute-done.2.refs_4_, ...), custom_call_target="tpu_custom_call" | custom-call | flops 20971520 | bytes 11534348 | tf_op jit(solution)/shard_map/pallas_call | solution.py:233
  15.4 2.6 %collective-permute-done.refs_0_.refs_1_ = f32[2,4,32,512]{3,2,1,0:T(8,128)S(1)} collective-permute-done((f32[2,4,32,512]{3,2,1,0:T(8,128)S(1)}, f32[2,4,32,512]{3,2,1,0:T(8,128)S(1)}, u32[]{:S(2)}, u32[]{:S(2)}) %collective-permute-start) | collective-permute-done | bytes 524320 | tf_op jit(solution)/shard_map/ppermute | solution.py:303
  18.1 0.1 shard_map.41.refs_3_.refs_4_
  18.1 0.7 shard_map.42
  18.8 2.1 %collective-permute-start.3 = (f32[2,2,32,512]{3,2,1,0:T(8,128)S(1)}, f32[2,2,32,512]{3,2,1,0:T(8,128)S(1)}, u32[]{:S(2)}, u32[]{:S(2)}) collective-permute-start(f32[2,2,32,512]{3,2,1,0:T(8,128)S(1)} %get-tuple-element.22), channel_id=1, source_target_pairs={{0,1},{1,0},{2,3},{3,2},{4,5},{5,4},{6,7},{7,6},{8,9},{9,8},{10,11... | collective-permute-start | bytes 786440 | tf_op jit(solution)/shard_map/ppermute | solution.py:294
  21.0 2.0 %collective-permute-start.9 = (f32[2,4,32,512]{3,2,1,0:T(8,128)S(1)}, f32[2,4,32,512]{3,2,1,0:T(8,128)S(1)}, u32[]{:S(2)}, u32[]{:S(2)}) collective-permute-start(f32[2,4,32,512]{3,2,1,0:T(8,128)S(1)} %shard_map.41.refs_3_.refs_4_), channel_id=1, source_target_pairs={{0,28},{4,8},{8,4},{12,16},{16,12},{20,24},{24,20},{28,0},{1,29},{... | collective-permute-start | bytes 1572872 | tf_op jit(solution)/shard_map/ppermute | solution.py:285
  23.0 3.3 %collective-permute-done.3.refs_1_ = f32[2,2,32,512]{3,2,1,0:T(8,128)S(1)} collective-permute-done((f32[2,2,32,512]{3,2,1,0:T(8,128)S(1)}, f32[2,2,32,512]{3,2,1,0:T(8,128)S(1)}, u32[]{:S(2)}, u32[]{:S(2)}) %collective-permute-start.3) | collective-permute-done | bytes 262176 | tf_op jit(solution)/shard_map/ppermute | solution.py:294
  26.3 2.9 %collective-permute-done.5.refs_0_.refs_1_ = f32[2,4,32,512]{3,2,1,0:T(8,128)S(1)} collective-permute-done((f32[2,4,32,512]{3,2,1,0:T(8,128)S(1)}, f32[2,4,32,512]{3,2,1,0:T(8,128)S(1)}, u32[]{:S(2)}, u32[]{:S(2)}) %collective-permute-start.5) | collective-permute-done | bytes 524320 | tf_op jit(solution)/shard_map/ppermute | solution.py:303
  29.3 0.1 shard_map.44
  29.4 0.7 shard_map.45
  30.1 2.1 %collective-permute-start.6 = (f32[2,2,32,512]{3,2,1,0:T(8,128)S(1)}, f32[2,2,32,512]{3,2,1,0:T(8,128)S(1)}, u32[]{:S(2)}, u32[]{:S(2)}) collective-permute-start(f32[2,2,32,512]{3,2,1,0:T(8,128)S(1)} %get-tuple-element.26), channel_id=1, source_target_pairs={{0,1},{1,0},{2,3},{3,2},{4,5},{5,4},{6,7},{7,6},{8,9},{9,8},{10,11... | collective-permute-start | bytes 786440 | tf_op jit(solution)/shard_map/ppermute | solution.py:294
  32.2 2.5 %collective-permute-start.4 = (f32[2,32,512]{2,1,0:T(8,128)S(1)}, f32[2,32,512]{2,1,0:T(8,128)S(1)}, u32[]{:S(2)}, u32[]{:S(2)}) collective-permute-start(f32[2,32,512]{2,1,0:T(8,128)S(1)} %shard_map.43.refs_2_), channel_id=1, source_target_pairs={{0,3},{1,2},{2,1},{3,0},{4,7},{5,6},{6,5},{7,4},{8,11},{9,10},{10,... | collective-permute-start | bytes 393224 | tf_op jit(solution)/shard_map/ppermute | solution.py:277
  34.7 1.8 %collective-permute-start.8 = (f32[2,4,16,512]{3,2,1,0:T(8,128)S(1)}, f32[2,4,16,512]{3,2,1,0:T(8,128)S(1)}, u32[]{:S(2)}, u32[]{:S(2)}) collective-permute-start(f32[2,4,16,512]{3,2,1,0:T(8,128)S(1)} %get-tuple-element.23.refs_3_.refs_5_), channel_id=1, source_target_pairs={{0,28},{4,8},{8,4},{12,16},{16,12},{20,24},{24,20},{28,0},{1,29},{... | collective-permute-start | bytes 786440 | tf_op jit(solution)/shard_map/ppermute | solution.py:285
  36.4 3.2 %shard_map.46.refs_3_ = f32[2,256,512]{2,1,0:T(8,128)S(1)} custom-call(f32[3]{0:T(128)S(1)} %copy-done.3, f32[4,256,512]{2,1,0:T(8,128)S(1)} %bitcast.10, f32[4,256,512]{2,1,0:T(8,128)S(1)} %copy-done.2, f32[2,256,512]{2,1,0:T(8,128)S(1)} %get-tuple-element.20.refs_2_.refs_3_, f32[2,4,32,512]{3,2,1,0:T(8,128)S(1)} %shard_map.41.refs_3_.refs_4_, ...), custom_call_target="tpu_custom_call" | custom-call | flops 10485760 | bytes 7340044 | tf_op jit(solution)/shard_map/pallas_call | solution.py:233
  39.6 3.0 %collective-permute-done.4.refs_2_ = f32[2,32,512]{2,1,0:T(8,128)S(1)} collective-permute-done((f32[2,32,512]{2,1,0:T(8,128)S(1)}, f32[2,32,512]{2,1,0:T(8,128)S(1)}, u32[]{:S(2)}, u32[]{:S(2)}) %collective-permute-start.4) | collective-permute-done | bytes 131104 | tf_op jit(solution)/shard_map/ppermute | solution.py:277
  42.6 0.0 collective-permute-done.6.refs_1_
  42.6 0.0 collective-permute-done.9.refs_1_
  42.6 0.6 shard_map.49
  43.3 0.1 collective-permute-start.10
  43.4 3.4 %collective-permute-start.13 = (f32[2,4,16,512]{3,2,1,0:T(8,128)S(1)}, f32[2,4,16,512]{3,2,1,0:T(8,128)S(1)}, u32[]{:S(2)}, u32[]{:S(2)}) collective-permute-start(f32[2,4,16,512]{3,2,1,0:T(8,128)S(1)} %get-tuple-element.24.refs_6_), channel_id=1, source_target_pairs={{0,28},{4,8},{8,4},{12,16},{16,12},{20,24},{24,20},{28,0},{1,29},{... | collective-permute-start | bytes 786440 | tf_op jit(solution)/shard_map/ppermute | solution.py:285
  46.8 1.6 %collective-permute-start.7 = (f32[2,32,512]{2,1,0:T(8,128)S(1)}, f32[2,32,512]{2,1,0:T(8,128)S(1)}, u32[]{:S(2)}, u32[]{:S(2)}) collective-permute-start(f32[2,32,512]{2,1,0:T(8,128)S(1)} %shard_map.48.refs_3_), channel_id=1, source_target_pairs={{0,3},{1,2},{2,1},{3,0},{4,7},{5,6},{6,5},{7,4},{8,11},{9,10},{10,... | collective-permute-start | bytes 393224 | tf_op jit(solution)/shard_map/ppermute | solution.py:277
  48.4 0.0 collective-permute-done.8.refs_1_
  48.4 0.6 shard_map.50
  49.0 0.8 %collective-permute-start.12 = (f32[2,2,16,512]{3,2,1,0:T(8,128)S(1)}, f32[2,2,16,512]{3,2,1,0:T(8,128)S(1)}, u32[]{:S(2)}, u32[]{:S(2)}) collective-permute-start(f32[2,2,16,512]{3,2,1,0:T(8,128)S(1)} %get-tuple-element.30), channel_id=1, source_target_pairs={{0,1},{1,0},{2,3},{3,2},{4,5},{5,4},{6,7},{7,6},{8,9},{9,8},{10,11... | collective-permute-start | bytes 393224 | tf_op jit(solution)/shard_map/ppermute | solution.py:294
  49.9 5.4 %collective-permute-done.7.refs_2_ = f32[2,32,512]{2,1,0:T(8,128)S(1)} collective-permute-done((f32[2,32,512]{2,1,0:T(8,128)S(1)}, f32[2,32,512]{2,1,0:T(8,128)S(1)}, u32[]{:S(2)}, u32[]{:S(2)}) %collective-permute-start.7) | collective-permute-done | bytes 131104 | tf_op jit(solution)/shard_map/ppermute | solution.py:277
  55.3 0.0 collective-permute-done.10.refs_1_
  55.3 1.4 %collective-permute-start.11 = (f32[2,32,512]{2,1,0:T(8,128)S(1)}, f32[2,32,512]{2,1,0:T(8,128)S(1)}, u32[]{:S(2)}, u32[]{:S(2)}) collective-permute-start(f32[2,32,512]{2,1,0:T(8,128)S(1)} %shard_map.52.refs_3_), channel_id=1, source_target_pairs={{0,3},{1,2},{2,1},{3,0},{4,7},{5,6},{6,5},{7,4},{8,11},{9,10},{10,... | collective-permute-start | bytes 393224 | tf_op jit(solution)/shard_map/ppermute | solution.py:277
  56.7 0.0 collective-permute-done.13.refs_1_
  56.7 0.6 shard_map.53
  57.3 0.1 collective-permute-start.15
  57.4 0.0 collective-permute-done.12.refs_1_
  57.4 2.5 %collective-permute-start.14 = (f32[2,16,512]{2,1,0:T(8,128)S(1)}, f32[2,16,512]{2,1,0:T(8,128)S(1)}, u32[]{:S(2)}, u32[]{:S(2)}) collective-permute-start(f32[2,16,512]{2,1,0:T(8,128)S(1)} %shard_map.54.refs_3_), channel_id=1, source_target_pairs={{0,3},{1,2},{2,1},{3,0},{4,7},{5,6},{6,5},{7,4},{8,11},{9,10},{10,... | collective-permute-start | bytes 196616 | tf_op jit(solution)/shard_map/ppermute | solution.py:277
  60.0 2.3 %collective-permute-done.11.refs_2_ = f32[2,32,512]{2,1,0:T(8,128)S(1)} collective-permute-done((f32[2,32,512]{2,1,0:T(8,128)S(1)}, f32[2,32,512]{2,1,0:T(8,128)S(1)}, u32[]{:S(2)}, u32[]{:S(2)}) %collective-permute-start.11) | collective-permute-done | bytes 131104 | tf_op jit(solution)/shard_map/ppermute | solution.py:277
  62.3 1.8 %collective-permute-done.15.refs_1_.refs_5_ = f32[2,2,16,512]{3,2,1,0:T(8,128)S(1)} collective-permute-done((f32[2,2,16,512]{3,2,1,0:T(8,128)S(1)}, f32[2,2,16,512]{3,2,1,0:T(8,128)S(1)}, u32[]{:S(2)}, u32[]{:S(2)}) %collective-permute-start.15) | collective-permute-done | bytes 131104 | tf_op jit(solution)/shard_map/ppermute | solution.py:294
  64.1 1.0 %collective-permute-start.16 = (f32[2,16,512]{2,1,0:T(8,128)S(1)}, f32[2,16,512]{2,1,0:T(8,128)S(1)}, u32[]{:S(2)}, u32[]{:S(2)}) collective-permute-start(f32[2,16,512]{2,1,0:T(8,128)S(1)} %shard_map.56.refs_3_), channel_id=1, source_target_pairs={{0,3},{1,2},{2,1},{3,0},{4,7},{5,6},{6,5},{7,4},{8,11},{9,10},{10,... | collective-permute-start | bytes 196616 | tf_op jit(solution)/shard_map/ppermute | solution.py:277
  65.1 0.0 collective-permute-done.14.refs_2_
  65.1 5.1 %collective-permute-done.16.refs_6_ = f32[2,16,512]{2,1,0:T(8,128)S(1)} collective-permute-done((f32[2,16,512]{2,1,0:T(8,128)S(1)}, f32[2,16,512]{2,1,0:T(8,128)S(1)}, u32[]{:S(2)}, u32[]{:S(2)}) %collective-permute-start.16) | collective-permute-done | bytes 65568 | tf_op jit(solution)/shard_map/ppermute | solution.py:277
  70.2 0.8 %shard_map.58 = f32[4,64,512]{2,1,0:T(8,128)} custom-call(f32[2,32,512]{2,1,0:T(8,128)S(1)} %shard_map.47.refs_2_.refs_0_, f32[2,32,512]{2,1,0:T(8,128)S(1)} %shard_map.51.refs_2_.refs_1_, f32[2,32,512]{2,1,0:T(8,128)S(1)} %shard_map.55.refs_2_, f32[2,16,512]{2,1,0:T(8,128)S(1)} %shard_map.57.refs_3_.refs_7_, ...), custom_call_target="tpu_custom_call" | custom-call | bytes 1310720 | tf_op jit(solution)/shard_map/pallas_call | solution.py:233
  (16 shorter events, 0.2 us)
Async XLA Ops:
  0.0 8.4 %collective-permute-start.1 = (f32[4,256,512]{2,1,0:T(8,128)}, f32[4,256,512]{2,1,0:T(8,128)S(1)}, u32[]{:S(2)}, u32[]{:S(2)}) collective-permute-start(f32[4,256,512]{2,1,0:T(8,128)} %bitcast.5), channel_id=1, source_target_pairs={{0,4},{4,0},{8,12},{12,8},{16,20},{20,16},{24,28},{28,24},{1,5},{5... | collective-permute-start | bytes 6291464 | tf_op jit(solution)/shard_map/ppermute | solution.py:296
  0.5 7.9 %collective-permute-start.2 = (f32[4,256,512]{2,1,0:T(8,128)}, f32[4,256,512]{2,1,0:T(8,128)S(1)}, u32[]{:S(2)}, u32[]{:S(2)}) collective-permute-start(f32[4,256,512]{2,1,0:T(8,128)} %refs_2_.3), channel_id=1, source_target_pairs={{0,4},{4,0},{8,12},{12,8},{16,20},{20,16},{24,28},{28,24},{1,5},{5... | collective-permute-start | bytes 6291464 | tf_op jit(solution)/shard_map/ppermute | solution.py:297
  0.5 1.6 %copy-start = (f32[1,4,256,512]{3,2,1,0:T(8,128)S(1)}, f32[1,4,256,512]{3,2,1,0:T(8,128)}, u32[]{:S(2)}) copy-start(f32[1,4,256,512]{3,2,1,0:T(8,128)} %param.3) | copy-start | bytes 6291460
  2.1 3.7 %copy-start.2 = (f32[4,256,512]{2,1,0:T(8,128)S(1)}, f32[4,256,512]{2,1,0:T(8,128)}, u32[]{:S(2)}) copy-start(f32[4,256,512]{2,1,0:T(8,128)} %refs_2_.3) | copy-start | bytes 6291460
  2.2 15.9 %collective-permute-start = (f32[2,4,32,512]{3,2,1,0:T(8,128)S(1)}, f32[2,4,32,512]{3,2,1,0:T(8,128)S(1)}, u32[]{:S(2)}, u32[]{:S(2)}) collective-permute-start(f32[2,4,32,512]{3,2,1,0:T(8,128)S(1)} %shard_map.37.refs_1_), channel_id=1, source_target_pairs={{0,28},{4,8},{8,4},{12,16},{16,12},{20,24},{24,20},{28,0},{1,29},{... | collective-permute-start | bytes 1572872 | tf_op jit(solution)/shard_map/ppermute | solution.py:303
  5.8 2.6 %copy-start.3 = (f32[3]{0:T(128)S(1)}, f32[3]{0:T(128)}, u32[]{:S(2)}) copy-start(f32[3]{0:T(128)} %refs_0_.13) | copy-start | bytes 40
  5.8 23.5 %collective-permute-start.5 = (f32[2,4,32,512]{3,2,1,0:T(8,128)S(1)}, f32[2,4,32,512]{3,2,1,0:T(8,128)S(1)}, u32[]{:S(2)}, u32[]{:S(2)}) collective-permute-start(f32[2,4,32,512]{3,2,1,0:T(8,128)S(1)} %shard_map.38.refs_2_), channel_id=1, source_target_pairs={{0,28},{4,8},{8,4},{12,16},{16,12},{20,24},{24,20},{28,0},{1,29},{... | collective-permute-start | bytes 1572872 | tf_op jit(solution)/shard_map/ppermute | solution.py:303
  18.8 7.5 %collective-permute-start.3 = (f32[2,2,32,512]{3,2,1,0:T(8,128)S(1)}, f32[2,2,32,512]{3,2,1,0:T(8,128)S(1)}, u32[]{:S(2)}, u32[]{:S(2)}) collective-permute-start(f32[2,2,32,512]{3,2,1,0:T(8,128)S(1)} %get-tuple-element.22), channel_id=1, source_target_pairs={{0,1},{1,0},{2,3},{3,2},{4,5},{5,4},{6,7},{7,6},{8,9},{9,8},{10,11... | collective-permute-start | bytes 786440 | tf_op jit(solution)/shard_map/ppermute | solution.py:294
  21.0 21.7 %collective-permute-start.9 = (f32[2,4,32,512]{3,2,1,0:T(8,128)S(1)}, f32[2,4,32,512]{3,2,1,0:T(8,128)S(1)}, u32[]{:S(2)}, u32[]{:S(2)}) collective-permute-start(f32[2,4,32,512]{3,2,1,0:T(8,128)S(1)} %shard_map.41.refs_3_.refs_4_), channel_id=1, source_target_pairs={{0,28},{4,8},{8,4},{12,16},{16,12},{20,24},{24,20},{28,0},{1,29},{... | collective-permute-start | bytes 1572872 | tf_op jit(solution)/shard_map/ppermute | solution.py:285
  26.3 10.1 %copy-start.1 = (f32[1,4,256,512]{3,2,1,0:T(8,128)S(1)}, f32[1,4,256,512]{3,2,1,0:T(8,128)}, u32[]{:S(2)}) copy-start(f32[1,4,256,512]{3,2,1,0:T(8,128)} %param.3) | copy-start | bytes 6291460
  30.1 12.5 %collective-permute-start.6 = (f32[2,2,32,512]{3,2,1,0:T(8,128)S(1)}, f32[2,2,32,512]{3,2,1,0:T(8,128)S(1)}, u32[]{:S(2)}, u32[]{:S(2)}) collective-permute-start(f32[2,2,32,512]{3,2,1,0:T(8,128)S(1)} %get-tuple-element.26), channel_id=1, source_target_pairs={{0,1},{1,0},{2,3},{3,2},{4,5},{5,4},{6,7},{7,6},{8,9},{9,8},{10,11... | collective-permute-start | bytes 786440 | tf_op jit(solution)/shard_map/ppermute | solution.py:294
  32.2 10.4 %collective-permute-start.4 = (f32[2,32,512]{2,1,0:T(8,128)S(1)}, f32[2,32,512]{2,1,0:T(8,128)S(1)}, u32[]{:S(2)}, u32[]{:S(2)}) collective-permute-start(f32[2,32,512]{2,1,0:T(8,128)S(1)} %shard_map.43.refs_2_), channel_id=1, source_target_pairs={{0,3},{1,2},{2,1},{3,0},{4,7},{5,6},{6,5},{7,4},{8,11},{9,10},{10,... | collective-permute-start | bytes 393224 | tf_op jit(solution)/shard_map/ppermute | solution.py:277
  34.7 13.8 %collective-permute-start.8 = (f32[2,4,16,512]{3,2,1,0:T(8,128)S(1)}, f32[2,4,16,512]{3,2,1,0:T(8,128)S(1)}, u32[]{:S(2)}, u32[]{:S(2)}) collective-permute-start(f32[2,4,16,512]{3,2,1,0:T(8,128)S(1)} %get-tuple-element.23.refs_3_.refs_5_), channel_id=1, source_target_pairs={{0,28},{4,8},{8,4},{12,16},{16,12},{20,24},{24,20},{28,0},{1,29},{... | collective-permute-start | bytes 786440 | tf_op jit(solution)/shard_map/ppermute | solution.py:285
  43.3 12.0 %collective-permute-start.10 = (f32[2,2,32,512]{3,2,1,0:T(8,128)S(1)}, f32[2,2,32,512]{3,2,1,0:T(8,128)S(1)}, u32[]{:S(2)}, u32[]{:S(2)}) collective-permute-start(f32[2,2,32,512]{3,2,1,0:T(8,128)S(1)} %get-tuple-element.29), channel_id=1, source_target_pairs={{0,1},{1,0},{2,3},{3,2},{4,5},{5,4},{6,7},{7,6},{8,9},{9,8},{10,11... | collective-permute-start | bytes 786440 | tf_op jit(solution)/shard_map/ppermute | solution.py:294
  43.4 13.4 %collective-permute-start.13 = (f32[2,4,16,512]{3,2,1,0:T(8,128)S(1)}, f32[2,4,16,512]{3,2,1,0:T(8,128)S(1)}, u32[]{:S(2)}, u32[]{:S(2)}) collective-permute-start(f32[2,4,16,512]{3,2,1,0:T(8,128)S(1)} %get-tuple-element.24.refs_6_), channel_id=1, source_target_pairs={{0,28},{4,8},{8,4},{12,16},{16,12},{20,24},{24,20},{28,0},{1,29},{... | collective-permute-start | bytes 786440 | tf_op jit(solution)/shard_map/ppermute | solution.py:285
  46.8 8.4 %collective-permute-start.7 = (f32[2,32,512]{2,1,0:T(8,128)S(1)}, f32[2,32,512]{2,1,0:T(8,128)S(1)}, u32[]{:S(2)}, u32[]{:S(2)}) collective-permute-start(f32[2,32,512]{2,1,0:T(8,128)S(1)} %shard_map.48.refs_3_), channel_id=1, source_target_pairs={{0,3},{1,2},{2,1},{3,0},{4,7},{5,6},{6,5},{7,4},{8,11},{9,10},{10,... | collective-permute-start | bytes 393224 | tf_op jit(solution)/shard_map/ppermute | solution.py:277
  49.0 8.4 %collective-permute-start.12 = (f32[2,2,16,512]{3,2,1,0:T(8,128)S(1)}, f32[2,2,16,512]{3,2,1,0:T(8,128)S(1)}, u32[]{:S(2)}, u32[]{:S(2)}) collective-permute-start(f32[2,2,16,512]{3,2,1,0:T(8,128)S(1)} %get-tuple-element.30), channel_id=1, source_target_pairs={{0,1},{1,0},{2,3},{3,2},{4,5},{5,4},{6,7},{7,6},{8,9},{9,8},{10,11... | collective-permute-start | bytes 393224 | tf_op jit(solution)/shard_map/ppermute | solution.py:294
  55.3 7.0 %collective-permute-start.11 = (f32[2,32,512]{2,1,0:T(8,128)S(1)}, f32[2,32,512]{2,1,0:T(8,128)S(1)}, u32[]{:S(2)}, u32[]{:S(2)}) collective-permute-start(f32[2,32,512]{2,1,0:T(8,128)S(1)} %shard_map.52.refs_3_), channel_id=1, source_target_pairs={{0,3},{1,2},{2,1},{3,0},{4,7},{5,6},{6,5},{7,4},{8,11},{9,10},{10,... | collective-permute-start | bytes 393224 | tf_op jit(solution)/shard_map/ppermute | solution.py:277
  57.3 6.7 %collective-permute-start.15 = (f32[2,2,16,512]{3,2,1,0:T(8,128)S(1)}, f32[2,2,16,512]{3,2,1,0:T(8,128)S(1)}, u32[]{:S(2)}, u32[]{:S(2)}) collective-permute-start(f32[2,2,16,512]{3,2,1,0:T(8,128)S(1)} %get-tuple-element.32), channel_id=1, source_target_pairs={{0,1},{1,0},{2,3},{3,2},{4,5},{5,4},{6,7},{7,6},{8,9},{9,8},{10,11... | collective-permute-start | bytes 393224 | tf_op jit(solution)/shard_map/ppermute | solution.py:294
  57.4 7.7 %collective-permute-start.14 = (f32[2,16,512]{2,1,0:T(8,128)S(1)}, f32[2,16,512]{2,1,0:T(8,128)S(1)}, u32[]{:S(2)}, u32[]{:S(2)}) collective-permute-start(f32[2,16,512]{2,1,0:T(8,128)S(1)} %shard_map.54.refs_3_), channel_id=1, source_target_pairs={{0,3},{1,2},{2,1},{3,0},{4,7},{5,6},{6,5},{7,4},{8,11},{9,10},{10,... | collective-permute-start | bytes 196616 | tf_op jit(solution)/shard_map/ppermute | solution.py:277
  64.1 6.1 %collective-permute-start.16 = (f32[2,16,512]{2,1,0:T(8,128)S(1)}, f32[2,16,512]{2,1,0:T(8,128)S(1)}, u32[]{:S(2)}, u32[]{:S(2)}) collective-permute-start(f32[2,16,512]{2,1,0:T(8,128)S(1)} %shard_map.56.refs_3_), channel_id=1, source_target_pairs={{0,3},{1,2},{2,1},{3,0},{4,7},{5,6},{6,5},{7,4},{8,11},{9,10},{10,... | collective-permute-start | bytes 196616 | tf_op jit(solution)/shard_map/ppermute | solution.py:277

commit v3 on v2

--- a/solution.py
+++ b/solution.py
@@ -59,12 +59,12 @@
     lax.fori_loop(0, rows // BLOCK, step, 0)
 
 
-def pack_kernel(chunk, psi, out):
-    odd = parity()
+def pack_kernel(chunk, psi, out, sem):
     lo, hi = chunk
-    for q in range(out.shape[0]):
-        for band in range(out.shape[1]):
-            out[q, band] = psi[2 * odd + q, band, lo:hi, :]
+    planes = pl.ds(2 * parity(), out.shape[0])
+    copy = pltpu.make_async_copy(psi.at[planes, :, pl.ds(lo, hi - lo), :], out, sem)
+    copy.start()
+    copy.wait()
 
 
 def start_kernel(psi, pot, g):
@@ -81,7 +81,7 @@
     blocks(psi.shape[1], body)
 
 
-def inner_kernel(c, psi, pot, psi_in, pot_in, g, t, h):
+def inner_kernel(c, psi, pot, psi_in, pot_in, g, t, h, row):
     odd = parity()
     at = [own(q, odd) for q in range(4)]
     base, one, two = c[0] - c[2], c[1], 2.0 * c[2]
@@ -109,6 +109,7 @@
         h[0, here, :] = base * p2 + one * t2 + two * s2
         h[1, here, :] = base * p3 + one * t3 + two * s3
 
+    row[...] = jnp.full(row.shape, two)
     blocks(psi.shape[1], first)
     blocks(psi.shape[1], second)
 
@@ -118,31 +119,32 @@
     return NEAR * near + FAR * far, FAR * near
 
 
+def square(x, bands):
+    return x * x * (1.0 / bands)
+
+
 def face_kernel(chunk, parts, halo, g, *fs):
     odd = parity()
-    for (lo, hi), f in zip(parts, fs):
-        in_halo = slice(lo - chunk[0], hi - chunk[0])
+    lo, hi = chunk
+    for (first, last), f in zip(parts, fs):
+        in_halo = slice(first - lo, last - lo)
         for band in range(halo.shape[1]):
             d0, d1 = halo_terms(halo, band, odd, in_halo)
-            f[0, band] = g[0, band, lo:hi, :] + d0
-            f[1, band] = g[1, band, lo:hi, :] + d1
-
-
-def square(x, bands):
-    return x * x * (1.0 / bands)
-
-
-def back_kernel(chunk, c, halo, h, keep, send):
+            f[0, band] = g[0, band, first:last, :] + d0
+            f[1, band] = g[1, band, first:last, :] + d1
+
+
+def back_kernel(chunk, row, halo, h, keep, send):
     odd = parity()
     lo, hi = chunk
-    two = 2.0 * c[2]
+    two = row[0:1, :]
     me = lax.axis_index("orb")
     bands = halo.shape[1]
 
     def part(band, out, slot):
         d0, d1 = halo_terms(halo, band, odd)
         v2 = h[0, band, lo:hi, :] + two * (NEAR * d1 + FAR * d0)
-        v3 = h[1, band, lo:hi, :] + (two * FAR) * d1
+        v3 = h[1, band, lo:hi, :] + two * (FAR * d1)
         out[slot, 0] = square(v2, bands)
         out[slot, 1] = square(v3, bands)
 
@@ -177,16 +179,16 @@
     blocks(rows, body)
 
 
-def last_kernel(chunk, c, halo, h, keep, send):
+def last_kernel(chunk, row, halo, h, keep, send):
     lo, hi = chunk
-    two = 2.0 * c[2]
+    two = row[0:1, :]
     me = lax.axis_index("orb")
     bands = halo.shape[1]
 
     def part(band, out, slot):
         near, far = halo[0, band], halo[1, band]
         v0 = h[0, band, lo:hi, :] + two * (NEAR * near + FAR * far)
-        v1 = h[1, band, lo:hi, :] + (two * FAR) * near
+        v1 = h[1, band, lo:hi, :] + two * (FAR * near)
         out[slot, 0] = square(v0, bands)
         out[slot, 1] = square(v1, bands)
 
@@ -219,7 +221,7 @@
     def __init__(self):
         self.last = []
 
-    def __call__(self, kernel, out, args, scalars=0, scratch=(), flops=0):
+    def __call__(self, kernel, out, args, scalars=0, scratch=(), flops=0, hbm=False):
         vmem = pl.BlockSpec(memory_space=pltpu.VMEM)
         smem = pl.BlockSpec(memory_space=pltpu.SMEM)
         many = isinstance(out, list)
@@ -234,7 +236,7 @@
             body,
             out_shape=shapes,
             in_specs=[smem] * scalars
-            + [vmem] * (first - scalars)
+            + [pl.BlockSpec(memory_space=pltpu.HBM) if hbm else vmem] * (first - scalars)
             + [pl.BlockSpec(memory_space=pl.ANY)] * len(last),
             out_specs=[vmem] * len(shapes),
             scratch_shapes=list(scratch),
@@ -276,35 +278,46 @@
         total = call(add_kernel, keep.shape[1:], (keep, came))
         return keep, came, lax.ppermute(total, "orb", far)
 
-    def face_of(chunk, halo, inside):
-        f = call(
-            functools.partial(face_kernel, chunk, inside),
-            [slab_shape(cut) for cut in inside],
+    def squares(cut, halo):
+        keep, send = call(
+            functools.partial(last_kernel, cut),
+            [pair_shape(cut)] * 2,
+            (row, halo, as_bands(h_front)),
+        )
+        return keep, lax.ppermute(send, "orb", near)
+
+    def back_squares(chunk, halo):
+        keep, send = call(
+            functools.partial(back_kernel, chunk),
+            [pair_shape(chunk)] * 2,
+            (row, halo, as_bands(h_back)),
+        )
+        return keep, lax.ppermute(send, "orb", near)
+
+    def faces(chunk, halo, parts):
+        fs = call(
+            functools.partial(face_kernel, chunk, parts),
+            [slab_shape(cut) for cut in parts],
             (halo, as_bands(g)),
         )
-        return f, [lax.ppermute(x, "slab", face) for x in f]
-
-    def squares(kernel, chunk, halo, h):
-        keep, send = call(
-            functools.partial(kernel, chunk),
-            [pair_shape(chunk)] * 2,
-            (coeffs, halo, as_bands(h)),
-            scalars=1,
-        )
-        return keep, lax.ppermute(send, "orb", near)
+        return fs, [lax.ppermute(x, "slab", face) for x in fs]
 
     psi_in = lax.ppermute(psi, "slab", partner)
     pot_in = lax.ppermute(potential, "slab", partner)
     halos = []
     for chunk in chunks:
         piece = call(
-            functools.partial(pack_kernel, chunk), slab_shape(chunk), (as_bands(psi),)
+            functools.partial(pack_kernel, chunk),
+            slab_shape(chunk),
+            (as_bands(psi),),
+            scratch=[pltpu.SemaphoreType.DMA],
+            hbm=True,
         )
         halos.append(lax.ppermute(piece, "slab", face))
     g = call(start_kernel, plane2, (psi, potential), flops=24 * cells)
-    t, h_back = call(
+    t, h_back, row = call(
         inner_kernel,
-        [plane2, plane2],
+        [plane2, plane2, (8, lanes)],
         (coeffs, psi, potential, psi_in, pot_in, g),
         scalars=1,
         flops=80 * cells,
@@ -314,11 +327,10 @@
         return call(sum_kernel, from_far.shape, (keep, came, from_far))
 
     cut_a, cut_b, cut_c = cuts
-    f0, (face_a,) = face_of(chunks[0], halos[0], [cut_a])
-    back0 = squares(back_kernel, chunks[0], halos[0], h_back)
+    f0, (face_a,) = faces(chunks[0], halos[0], [cut_a])
+    back0 = back_squares(chunks[0], halos[0])
     back0 = add_far(*back0)
-    f1, (face_b, face_c) = face_of(chunks[1], halos[1], [cut_b, cut_c])
-    back1 = squares(back_kernel, chunks[1], halos[1], h_back)
+    f1, (face_b, face_c) = faces(chunks[1], halos[1], [cut_b, cut_c])
     h_front = call(
         functools.partial(front_kernel, cuts),
         plane2,
@@ -328,12 +340,13 @@
         flops=40 * cells,
     )
     back0 = summed(*back0)
+    back1 = back_squares(chunks[1], halos[1])
     back1 = add_far(*back1)
-    front_a = squares(last_kernel, cut_a, face_a, h_front)
-    front_b = squares(last_kernel, cut_b, face_b, h_front)
+    front_a = squares(cut_a, face_a)
     back1 = summed(*back1)
+    front_b = squares(cut_b, face_b)
     front_a = add_far(*front_a)
-    front_c = squares(last_kernel, cut_c, face_c, h_front)
+    front_c = squares(cut_c, face_c)
     front_b = add_far(*front_b)
     front_a = summed(*front_a)
     front_c = add_far(*front_c)

time: 71.9 us -> 72.3 us (level); the launches traced: 71 us -> 72.2 us
  starting transfers between devices: 25.7 us -> 37.3 us
  waiting for transfers between devices: 26.4 us -> 18.6 us
  Pallas kernels: 17.1 us -> 14.5 us
    ppermute x5, starting transfers between devices: 9.09 us -> 17.2 us  [add_far(): return (keep, came, lax.ppermute(total, 'orb', far))]
    ppermute x5, waiting for transfers between devices: 15.7 us -> 9.2 us  [add_far(): return (keep, came, lax.ppermute(total, 'orb', far))]
    ppermute x3 -> x5, starting transfers between devices: 7.23 us -> 12.4 us  [the longest x3 8.55 us: faces(): return (fs, [lax.ppermute(x, 'slab', face) for x in fs])]
    ppermute x3 -> x5, waiting for transfers between devices: 0.01 us -> 5.18 us  [the longest x2 4.95 us: back_squares(): return (keep, lax.ppermute(send, 'orb', near))]
    ppermute x5 -> x3, waiting for transfers between devices: 5.13 us -> 1.61 us  [squares(): return (keep, lax.ppermute(send, 'orb', near))]
    ppermute x2, waiting for transfers between devices: 5.59 us -> 2.62 us  [shards(): halos.append(lax.ppermute(piece, 'slab', face))]
    pallas_call x22, Pallas kernels: 17.1 us -> 14.5 us  [__call__(): pl.pallas_call(body, out_shape=shapes, in_specs=[smem] * scalars + [pl.Bl...]
    ppermute x5 -> x3, starting transfers between devices: 5.25 us -> 3.46 us  [squares(): return (keep, lax.ppermute(send, 'orb', near))]
  transfers between devices with their start and end apart: 17 -> 17, of which waited for: 8 -> 9; matrix products, arithmetic and copies ran while one was open for 0% -> 0% of each run, Pallas kernels for 23% -> 19%
where the time goes in v3:
time: 72.3 us; the launch traced here: 72.2 us
  starting transfers between devices  37.3 us (52%)
  waiting for transfers between devices  18.6 us (26%)
  Pallas kernels  14.5 us (20%)
  local copies, waits for them, and re-layouts  1.61 us (2%)
    ppermute x5, starting transfers between devices, add_far(): return (keep, came, lax.ppermute(total, 'orb', far))  17.2 us
    pallas_call x22, Pallas kernels, __call__(): pl.pallas_call(body, out_shape=shapes, in_specs=[smem] * scalars + [pl.Bl...  14.5 us
    ppermute x5, waiting for transfers between devices, add_far(): return (keep, came, lax.ppermute(total, 'orb', far))  9.2 us
    ppermute x3, starting transfers between devices, faces(): return (fs, [lax.ppermute(x, 'slab', face) for x in fs])  8.55 us
    ppermute x2, waiting for transfers between devices, back_squares(): return (keep, lax.ppermute(send, 'orb', near))  4.95 us
    ppermute x2, starting transfers between devices, back_squares(): return (keep, lax.ppermute(send, 'orb', near))  3.89 us
    ppermute x2, starting transfers between devices, shards(): halos.append(lax.ppermute(piece, 'slab', face))  3.66 us
    ppermute x3, starting transfers between devices, squares(): return (keep, lax.ppermute(send, 'orb', near))  3.46 us
  transfers between devices with their start and end apart: 17, of which 9 were waited for; matrix products, arithmetic and copies ran while one was open for 0% of the time, Pallas kernels for 19%

profile of v3, /device:TPU:0, one launch (start us, length us, event | category | flops | bytes accessed | tf_op | source)
XLA Modules:
  0.0 72.2 jit_solution(8246770003962808153)
XLA Ops:
  0.0 0.5 collective-permute-start
  0.5 0.1 collective-permute-start.1
  0.5 1.6 %copy-done = f32[1,4,256,512]{3,2,1,0:T(8,128)S(1)} copy-done((f32[1,4,256,512]{3,2,1,0:T(8,128)S(1)}, f32[1,4,256,512]{3,2,1,0:T(8,128)}, u32[]{:S(2)}) %copy-start) | copy-done | bytes 2097176
  2.2 0.0 copy-start.2
  2.2 3.6 %collective-permute-start.2 = (f32[2,4,32,512]{3,2,1,0:T(8,128)S(1)}, f32[2,4,32,512]{3,2,1,0:T(8,128)S(1)}, u32[]{:S(2)}, u32[]{:S(2)}) collective-permute-start(f32[2,4,32,512]{3,2,1,0:T(8,128)S(1)} %shard_map.37.refs_1_), channel_id=1, source_target_pairs={{0,28},{4,8},{8,4},{12,16},{16,12},{20,24},{24,20},{28,0},{1,29},{... | collective-permute-start | bytes 1572872 | tf_op jit(solution)/shard_map/ppermute | solution.py:316
  5.8 0.0 copy-start.3
  5.8 0.1 collective-permute-start.5
  5.9 2.5 %shard_map.39.refs_5_.refs_6_ = f32[2,256,512]{2,1,0:T(8,128)S(1)} custom-call(f32[4,256,512]{2,1,0:T(8,128)S(1)} %bitcast.8, f32[4,256,512]{2,1,0:T(8,128)S(1)} %copy-done.2, f32[2,4,32,512]{3,2,1,0:T(8,128)S(1)} %shard_map.38.refs_2_), custom_call_target="tpu_custom_call" | custom-call | flops 6291456 | bytes 5242880 | tf_op jit(solution)/shard_map/pallas_call | solution.py:235
  8.4 0.0 collective-permute-done.refs_3_
  8.4 0.0 collective-permute-done.1.refs_4_
  8.4 7.0 %shard_map.40 = (f32[2,256,512]{2,1,0:T(8,128)S(1)}, f32[2,256,512]{2,1,0:T(8,128)S(1)}, f32[8,512]{1,0:T(8,128)S(1)}) custom-call(f32[3]{0:T(128)S(1)} %copy-done.3, f32[4,256,512]{2,1,0:T(8,128)S(1)} %bitcast.9, f32[4,256,512]{2,1,0:T(8,128)S(1)} %copy-done.2, f32[4,256,512]{2,1,0:T(8,128)S(1)} %collective-permute-done.refs_3_, ...), custom_call_target="tpu_custom_call" | custom-call | flops 20971520 | bytes 11550732 | tf_op jit(solution)/shard_map/pallas_call | solution.py:235
  15.4 2.6 %collective-permute-done.2.refs_0_.refs_1_ = f32[2,4,32,512]{3,2,1,0:T(8,128)S(1)} collective-permute-done((f32[2,4,32,512]{3,2,1,0:T(8,128)S(1)}, f32[2,4,32,512]{3,2,1,0:T(8,128)S(1)}, u32[]{:S(2)}, u32[]{:S(2)}) %collective-permute-start.2) | collective-permute-done | bytes 524320 | tf_op jit(solution)/shard_map/ppermute | solution.py:316
  18.1 0.1 shard_map.41.refs_3_.refs_4_
  18.2 0.0 copy-start.1
  18.2 0.2 shard_map.42
  18.3 2.1 %collective-permute-start.3 = (f32[2,2,32,512]{3,2,1,0:T(8,128)S(1)}, f32[2,2,32,512]{3,2,1,0:T(8,128)S(1)}, u32[]{:S(2)}, u32[]{:S(2)}) collective-permute-start(f32[2,2,32,512]{3,2,1,0:T(8,128)S(1)} %get-tuple-element.24), channel_id=1, source_target_pairs={{0,1},{1,0},{2,3},{3,2},{4,5},{5,4},{6,7},{7,6},{8,9},{9,8},{10,11... | collective-permute-start | bytes 786440 | tf_op jit(solution)/shard_map/ppermute | solution.py:295
  20.5 2.0 %collective-permute-start.8 = (f32[2,4,32,512]{3,2,1,0:T(8,128)S(1)}, f32[2,4,32,512]{3,2,1,0:T(8,128)S(1)}, u32[]{:S(2)}, u32[]{:S(2)}) collective-permute-start(f32[2,4,32,512]{3,2,1,0:T(8,128)S(1)} %shard_map.41.refs_3_.refs_4_), channel_id=1, source_target_pairs={{0,28},{4,8},{8,4},{12,16},{16,12},{20,24},{24,20},{28,0},{1,29},{... | collective-permute-start | bytes 1572872 | tf_op jit(solution)/shard_map/ppermute | solution.py:303
  22.5 3.3 %collective-permute-done.3.refs_1_ = f32[2,2,32,512]{3,2,1,0:T(8,128)S(1)} collective-permute-done((f32[2,2,32,512]{3,2,1,0:T(8,128)S(1)}, f32[2,2,32,512]{3,2,1,0:T(8,128)S(1)}, u32[]{:S(2)}, u32[]{:S(2)}) %collective-permute-start.3) | collective-permute-done | bytes 262176 | tf_op jit(solution)/shard_map/ppermute | solution.py:295
  25.9 3.8 %collective-permute-start.4 = (f32[2,32,512]{2,1,0:T(8,128)S(1)}, f32[2,32,512]{2,1,0:T(8,128)S(1)}, u32[]{:S(2)}, u32[]{:S(2)}) collective-permute-start(f32[2,32,512]{2,1,0:T(8,128)S(1)} %shard_map.43.refs_2_), channel_id=1, source_target_pairs={{0,3},{1,2},{2,1},{3,0},{4,7},{5,6},{6,5},{7,4},{8,11},{9,10},{10,... | collective-permute-start | bytes 393224 | tf_op jit(solution)/shard_map/ppermute | solution.py:279
  29.7 0.0 collective-permute-done.5.refs_0_.refs_1_
  29.7 0.1 shard_map.44
  29.8 3.2 %shard_map.45.refs_3_ = f32[2,256,512]{2,1,0:T(8,128)S(1)} custom-call(f32[3]{0:T(128)S(1)} %copy-done.3, f32[4,256,512]{2,1,0:T(8,128)S(1)} %bitcast.10, f32[4,256,512]{2,1,0:T(8,128)S(1)} %copy-done.2, f32[2,256,512]{2,1,0:T(8,128)S(1)} %get-tuple-element.22.refs_2_.refs_3_, f32[2,4,32,512]{3,2,1,0:T(8,128)S(1)} %shard_map.41.refs_3_.refs_4_, ...), custom_call_target="tpu_custom_call" | custom-call | flops 10485760 | bytes 7340044 | tf_op jit(solution)/shard_map/pallas_call | solution.py:235
  33.0 0.0 collective-permute-done.4.refs_2_
  33.0 0.2 shard_map.47
  33.2 1.8 %collective-permute-start.6 = (f32[2,2,32,512]{3,2,1,0:T(8,128)S(1)}, f32[2,2,32,512]{3,2,1,0:T(8,128)S(1)}, u32[]{:S(2)}, u32[]{:S(2)}) collective-permute-start(f32[2,2,32,512]{3,2,1,0:T(8,128)S(1)} %get-tuple-element.28), channel_id=1, source_target_pairs={{0,1},{1,0},{2,3},{3,2},{4,5},{5,4},{6,7},{7,6},{8,9},{9,8},{10,11... | collective-permute-start | bytes 786440 | tf_op jit(solution)/shard_map/ppermute | solution.py:295
  34.9 3.8 %collective-permute-start.10 = (f32[2,4,16,512]{3,2,1,0:T(8,128)S(1)}, f32[2,4,16,512]{3,2,1,0:T(8,128)S(1)}, u32[]{:S(2)}, u32[]{:S(2)}) collective-permute-start(f32[2,4,16,512]{3,2,1,0:T(8,128)S(1)} %get-tuple-element.25.refs_5_.refs_7_), channel_id=1, source_target_pairs={{0,28},{4,8},{8,4},{12,16},{16,12},{20,24},{24,20},{28,0},{1,29},{... | collective-permute-start | bytes 786440 | tf_op jit(solution)/shard_map/ppermute | solution.py:303
  38.7 1.6 %collective-permute-done.6.refs_1_ = f32[2,2,32,512]{3,2,1,0:T(8,128)S(1)} collective-permute-done((f32[2,2,32,512]{3,2,1,0:T(8,128)S(1)}, f32[2,2,32,512]{3,2,1,0:T(8,128)S(1)}, u32[]{:S(2)}, u32[]{:S(2)}) %collective-permute-start.6) | collective-permute-done | bytes 262176 | tf_op jit(solution)/shard_map/ppermute | solution.py:295
  40.3 0.2 collective-permute-done.8.refs_1_
  40.5 0.1 shard_map.49
  40.7 2.1 %collective-permute-start.9 = (f32[2,2,32,512]{3,2,1,0:T(8,128)S(1)}, f32[2,2,32,512]{3,2,1,0:T(8,128)S(1)}, u32[]{:S(2)}, u32[]{:S(2)}) collective-permute-start(f32[2,2,32,512]{3,2,1,0:T(8,128)S(1)} %get-tuple-element.30), channel_id=1, source_target_pairs={{0,1},{1,0},{2,3},{3,2},{4,5},{5,4},{6,7},{7,6},{8,9},{9,8},{10,11... | collective-permute-start | bytes 786440 | tf_op jit(solution)/shard_map/ppermute | solution.py:287
  42.8 2.8 %collective-permute-start.13 = (f32[2,4,16,512]{3,2,1,0:T(8,128)S(1)}, f32[2,4,16,512]{3,2,1,0:T(8,128)S(1)}, u32[]{:S(2)}, u32[]{:S(2)}) collective-permute-start(f32[2,4,16,512]{3,2,1,0:T(8,128)S(1)} %get-tuple-element.26.refs_6_), channel_id=1, source_target_pairs={{0,28},{4,8},{8,4},{12,16},{16,12},{20,24},{24,20},{28,0},{1,29},{... | collective-permute-start | bytes 786440 | tf_op jit(solution)/shard_map/ppermute | solution.py:303
  45.6 2.5 %collective-permute-start.7 = (f32[2,32,512]{2,1,0:T(8,128)S(1)}, f32[2,32,512]{2,1,0:T(8,128)S(1)}, u32[]{:S(2)}, u32[]{:S(2)}) collective-permute-start(f32[2,32,512]{2,1,0:T(8,128)S(1)} %shard_map.48.refs_3_), channel_id=1, source_target_pairs={{0,3},{1,2},{2,1},{3,0},{4,7},{5,6},{6,5},{7,4},{8,11},{9,10},{10,... | collective-permute-start | bytes 393224 | tf_op jit(solution)/shard_map/ppermute | solution.py:279
  48.0 5.7 %collective-permute-done.7.refs_2_ = f32[2,32,512]{2,1,0:T(8,128)S(1)} collective-permute-done((f32[2,32,512]{2,1,0:T(8,128)S(1)}, f32[2,32,512]{2,1,0:T(8,128)S(1)}, u32[]{:S(2)}, u32[]{:S(2)}) %collective-permute-start.7) | collective-permute-done | bytes 131104 | tf_op jit(solution)/shard_map/ppermute | solution.py:279
  53.7 0.0 collective-permute-done.10.refs_1_
  53.8 0.1 shard_map.51
  53.8 1.3 %collective-permute-start.12 = (f32[2,2,16,512]{3,2,1,0:T(8,128)S(1)}, f32[2,2,16,512]{3,2,1,0:T(8,128)S(1)}, u32[]{:S(2)}, u32[]{:S(2)}) collective-permute-start(f32[2,2,16,512]{3,2,1,0:T(8,128)S(1)} %get-tuple-element.32), channel_id=1, source_target_pairs={{0,1},{1,0},{2,3},{3,2},{4,5},{5,4},{6,7},{7,6},{8,9},{9,8},{10,11... | collective-permute-start | bytes 393224 | tf_op jit(solution)/shard_map/ppermute | solution.py:287
  55.1 0.0 collective-permute-done.9.refs_1_
  55.1 2.7 %collective-permute-start.11 = (f32[2,32,512]{2,1,0:T(8,128)S(1)}, f32[2,32,512]{2,1,0:T(8,128)S(1)}, u32[]{:S(2)}, u32[]{:S(2)}) collective-permute-start(f32[2,32,512]{2,1,0:T(8,128)S(1)} %shard_map.52.refs_3_), channel_id=1, source_target_pairs={{0,3},{1,2},{2,1},{3,0},{4,7},{5,6},{6,5},{7,4},{8,11},{9,10},{10,... | collective-permute-start | bytes 393224 | tf_op jit(solution)/shard_map/ppermute | solution.py:279
  57.8 0.0 collective-permute-done.13.refs_1_
  57.8 0.1 shard_map.53
  57.8 0.1 collective-permute-start.15
  57.9 1.3 %collective-permute-done.12.refs_1_ = f32[2,2,16,512]{3,2,1,0:T(8,128)S(1)} collective-permute-done((f32[2,2,16,512]{3,2,1,0:T(8,128)S(1)}, f32[2,2,16,512]{3,2,1,0:T(8,128)S(1)}, u32[]{:S(2)}, u32[]{:S(2)}) %collective-permute-start.12) | collective-permute-done | bytes 131104 | tf_op jit(solution)/shard_map/ppermute | solution.py:287
  59.3 5.3 %collective-permute-start.14 = (f32[2,16,512]{2,1,0:T(8,128)S(1)}, f32[2,16,512]{2,1,0:T(8,128)S(1)}, u32[]{:S(2)}, u32[]{:S(2)}) collective-permute-start(f32[2,16,512]{2,1,0:T(8,128)S(1)} %shard_map.54.refs_3_), channel_id=1, source_target_pairs={{0,3},{1,2},{2,1},{3,0},{4,7},{5,6},{6,5},{7,4},{8,11},{9,10},{10,... | collective-permute-start | bytes 196616 | tf_op jit(solution)/shard_map/ppermute | solution.py:279
  64.6 0.3 collective-permute-done.11.refs_2_
  64.9 0.3 collective-permute-done.15.refs_1_.refs_5_
  65.2 2.9 %collective-permute-start.16 = (f32[2,16,512]{2,1,0:T(8,128)S(1)}, f32[2,16,512]{2,1,0:T(8,128)S(1)}, u32[]{:S(2)}, u32[]{:S(2)}) collective-permute-start(f32[2,16,512]{2,1,0:T(8,128)S(1)} %shard_map.56.refs_3_), channel_id=1, source_target_pairs={{0,3},{1,2},{2,1},{3,0},{4,7},{5,6},{6,5},{7,4},{8,11},{9,10},{10,... | collective-permute-start | bytes 196616 | tf_op jit(solution)/shard_map/ppermute | solution.py:279
  68.1 3.2 %collective-permute-done.16.refs_6_ = f32[2,16,512]{2,1,0:T(8,128)S(1)} collective-permute-done((f32[2,16,512]{2,1,0:T(8,128)S(1)}, f32[2,16,512]{2,1,0:T(8,128)S(1)}, u32[]{:S(2)}, u32[]{:S(2)}) %collective-permute-start.16) | collective-permute-done | bytes 65568 | tf_op jit(solution)/shard_map/ppermute | solution.py:279
  71.3 0.8 %shard_map.58 = f32[4,64,512]{2,1,0:T(8,128)} custom-call(f32[2,32,512]{2,1,0:T(8,128)S(1)} %shard_map.46.refs_3_.refs_0_, f32[2,32,512]{2,1,0:T(8,128)S(1)} %shard_map.50.refs_3_.refs_1_, f32[2,32,512]{2,1,0:T(8,128)S(1)} %shard_map.55.refs_2_, f32[2,16,512]{2,1,0:T(8,128)S(1)} %shard_map.57.refs_3_.refs_7_, ...), custom_call_target="tpu_custom_call" | custom-call | bytes 1310720 | tf_op jit(solution)/shard_map/pallas_call | solution.py:235
  (16 shorter events, 0.2 us)
Async XLA Ops:
  0.0 8.4 %collective-permute-start = (f32[4,256,512]{2,1,0:T(8,128)}, f32[4,256,512]{2,1,0:T(8,128)S(1)}, u32[]{:S(2)}, u32[]{:S(2)}) collective-permute-start(f32[4,256,512]{2,1,0:T(8,128)} %bitcast.5), channel_id=1, source_target_pairs={{0,4},{4,0},{8,12},{12,8},{16,20},{20,16},{24,28},{28,24},{1,5},{5... | collective-permute-start | bytes 6291464 | tf_op jit(solution)/shard_map/ppermute | solution.py:305
  0.5 8.0 %collective-permute-start.1 = (f32[4,256,512]{2,1,0:T(8,128)}, f32[4,256,512]{2,1,0:T(8,128)S(1)}, u32[]{:S(2)}, u32[]{:S(2)}) collective-permute-start(f32[4,256,512]{2,1,0:T(8,128)} %refs_2_.3), channel_id=1, source_target_pairs={{0,4},{4,0},{8,12},{12,8},{16,20},{20,16},{24,28},{28,24},{1,5},{5... | collective-permute-start | bytes 6291464 | tf_op jit(solution)/shard_map/ppermute | solution.py:306
  0.5 1.6 %copy-start = (f32[1,4,256,512]{3,2,1,0:T(8,128)S(1)}, f32[1,4,256,512]{3,2,1,0:T(8,128)}, u32[]{:S(2)}) copy-start(f32[1,4,256,512]{3,2,1,0:T(8,128)} %param.3) | copy-start | bytes 6291460
  2.2 3.7 %copy-start.2 = (f32[4,256,512]{2,1,0:T(8,128)S(1)}, f32[4,256,512]{2,1,0:T(8,128)}, u32[]{:S(2)}) copy-start(f32[4,256,512]{2,1,0:T(8,128)} %refs_2_.3) | copy-start | bytes 6291460
  2.2 15.9 %collective-permute-start.2 = (f32[2,4,32,512]{3,2,1,0:T(8,128)S(1)}, f32[2,4,32,512]{3,2,1,0:T(8,128)S(1)}, u32[]{:S(2)}, u32[]{:S(2)}) collective-permute-start(f32[2,4,32,512]{3,2,1,0:T(8,128)S(1)} %shard_map.37.refs_1_), channel_id=1, source_target_pairs={{0,28},{4,8},{8,4},{12,16},{16,12},{20,24},{24,20},{28,0},{1,29},{... | collective-permute-start | bytes 1572872 | tf_op jit(solution)/shard_map/ppermute | solution.py:316
  5.8 2.6 %copy-start.3 = (f32[3]{0:T(128)S(1)}, f32[3]{0:T(128)}, u32[]{:S(2)}) copy-start(f32[3]{0:T(128)} %refs_0_.3) | copy-start | bytes 40
  5.8 23.9 %collective-permute-start.5 = (f32[2,4,32,512]{3,2,1,0:T(8,128)S(1)}, f32[2,4,32,512]{3,2,1,0:T(8,128)S(1)}, u32[]{:S(2)}, u32[]{:S(2)}) collective-permute-start(f32[2,4,32,512]{3,2,1,0:T(8,128)S(1)} %shard_map.38.refs_2_), channel_id=1, source_target_pairs={{0,28},{4,8},{8,4},{12,16},{16,12},{20,24},{24,20},{28,0},{1,29},{... | collective-permute-start | bytes 1572872 | tf_op jit(solution)/shard_map/ppermute | solution.py:316
  18.2 11.6 %copy-start.1 = (f32[1,4,256,512]{3,2,1,0:T(8,128)S(1)}, f32[1,4,256,512]{3,2,1,0:T(8,128)}, u32[]{:S(2)}) copy-start(f32[1,4,256,512]{3,2,1,0:T(8,128)} %param.3) | copy-start | bytes 6291460
  18.3 7.5 %collective-permute-start.3 = (f32[2,2,32,512]{3,2,1,0:T(8,128)S(1)}, f32[2,2,32,512]{3,2,1,0:T(8,128)S(1)}, u32[]{:S(2)}, u32[]{:S(2)}) collective-permute-start(f32[2,2,32,512]{3,2,1,0:T(8,128)S(1)} %get-tuple-element.24), channel_id=1, source_target_pairs={{0,1},{1,0},{2,3},{3,2},{4,5},{5,4},{6,7},{7,6},{8,9},{9,8},{10,11... | collective-permute-start | bytes 786440 | tf_op jit(solution)/shard_map/ppermute | solution.py:295
  20.5 20.1 %collective-permute-start.8 = (f32[2,4,32,512]{3,2,1,0:T(8,128)S(1)}, f32[2,4,32,512]{3,2,1,0:T(8,128)S(1)}, u32[]{:S(2)}, u32[]{:S(2)}) collective-permute-start(f32[2,4,32,512]{3,2,1,0:T(8,128)S(1)} %shard_map.41.refs_3_.refs_4_), channel_id=1, source_target_pairs={{0,28},{4,8},{8,4},{12,16},{16,12},{20,24},{24,20},{28,0},{1,29},{... | collective-permute-start | bytes 1572872 | tf_op jit(solution)/shard_map/ppermute | solution.py:303
  25.9 7.1 %collective-permute-start.4 = (f32[2,32,512]{2,1,0:T(8,128)S(1)}, f32[2,32,512]{2,1,0:T(8,128)S(1)}, u32[]{:S(2)}, u32[]{:S(2)}) collective-permute-start(f32[2,32,512]{2,1,0:T(8,128)S(1)} %shard_map.43.refs_2_), channel_id=1, source_target_pairs={{0,3},{1,2},{2,1},{3,0},{4,7},{5,6},{6,5},{7,4},{8,11},{9,10},{10,... | collective-permute-start | bytes 393224 | tf_op jit(solution)/shard_map/ppermute | solution.py:279
  33.2 7.1 %collective-permute-start.6 = (f32[2,2,32,512]{3,2,1,0:T(8,128)S(1)}, f32[2,2,32,512]{3,2,1,0:T(8,128)S(1)}, u32[]{:S(2)}, u32[]{:S(2)}) collective-permute-start(f32[2,2,32,512]{3,2,1,0:T(8,128)S(1)} %get-tuple-element.28), channel_id=1, source_target_pairs={{0,1},{1,0},{2,3},{3,2},{4,5},{5,4},{6,7},{7,6},{8,9},{9,8},{10,11... | collective-permute-start | bytes 786440 | tf_op jit(solution)/shard_map/ppermute | solution.py:295
  34.9 18.8 %collective-permute-start.10 = (f32[2,4,16,512]{3,2,1,0:T(8,128)S(1)}, f32[2,4,16,512]{3,2,1,0:T(8,128)S(1)}, u32[]{:S(2)}, u32[]{:S(2)}) collective-permute-start(f32[2,4,16,512]{3,2,1,0:T(8,128)S(1)} %get-tuple-element.25.refs_5_.refs_7_), channel_id=1, source_target_pairs={{0,28},{4,8},{8,4},{12,16},{16,12},{20,24},{24,20},{28,0},{1,29},{... | collective-permute-start | bytes 786440 | tf_op jit(solution)/shard_map/ppermute | solution.py:303
  40.7 14.4 %collective-permute-start.9 = (f32[2,2,32,512]{3,2,1,0:T(8,128)S(1)}, f32[2,2,32,512]{3,2,1,0:T(8,128)S(1)}, u32[]{:S(2)}, u32[]{:S(2)}) collective-permute-start(f32[2,2,32,512]{3,2,1,0:T(8,128)S(1)} %get-tuple-element.30), channel_id=1, source_target_pairs={{0,1},{1,0},{2,3},{3,2},{4,5},{5,4},{6,7},{7,6},{8,9},{9,8},{10,11... | collective-permute-start | bytes 786440 | tf_op jit(solution)/shard_map/ppermute | solution.py:287
  42.8 15.0 %collective-permute-start.13 = (f32[2,4,16,512]{3,2,1,0:T(8,128)S(1)}, f32[2,4,16,512]{3,2,1,0:T(8,128)S(1)}, u32[]{:S(2)}, u32[]{:S(2)}) collective-permute-start(f32[2,4,16,512]{3,2,1,0:T(8,128)S(1)} %get-tuple-element.26.refs_6_), channel_id=1, source_target_pairs={{0,28},{4,8},{8,4},{12,16},{16,12},{20,24},{24,20},{28,0},{1,29},{... | collective-permute-start | bytes 786440 | tf_op jit(solution)/shard_map/ppermute | solution.py:303
  45.6 8.2 %collective-permute-start.7 = (f32[2,32,512]{2,1,0:T(8,128)S(1)}, f32[2,32,512]{2,1,0:T(8,128)S(1)}, u32[]{:S(2)}, u32[]{:S(2)}) collective-permute-start(f32[2,32,512]{2,1,0:T(8,128)S(1)} %shard_map.48.refs_3_), channel_id=1, source_target_pairs={{0,3},{1,2},{2,1},{3,0},{4,7},{5,6},{6,5},{7,4},{8,11},{9,10},{10,... | collective-permute-start | bytes 393224 | tf_op jit(solution)/shard_map/ppermute | solution.py:279
  53.8 5.4 %collective-permute-start.12 = (f32[2,2,16,512]{3,2,1,0:T(8,128)S(1)}, f32[2,2,16,512]{3,2,1,0:T(8,128)S(1)}, u32[]{:S(2)}, u32[]{:S(2)}) collective-permute-start(f32[2,2,16,512]{3,2,1,0:T(8,128)S(1)} %get-tuple-element.32), channel_id=1, source_target_pairs={{0,1},{1,0},{2,3},{3,2},{4,5},{5,4},{6,7},{7,6},{8,9},{9,8},{10,11... | collective-permute-start | bytes 393224 | tf_op jit(solution)/shard_map/ppermute | solution.py:287
  55.1 9.8 %collective-permute-start.11 = (f32[2,32,512]{2,1,0:T(8,128)S(1)}, f32[2,32,512]{2,1,0:T(8,128)S(1)}, u32[]{:S(2)}, u32[]{:S(2)}) collective-permute-start(f32[2,32,512]{2,1,0:T(8,128)S(1)} %shard_map.52.refs_3_), channel_id=1, source_target_pairs={{0,3},{1,2},{2,1},{3,0},{4,7},{5,6},{6,5},{7,4},{8,11},{9,10},{10,... | collective-permute-start | bytes 393224 | tf_op jit(solution)/shard_map/ppermute | solution.py:279
  57.8 7.3 %collective-permute-start.15 = (f32[2,2,16,512]{3,2,1,0:T(8,128)S(1)}, f32[2,2,16,512]{3,2,1,0:T(8,128)S(1)}, u32[]{:S(2)}, u32[]{:S(2)}) collective-permute-start(f32[2,2,16,512]{3,2,1,0:T(8,128)S(1)} %get-tuple-element.34), channel_id=1, source_target_pairs={{0,1},{1,0},{2,3},{3,2},{4,5},{5,4},{6,7},{7,6},{8,9},{9,8},{10,11... | collective-permute-start | bytes 393224 | tf_op jit(solution)/shard_map/ppermute | solution.py:287
  59.3 8.9 %collective-permute-start.14 = (f32[2,16,512]{2,1,0:T(8,128)S(1)}, f32[2,16,512]{2,1,0:T(8,128)S(1)}, u32[]{:S(2)}, u32[]{:S(2)}) collective-permute-start(f32[2,16,512]{2,1,0:T(8,128)S(1)} %shard_map.54.refs_3_), channel_id=1, source_target_pairs={{0,3},{1,2},{2,1},{3,0},{4,7},{5,6},{6,5},{7,4},{8,11},{9,10},{10,... | collective-permute-start | bytes 196616 | tf_op jit(solution)/shard_map/ppermute | solution.py:279
  65.2 6.1 %collective-permute-start.16 = (f32[2,16,512]{2,1,0:T(8,128)S(1)}, f32[2,16,512]{2,1,0:T(8,128)S(1)}, u32[]{:S(2)}, u32[]{:S(2)}) collective-permute-start(f32[2,16,512]{2,1,0:T(8,128)S(1)} %shard_map.56.refs_3_), channel_id=1, source_target_pairs={{0,3},{1,2},{2,1},{3,0},{4,7},{5,6},{6,5},{7,4},{8,11},{9,10},{10,... | collective-permute-start | bytes 196616 | tf_op jit(solution)/shard_map/ppermute | solution.py:279

commit v4 on v3

--- a/solution.py
+++ b/solution.py
@@ -152,6 +152,26 @@
     part(me ^ 2, send, 1)
     part(me, keep, 0)
     part(me ^ 3, keep, 1)
+
+
+def back_all_kernel(chunk, row, halo, h, out):
+    odd = parity()
+    lo, hi = chunk
+    two = row[0:1, :]
+    bands = halo.shape[1]
+    for band in range(bands):
+        d0, d1 = halo_terms(halo, band, odd)
+        v2 = h[0, band, lo:hi, :] + two * (NEAR * d1 + FAR * d0)
+        v3 = h[1, band, lo:hi, :] + two * (FAR * d1)
+        out[band, 0] = square(v2, bands)
+        out[band, 1] = square(v3, bands)
+
+
+def sum_all_kernel(came, out):
+    total = came[0]
+    for band in range(1, came.shape[0]):
+        total = total + came[band]
+    out[...] = total
 
 
 def front_kernel(chunks, c, psi, pot, t, *rest):
@@ -287,12 +307,15 @@
         return keep, lax.ppermute(send, "orb", near)
 
     def back_squares(chunk, halo):
-        keep, send = call(
-            functools.partial(back_kernel, chunk),
-            [pair_shape(chunk)] * 2,
+        out = call(
+            functools.partial(back_all_kernel, chunk),
+            (bands,) + pair_shape(chunk)[1:],
             (row, halo, as_bands(h_back)),
         )
-        return keep, lax.ppermute(send, "orb", near)
+        return lax.all_to_all(out, "orb", 0, 0, tiled=True)
+
+    def sum_all(came):
+        return call(sum_all_kernel, came.shape[1:], (came,))
 
     def faces(chunk, halo, parts):
         fs = call(
@@ -329,8 +352,8 @@
     cut_a, cut_b, cut_c = cuts
     f0, (face_a,) = faces(chunks[0], halos[0], [cut_a])
     back0 = back_squares(chunks[0], halos[0])
-    back0 = add_far(*back0)
     f1, (face_b, face_c) = faces(chunks[1], halos[1], [cut_b, cut_c])
+    back1 = back_squares(chunks[1], halos[1])
     h_front = call(
         functools.partial(front_kernel, cuts),
         plane2,
@@ -339,12 +362,10 @@
         scratch=[pltpu.VMEM(plane2, jnp.float32)],
         flops=40 * cells,
     )
-    back0 = summed(*back0)
-    back1 = back_squares(chunks[1], halos[1])
-    back1 = add_far(*back1)
+    back0 = sum_all(back0)
     front_a = squares(cut_a, face_a)
-    back1 = summed(*back1)
     front_b = squares(cut_b, face_b)
+    back1 = sum_all(back1)
     front_a = add_far(*front_a)
     front_c = squares(cut_c, face_c)
     front_b = add_far(*front_b)

time: 72.3 us -> 82.4 us (1.14)
  Pallas kernels: 14.5 us -> 21.2 us
  starting transfers between devices: 37.3 us -> 31.7 us
  waiting for transfers between devices: 18.6 us -> 23.4 us
  local copies, waits for them, and re-layouts: 1.61 us -> 5.43 us
    ppermute x2, waiting for transfers between devices: 2.62 us -> 14.5 us  [shards(): halos.append(lax.ppermute(piece, 'slab', face))]
    all_to_all x0 -> x2, starting transfers between devices: none -> 11.1 us  [back_squares(): return lax.all_to_all(out, 'orb', 0, 0, tiled=True)]
    ppermute x5 -> x3, starting transfers between devices: 17.2 us -> 8.31 us  [add_far(): return (keep, came, lax.ppermute(total, 'orb', far))]
    pallas_call x22 -> x20, Pallas kernels: 14.5 us -> 21.2 us  [__call__(): pl.pallas_call(body, out_shape=shapes, in_specs=[smem] * scalars + [pl.Bl...]
    ppermute x2 -> x0, waiting for transfers between devices: 4.95 us -> none  [back_squares(): return (keep, lax.ppermute(send, 'orb', near))]
    ppermute x5 -> x3, waiting for transfers between devices: 9.2 us -> 4.96 us  [add_far(): return (keep, came, lax.ppermute(total, 'orb', far))]
    ppermute x3, starting transfers between devices: 8.55 us -> 4.38 us  [faces(): return (fs, [lax.ppermute(x, 'slab', face) for x in fs])]
    ppermute x2 -> x0, starting transfers between devices: 3.89 us -> none  [back_squares(): return (keep, lax.ppermute(send, 'orb', near))]
  transfers between devices with their start and end apart: 17 -> 15, of which waited for: 9 -> 6; matrix products, arithmetic and copies ran while one was open for 0% -> 0% of each run, Pallas kernels for 19% -> 23%
where the time goes in v4:
time: 82.4 us; the launch traced here: 81.9 us
  starting transfers between devices  31.7 us (38%)
  waiting for transfers between devices  23.4 us (28%)
  Pallas kernels  21.2 us (26%)
  local copies, waits for them, and re-layouts  5.43 us (7%)
    pallas_call x20, Pallas kernels, __call__(): pl.pallas_call(body, out_shape=shapes, in_specs=[smem] * scalars + [pl.Bl...  21.2 us
    ppermute x2, waiting for transfers between devices, shards(): halos.append(lax.ppermute(piece, 'slab', face))  14.5 us
    all_to_all x2, starting transfers between devices, back_squares(): return lax.all_to_all(out, 'orb', 0, 0, tiled=True)  11.1 us
    ppermute x3, starting transfers between devices, add_far(): return (keep, came, lax.ppermute(total, 'orb', far))  8.31 us
    unnamed x14, local copies, waits for them, and re-layouts  5.43 us
    ppermute x3, waiting for transfers between devices, add_far(): return (keep, came, lax.ppermute(total, 'orb', far))  4.96 us
    ppermute x2, starting transfers between devices, shards(): halos.append(lax.ppermute(piece, 'slab', face))  4.45 us
    ppermute x3, starting transfers between devices, faces(): return (fs, [lax.ppermute(x, 'slab', face) for x in fs])  4.38 us
  transfers between devices with their start and end apart: 15, of which 6 were waited for; matrix products, arithmetic and copies ran while one was open for 0% of the time, Pallas kernels for 23%

profile of v4, /device:TPU:0, one launch (start us, length us, event | category | flops | bytes accessed | tf_op | source)
XLA Modules:
  0.0 81.9 jit_solution(17655394656655689379)
XLA Ops:
  0.0 0.5 collective-permute-start
  0.5 0.1 collective-permute-start.1
  0.5 1.6 %copy-done = f32[1,4,256,512]{3,2,1,0:T(8,128)S(1)} copy-done((f32[1,4,256,512]{3,2,1,0:T(8,128)S(1)}, f32[1,4,256,512]{3,2,1,0:T(8,128)}, u32[]{:S(2)}) %copy-start) | copy-done | bytes 2097176
  2.2 0.0 copy-start.2
  2.2 3.6 %collective-permute-start.2 = (f32[2,4,32,512]{3,2,1,0:T(8,128)S(1)}, f32[2,4,32,512]{3,2,1,0:T(8,128)S(1)}, u32[]{:S(2)}, u32[]{:S(2)}) collective-permute-start(f32[2,4,32,512]{3,2,1,0:T(8,128)S(1)} %shard_map.37.refs_1_), channel_id=1, source_target_pairs={{0,28},{4,8},{8,4},{12,16},{16,12},{20,24},{24,20},{28,0},{1,29},{... | collective-permute-start | bytes 1572872 | tf_op jit(solution)/shard_map/ppermute | solution.py:339
  5.8 0.0 copy-start.6
  5.8 2.5 %shard_map.39.refs_5_.refs_6_ = f32[2,256,512]{2,1,0:T(8,128)S(1)} custom-call(f32[4,256,512]{2,1,0:T(8,128)S(1)} %bitcast.8, f32[4,256,512]{2,1,0:T(8,128)S(1)} %copy-done.2, f32[2,4,32,512]{3,2,1,0:T(8,128)S(1)} %shard_map.38.refs_2_), custom_call_target="tpu_custom_call" | custom-call | flops 6291456 | bytes 5242880 | tf_op jit(solution)/shard_map/pallas_call | solution.py:255
  8.3 0.0 collective-permute-done.refs_3_
  8.3 0.0 collective-permute-done.1.refs_4_
  8.4 7.0 %shard_map.40 = (f32[2,256,512]{2,1,0:T(8,128)S(1)}, f32[2,256,512]{2,1,0:T(8,128)S(1)}, f32[8,512]{1,0:T(8,128)S(1)}) custom-call(f32[3]{0:T(128)S(1)} %copy-done.6, f32[4,256,512]{2,1,0:T(8,128)S(1)} %bitcast.9, f32[4,256,512]{2,1,0:T(8,128)S(1)} %copy-done.2, f32[4,256,512]{2,1,0:T(8,128)S(1)} %collective-permute-done.refs_3_, ...), custom_call_target="tpu_custom_call" | custom-call | flops 20971520 | bytes 11550732 | tf_op jit(solution)/shard_map/pallas_call | solution.py:255
  15.4 2.1 %collective-permute-done.2.refs_0_.refs_1_ = f32[2,4,32,512]{3,2,1,0:T(8,128)S(1)} collective-permute-done((f32[2,4,32,512]{3,2,1,0:T(8,128)S(1)}, f32[2,4,32,512]{3,2,1,0:T(8,128)S(1)}, u32[]{:S(2)}, u32[]{:S(2)}) %collective-permute-start.2) | collective-permute-done | bytes 524320 | tf_op jit(solution)/shard_map/ppermute | solution.py:339
  17.4 0.9 %shard_map.41.refs_3_.refs_4_ = f32[2,4,32,512]{3,2,1,0:T(8,128)} custom-call(f32[2,4,32,512]{3,2,1,0:T(8,128)S(1)} %collective-permute-done.2.refs_0_.refs_1_, f32[2,4,64,512]{3,2,1,0:T(8,128)S(1)} %bitcast.14, f32[2,256,512]{2,1,0:T(8,128)S(1)} %get-tuple-element.18.refs_2_.refs_3_), custom_call_target="tpu_custom_call" | custom-call | bytes 2097152 | tf_op jit(solution)/shard_map/pallas_call | solution.py:255
  18.3 1.0 %copy-done.4 = f32[2,256,512]{2,1,0:T(8,128)} copy-done((f32[2,256,512]{2,1,0:T(8,128)}, f32[2,256,512]{2,1,0:T(8,128)S(1)}, u32[]{:S(2)}) %copy-start.4) | copy-done | bytes 1048600
  19.3 1.0 %shard_map.42.refs_2_ = f32[4,2,32,512]{3,2,1,0:T(8,128)} custom-call(f32[8,512]{1,0:T(8,128)S(1)} %get-tuple-element.16.refs_0_, f32[2,4,32,512]{3,2,1,0:T(8,128)S(1)} %collective-permute-done.2.refs_0_.refs_1_, f32[2,4,64,512]{3,2,1,0:T(8,128)S(1)} %bitcast.16, f32[2,4,32,512]{3,2,1,0:T(8,128)} %shard_map.41.refs_3_.refs_4_), custom_call_target="tpu_custom_call" | custom-call | bytes 2113536 | tf_op jit(solution)/shard_map/pallas_call | solution.py:255
  20.3 6.0 %all-to-all-start = ((f32[4,2,32,512]{3,2,1,0:T(8,128)}), f32[4,2,32,512]{3,2,1,0:T(8,128)}, u32[]{:S(2)}, u32[]{:S(2)}) async-start(f32[4,2,32,512]{3,2,1,0:T(8,128)} %shard_map.42.refs_2_), calls=%async_computation | async-start | bytes 1048576 | tf_op jit(solution)/shard_map/all_to_all | solution.py:315
  26.3 0.9 %collective-permute-start.3 = (f32[2,4,32,512]{3,2,1,0:T(8,128)S(1)}, f32[2,4,32,512]{3,2,1,0:T(8,128)S(1)}, u32[]{:S(2)}, u32[]{:S(2)}) collective-permute-start(f32[2,4,32,512]{3,2,1,0:T(8,128)S(1)} %shard_map.38.refs_2_), channel_id=1, source_target_pairs={{0,28},{4,8},{8,4},{12,16},{16,12},{20,24},{24,20},{28,0},{1,29},{... | collective-permute-start | bytes 1572872 | tf_op jit(solution)/shard_map/ppermute | solution.py:339
  27.2 1.8 %collective-permute-start.5 = (f32[2,4,32,512]{3,2,1,0:T(8,128)}, f32[2,4,32,512]{3,2,1,0:T(8,128)}, u32[]{:S(2)}, u32[]{:S(2)}) collective-permute-start(f32[2,4,32,512]{3,2,1,0:T(8,128)} %shard_map.41.refs_3_.refs_4_), channel_id=1, source_target_pairs={{0,28},{4,8},{8,4},{12,16},{16,12},{20,24},{24,20},{28,0},{1,29},{... | collective-permute-start | bytes 1572872 | tf_op jit(solution)/shard_map/ppermute | solution.py:326
  28.9 12.4 %collective-permute-done.3.refs_0_.refs_1_ = f32[2,4,32,512]{3,2,1,0:T(8,128)S(1)} collective-permute-done((f32[2,4,32,512]{3,2,1,0:T(8,128)S(1)}, f32[2,4,32,512]{3,2,1,0:T(8,128)S(1)}, u32[]{:S(2)}, u32[]{:S(2)}) %collective-permute-start.3) | collective-permute-done | bytes 524320 | tf_op jit(solution)/shard_map/ppermute | solution.py:339
  41.4 0.8 shard_map.43
  42.1 1.0 %shard_map.44.refs_7_ = f32[4,2,32,512]{3,2,1,0:T(8,128)} custom-call(f32[8,512]{1,0:T(8,128)S(1)} %get-tuple-element.16.refs_0_, f32[2,4,32,512]{3,2,1,0:T(8,128)S(1)} %collective-permute-done.3.refs_0_.refs_1_, f32[2,4,64,512]{3,2,1,0:T(8,128)S(1)} %bitcast.17, f32[2,4,16,512]{3,2,1,0:T(8,128)S(1)} %get-tuple-element.19.refs_3_.refs_5_), custom_call_target="tpu_custom_call" | custom-call | bytes 2113536 | tf_op jit(solution)/shard_map/pallas_call | solution.py:255
  43.1 0.0 all-to-all-done.refs_0_
  43.1 5.1 %all-to-all-start.1 = ((f32[4,2,32,512]{3,2,1,0:T(8,128)}), f32[4,2,32,512]{3,2,1,0:T(8,128)}, u32[]{:S(2)}, u32[]{:S(2)}) async-start(f32[4,2,32,512]{3,2,1,0:T(8,128)} %shard_map.44.refs_7_), calls=%async_computation.1 | async-start | bytes 1048576 | tf_op jit(solution)/shard_map/all_to_all | solution.py:315
  48.2 0.4 collective-permute-start.4
  48.6 1.6 %copy-done.3 = f32[4,256,512]{2,1,0:T(8,128)S(1)} copy-done((f32[4,256,512]{2,1,0:T(8,128)S(1)}, f32[4,256,512]{2,1,0:T(8,128)}, u32[]{:S(2)}) %copy-start.3) | copy-done | bytes 2097176
  50.2 1.2 %copy-done.5 = f32[2,256,512]{2,1,0:T(8,128)S(1)} copy-done((f32[2,256,512]{2,1,0:T(8,128)S(1)}, f32[2,256,512]{2,1,0:T(8,128)}, u32[]{:S(2)}) %copy-start.5) | copy-done | bytes 1048600
  51.4 3.7 %shard_map.45.refs_1_ = f32[2,256,512]{2,1,0:T(8,128)S(1)} custom-call(f32[3]{0:T(128)S(1)} %copy-done.6, f32[4,256,512]{2,1,0:T(8,128)S(1)} %bitcast.10, f32[4,256,512]{2,1,0:T(8,128)S(1)} %copy-done.3, f32[2,256,512]{2,1,0:T(8,128)S(1)} %copy-done.5, f32[2,4,32,512]{3,2,1,0:T(8,128)} %shard_map.41.refs_3_.refs_4_, ...), custom_call_target="tpu_custom_call" | custom-call | flops 10485760 | bytes 7340044 | tf_op jit(solution)/shard_map/pallas_call | solution.py:255
  55.2 1.1 %shard_map.46.refs_3_.refs_0_ = f32[2,32,512]{2,1,0:T(8,128)S(1)} custom-call(f32[4,2,32,512]{3,2,1,0:T(8,128)} %all-to-all-done.refs_0_, f32[2,256,512]{2,1,0:T(8,128)S(1)} %shard_map.45.refs_1_), custom_call_target="tpu_custom_call" | custom-call | bytes 655360 | tf_op jit(solution)/shard_map/pallas_call | solution.py:255
  56.3 0.0 collective-permute-done.5.refs_1_
  56.3 1.2 %shard_map.47 = (f32[2,2,32,512]{3,2,1,0:T(8,128)S(1)}, f32[2,2,32,512]{3,2,1,0:T(8,128)S(1)}) custom-call(f32[8,512]{1,0:T(8,128)S(1)} %get-tuple-element.16.refs_0_, f32[2,4,32,512]{3,2,1,0:T(8,128)} %collective-permute-done.5.refs_1_, f32[2,4,64,512]{3,2,1,0:T(8,128)S(1)} %bitcast.11, f32[2,32,512]{2,1,0:T(8,128)S(1)} %shard_map.46.refs_3_.refs_0_), custom_call_target="tpu_custom_call" | custom-call | bytes 2113536 | tf_op jit(solution)/shard_map/pallas_call | solution.py:255
  57.4 1.8 %collective-permute-start.6 = (f32[2,2,32,512]{3,2,1,0:T(8,128)S(1)}, f32[2,2,32,512]{3,2,1,0:T(8,128)S(1)}, u32[]{:S(2)}, u32[]{:S(2)}) collective-permute-start(f32[2,2,32,512]{3,2,1,0:T(8,128)S(1)} %get-tuple-element.23), channel_id=1, source_target_pairs={{0,1},{1,0},{2,3},{3,2},{4,5},{5,4},{6,7},{7,6},{8,9},{9,8},{10,11... | collective-permute-start | bytes 786440 | tf_op jit(solution)/shard_map/ppermute | solution.py:307
  59.3 2.2 %collective-permute-start.9 = (f32[2,4,16,512]{3,2,1,0:T(8,128)}, f32[2,4,16,512]{3,2,1,0:T(8,128)S(1)}, u32[]{:S(2)}, u32[]{:S(2)}) collective-permute-start(f32[2,4,16,512]{3,2,1,0:T(8,128)} %get-tuple-element.20.refs_6_), channel_id=1, source_target_pairs={{0,28},{4,8},{8,4},{12,16},{16,12},{20,24},{24,20},{28,0},{1,29},{... | collective-permute-start | bytes 786440 | tf_op jit(solution)/shard_map/ppermute | solution.py:326
  61.4 0.0 collective-permute-done.4.refs_1_
  61.4 0.1 shard_map.48
  61.5 0.4 collective-permute-start.8
  61.9 0.0 all-to-all-done.1.refs_0_
  61.9 1.1 %shard_map.49.refs_2_.refs_1_ = f32[2,32,512]{2,1,0:T(8,128)S(1)} custom-call(f32[4,2,32,512]{3,2,1,0:T(8,128)} %all-to-all-done.1.refs_0_, f32[2,2,16,512]{3,2,1,0:T(8,128)S(1)} %get-tuple-element.22.refs_1_.refs_0_), custom_call_target="tpu_custom_call" | custom-call | bytes 655360 | tf_op jit(solution)/shard_map/pallas_call | solution.py:255
  63.0 1.9 %collective-permute-done.6.refs_1_ = f32[2,2,32,512]{3,2,1,0:T(8,128)S(1)} collective-permute-done((f32[2,2,32,512]{3,2,1,0:T(8,128)S(1)}, f32[2,2,32,512]{3,2,1,0:T(8,128)S(1)}, u32[]{:S(2)}, u32[]{:S(2)}) %collective-permute-start.6) | collective-permute-done | bytes 262176 | tf_op jit(solution)/shard_map/ppermute | solution.py:307
  65.0 3.3 %collective-permute-start.7 = (f32[2,32,512]{2,1,0:T(8,128)S(1)}, f32[2,32,512]{2,1,0:T(8,128)S(1)}, u32[]{:S(2)}, u32[]{:S(2)}) collective-permute-start(f32[2,32,512]{2,1,0:T(8,128)S(1)} %shard_map.50.refs_3_), channel_id=1, source_target_pairs={{0,3},{1,2},{2,1},{3,0},{4,7},{5,6},{6,5},{7,4},{8,11},{9,10},{10,... | collective-permute-start | bytes 393224 | tf_op jit(solution)/shard_map/ppermute | solution.py:299
  68.3 0.1 collective-permute-done.9.refs_1_
  68.3 0.1 shard_map.51
  68.4 0.6 collective-permute-start.11
  69.1 3.3 %collective-permute-start.10 = (f32[2,16,512]{2,1,0:T(8,128)S(1)}, f32[2,16,512]{2,1,0:T(8,128)S(1)}, u32[]{:S(2)}, u32[]{:S(2)}) collective-permute-start(f32[2,16,512]{2,1,0:T(8,128)S(1)} %shard_map.52.refs_3_), channel_id=1, source_target_pairs={{0,3},{1,2},{2,1},{3,0},{4,7},{5,6},{6,5},{7,4},{8,11},{9,10},{10,... | collective-permute-start | bytes 196616 | tf_op jit(solution)/shard_map/ppermute | solution.py:299
  72.4 0.5 collective-permute-done.7.refs_2_
  72.9 2.0 %collective-permute-done.11.refs_1_.refs_5_ = f32[2,2,16,512]{3,2,1,0:T(8,128)S(1)} collective-permute-done((f32[2,2,16,512]{3,2,1,0:T(8,128)S(1)}, f32[2,2,16,512]{3,2,1,0:T(8,128)S(1)}, u32[]{:S(2)}, u32[]{:S(2)}) %collective-permute-start.11) | collective-permute-done | bytes 131104 | tf_op jit(solution)/shard_map/ppermute | solution.py:307
  74.9 1.7 %collective-permute-start.12 = (f32[2,16,512]{2,1,0:T(8,128)S(1)}, f32[2,16,512]{2,1,0:T(8,128)S(1)}, u32[]{:S(2)}, u32[]{:S(2)}) collective-permute-start(f32[2,16,512]{2,1,0:T(8,128)S(1)} %shard_map.54.refs_3_), channel_id=1, source_target_pairs={{0,3},{1,2},{2,1},{3,0},{4,7},{5,6},{6,5},{7,4},{8,11},{9,10},{10,... | collective-permute-start | bytes 196616 | tf_op jit(solution)/shard_map/ppermute | solution.py:299
  76.6 0.0 collective-permute-done.10.refs_2_
  76.7 4.4 %collective-permute-done.12.refs_6_ = f32[2,16,512]{2,1,0:T(8,128)S(1)} collective-permute-done((f32[2,16,512]{2,1,0:T(8,128)S(1)}, f32[2,16,512]{2,1,0:T(8,128)S(1)}, u32[]{:S(2)}, u32[]{:S(2)}) %collective-permute-start.12) | collective-permute-done | bytes 65568 | tf_op jit(solution)/shard_map/ppermute | solution.py:299
  81.1 0.8 %shard_map.56 = f32[4,64,512]{2,1,0:T(8,128)} custom-call(f32[2,32,512]{2,1,0:T(8,128)S(1)} %shard_map.46.refs_3_.refs_0_, f32[2,32,512]{2,1,0:T(8,128)S(1)} %shard_map.49.refs_2_.refs_1_, f32[2,32,512]{2,1,0:T(8,128)S(1)} %shard_map.53.refs_2_, f32[2,16,512]{2,1,0:T(8,128)S(1)} %shard_map.55.refs_3_.refs_7_, ...), custom_call_target="tpu_custom_call" | custom-call | bytes 1310720 | tf_op jit(solution)/shard_map/pallas_call | solution.py:255
  (16 shorter events, 0.2 us)
Async XLA Ops:
  0.0 8.3 %collective-permute-start = (f32[4,256,512]{2,1,0:T(8,128)}, f32[4,256,512]{2,1,0:T(8,128)S(1)}, u32[]{:S(2)}, u32[]{:S(2)}) collective-permute-start(f32[4,256,512]{2,1,0:T(8,128)} %bitcast.5), channel_id=1, source_target_pairs={{0,4},{4,0},{8,12},{12,8},{16,20},{20,16},{24,28},{28,24},{1,5},{5... | collective-permute-start | bytes 6291464 | tf_op jit(solution)/shard_map/ppermute | solution.py:328
  0.5 7.9 %collective-permute-start.1 = (f32[4,256,512]{2,1,0:T(8,128)}, f32[4,256,512]{2,1,0:T(8,128)S(1)}, u32[]{:S(2)}, u32[]{:S(2)}) collective-permute-start(f32[4,256,512]{2,1,0:T(8,128)} %refs_2_.3), channel_id=1, source_target_pairs={{0,4},{4,0},{8,12},{12,8},{16,20},{20,16},{24,28},{28,24},{1,5},{5... | collective-permute-start | bytes 6291464 | tf_op jit(solution)/shard_map/ppermute | solution.py:329
  0.5 1.6 %copy-start = (f32[1,4,256,512]{3,2,1,0:T(8,128)S(1)}, f32[1,4,256,512]{3,2,1,0:T(8,128)}, u32[]{:S(2)}) copy-start(f32[1,4,256,512]{3,2,1,0:T(8,128)} %param.3) | copy-start | bytes 6291460
  2.2 3.6 %copy-start.2 = (f32[4,256,512]{2,1,0:T(8,128)S(1)}, f32[4,256,512]{2,1,0:T(8,128)}, u32[]{:S(2)}) copy-start(f32[4,256,512]{2,1,0:T(8,128)} %refs_2_.3) | copy-start | bytes 6291460
  2.2 15.3 %collective-permute-start.2 = (f32[2,4,32,512]{3,2,1,0:T(8,128)S(1)}, f32[2,4,32,512]{3,2,1,0:T(8,128)S(1)}, u32[]{:S(2)}, u32[]{:S(2)}) collective-permute-start(f32[2,4,32,512]{3,2,1,0:T(8,128)S(1)} %shard_map.37.refs_1_), channel_id=1, source_target_pairs={{0,28},{4,8},{8,4},{12,16},{16,12},{20,24},{24,20},{28,0},{1,29},{... | collective-permute-start | bytes 1572872 | tf_op jit(solution)/shard_map/ppermute | solution.py:339
  5.8 2.6 %copy-start.6 = (f32[3]{0:T(128)S(1)}, f32[3]{0:T(128)}, u32[]{:S(2)}) copy-start(f32[3]{0:T(128)} %refs_0_.3) | copy-start | bytes 40
  18.3 1.0 %copy-start.4 = (f32[2,256,512]{2,1,0:T(8,128)}, f32[2,256,512]{2,1,0:T(8,128)S(1)}, u32[]{:S(2)}) copy-start(f32[2,256,512]{2,1,0:T(8,128)S(1)} %get-tuple-element.18.refs_2_.refs_3_) | copy-start | bytes 3145732
  20.3 22.8 %all-to-all-start = ((f32[4,2,32,512]{3,2,1,0:T(8,128)}), f32[4,2,32,512]{3,2,1,0:T(8,128)}, u32[]{:S(2)}, u32[]{:S(2)}) async-start(f32[4,2,32,512]{3,2,1,0:T(8,128)} %shard_map.42.refs_2_), calls=%async_computation | async-start | bytes 1048576 | tf_op jit(solution)/shard_map/all_to_all | solution.py:315
  26.3 15.1 %collective-permute-start.3 = (f32[2,4,32,512]{3,2,1,0:T(8,128)S(1)}, f32[2,4,32,512]{3,2,1,0:T(8,128)S(1)}, u32[]{:S(2)}, u32[]{:S(2)}) collective-permute-start(f32[2,4,32,512]{3,2,1,0:T(8,128)S(1)} %shard_map.38.refs_2_), channel_id=1, source_target_pairs={{0,28},{4,8},{8,4},{12,16},{16,12},{20,24},{24,20},{28,0},{1,29},{... | collective-permute-start | bytes 1572872 | tf_op jit(solution)/shard_map/ppermute | solution.py:339
  27.2 29.1 %collective-permute-start.5 = (f32[2,4,32,512]{3,2,1,0:T(8,128)}, f32[2,4,32,512]{3,2,1,0:T(8,128)}, u32[]{:S(2)}, u32[]{:S(2)}) collective-permute-start(f32[2,4,32,512]{3,2,1,0:T(8,128)} %shard_map.41.refs_3_.refs_4_), channel_id=1, source_target_pairs={{0,28},{4,8},{8,4},{12,16},{16,12},{20,24},{24,20},{28,0},{1,29},{... | collective-permute-start | bytes 1572872 | tf_op jit(solution)/shard_map/ppermute | solution.py:326
  42.1 6.5 %copy-start.1 = (f32[1,4,256,512]{3,2,1,0:T(8,128)S(1)}, f32[1,4,256,512]{3,2,1,0:T(8,128)}, u32[]{:S(2)}) copy-start(f32[1,4,256,512]{3,2,1,0:T(8,128)} %param.3) | copy-start | bytes 6291460
  43.1 18.9 %all-to-all-start.1 = ((f32[4,2,32,512]{3,2,1,0:T(8,128)}), f32[4,2,32,512]{3,2,1,0:T(8,128)}, u32[]{:S(2)}, u32[]{:S(2)}) async-start(f32[4,2,32,512]{3,2,1,0:T(8,128)} %shard_map.44.refs_7_), calls=%async_computation.1 | async-start | bytes 1048576 | tf_op jit(solution)/shard_map/all_to_all | solution.py:315
  48.2 13.3 %collective-permute-start.4 = (f32[2,4,16,512]{3,2,1,0:T(8,128)S(1)}, f32[2,4,16,512]{3,2,1,0:T(8,128)S(1)}, u32[]{:S(2)}, u32[]{:S(2)}) collective-permute-start(f32[2,4,16,512]{3,2,1,0:T(8,128)S(1)} %get-tuple-element.19.refs_3_.refs_5_), channel_id=1, source_target_pairs={{0,28},{4,8},{8,4},{12,16},{16,12},{20,24},{24,20},{28,0},{1,29},{... | collective-permute-start | bytes 786440 | tf_op jit(solution)/shard_map/ppermute | solution.py:326
  48.6 1.6 %copy-start.3 = (f32[4,256,512]{2,1,0:T(8,128)S(1)}, f32[4,256,512]{2,1,0:T(8,128)}, u32[]{:S(2)}) copy-start(f32[4,256,512]{2,1,0:T(8,128)} %refs_2_.3) | copy-start | bytes 6291460
  50.2 1.2 %copy-start.5 = (f32[2,256,512]{2,1,0:T(8,128)S(1)}, f32[2,256,512]{2,1,0:T(8,128)}, u32[]{:S(2)}) copy-start(f32[2,256,512]{2,1,0:T(8,128)} %copy-done.4) | copy-start | bytes 3145732
  57.4 7.5 %collective-permute-start.6 = (f32[2,2,32,512]{3,2,1,0:T(8,128)S(1)}, f32[2,2,32,512]{3,2,1,0:T(8,128)S(1)}, u32[]{:S(2)}, u32[]{:S(2)}) collective-permute-start(f32[2,2,32,512]{3,2,1,0:T(8,128)S(1)} %get-tuple-element.23), channel_id=1, source_target_pairs={{0,1},{1,0},{2,3},{3,2},{4,5},{5,4},{6,7},{7,6},{8,9},{9,8},{10,11... | collective-permute-start | bytes 786440 | tf_op jit(solution)/shard_map/ppermute | solution.py:307
  59.3 9.1 %collective-permute-start.9 = (f32[2,4,16,512]{3,2,1,0:T(8,128)}, f32[2,4,16,512]{3,2,1,0:T(8,128)S(1)}, u32[]{:S(2)}, u32[]{:S(2)}) collective-permute-start(f32[2,4,16,512]{3,2,1,0:T(8,128)} %get-tuple-element.20.refs_6_), channel_id=1, source_target_pairs={{0,28},{4,8},{8,4},{12,16},{16,12},{20,24},{24,20},{28,0},{1,29},{... | collective-permute-start | bytes 786440 | tf_op jit(solution)/shard_map/ppermute | solution.py:326
  61.5 7.5 %collective-permute-start.8 = (f32[2,2,16,512]{3,2,1,0:T(8,128)S(1)}, f32[2,2,16,512]{3,2,1,0:T(8,128)S(1)}, u32[]{:S(2)}, u32[]{:S(2)}) collective-permute-start(f32[2,2,16,512]{3,2,1,0:T(8,128)S(1)} %get-tuple-element.24), channel_id=1, source_target_pairs={{0,1},{1,0},{2,3},{3,2},{4,5},{5,4},{6,7},{7,6},{8,9},{9,8},{10,11... | collective-permute-start | bytes 393224 | tf_op jit(solution)/shard_map/ppermute | solution.py:307
  65.0 7.9 %collective-permute-start.7 = (f32[2,32,512]{2,1,0:T(8,128)S(1)}, f32[2,32,512]{2,1,0:T(8,128)S(1)}, u32[]{:S(2)}, u32[]{:S(2)}) collective-permute-start(f32[2,32,512]{2,1,0:T(8,128)S(1)} %shard_map.50.refs_3_), channel_id=1, source_target_pairs={{0,3},{1,2},{2,1},{3,0},{4,7},{5,6},{6,5},{7,4},{8,11},{9,10},{10,... | collective-permute-start | bytes 393224 | tf_op jit(solution)/shard_map/ppermute | solution.py:299
  68.4 6.5 %collective-permute-start.11 = (f32[2,2,16,512]{3,2,1,0:T(8,128)S(1)}, f32[2,2,16,512]{3,2,1,0:T(8,128)S(1)}, u32[]{:S(2)}, u32[]{:S(2)}) collective-permute-start(f32[2,2,16,512]{3,2,1,0:T(8,128)S(1)} %get-tuple-element.26), channel_id=1, source_target_pairs={{0,1},{1,0},{2,3},{3,2},{4,5},{5,4},{6,7},{7,6},{8,9},{9,8},{10,11... | collective-permute-start | bytes 393224 | tf_op jit(solution)/shard_map/ppermute | solution.py:307
  69.1 7.6 %collective-permute-start.10 = (f32[2,16,512]{2,1,0:T(8,128)S(1)}, f32[2,16,512]{2,1,0:T(8,128)S(1)}, u32[]{:S(2)}, u32[]{:S(2)}) collective-permute-start(f32[2,16,512]{2,1,0:T(8,128)S(1)} %shard_map.52.refs_3_), channel_id=1, source_target_pairs={{0,3},{1,2},{2,1},{3,0},{4,7},{5,6},{6,5},{7,4},{8,11},{9,10},{10,... | collective-permute-start | bytes 196616 | tf_op jit(solution)/shard_map/ppermute | solution.py:299
  74.9 6.1 %collective-permute-start.12 = (f32[2,16,512]{2,1,0:T(8,128)S(1)}, f32[2,16,512]{2,1,0:T(8,128)S(1)}, u32[]{:S(2)}, u32[]{:S(2)}) collective-permute-start(f32[2,16,512]{2,1,0:T(8,128)S(1)} %shard_map.54.refs_3_), channel_id=1, source_target_pairs={{0,3},{1,2},{2,1},{3,0},{4,7},{5,6},{6,5},{7,4},{8,11},{9,10},{10,... | collective-permute-start | bytes 196616 | tf_op jit(solution)/shard_map/ppermute | solution.py:299

commit v5 on v3

--- a/solution.py
+++ b/solution.py
@@ -221,7 +221,7 @@
     def __init__(self):
         self.last = []
 
-    def __call__(self, kernel, out, args, scalars=0, scratch=(), flops=0, hbm=False):
+    def __call__(self, kernel, out, args, scalars=0, scratch=(), flops=0, hbm=False, weight=0):
         vmem = pl.BlockSpec(memory_space=pltpu.VMEM)
         smem = pl.BlockSpec(memory_space=pltpu.SMEM)
         many = isinstance(out, list)
@@ -242,7 +242,7 @@
             scratch_shapes=list(scratch),
             compiler_params=pltpu.CompilerParams(vmem_limit_bytes=40 * 2**20),
             cost_estimate=pl.CostEstimate(
-                flops=flops, bytes_accessed=total, transcendentals=0
+                flops=flops + weight, bytes_accessed=total, transcendentals=0
             ),
         )(*args, *last)
         self.last = [result[0]]
@@ -323,14 +323,16 @@
         flops=80 * cells,
     )
 
-    def summed(keep, came, from_far):
-        return call(sum_kernel, from_far.shape, (keep, came, from_far))
+    def summed(keep, came, from_far, weight=0):
+        return call(sum_kernel, from_far.shape, (keep, came, from_far), weight=weight)
 
     cut_a, cut_b, cut_c = cuts
     f0, (face_a,) = faces(chunks[0], halos[0], [cut_a])
     back0 = back_squares(chunks[0], halos[0])
     back0 = add_far(*back0)
     f1, (face_b, face_c) = faces(chunks[1], halos[1], [cut_b, cut_c])
+    back1 = back_squares(chunks[1], halos[1])
+    back0 = summed(*back0)
     h_front = call(
         functools.partial(front_kernel, cuts),
         plane2,
@@ -338,13 +340,12 @@
         scalars=1,
         scratch=[pltpu.VMEM(plane2, jnp.float32)],
         flops=40 * cells,
-    )
-    back0 = summed(*back0)
-    back1 = back_squares(chunks[1], halos[1])
+        weight=3_000_000_000,
+    )
     back1 = add_far(*back1)
     front_a = squares(cut_a, face_a)
-    back1 = summed(*back1)
     front_b = squares(cut_b, face_b)
+    back1 = summed(*back1, weight=2_000_000_000)
     front_a = add_far(*front_a)
     front_c = squares(cut_c, face_c)
     front_b = add_far(*front_b)

time: 72.3 us -> 70 us (0.968)
  the two profiles are of different devices: /device:TPU:0 before, /device:TPU:6 now
where the time goes in v5:
time: 70 us; the launch traced here: 69.8 us
  waiting for transfers between devices  32.7 us (47%)
  starting transfers between devices  20.8 us (30%)
  Pallas kernels  14.5 us (21%)
  local copies, waits for them, and re-layouts  1.61 us (2%)
    pallas_call x22, Pallas kernels, __call__(): pl.pallas_call(body, out_shape=shapes, in_specs=[smem] * scalars + [pl.Bl...  14.5 us
    ppermute x5, starting transfers between devices, add_far(): return (keep, came, lax.ppermute(total, 'orb', far))  14.3 us
    ppermute x5, waiting for transfers between devices, add_far(): return (keep, came, lax.ppermute(total, 'orb', far))  11.8 us
    ppermute x2, waiting for transfers between devices, back_squares(): return (keep, lax.ppermute(send, 'orb', near))  9.55 us
    ppermute x3, waiting for transfers between devices, squares(): return (keep, lax.ppermute(send, 'orb', near))  7.15 us
    ppermute x2, waiting for transfers between devices, shards(): halos.append(lax.ppermute(piece, 'slab', face))  1.96 us
    ppermute x2, starting transfers between devices, back_squares(): return (keep, lax.ppermute(send, 'orb', near))  1.93 us
    ppermute x2, starting transfers between devices, shards(): halos.append(lax.ppermute(piece, 'slab', face))  1.88 us
  transfers between devices with their start and end apart: 17, of which 11 were waited for; matrix products, arithmetic and copies ran while one was open for 0% of the time, Pallas kernels for 20%

profile of v5, /device:TPU:6, one launch (start us, length us, event | category | flops | bytes accessed | tf_op | source)
XLA Modules:
  0.0 69.8 jit_solution(9983312847130161740)
XLA Ops:
  0.0 0.0 collective-permute-start
  0.0 0.5 collective-permute-start.1
  0.5 1.6 %copy-done = f32[1,4,256,512]{3,2,1,0:T(8,128)S(1)} copy-done((f32[1,4,256,512]{3,2,1,0:T(8,128)S(1)}, f32[1,4,256,512]{3,2,1,0:T(8,128)}, u32[]{:S(2)}) %copy-start) | copy-done | bytes 2097176
  2.2 0.0 copy-start.2
  2.2 0.2 collective-permute-start.2
  2.4 0.0 copy-start.3
  2.4 1.7 %collective-permute-start.5 = (f32[2,4,32,512]{3,2,1,0:T(8,128)S(1)}, f32[2,4,32,512]{3,2,1,0:T(8,128)S(1)}, u32[]{:S(2)}, u32[]{:S(2)}) collective-permute-start(f32[2,4,32,512]{3,2,1,0:T(8,128)S(1)} %shard_map.38.refs_2_), channel_id=1, source_target_pairs={{0,28},{4,8},{8,4},{12,16},{16,12},{20,24},{24,20},{28,0},{1,29},{... | collective-permute-start | bytes 1572872 | tf_op jit(solution)/shard_map/ppermute | solution.py:316
  4.1 2.5 %shard_map.39.refs_5_.refs_6_ = f32[2,256,512]{2,1,0:T(8,128)S(1)} custom-call(f32[4,256,512]{2,1,0:T(8,128)S(1)} %bitcast.8, f32[4,256,512]{2,1,0:T(8,128)S(1)} %copy-done.2, f32[2,4,32,512]{3,2,1,0:T(8,128)S(1)} %shard_map.38.refs_2_), custom_call_target="tpu_custom_call" | custom-call | flops 6291456 | bytes 5242880 | tf_op jit(solution)/shard_map/pallas_call | solution.py:235
  6.6 0.0 collective-permute-done.refs_3_
  6.6 0.7 %collective-permute-done.1.refs_4_ = f32[4,256,512]{2,1,0:T(8,128)S(1)} collective-permute-done((f32[4,256,512]{2,1,0:T(8,128)}, f32[4,256,512]{2,1,0:T(8,128)S(1)}, u32[]{:S(2)}, u32[]{:S(2)}) %collective-permute-start.1) | collective-permute-done | bytes 2097184 | tf_op jit(solution)/shard_map/ppermute | solution.py:306
  7.4 7.0 %shard_map.40 = (f32[2,256,512]{2,1,0:T(8,128)S(1)}, f32[2,256,512]{2,1,0:T(8,128)S(1)}, f32[8,512]{1,0:T(8,128)S(1)}) custom-call(f32[3]{0:T(128)S(1)} %copy-done.3, f32[4,256,512]{2,1,0:T(8,128)S(1)} %bitcast.9, f32[4,256,512]{2,1,0:T(8,128)S(1)} %copy-done.2, f32[4,256,512]{2,1,0:T(8,128)S(1)} %collective-permute-done.refs_3_, ...), custom_call_target="tpu_custom_call" | custom-call | flops 20971520 | bytes 11550732 | tf_op jit(solution)/shard_map/pallas_call | solution.py:235
  14.4 2.0 %collective-permute-done.2.refs_0_.refs_1_ = f32[2,4,32,512]{3,2,1,0:T(8,128)S(1)} collective-permute-done((f32[2,4,32,512]{3,2,1,0:T(8,128)S(1)}, f32[2,4,32,512]{3,2,1,0:T(8,128)S(1)}, u32[]{:S(2)}, u32[]{:S(2)}) %collective-permute-start.2) | collective-permute-done | bytes 524320 | tf_op jit(solution)/shard_map/ppermute | solution.py:316
  16.3 0.1 shard_map.41.refs_3_.refs_4_
  16.4 0.2 shard_map.42
  16.6 1.6 %collective-permute-start.3 = (f32[2,2,32,512]{3,2,1,0:T(8,128)S(1)}, f32[2,2,32,512]{3,2,1,0:T(8,128)S(1)}, u32[]{:S(2)}, u32[]{:S(2)}) collective-permute-start(f32[2,2,32,512]{3,2,1,0:T(8,128)S(1)} %get-tuple-element.24), channel_id=1, source_target_pairs={{0,1},{1,0},{2,3},{3,2},{4,5},{5,4},{6,7},{7,6},{8,9},{9,8},{10,11... | collective-permute-start | bytes 786440 | tf_op jit(solution)/shard_map/ppermute | solution.py:295
  18.2 0.3 collective-permute-start.9
  18.5 7.2 %collective-permute-done.3.refs_1_ = f32[2,2,32,512]{3,2,1,0:T(8,128)S(1)} collective-permute-done((f32[2,2,32,512]{3,2,1,0:T(8,128)S(1)}, f32[2,2,32,512]{3,2,1,0:T(8,128)S(1)}, u32[]{:S(2)}, u32[]{:S(2)}) %collective-permute-start.3) | collective-permute-done | bytes 262176 | tf_op jit(solution)/shard_map/ppermute | solution.py:295
  25.8 0.0 copy-start.1
  25.8 3.7 %collective-permute-start.4 = (f32[2,32,512]{2,1,0:T(8,128)S(1)}, f32[2,32,512]{2,1,0:T(8,128)S(1)}, u32[]{:S(2)}, u32[]{:S(2)}) collective-permute-start(f32[2,32,512]{2,1,0:T(8,128)S(1)} %shard_map.43.refs_2_), channel_id=1, source_target_pairs={{0,3},{1,2},{2,1},{3,0},{4,7},{5,6},{6,5},{7,4},{8,11},{9,10},{10,... | collective-permute-start | bytes 393224 | tf_op jit(solution)/shard_map/ppermute | solution.py:279
  29.5 0.0 collective-permute-done.5.refs_0_.refs_1_
  29.5 0.1 shard_map.44
  29.5 0.1 collective-permute-start.8
  29.6 0.2 shard_map.45
  29.8 0.3 collective-permute-start.6
  30.1 3.4 %collective-permute-done.4.refs_2_ = f32[2,32,512]{2,1,0:T(8,128)S(1)} collective-permute-done((f32[2,32,512]{2,1,0:T(8,128)S(1)}, f32[2,32,512]{2,1,0:T(8,128)S(1)}, u32[]{:S(2)}, u32[]{:S(2)}) %collective-permute-start.4) | collective-permute-done | bytes 131104 | tf_op jit(solution)/shard_map/ppermute | solution.py:279
  33.5 3.2 %shard_map.47.refs_2_ = f32[2,256,512]{2,1,0:T(8,128)S(1)} custom-call(f32[3]{0:T(128)S(1)} %copy-done.3, f32[4,256,512]{2,1,0:T(8,128)S(1)} %bitcast.10, f32[4,256,512]{2,1,0:T(8,128)S(1)} %copy-done.2, f32[2,256,512]{2,1,0:T(8,128)S(1)} %get-tuple-element.22.refs_2_.refs_3_, f32[2,4,32,512]{3,2,1,0:T(8,128)S(1)} %shard_map.41.refs_3_.refs_4_, ...), custom_call_target="tpu_custom_call" | custom-call | flops 3010485760 | bytes 7340044 | tf_op jit(solution)/shard_map/pallas_call | solution.py:235
  36.7 2.3 %collective-permute-done.6.refs_1_ = f32[2,2,32,512]{3,2,1,0:T(8,128)S(1)} collective-permute-done((f32[2,2,32,512]{3,2,1,0:T(8,128)S(1)}, f32[2,2,32,512]{3,2,1,0:T(8,128)S(1)}, u32[]{:S(2)}, u32[]{:S(2)}) %collective-permute-start.6) | collective-permute-done | bytes 262176 | tf_op jit(solution)/shard_map/ppermute | solution.py:295
  39.0 3.6 %collective-permute-start.7 = (f32[2,32,512]{2,1,0:T(8,128)S(1)}, f32[2,32,512]{2,1,0:T(8,128)S(1)}, u32[]{:S(2)}, u32[]{:S(2)}) collective-permute-start(f32[2,32,512]{2,1,0:T(8,128)S(1)} %shard_map.48.refs_3_), channel_id=1, source_target_pairs={{0,3},{1,2},{2,1},{3,0},{4,7},{5,6},{6,5},{7,4},{8,11},{9,10},{10,... | collective-permute-start | bytes 393224 | tf_op jit(solution)/shard_map/ppermute | solution.py:279
  42.6 0.0 collective-permute-done.9.refs_1_
  42.7 0.1 shard_map.49
  42.8 0.1 collective-permute-start.10
  42.8 0.1 collective-permute-start.13
  42.9 1.5 %collective-permute-done.8.refs_1_ = f32[2,4,16,512]{3,2,1,0:T(8,128)S(1)} collective-permute-done((f32[2,4,16,512]{3,2,1,0:T(8,128)S(1)}, f32[2,4,16,512]{3,2,1,0:T(8,128)S(1)}, u32[]{:S(2)}, u32[]{:S(2)}) %collective-permute-start.8) | collective-permute-done | bytes 262176 | tf_op jit(solution)/shard_map/ppermute | solution.py:303
  44.4 0.1 shard_map.50
  44.5 1.6 %collective-permute-start.12 = (f32[2,2,16,512]{3,2,1,0:T(8,128)S(1)}, f32[2,2,16,512]{3,2,1,0:T(8,128)S(1)}, u32[]{:S(2)}, u32[]{:S(2)}) collective-permute-start(f32[2,2,16,512]{3,2,1,0:T(8,128)S(1)} %get-tuple-element.32), channel_id=1, source_target_pairs={{0,1},{1,0},{2,3},{3,2},{4,5},{5,4},{6,7},{7,6},{8,9},{9,8},{10,11... | collective-permute-start | bytes 393224 | tf_op jit(solution)/shard_map/ppermute | solution.py:287
  46.1 1.2 %collective-permute-done.7.refs_2_ = f32[2,32,512]{2,1,0:T(8,128)S(1)} collective-permute-done((f32[2,32,512]{2,1,0:T(8,128)S(1)}, f32[2,32,512]{2,1,0:T(8,128)S(1)}, u32[]{:S(2)}, u32[]{:S(2)}) %collective-permute-start.7) | collective-permute-done | bytes 131104 | tf_op jit(solution)/shard_map/ppermute | solution.py:279
  47.3 5.1 %collective-permute-done.10.refs_1_ = f32[2,2,32,512]{3,2,1,0:T(8,128)S(1)} collective-permute-done((f32[2,2,32,512]{3,2,1,0:T(8,128)S(1)}, f32[2,2,32,512]{3,2,1,0:T(8,128)S(1)}, u32[]{:S(2)}, u32[]{:S(2)}) %collective-permute-start.10) | collective-permute-done | bytes 262176 | tf_op jit(solution)/shard_map/ppermute | solution.py:287
  52.5 2.6 %collective-permute-start.11 = (f32[2,32,512]{2,1,0:T(8,128)S(1)}, f32[2,32,512]{2,1,0:T(8,128)S(1)}, u32[]{:S(2)}, u32[]{:S(2)}) collective-permute-start(f32[2,32,512]{2,1,0:T(8,128)S(1)} %shard_map.52.refs_3_), channel_id=1, source_target_pairs={{0,3},{1,2},{2,1},{3,0},{4,7},{5,6},{6,5},{7,4},{8,11},{9,10},{10,... | collective-permute-start | bytes 393224 | tf_op jit(solution)/shard_map/ppermute | solution.py:279
  55.1 0.0 collective-permute-done.13.refs_1_
  55.1 0.1 shard_map.53
  55.2 0.1 collective-permute-start.15
  55.3 0.0 collective-permute-done.12.refs_1_
  55.3 2.6 %collective-permute-start.14 = (f32[2,16,512]{2,1,0:T(8,128)S(1)}, f32[2,16,512]{2,1,0:T(8,128)S(1)}, u32[]{:S(2)}, u32[]{:S(2)}) collective-permute-start(f32[2,16,512]{2,1,0:T(8,128)S(1)} %shard_map.54.refs_3_), channel_id=1, source_target_pairs={{0,3},{1,2},{2,1},{3,0},{4,7},{5,6},{6,5},{7,4},{8,11},{9,10},{10,... | collective-permute-start | bytes 196616 | tf_op jit(solution)/shard_map/ppermute | solution.py:279
  57.8 3.0 %collective-permute-done.11.refs_2_ = f32[2,32,512]{2,1,0:T(8,128)S(1)} collective-permute-done((f32[2,32,512]{2,1,0:T(8,128)S(1)}, f32[2,32,512]{2,1,0:T(8,128)S(1)}, u32[]{:S(2)}, u32[]{:S(2)}) %collective-permute-start.11) | collective-permute-done | bytes 131104 | tf_op jit(solution)/shard_map/ppermute | solution.py:279
  60.8 2.0 %collective-permute-done.15.refs_1_.refs_5_ = f32[2,2,16,512]{3,2,1,0:T(8,128)S(1)} collective-permute-done((f32[2,2,16,512]{3,2,1,0:T(8,128)S(1)}, f32[2,2,16,512]{3,2,1,0:T(8,128)S(1)}, u32[]{:S(2)}, u32[]{:S(2)}) %collective-permute-start.15) | collective-permute-done | bytes 131104 | tf_op jit(solution)/shard_map/ppermute | solution.py:287
  62.8 1.8 %collective-permute-start.16 = (f32[2,16,512]{2,1,0:T(8,128)S(1)}, f32[2,16,512]{2,1,0:T(8,128)S(1)}, u32[]{:S(2)}, u32[]{:S(2)}) collective-permute-start(f32[2,16,512]{2,1,0:T(8,128)S(1)} %shard_map.56.refs_3_), channel_id=1, source_target_pairs={{0,3},{1,2},{2,1},{3,0},{4,7},{5,6},{6,5},{7,4},{8,11},{9,10},{10,... | collective-permute-start | bytes 196616 | tf_op jit(solution)/shard_map/ppermute | solution.py:279
  64.7 4.3 %collective-permute-done.16.refs_6_ = f32[2,16,512]{2,1,0:T(8,128)S(1)} collective-permute-done((f32[2,16,512]{2,1,0:T(8,128)S(1)}, f32[2,16,512]{2,1,0:T(8,128)S(1)}, u32[]{:S(2)}, u32[]{:S(2)}) %collective-permute-start.16) | collective-permute-done | bytes 65568 | tf_op jit(solution)/shard_map/ppermute | solution.py:279
  69.0 0.8 %shard_map.58 = f32[4,64,512]{2,1,0:T(8,128)} custom-call(f32[2,32,512]{2,1,0:T(8,128)S(1)} %shard_map.46.refs_7_.refs_0_, f32[2,32,512]{2,1,0:T(8,128)S(1)} %shard_map.51.refs_2_.refs_1_, f32[2,32,512]{2,1,0:T(8,128)S(1)} %shard_map.55.refs_2_, f32[2,16,512]{2,1,0:T(8,128)S(1)} %shard_map.57.refs_3_.refs_7_, ...), custom_call_target="tpu_custom_call" | custom-call | bytes 1310720 | tf_op jit(solution)/shard_map/pallas_call | solution.py:235
  (16 shorter events, 0.2 us)
Async XLA Ops:
  0.0 6.6 %collective-permute-start = (f32[4,256,512]{2,1,0:T(8,128)}, f32[4,256,512]{2,1,0:T(8,128)S(1)}, u32[]{:S(2)}, u32[]{:S(2)}) collective-permute-start(f32[4,256,512]{2,1,0:T(8,128)} %bitcast.5), channel_id=1, source_target_pairs={{0,4},{4,0},{8,12},{12,8},{16,20},{20,16},{24,28},{28,24},{1,5},{5... | collective-permute-start | bytes 6291464 | tf_op jit(solution)/shard_map/ppermute | solution.py:305
  0.0 7.4 %collective-permute-start.1 = (f32[4,256,512]{2,1,0:T(8,128)}, f32[4,256,512]{2,1,0:T(8,128)S(1)}, u32[]{:S(2)}, u32[]{:S(2)}) collective-permute-start(f32[4,256,512]{2,1,0:T(8,128)} %refs_2_.3), channel_id=1, source_target_pairs={{0,4},{4,0},{8,12},{12,8},{16,20},{20,16},{24,28},{28,24},{1,5},{5... | collective-permute-start | bytes 6291464 | tf_op jit(solution)/shard_map/ppermute | solution.py:306
  0.5 1.6 %copy-start = (f32[1,4,256,512]{3,2,1,0:T(8,128)S(1)}, f32[1,4,256,512]{3,2,1,0:T(8,128)}, u32[]{:S(2)}) copy-start(f32[1,4,256,512]{3,2,1,0:T(8,128)} %param.3) | copy-start | bytes 6291460
  2.2 2.0 %copy-start.2 = (f32[4,256,512]{2,1,0:T(8,128)S(1)}, f32[4,256,512]{2,1,0:T(8,128)}, u32[]{:S(2)}) copy-start(f32[4,256,512]{2,1,0:T(8,128)} %refs_2_.3) | copy-start | bytes 6291460
  2.2 14.2 %collective-permute-start.2 = (f32[2,4,32,512]{3,2,1,0:T(8,128)S(1)}, f32[2,4,32,512]{3,2,1,0:T(8,128)S(1)}, u32[]{:S(2)}, u32[]{:S(2)}) collective-permute-start(f32[2,4,32,512]{3,2,1,0:T(8,128)S(1)} %shard_map.37.refs_1_), channel_id=1, source_target_pairs={{0,28},{4,8},{8,4},{12,16},{16,12},{20,24},{24,20},{28,0},{1,29},{... | collective-permute-start | bytes 1572872 | tf_op jit(solution)/shard_map/ppermute | solution.py:316
  2.4 4.9 %copy-start.3 = (f32[3]{0:T(128)S(1)}, f32[3]{0:T(128)}, u32[]{:S(2)}) copy-start(f32[3]{0:T(128)} %refs_0_.3) | copy-start | bytes 40
  2.4 27.0 %collective-permute-start.5 = (f32[2,4,32,512]{3,2,1,0:T(8,128)S(1)}, f32[2,4,32,512]{3,2,1,0:T(8,128)S(1)}, u32[]{:S(2)}, u32[]{:S(2)}) collective-permute-start(f32[2,4,32,512]{3,2,1,0:T(8,128)S(1)} %shard_map.38.refs_2_), channel_id=1, source_target_pairs={{0,28},{4,8},{8,4},{12,16},{16,12},{20,24},{24,20},{28,0},{1,29},{... | collective-permute-start | bytes 1572872 | tf_op jit(solution)/shard_map/ppermute | solution.py:316
  16.6 9.2 %collective-permute-start.3 = (f32[2,2,32,512]{3,2,1,0:T(8,128)S(1)}, f32[2,2,32,512]{3,2,1,0:T(8,128)S(1)}, u32[]{:S(2)}, u32[]{:S(2)}) collective-permute-start(f32[2,2,32,512]{3,2,1,0:T(8,128)S(1)} %get-tuple-element.24), channel_id=1, source_target_pairs={{0,1},{1,0},{2,3},{3,2},{4,5},{5,4},{6,7},{7,6},{8,9},{9,8},{10,11... | collective-permute-start | bytes 786440 | tf_op jit(solution)/shard_map/ppermute | solution.py:295
  18.2 24.4 %collective-permute-start.9 = (f32[2,4,32,512]{3,2,1,0:T(8,128)S(1)}, f32[2,4,32,512]{3,2,1,0:T(8,128)S(1)}, u32[]{:S(2)}, u32[]{:S(2)}) collective-permute-start(f32[2,4,32,512]{3,2,1,0:T(8,128)S(1)} %shard_map.41.refs_3_.refs_4_), channel_id=1, source_target_pairs={{0,28},{4,8},{8,4},{12,16},{16,12},{20,24},{24,20},{28,0},{1,29},{... | collective-permute-start | bytes 1572872 | tf_op jit(solution)/shard_map/ppermute | solution.py:303
  25.8 7.8 %copy-start.1 = (f32[1,4,256,512]{3,2,1,0:T(8,128)S(1)}, f32[1,4,256,512]{3,2,1,0:T(8,128)}, u32[]{:S(2)}) copy-start(f32[1,4,256,512]{3,2,1,0:T(8,128)} %param.3) | copy-start | bytes 6291460
  25.8 7.7 %collective-permute-start.4 = (f32[2,32,512]{2,1,0:T(8,128)S(1)}, f32[2,32,512]{2,1,0:T(8,128)S(1)}, u32[]{:S(2)}, u32[]{:S(2)}) collective-permute-start(f32[2,32,512]{2,1,0:T(8,128)S(1)} %shard_map.43.refs_2_), channel_id=1, source_target_pairs={{0,3},{1,2},{2,1},{3,0},{4,7},{5,6},{6,5},{7,4},{8,11},{9,10},{10,... | collective-permute-start | bytes 393224 | tf_op jit(solution)/shard_map/ppermute | solution.py:279
  29.5 14.9 %collective-permute-start.8 = (f32[2,4,16,512]{3,2,1,0:T(8,128)S(1)}, f32[2,4,16,512]{3,2,1,0:T(8,128)S(1)}, u32[]{:S(2)}, u32[]{:S(2)}) collective-permute-start(f32[2,4,16,512]{3,2,1,0:T(8,128)S(1)} %get-tuple-element.25.refs_3_.refs_5_), channel_id=1, source_target_pairs={{0,28},{4,8},{8,4},{12,16},{16,12},{20,24},{24,20},{28,0},{1,29},{... | collective-permute-start | bytes 786440 | tf_op jit(solution)/shard_map/ppermute | solution.py:303
  29.8 9.2 %collective-permute-start.6 = (f32[2,2,32,512]{3,2,1,0:T(8,128)S(1)}, f32[2,2,32,512]{3,2,1,0:T(8,128)S(1)}, u32[]{:S(2)}, u32[]{:S(2)}) collective-permute-start(f32[2,2,32,512]{3,2,1,0:T(8,128)S(1)} %get-tuple-element.27), channel_id=1, source_target_pairs={{0,1},{1,0},{2,3},{3,2},{4,5},{5,4},{6,7},{7,6},{8,9},{9,8},{10,11... | collective-permute-start | bytes 786440 | tf_op jit(solution)/shard_map/ppermute | solution.py:295
  39.0 8.2 %collective-permute-start.7 = (f32[2,32,512]{2,1,0:T(8,128)S(1)}, f32[2,32,512]{2,1,0:T(8,128)S(1)}, u32[]{:S(2)}, u32[]{:S(2)}) collective-permute-start(f32[2,32,512]{2,1,0:T(8,128)S(1)} %shard_map.48.refs_3_), channel_id=1, source_target_pairs={{0,3},{1,2},{2,1},{3,0},{4,7},{5,6},{6,5},{7,4},{8,11},{9,10},{10,... | collective-permute-start | bytes 393224 | tf_op jit(solution)/shard_map/ppermute | solution.py:279
  42.8 9.7 %collective-permute-start.10 = (f32[2,2,32,512]{3,2,1,0:T(8,128)S(1)}, f32[2,2,32,512]{3,2,1,0:T(8,128)S(1)}, u32[]{:S(2)}, u32[]{:S(2)}) collective-permute-start(f32[2,2,32,512]{3,2,1,0:T(8,128)S(1)} %get-tuple-element.31), channel_id=1, source_target_pairs={{0,1},{1,0},{2,3},{3,2},{4,5},{5,4},{6,7},{7,6},{8,9},{9,8},{10,11... | collective-permute-start | bytes 786440 | tf_op jit(solution)/shard_map/ppermute | solution.py:287
  42.8 12.3 %collective-permute-start.13 = (f32[2,4,16,512]{3,2,1,0:T(8,128)S(1)}, f32[2,4,16,512]{3,2,1,0:T(8,128)S(1)}, u32[]{:S(2)}, u32[]{:S(2)}) collective-permute-start(f32[2,4,16,512]{3,2,1,0:T(8,128)S(1)} %get-tuple-element.28.refs_6_), channel_id=1, source_target_pairs={{0,28},{4,8},{8,4},{12,16},{16,12},{20,24},{24,20},{28,0},{1,29},{... | collective-permute-start | bytes 786440 | tf_op jit(solution)/shard_map/ppermute | solution.py:303
  44.5 10.8 %collective-permute-start.12 = (f32[2,2,16,512]{3,2,1,0:T(8,128)S(1)}, f32[2,2,16,512]{3,2,1,0:T(8,128)S(1)}, u32[]{:S(2)}, u32[]{:S(2)}) collective-permute-start(f32[2,2,16,512]{3,2,1,0:T(8,128)S(1)} %get-tuple-element.32), channel_id=1, source_target_pairs={{0,1},{1,0},{2,3},{3,2},{4,5},{5,4},{6,7},{7,6},{8,9},{9,8},{10,11... | collective-permute-start | bytes 393224 | tf_op jit(solution)/shard_map/ppermute | solution.py:287
  52.5 8.3 %collective-permute-start.11 = (f32[2,32,512]{2,1,0:T(8,128)S(1)}, f32[2,32,512]{2,1,0:T(8,128)S(1)}, u32[]{:S(2)}, u32[]{:S(2)}) collective-permute-start(f32[2,32,512]{2,1,0:T(8,128)S(1)} %shard_map.52.refs_3_), channel_id=1, source_target_pairs={{0,3},{1,2},{2,1},{3,0},{4,7},{5,6},{6,5},{7,4},{8,11},{9,10},{10,... | collective-permute-start | bytes 393224 | tf_op jit(solution)/shard_map/ppermute | solution.py:279
  55.2 7.7 %collective-permute-start.15 = (f32[2,2,16,512]{3,2,1,0:T(8,128)S(1)}, f32[2,2,16,512]{3,2,1,0:T(8,128)S(1)}, u32[]{:S(2)}, u32[]{:S(2)}) collective-permute-start(f32[2,2,16,512]{3,2,1,0:T(8,128)S(1)} %get-tuple-element.34), channel_id=1, source_target_pairs={{0,1},{1,0},{2,3},{3,2},{4,5},{5,4},{6,7},{7,6},{8,9},{9,8},{10,11... | collective-permute-start | bytes 393224 | tf_op jit(solution)/shard_map/ppermute | solution.py:287
  55.3 9.4 %collective-permute-start.14 = (f32[2,16,512]{2,1,0:T(8,128)S(1)}, f32[2,16,512]{2,1,0:T(8,128)S(1)}, u32[]{:S(2)}, u32[]{:S(2)}) collective-permute-start(f32[2,16,512]{2,1,0:T(8,128)S(1)} %shard_map.54.refs_3_), channel_id=1, source_target_pairs={{0,3},{1,2},{2,1},{3,0},{4,7},{5,6},{6,5},{7,4},{8,11},{9,10},{10,... | collective-permute-start | bytes 196616 | tf_op jit(solution)/shard_map/ppermute | solution.py:279
  62.8 6.1 %collective-permute-start.16 = (f32[2,16,512]{2,1,0:T(8,128)S(1)}, f32[2,16,512]{2,1,0:T(8,128)S(1)}, u32[]{:S(2)}, u32[]{:S(2)}) collective-permute-start(f32[2,16,512]{2,1,0:T(8,128)S(1)} %shard_map.56.refs_3_), channel_id=1, source_target_pairs={{0,3},{1,2},{2,1},{3,0},{4,7},{5,6},{6,5},{7,4},{8,11},{9,10},{10,... | collective-permute-start | bytes 196616 | tf_op jit(solution)/shard_map/ppermute | solution.py:279

commit v6 on v5

--- a/solution.py
+++ b/solution.py
@@ -134,24 +134,23 @@
             f[1, band] = g[1, band, first:last, :] + d1
 
 
-def back_kernel(chunk, row, halo, h, keep, send):
+def offsets(bands):
+    return [0, *range(bands - 1, 0, -1)]
+
+
+def back_kernel(chunk, row, halo, h, *outs):
     odd = parity()
     lo, hi = chunk
     two = row[0:1, :]
     me = lax.axis_index("orb")
     bands = halo.shape[1]
-
-    def part(band, out, slot):
+    for d, out in zip(offsets(bands), outs):
+        band = me ^ d
         d0, d1 = halo_terms(halo, band, odd)
         v2 = h[0, band, lo:hi, :] + two * (NEAR * d1 + FAR * d0)
         v3 = h[1, band, lo:hi, :] + two * (FAR * d1)
-        out[slot, 0] = square(v2, bands)
-        out[slot, 1] = square(v3, bands)
-
-    part(me ^ 1, send, 0)
-    part(me ^ 2, send, 1)
-    part(me, keep, 0)
-    part(me ^ 3, keep, 1)
+        out[0] = square(v2, bands)
+        out[1] = square(v3, bands)
 
 
 def front_kernel(chunks, c, psi, pot, t, *rest):
@@ -204,6 +203,13 @@
 
 def sum_kernel(keep, came, far, out):
     out[...] = keep[0] + came[0] + far[...]
+
+
+def sum_all_kernel(*refs):
+    total = refs[0][...]
+    for ref in refs[1:-1]:
+        total = total + ref[...]
+    refs[-1][...] = total
 
 
 def join_kernel(places, *refs):
@@ -287,12 +293,19 @@
         return keep, lax.ppermute(send, "orb", near)
 
     def back_squares(chunk, halo):
-        keep, send = call(
+        keep, *sends = call(
             functools.partial(back_kernel, chunk),
-            [pair_shape(chunk)] * 2,
+            [pair_shape(chunk)[1:]] * bands,
             (row, halo, as_bands(h_back)),
         )
-        return keep, lax.ppermute(send, "orb", near)
+        came = [
+            lax.ppermute(x, "orb", [(i, i ^ d) for i in range(bands)])
+            for d, x in zip(offsets(bands)[1:], sends)
+        ]
+        return keep, *came
+
+    def sum_all(keep, *came, weight=0):
+        return call(sum_all_kernel, keep.shape, (keep, *came), weight=weight)
 
     def faces(chunk, halo, parts):
         fs = call(
@@ -329,10 +342,9 @@
     cut_a, cut_b, cut_c = cuts
     f0, (face_a,) = faces(chunks[0], halos[0], [cut_a])
     back0 = back_squares(chunks[0], halos[0])
-    back0 = add_far(*back0)
     f1, (face_b, face_c) = faces(chunks[1], halos[1], [cut_b, cut_c])
     back1 = back_squares(chunks[1], halos[1])
-    back0 = summed(*back0)
+    back0 = sum_all(*back0)
     h_front = call(
         functools.partial(front_kernel, cuts),
         plane2,
@@ -342,10 +354,9 @@
         flops=40 * cells,
         weight=3_000_000_000,
     )
-    back1 = add_far(*back1)
     front_a = squares(cut_a, face_a)
     front_b = squares(cut_b, face_b)
-    back1 = summed(*back1, weight=2_000_000_000)
+    back1 = sum_all(*back1, weight=2_000_000_000)
     front_a = add_far(*front_a)
     front_c = squares(cut_c, face_c)
     front_b = add_far(*front_b)

time: 70 us -> 68.4 us (0.977)
  the two profiles are of different devices: /device:TPU:6 before, /device:TPU:0 now
where the time goes in v6:
time: 68.4 us; the launch traced here: 68.3 us
  starting transfers between devices  36.3 us (53%)
  waiting for transfers between devices  15.8 us (23%)
  Pallas kernels  14.4 us (21%)
  local copies, waits for them, and re-layouts  1.61 us (2%)
    pallas_call x20, Pallas kernels, __call__(): pl.pallas_call(body, out_shape=shapes, in_specs=[smem] * scalars + [pl.Bl...  14.4 us
    ppermute x6, starting transfers between devices, back_squares(): lax.ppermute(x, 'orb', [(i, i ^ d) for i in range(bands)])  8.9 us
    ppermute x3, starting transfers between devices, add_far(): return (keep, came, lax.ppermute(total, 'orb', far))  8.55 us
    ppermute x3, starting transfers between devices, faces(): return (fs, [lax.ppermute(x, 'slab', face) for x in fs])  8.04 us
    ppermute x3, starting transfers between devices, squares(): return (keep, lax.ppermute(send, 'orb', near))  6.59 us
    ppermute x2, waiting for transfers between devices, shards(): halos.append(lax.ppermute(piece, 'slab', face))  6.3 us
    ppermute x3, waiting for transfers between devices, faces(): return (fs, [lax.ppermute(x, 'slab', face) for x in fs])  4.51 us
    ppermute x2, starting transfers between devices, shards(): halos.append(lax.ppermute(piece, 'slab', face))  3.66 us
  transfers between devices with their start and end apart: 19, of which 8 were waited for; matrix products, arithmetic and copies ran while one was open for 0% of the time, Pallas kernels for 20%

profile of v6, /device:TPU:0, one launch (start us, length us, event | category | flops | bytes accessed | tf_op | source)
XLA Modules:
  0.0 68.3 jit_solution(3343805994977850476)
XLA Ops:
  0.0 0.5 collective-permute-start
  0.5 0.1 collective-permute-start.1
  0.5 1.6 %copy-done = f32[1,4,256,512]{3,2,1,0:T(8,128)S(1)} copy-done((f32[1,4,256,512]{3,2,1,0:T(8,128)S(1)}, f32[1,4,256,512]{3,2,1,0:T(8,128)}, u32[]{:S(2)}) %copy-start) | copy-done | bytes 2097176
  2.2 0.0 copy-start.2
  2.2 3.6 %collective-permute-start.2 = (f32[2,4,32,512]{3,2,1,0:T(8,128)S(1)}, f32[2,4,32,512]{3,2,1,0:T(8,128)S(1)}, u32[]{:S(2)}, u32[]{:S(2)}) collective-permute-start(f32[2,4,32,512]{3,2,1,0:T(8,128)S(1)} %shard_map.37.refs_1_), channel_id=1, source_target_pairs={{0,28},{4,8},{8,4},{12,16},{16,12},{20,24},{24,20},{28,0},{1,29},{... | collective-permute-start | bytes 1572872 | tf_op jit(solution)/shard_map/ppermute | solution.py:329
  5.8 0.0 copy-start.3
  5.8 0.1 collective-permute-start.6
  5.9 2.5 %shard_map.39.refs_5_.refs_6_ = f32[2,256,512]{2,1,0:T(8,128)S(1)} custom-call(f32[4,256,512]{2,1,0:T(8,128)S(1)} %bitcast.8, f32[4,256,512]{2,1,0:T(8,128)S(1)} %copy-done.2, f32[2,4,32,512]{3,2,1,0:T(8,128)S(1)} %shard_map.38.refs_2_), custom_call_target="tpu_custom_call" | custom-call | flops 6291456 | bytes 5242880 | tf_op jit(solution)/shard_map/pallas_call | solution.py:241
  8.4 0.0 collective-permute-done.refs_3_
  8.4 0.0 collective-permute-done.1.refs_4_
  8.4 7.0 %shard_map.40 = (f32[2,256,512]{2,1,0:T(8,128)S(1)}, f32[2,256,512]{2,1,0:T(8,128)S(1)}, f32[8,512]{1,0:T(8,128)S(1)}) custom-call(f32[3]{0:T(128)S(1)} %copy-done.3, f32[4,256,512]{2,1,0:T(8,128)S(1)} %bitcast.9, f32[4,256,512]{2,1,0:T(8,128)S(1)} %copy-done.2, f32[4,256,512]{2,1,0:T(8,128)S(1)} %collective-permute-done.refs_3_, ...), custom_call_target="tpu_custom_call" | custom-call | flops 20971520 | bytes 11550732 | tf_op jit(solution)/shard_map/pallas_call | solution.py:241
  15.4 2.6 %collective-permute-done.2.refs_0_.refs_1_ = f32[2,4,32,512]{3,2,1,0:T(8,128)S(1)} collective-permute-done((f32[2,4,32,512]{3,2,1,0:T(8,128)S(1)}, f32[2,4,32,512]{3,2,1,0:T(8,128)S(1)}, u32[]{:S(2)}, u32[]{:S(2)}) %collective-permute-start.2) | collective-permute-done | bytes 524320 | tf_op jit(solution)/shard_map/ppermute | solution.py:329
  18.1 0.1 shard_map.41.refs_3_.refs_4_
  18.2 2.9 %collective-permute-start.11 = (f32[2,4,32,512]{3,2,1,0:T(8,128)S(1)}, f32[2,4,32,512]{3,2,1,0:T(8,128)S(1)}, u32[]{:S(2)}, u32[]{:S(2)}) collective-permute-start(f32[2,4,32,512]{3,2,1,0:T(8,128)S(1)} %shard_map.41.refs_3_.refs_4_), channel_id=1, source_target_pairs={{0,28},{4,8},{8,4},{12,16},{16,12},{20,24},{24,20},{28,0},{1,29},{... | collective-permute-start | bytes 1572872 | tf_op jit(solution)/shard_map/ppermute | solution.py:316
  21.0 0.1 shard_map.42
  21.2 3.7 %collective-permute-start.3 = (f32[2,32,512]{2,1,0:T(8,128)S(1)}, f32[2,32,512]{2,1,0:T(8,128)S(1)}, u32[]{:S(2)}, u32[]{:S(2)}) collective-permute-start(f32[2,32,512]{2,1,0:T(8,128)S(1)} %get-tuple-element.28), channel_id=1, source_target_pairs={{0,3},{1,2},{2,1},{3,0},{4,7},{5,6},{6,5},{7,4},{8,11},{9,10},{10,... | collective-permute-start | bytes 393224 | tf_op jit(solution)/shard_map/ppermute | solution.py:302
  24.8 0.0 collective-permute-start.4
  24.8 0.8 %collective-permute-start.5 = (f32[2,32,512]{2,1,0:T(8,128)S(1)}, f32[2,32,512]{2,1,0:T(8,128)S(1)}, u32[]{:S(2)}, u32[]{:S(2)}) collective-permute-start(f32[2,32,512]{2,1,0:T(8,128)S(1)} %get-tuple-element.30), channel_id=1, source_target_pairs={{0,1},{1,0},{2,3},{3,2},{4,5},{5,4},{6,7},{7,6},{8,9},{9,8},{10,11... | collective-permute-start | bytes 393224 | tf_op jit(solution)/shard_map/ppermute | solution.py:302
  25.6 3.7 %collective-permute-done.6.refs_0_.refs_1_ = f32[2,4,32,512]{3,2,1,0:T(8,128)S(1)} collective-permute-done((f32[2,4,32,512]{3,2,1,0:T(8,128)S(1)}, f32[2,4,32,512]{3,2,1,0:T(8,128)S(1)}, u32[]{:S(2)}, u32[]{:S(2)}) %collective-permute-start.6) | collective-permute-done | bytes 524320 | tf_op jit(solution)/shard_map/ppermute | solution.py:329
  29.3 0.1 shard_map.43
  29.4 2.9 %collective-permute-start.10 = (f32[2,4,16,512]{3,2,1,0:T(8,128)S(1)}, f32[2,4,16,512]{3,2,1,0:T(8,128)S(1)}, u32[]{:S(2)}, u32[]{:S(2)}) collective-permute-start(f32[2,4,16,512]{3,2,1,0:T(8,128)S(1)} %get-tuple-element.31.refs_3_.refs_5_), channel_id=1, source_target_pairs={{0,28},{4,8},{8,4},{12,16},{16,12},{20,24},{24,20},{28,0},{1,29},{... | collective-permute-start | bytes 786440 | tf_op jit(solution)/shard_map/ppermute | solution.py:316
  32.3 0.1 shard_map.44
  32.4 0.0 collective-permute-done.3.refs_1_
  32.4 3.7 %collective-permute-start.7 = (f32[2,32,512]{2,1,0:T(8,128)S(1)}, f32[2,32,512]{2,1,0:T(8,128)S(1)}, u32[]{:S(2)}, u32[]{:S(2)}) collective-permute-start(f32[2,32,512]{2,1,0:T(8,128)S(1)} %get-tuple-element.33), channel_id=1, source_target_pairs={{0,3},{1,2},{2,1},{3,0},{4,7},{5,6},{6,5},{7,4},{8,11},{9,10},{10,... | collective-permute-start | bytes 393224 | tf_op jit(solution)/shard_map/ppermute | solution.py:302
  36.1 0.0 collective-permute-done.4.refs_2_
  36.1 0.0 collective-permute-start.8
  36.1 0.0 collective-permute-done.5.refs_3_
  36.1 0.8 %collective-permute-start.9 = (f32[2,32,512]{2,1,0:T(8,128)S(1)}, f32[2,32,512]{2,1,0:T(8,128)S(1)}, u32[]{:S(2)}, u32[]{:S(2)}) collective-permute-start(f32[2,32,512]{2,1,0:T(8,128)S(1)} %get-tuple-element.35), channel_id=1, source_target_pairs={{0,1},{1,0},{2,3},{3,2},{4,5},{5,4},{6,7},{7,6},{8,9},{9,8},{10,11... | collective-permute-start | bytes 393224 | tf_op jit(solution)/shard_map/ppermute | solution.py:302
  36.9 3.2 %shard_map.46.refs_3_ = f32[2,256,512]{2,1,0:T(8,128)S(1)} custom-call(f32[3]{0:T(128)S(1)} %copy-done.3, f32[4,256,512]{2,1,0:T(8,128)S(1)} %bitcast.10, f32[4,256,512]{2,1,0:T(8,128)S(1)} %copy-done.2, f32[2,256,512]{2,1,0:T(8,128)S(1)} %get-tuple-element.26.refs_2_.refs_3_, f32[2,4,32,512]{3,2,1,0:T(8,128)S(1)} %shard_map.41.refs_3_.refs_4_, ...), custom_call_target="tpu_custom_call" | custom-call | flops 3010485760 | bytes 7340044 | tf_op jit(solution)/shard_map/pallas_call | solution.py:241
  40.1 0.4 collective-permute-done.11.refs_1_
  40.5 0.1 shard_map.47
  40.7 2.1 %collective-permute-start.12 = (f32[2,2,32,512]{3,2,1,0:T(8,128)S(1)}, f32[2,2,32,512]{3,2,1,0:T(8,128)S(1)}, u32[]{:S(2)}, u32[]{:S(2)}) collective-permute-start(f32[2,2,32,512]{3,2,1,0:T(8,128)S(1)} %get-tuple-element.39), channel_id=1, source_target_pairs={{0,1},{1,0},{2,3},{3,2},{4,5},{5,4},{6,7},{7,6},{8,9},{9,8},{10,11... | collective-permute-start | bytes 786440 | tf_op jit(solution)/shard_map/ppermute | solution.py:293
  42.8 2.7 %collective-permute-done.10.refs_1_ = f32[2,4,16,512]{3,2,1,0:T(8,128)S(1)} collective-permute-done((f32[2,4,16,512]{3,2,1,0:T(8,128)S(1)}, f32[2,4,16,512]{3,2,1,0:T(8,128)S(1)}, u32[]{:S(2)}, u32[]{:S(2)}) %collective-permute-start.10) | collective-permute-done | bytes 262176 | tf_op jit(solution)/shard_map/ppermute | solution.py:316
  45.5 2.3 %collective-permute-start.15 = (f32[2,4,16,512]{3,2,1,0:T(8,128)S(1)}, f32[2,4,16,512]{3,2,1,0:T(8,128)S(1)}, u32[]{:S(2)}, u32[]{:S(2)}) collective-permute-start(f32[2,4,16,512]{3,2,1,0:T(8,128)S(1)} %get-tuple-element.36.refs_6_), channel_id=1, source_target_pairs={{0,28},{4,8},{8,4},{12,16},{16,12},{20,24},{24,20},{28,0},{1,29},{... | collective-permute-start | bytes 786440 | tf_op jit(solution)/shard_map/ppermute | solution.py:316
  47.8 0.1 shard_map.48
  47.9 0.0 collective-permute-done.7.refs_1_
  47.9 1.6 %collective-permute-start.14 = (f32[2,2,16,512]{3,2,1,0:T(8,128)S(1)}, f32[2,2,16,512]{3,2,1,0:T(8,128)S(1)}, u32[]{:S(2)}, u32[]{:S(2)}) collective-permute-start(f32[2,2,16,512]{3,2,1,0:T(8,128)S(1)} %get-tuple-element.40), channel_id=1, source_target_pairs={{0,1},{1,0},{2,3},{3,2},{4,5},{5,4},{6,7},{7,6},{8,9},{9,8},{10,11... | collective-permute-start | bytes 393224 | tf_op jit(solution)/shard_map/ppermute | solution.py:293
  49.5 0.0 collective-permute-done.8.refs_2_
  49.6 1.0 %collective-permute-done.12.refs_1_ = f32[2,2,32,512]{3,2,1,0:T(8,128)S(1)} collective-permute-done((f32[2,2,32,512]{3,2,1,0:T(8,128)S(1)}, f32[2,2,32,512]{3,2,1,0:T(8,128)S(1)}, u32[]{:S(2)}, u32[]{:S(2)}) %collective-permute-start.12) | collective-permute-done | bytes 262176 | tf_op jit(solution)/shard_map/ppermute | solution.py:293
  50.5 2.7 %collective-permute-start.13 = (f32[2,32,512]{2,1,0:T(8,128)S(1)}, f32[2,32,512]{2,1,0:T(8,128)S(1)}, u32[]{:S(2)}, u32[]{:S(2)}) collective-permute-start(f32[2,32,512]{2,1,0:T(8,128)S(1)} %shard_map.50.refs_3_), channel_id=1, source_target_pairs={{0,3},{1,2},{2,1},{3,0},{4,7},{5,6},{6,5},{7,4},{8,11},{9,10},{10,... | collective-permute-start | bytes 393224 | tf_op jit(solution)/shard_map/ppermute | solution.py:285
  53.3 1.4 %collective-permute-done.15.refs_1_ = f32[2,4,16,512]{3,2,1,0:T(8,128)S(1)} collective-permute-done((f32[2,4,16,512]{3,2,1,0:T(8,128)S(1)}, f32[2,4,16,512]{3,2,1,0:T(8,128)S(1)}, u32[]{:S(2)}, u32[]{:S(2)}) %collective-permute-start.15) | collective-permute-done | bytes 262176 | tf_op jit(solution)/shard_map/ppermute | solution.py:316
  54.6 0.1 shard_map.51
  54.7 2.8 %collective-permute-start.17 = (f32[2,2,16,512]{3,2,1,0:T(8,128)S(1)}, f32[2,2,16,512]{3,2,1,0:T(8,128)S(1)}, u32[]{:S(2)}, u32[]{:S(2)}) collective-permute-start(f32[2,2,16,512]{3,2,1,0:T(8,128)S(1)} %get-tuple-element.42), channel_id=1, source_target_pairs={{0,1},{1,0},{2,3},{3,2},{4,5},{5,4},{6,7},{7,6},{8,9},{9,8},{10,11... | collective-permute-start | bytes 393224 | tf_op jit(solution)/shard_map/ppermute | solution.py:293
  57.5 2.5 %collective-permute-start.16 = (f32[2,16,512]{2,1,0:T(8,128)S(1)}, f32[2,16,512]{2,1,0:T(8,128)S(1)}, u32[]{:S(2)}, u32[]{:S(2)}) collective-permute-start(f32[2,16,512]{2,1,0:T(8,128)S(1)} %shard_map.52.refs_3_), channel_id=1, source_target_pairs={{0,3},{1,2},{2,1},{3,0},{4,7},{5,6},{6,5},{7,4},{8,11},{9,10},{10,... | collective-permute-start | bytes 196616 | tf_op jit(solution)/shard_map/ppermute | solution.py:285
  60.1 1.2 %collective-permute-done.17.refs_1_.refs_5_ = f32[2,2,16,512]{3,2,1,0:T(8,128)S(1)} collective-permute-done((f32[2,2,16,512]{3,2,1,0:T(8,128)S(1)}, f32[2,2,16,512]{3,2,1,0:T(8,128)S(1)}, u32[]{:S(2)}, u32[]{:S(2)}) %collective-permute-start.17) | collective-permute-done | bytes 131104 | tf_op jit(solution)/shard_map/ppermute | solution.py:293
  61.3 3.3 %collective-permute-start.18 = (f32[2,16,512]{2,1,0:T(8,128)S(1)}, f32[2,16,512]{2,1,0:T(8,128)S(1)}, u32[]{:S(2)}, u32[]{:S(2)}) collective-permute-start(f32[2,16,512]{2,1,0:T(8,128)S(1)} %shard_map.54.refs_3_), channel_id=1, source_target_pairs={{0,3},{1,2},{2,1},{3,0},{4,7},{5,6},{6,5},{7,4},{8,11},{9,10},{10,... | collective-permute-start | bytes 196616 | tf_op jit(solution)/shard_map/ppermute | solution.py:285
  64.6 2.8 %collective-permute-done.18.refs_6_ = f32[2,16,512]{2,1,0:T(8,128)S(1)} collective-permute-done((f32[2,16,512]{2,1,0:T(8,128)S(1)}, f32[2,16,512]{2,1,0:T(8,128)S(1)}, u32[]{:S(2)}, u32[]{:S(2)}) %collective-permute-start.18) | collective-permute-done | bytes 65568 | tf_op jit(solution)/shard_map/ppermute | solution.py:285
  67.4 0.8 %shard_map.56 = f32[4,64,512]{2,1,0:T(8,128)} custom-call(f32[2,32,512]{2,1,0:T(8,128)S(1)} %shard_map.45.refs_7_.refs_0_, f32[2,32,512]{2,1,0:T(8,128)S(1)} %shard_map.49.refs_2_.refs_1_, f32[2,32,512]{2,1,0:T(8,128)S(1)} %shard_map.53.refs_2_, f32[2,16,512]{2,1,0:T(8,128)S(1)} %shard_map.55.refs_3_.refs_7_, ...), custom_call_target="tpu_custom_call" | custom-call | bytes 1310720 | tf_op jit(solution)/shard_map/pallas_call | solution.py:241
  (18 shorter events, 0.2 us)
Async XLA Ops:
  0.0 8.4 %collective-permute-start = (f32[4,256,512]{2,1,0:T(8,128)}, f32[4,256,512]{2,1,0:T(8,128)S(1)}, u32[]{:S(2)}, u32[]{:S(2)}) collective-permute-start(f32[4,256,512]{2,1,0:T(8,128)} %bitcast.5), channel_id=1, source_target_pairs={{0,4},{4,0},{8,12},{12,8},{16,20},{20,16},{24,28},{28,24},{1,5},{5... | collective-permute-start | bytes 6291464 | tf_op jit(solution)/shard_map/ppermute | solution.py:318
  0.5 8.0 %collective-permute-start.1 = (f32[4,256,512]{2,1,0:T(8,128)}, f32[4,256,512]{2,1,0:T(8,128)S(1)}, u32[]{:S(2)}, u32[]{:S(2)}) collective-permute-start(f32[4,256,512]{2,1,0:T(8,128)} %refs_2_.3), channel_id=1, source_target_pairs={{0,4},{4,0},{8,12},{12,8},{16,20},{20,16},{24,28},{28,24},{1,5},{5... | collective-permute-start | bytes 6291464 | tf_op jit(solution)/shard_map/ppermute | solution.py:319
  0.5 1.6 %copy-start = (f32[1,4,256,512]{3,2,1,0:T(8,128)S(1)}, f32[1,4,256,512]{3,2,1,0:T(8,128)}, u32[]{:S(2)}) copy-start(f32[1,4,256,512]{3,2,1,0:T(8,128)} %param.3) | copy-start | bytes 6291460
  2.2 3.7 %copy-start.2 = (f32[4,256,512]{2,1,0:T(8,128)S(1)}, f32[4,256,512]{2,1,0:T(8,128)}, u32[]{:S(2)}) copy-start(f32[4,256,512]{2,1,0:T(8,128)} %refs_2_.3) | copy-start | bytes 6291460
  2.2 15.9 %collective-permute-start.2 = (f32[2,4,32,512]{3,2,1,0:T(8,128)S(1)}, f32[2,4,32,512]{3,2,1,0:T(8,128)S(1)}, u32[]{:S(2)}, u32[]{:S(2)}) collective-permute-start(f32[2,4,32,512]{3,2,1,0:T(8,128)S(1)} %shard_map.37.refs_1_), channel_id=1, source_target_pairs={{0,28},{4,8},{8,4},{12,16},{16,12},{20,24},{24,20},{28,0},{1,29},{... | collective-permute-start | bytes 1572872 | tf_op jit(solution)/shard_map/ppermute | solution.py:329
  5.8 2.6 %copy-start.3 = (f32[3]{0:T(128)S(1)}, f32[3]{0:T(128)}, u32[]{:S(2)}) copy-start(f32[3]{0:T(128)} %refs_0_.3) | copy-start | bytes 40
  5.8 23.5 %collective-permute-start.6 = (f32[2,4,32,512]{3,2,1,0:T(8,128)S(1)}, f32[2,4,32,512]{3,2,1,0:T(8,128)S(1)}, u32[]{:S(2)}, u32[]{:S(2)}) collective-permute-start(f32[2,4,32,512]{3,2,1,0:T(8,128)S(1)} %shard_map.38.refs_2_), channel_id=1, source_target_pairs={{0,28},{4,8},{8,4},{12,16},{16,12},{20,24},{24,20},{28,0},{1,29},{... | collective-permute-start | bytes 1572872 | tf_op jit(solution)/shard_map/ppermute | solution.py:329
  18.2 22.4 %collective-permute-start.11 = (f32[2,4,32,512]{3,2,1,0:T(8,128)S(1)}, f32[2,4,32,512]{3,2,1,0:T(8,128)S(1)}, u32[]{:S(2)}, u32[]{:S(2)}) collective-permute-start(f32[2,4,32,512]{3,2,1,0:T(8,128)S(1)} %shard_map.41.refs_3_.refs_4_), channel_id=1, source_target_pairs={{0,28},{4,8},{8,4},{12,16},{16,12},{20,24},{24,20},{28,0},{1,29},{... | collective-permute-start | bytes 1572872 | tf_op jit(solution)/shard_map/ppermute | solution.py:316
  21.2 11.2 %collective-permute-start.3 = (f32[2,32,512]{2,1,0:T(8,128)S(1)}, f32[2,32,512]{2,1,0:T(8,128)S(1)}, u32[]{:S(2)}, u32[]{:S(2)}) collective-permute-start(f32[2,32,512]{2,1,0:T(8,128)S(1)} %get-tuple-element.28), channel_id=1, source_target_pairs={{0,3},{1,2},{2,1},{3,0},{4,7},{5,6},{6,5},{7,4},{8,11},{9,10},{10,... | collective-permute-start | bytes 393224 | tf_op jit(solution)/shard_map/ppermute | solution.py:302
  24.8 11.3 %collective-permute-start.4 = (f32[2,32,512]{2,1,0:T(8,128)S(1)}, f32[2,32,512]{2,1,0:T(8,128)S(1)}, u32[]{:S(2)}, u32[]{:S(2)}) collective-permute-start(f32[2,32,512]{2,1,0:T(8,128)S(1)} %get-tuple-element.29), channel_id=1, source_target_pairs={{0,2},{1,3},{2,0},{3,1},{4,6},{5,7},{6,4},{7,5},{8,10},{9,11},{10,... | collective-permute-start | bytes 393224 | tf_op jit(solution)/shard_map/ppermute | solution.py:302
  24.8 11.3 %collective-permute-start.5 = (f32[2,32,512]{2,1,0:T(8,128)S(1)}, f32[2,32,512]{2,1,0:T(8,128)S(1)}, u32[]{:S(2)}, u32[]{:S(2)}) collective-permute-start(f32[2,32,512]{2,1,0:T(8,128)S(1)} %get-tuple-element.30), channel_id=1, source_target_pairs={{0,1},{1,0},{2,3},{3,2},{4,5},{5,4},{6,7},{7,6},{8,9},{9,8},{10,11... | collective-permute-start | bytes 393224 | tf_op jit(solution)/shard_map/ppermute | solution.py:302
  29.3 7.6 %copy-start.1 = (f32[1,4,256,512]{3,2,1,0:T(8,128)S(1)}, f32[1,4,256,512]{3,2,1,0:T(8,128)}, u32[]{:S(2)}) copy-start(f32[1,4,256,512]{3,2,1,0:T(8,128)} %param.3) | copy-start | bytes 6291460
  29.4 16.1 %collective-permute-start.10 = (f32[2,4,16,512]{3,2,1,0:T(8,128)S(1)}, f32[2,4,16,512]{3,2,1,0:T(8,128)S(1)}, u32[]{:S(2)}, u32[]{:S(2)}) collective-permute-start(f32[2,4,16,512]{3,2,1,0:T(8,128)S(1)} %get-tuple-element.31.refs_3_.refs_5_), channel_id=1, source_target_pairs={{0,28},{4,8},{8,4},{12,16},{16,12},{20,24},{24,20},{28,0},{1,29},{... | collective-permute-start | bytes 786440 | tf_op jit(solution)/shard_map/ppermute | solution.py:316
  32.4 15.4 %collective-permute-start.7 = (f32[2,32,512]{2,1,0:T(8,128)S(1)}, f32[2,32,512]{2,1,0:T(8,128)S(1)}, u32[]{:S(2)}, u32[]{:S(2)}) collective-permute-start(f32[2,32,512]{2,1,0:T(8,128)S(1)} %get-tuple-element.33), channel_id=1, source_target_pairs={{0,3},{1,2},{2,1},{3,0},{4,7},{5,6},{6,5},{7,4},{8,11},{9,10},{10,... | collective-permute-start | bytes 393224 | tf_op jit(solution)/shard_map/ppermute | solution.py:302
  36.1 13.4 %collective-permute-start.8 = (f32[2,32,512]{2,1,0:T(8,128)S(1)}, f32[2,32,512]{2,1,0:T(8,128)S(1)}, u32[]{:S(2)}, u32[]{:S(2)}) collective-permute-start(f32[2,32,512]{2,1,0:T(8,128)S(1)} %get-tuple-element.34), channel_id=1, source_target_pairs={{0,2},{1,3},{2,0},{3,1},{4,6},{5,7},{6,4},{7,5},{8,10},{9,11},{10,... | collective-permute-start | bytes 393224 | tf_op jit(solution)/shard_map/ppermute | solution.py:302
  36.1 13.4 %collective-permute-start.9 = (f32[2,32,512]{2,1,0:T(8,128)S(1)}, f32[2,32,512]{2,1,0:T(8,128)S(1)}, u32[]{:S(2)}, u32[]{:S(2)}) collective-permute-start(f32[2,32,512]{2,1,0:T(8,128)S(1)} %get-tuple-element.35), channel_id=1, source_target_pairs={{0,1},{1,0},{2,3},{3,2},{4,5},{5,4},{6,7},{7,6},{8,9},{9,8},{10,11... | collective-permute-start | bytes 393224 | tf_op jit(solution)/shard_map/ppermute | solution.py:302
  40.7 9.9 %collective-permute-start.12 = (f32[2,2,32,512]{3,2,1,0:T(8,128)S(1)}, f32[2,2,32,512]{3,2,1,0:T(8,128)S(1)}, u32[]{:S(2)}, u32[]{:S(2)}) collective-permute-start(f32[2,2,32,512]{3,2,1,0:T(8,128)S(1)} %get-tuple-element.39), channel_id=1, source_target_pairs={{0,1},{1,0},{2,3},{3,2},{4,5},{5,4},{6,7},{7,6},{8,9},{9,8},{10,11... | collective-permute-start | bytes 786440 | tf_op jit(solution)/shard_map/ppermute | solution.py:293
  45.5 9.1 %collective-permute-start.15 = (f32[2,4,16,512]{3,2,1,0:T(8,128)S(1)}, f32[2,4,16,512]{3,2,1,0:T(8,128)S(1)}, u32[]{:S(2)}, u32[]{:S(2)}) collective-permute-start(f32[2,4,16,512]{3,2,1,0:T(8,128)S(1)} %get-tuple-element.36.refs_6_), channel_id=1, source_target_pairs={{0,28},{4,8},{8,4},{12,16},{16,12},{20,24},{24,20},{28,0},{1,29},{... | collective-permute-start | bytes 786440 | tf_op jit(solution)/shard_map/ppermute | solution.py:316
  47.9 9.6 %collective-permute-start.14 = (f32[2,2,16,512]{3,2,1,0:T(8,128)S(1)}, f32[2,2,16,512]{3,2,1,0:T(8,128)S(1)}, u32[]{:S(2)}, u32[]{:S(2)}) collective-permute-start(f32[2,2,16,512]{3,2,1,0:T(8,128)S(1)} %get-tuple-element.40), channel_id=1, source_target_pairs={{0,1},{1,0},{2,3},{3,2},{4,5},{5,4},{6,7},{7,6},{8,9},{9,8},{10,11... | collective-permute-start | bytes 393224 | tf_op jit(solution)/shard_map/ppermute | solution.py:293
  50.5 9.5 %collective-permute-start.13 = (f32[2,32,512]{2,1,0:T(8,128)S(1)}, f32[2,32,512]{2,1,0:T(8,128)S(1)}, u32[]{:S(2)}, u32[]{:S(2)}) collective-permute-start(f32[2,32,512]{2,1,0:T(8,128)S(1)} %shard_map.50.refs_3_), channel_id=1, source_target_pairs={{0,3},{1,2},{2,1},{3,0},{4,7},{5,6},{6,5},{7,4},{8,11},{9,10},{10,... | collective-permute-start | bytes 393224 | tf_op jit(solution)/shard_map/ppermute | solution.py:285
  54.7 6.6 %collective-permute-start.17 = (f32[2,2,16,512]{3,2,1,0:T(8,128)S(1)}, f32[2,2,16,512]{3,2,1,0:T(8,128)S(1)}, u32[]{:S(2)}, u32[]{:S(2)}) collective-permute-start(f32[2,2,16,512]{3,2,1,0:T(8,128)S(1)} %get-tuple-element.42), channel_id=1, source_target_pairs={{0,1},{1,0},{2,3},{3,2},{4,5},{5,4},{6,7},{7,6},{8,9},{9,8},{10,11... | collective-permute-start | bytes 393224 | tf_op jit(solution)/shard_map/ppermute | solution.py:293
  57.5 7.1 %collective-permute-start.16 = (f32[2,16,512]{2,1,0:T(8,128)S(1)}, f32[2,16,512]{2,1,0:T(8,128)S(1)}, u32[]{:S(2)}, u32[]{:S(2)}) collective-permute-start(f32[2,16,512]{2,1,0:T(8,128)S(1)} %shard_map.52.refs_3_), channel_id=1, source_target_pairs={{0,3},{1,2},{2,1},{3,0},{4,7},{5,6},{6,5},{7,4},{8,11},{9,10},{10,... | collective-permute-start | bytes 196616 | tf_op jit(solution)/shard_map/ppermute | solution.py:285
  61.3 6.1 %collective-permute-start.18 = (f32[2,16,512]{2,1,0:T(8,128)S(1)}, f32[2,16,512]{2,1,0:T(8,128)S(1)}, u32[]{:S(2)}, u32[]{:S(2)}) collective-permute-start(f32[2,16,512]{2,1,0:T(8,128)S(1)} %shard_map.54.refs_3_), channel_id=1, source_target_pairs={{0,3},{1,2},{2,1},{3,0},{4,7},{5,6},{6,5},{7,4},{8,11},{9,10},{10,... | collective-permute-start | bytes 196616 | tf_op jit(solution)/shard_map/ppermute | solution.py:285

commit v7 on v6

--- a/solution.py
+++ b/solution.py
@@ -354,9 +354,9 @@
         flops=40 * cells,
         weight=3_000_000_000,
     )
+    back1 = sum_all(*back1)
     front_a = squares(cut_a, face_a)
     front_b = squares(cut_b, face_b)
-    back1 = sum_all(*back1, weight=2_000_000_000)
     front_a = add_far(*front_a)
     front_c = squares(cut_c, face_c)
     front_b = add_far(*front_b)

time: 68.4 us -> 70.1 us (1.025); the launches traced: 68.3 us -> 69 us
  waiting for transfers between devices: 15.8 us -> 25.4 us
  starting transfers between devices: 36.3 us -> 27.4 us
    ppermute x3, waiting for transfers between devices: 2.15 us -> 8.02 us  [squares(): return (keep, lax.ppermute(send, 'orb', near))]
    ppermute x3, starting transfers between devices: 6.59 us -> 1.85 us  [squares(): return (keep, lax.ppermute(send, 'orb', near))]
    ppermute x6, waiting for transfers between devices: 0.02 us -> 4.72 us  [back_squares(): lax.ppermute(x, 'orb', [(i, i ^ d) for i in range(bands)])]
    ppermute x3, waiting for transfers between devices: 4.51 us -> 0.01 us  [faces(): return (fs, [lax.ppermute(x, 'slab', face) for x in fs])]
    ppermute x3, starting transfers between devices: 8.55 us -> 4.35 us  [add_far(): return (keep, came, lax.ppermute(total, 'orb', far))]
    ppermute x3, waiting for transfers between devices: 2.83 us -> 6.31 us  [add_far(): return (keep, came, lax.ppermute(total, 'orb', far))]
  transfers between devices with their start and end apart: 19 -> 19, of which waited for: 8 -> 10; matrix products, arithmetic and copies ran while one was open for 0% -> 0% of each run, Pallas kernels for 20% -> 20%
where the time goes in v7:
time: 70.1 us; the launch traced here: 69 us
  starting transfers between devices  27.4 us (39%)
  waiting for transfers between devices  25.4 us (36%)
  Pallas kernels  14.4 us (21%)
  local copies, waits for them, and re-layouts  1.61 us (2%)
    pallas_call x20, Pallas kernels, __call__(): pl.pallas_call(body, out_shape=shapes, in_specs=[smem] * scalars + [pl.Bl...  14.4 us
    ppermute x6, starting transfers between devices, back_squares(): lax.ppermute(x, 'orb', [(i, i ^ d) for i in range(bands)])  8.9 us
    ppermute x3, starting transfers between devices, faces(): return (fs, [lax.ppermute(x, 'slab', face) for x in fs])  8.13 us
    ppermute x3, waiting for transfers between devices, squares(): return (keep, lax.ppermute(send, 'orb', near))  8.02 us
    ppermute x3, waiting for transfers between devices, add_far(): return (keep, came, lax.ppermute(total, 'orb', far))  6.31 us
    ppermute x2, waiting for transfers between devices, shards(): halos.append(lax.ppermute(piece, 'slab', face))  6.3 us
    ppermute x6, waiting for transfers between devices, back_squares(): lax.ppermute(x, 'orb', [(i, i ^ d) for i in range(bands)])  4.72 us
    ppermute x3, starting transfers between devices, add_far(): return (keep, came, lax.ppermute(total, 'orb', far))  4.35 us
  transfers between devices with their start and end apart: 19, of which 10 were waited for; matrix products, arithmetic and copies ran while one was open for 0% of the time, Pallas kernels for 20%

profile of v7, /device:TPU:0, one launch (start us, length us, event | category | flops | bytes accessed | tf_op | source)
XLA Modules:
  0.0 69.0 jit_solution(16199001960153090569)
XLA Ops:
  0.0 0.5 collective-permute-start
  0.5 0.1 collective-permute-start.1
  0.5 1.6 %copy-done = f32[1,4,256,512]{3,2,1,0:T(8,128)S(1)} copy-done((f32[1,4,256,512]{3,2,1,0:T(8,128)S(1)}, f32[1,4,256,512]{3,2,1,0:T(8,128)}, u32[]{:S(2)}) %copy-start) | copy-done | bytes 2097176
  2.2 0.0 copy-start.2
  2.2 3.6 %collective-permute-start.2 = (f32[2,4,32,512]{3,2,1,0:T(8,128)S(1)}, f32[2,4,32,512]{3,2,1,0:T(8,128)S(1)}, u32[]{:S(2)}, u32[]{:S(2)}) collective-permute-start(f32[2,4,32,512]{3,2,1,0:T(8,128)S(1)} %shard_map.37.refs_1_), channel_id=1, source_target_pairs={{0,28},{4,8},{8,4},{12,16},{16,12},{20,24},{24,20},{28,0},{1,29},{... | collective-permute-start | bytes 1572872 | tf_op jit(solution)/shard_map/ppermute | solution.py:329
  5.8 0.0 copy-start.3
  5.8 0.1 collective-permute-start.6
  5.9 2.5 %shard_map.39.refs_5_.refs_6_ = f32[2,256,512]{2,1,0:T(8,128)S(1)} custom-call(f32[4,256,512]{2,1,0:T(8,128)S(1)} %bitcast.8, f32[4,256,512]{2,1,0:T(8,128)S(1)} %copy-done.2, f32[2,4,32,512]{3,2,1,0:T(8,128)S(1)} %shard_map.38.refs_2_), custom_call_target="tpu_custom_call" | custom-call | flops 6291456 | bytes 5242880 | tf_op jit(solution)/shard_map/pallas_call | solution.py:241
  8.4 0.0 collective-permute-done.refs_3_
  8.4 0.0 collective-permute-done.1.refs_4_
  8.4 7.0 %shard_map.40 = (f32[2,256,512]{2,1,0:T(8,128)S(1)}, f32[2,256,512]{2,1,0:T(8,128)S(1)}, f32[8,512]{1,0:T(8,128)S(1)}) custom-call(f32[3]{0:T(128)S(1)} %copy-done.3, f32[4,256,512]{2,1,0:T(8,128)S(1)} %bitcast.9, f32[4,256,512]{2,1,0:T(8,128)S(1)} %copy-done.2, f32[4,256,512]{2,1,0:T(8,128)S(1)} %collective-permute-done.refs_3_, ...), custom_call_target="tpu_custom_call" | custom-call | flops 20971520 | bytes 11550732 | tf_op jit(solution)/shard_map/pallas_call | solution.py:241
  15.4 2.6 %collective-permute-done.2.refs_0_.refs_1_ = f32[2,4,32,512]{3,2,1,0:T(8,128)S(1)} collective-permute-done((f32[2,4,32,512]{3,2,1,0:T(8,128)S(1)}, f32[2,4,32,512]{3,2,1,0:T(8,128)S(1)}, u32[]{:S(2)}, u32[]{:S(2)}) %collective-permute-start.2) | collective-permute-done | bytes 524320 | tf_op jit(solution)/shard_map/ppermute | solution.py:329
  18.1 0.1 shard_map.41.refs_3_.refs_4_
  18.2 2.9 %collective-permute-start.10 = (f32[2,4,32,512]{3,2,1,0:T(8,128)S(1)}, f32[2,4,32,512]{3,2,1,0:T(8,128)S(1)}, u32[]{:S(2)}, u32[]{:S(2)}) collective-permute-start(f32[2,4,32,512]{3,2,1,0:T(8,128)S(1)} %shard_map.41.refs_3_.refs_4_), channel_id=1, source_target_pairs={{0,28},{4,8},{8,4},{12,16},{16,12},{20,24},{24,20},{28,0},{1,29},{... | collective-permute-start | bytes 1572872 | tf_op jit(solution)/shard_map/ppermute | solution.py:316
  21.0 0.1 shard_map.42
  21.2 3.7 %collective-permute-start.3 = (f32[2,32,512]{2,1,0:T(8,128)S(1)}, f32[2,32,512]{2,1,0:T(8,128)S(1)}, u32[]{:S(2)}, u32[]{:S(2)}) collective-permute-start(f32[2,32,512]{2,1,0:T(8,128)S(1)} %get-tuple-element.28), channel_id=1, source_target_pairs={{0,3},{1,2},{2,1},{3,0},{4,7},{5,6},{6,5},{7,4},{8,11},{9,10},{10,... | collective-permute-start | bytes 393224 | tf_op jit(solution)/shard_map/ppermute | solution.py:302
  24.8 0.0 collective-permute-start.4
  24.8 0.8 %collective-permute-start.5 = (f32[2,32,512]{2,1,0:T(8,128)S(1)}, f32[2,32,512]{2,1,0:T(8,128)S(1)}, u32[]{:S(2)}, u32[]{:S(2)}) collective-permute-start(f32[2,32,512]{2,1,0:T(8,128)S(1)} %get-tuple-element.30), channel_id=1, source_target_pairs={{0,1},{1,0},{2,3},{3,2},{4,5},{5,4},{6,7},{7,6},{8,9},{9,8},{10,11... | collective-permute-start | bytes 393224 | tf_op jit(solution)/shard_map/ppermute | solution.py:302
  25.6 3.7 %collective-permute-done.6.refs_0_.refs_1_ = f32[2,4,32,512]{3,2,1,0:T(8,128)S(1)} collective-permute-done((f32[2,4,32,512]{3,2,1,0:T(8,128)S(1)}, f32[2,4,32,512]{3,2,1,0:T(8,128)S(1)}, u32[]{:S(2)}, u32[]{:S(2)}) %collective-permute-start.6) | collective-permute-done | bytes 524320 | tf_op jit(solution)/shard_map/ppermute | solution.py:329
  29.3 0.1 shard_map.43
  29.4 2.9 %collective-permute-start.12 = (f32[2,4,16,512]{3,2,1,0:T(8,128)S(1)}, f32[2,4,16,512]{3,2,1,0:T(8,128)S(1)}, u32[]{:S(2)}, u32[]{:S(2)}) collective-permute-start(f32[2,4,16,512]{3,2,1,0:T(8,128)S(1)} %get-tuple-element.31.refs_3_.refs_5_), channel_id=1, source_target_pairs={{0,28},{4,8},{8,4},{12,16},{16,12},{20,24},{24,20},{28,0},{1,29},{... | collective-permute-start | bytes 786440 | tf_op jit(solution)/shard_map/ppermute | solution.py:316
  32.3 0.1 shard_map.44
  32.4 0.0 collective-permute-done.3.refs_1_
  32.4 3.7 %collective-permute-start.7 = (f32[2,32,512]{2,1,0:T(8,128)S(1)}, f32[2,32,512]{2,1,0:T(8,128)S(1)}, u32[]{:S(2)}, u32[]{:S(2)}) collective-permute-start(f32[2,32,512]{2,1,0:T(8,128)S(1)} %get-tuple-element.33), channel_id=1, source_target_pairs={{0,3},{1,2},{2,1},{3,0},{4,7},{5,6},{6,5},{7,4},{8,11},{9,10},{10,... | collective-permute-start | bytes 393224 | tf_op jit(solution)/shard_map/ppermute | solution.py:302
  36.1 0.0 collective-permute-done.4.refs_2_
  36.1 0.0 collective-permute-done.5.refs_3_
  36.1 0.8 %collective-permute-start.9 = (f32[2,32,512]{2,1,0:T(8,128)S(1)}, f32[2,32,512]{2,1,0:T(8,128)S(1)}, u32[]{:S(2)}, u32[]{:S(2)}) collective-permute-start(f32[2,32,512]{2,1,0:T(8,128)S(1)} %get-tuple-element.35), channel_id=1, source_target_pairs={{0,1},{1,0},{2,3},{3,2},{4,5},{5,4},{6,7},{7,6},{8,9},{9,8},{10,11... | collective-permute-start | bytes 393224 | tf_op jit(solution)/shard_map/ppermute | solution.py:302
  36.9 3.2 %shard_map.46.refs_4_ = f32[2,256,512]{2,1,0:T(8,128)S(1)} custom-call(f32[3]{0:T(128)S(1)} %copy-done.3, f32[4,256,512]{2,1,0:T(8,128)S(1)} %bitcast.10, f32[4,256,512]{2,1,0:T(8,128)S(1)} %copy-done.2, f32[2,256,512]{2,1,0:T(8,128)S(1)} %get-tuple-element.26.refs_2_.refs_3_, f32[2,4,32,512]{3,2,1,0:T(8,128)S(1)} %shard_map.41.refs_3_.refs_4_, ...), custom_call_target="tpu_custom_call" | custom-call | flops 3010485760 | bytes 7340044 | tf_op jit(solution)/shard_map/pallas_call | solution.py:241
  40.1 0.4 collective-permute-done.7.refs_1_
  40.5 4.3 %collective-permute-done.8.refs_2_ = f32[2,32,512]{2,1,0:T(8,128)S(1)} collective-permute-done((f32[2,32,512]{2,1,0:T(8,128)S(1)}, f32[2,32,512]{2,1,0:T(8,128)S(1)}, u32[]{:S(2)}, u32[]{:S(2)}) %collective-permute-start.8) | collective-permute-done | bytes 131104 | tf_op jit(solution)/shard_map/ppermute | solution.py:302
  44.9 0.0 collective-permute-done.10.refs_1_
  44.9 0.1 shard_map.48
  45.0 0.1 collective-permute-start.11
  45.1 2.4 %collective-permute-start.15 = (f32[2,4,16,512]{3,2,1,0:T(8,128)S(1)}, f32[2,4,16,512]{3,2,1,0:T(8,128)S(1)}, u32[]{:S(2)}, u32[]{:S(2)}) collective-permute-start(f32[2,4,16,512]{3,2,1,0:T(8,128)S(1)} %get-tuple-element.36.refs_6_), channel_id=1, source_target_pairs={{0,28},{4,8},{8,4},{12,16},{16,12},{20,24},{24,20},{28,0},{1,29},{... | collective-permute-start | bytes 786440 | tf_op jit(solution)/shard_map/ppermute | solution.py:316
  47.5 0.1 shard_map.49
  47.5 1.5 %collective-permute-start.14 = (f32[2,2,16,512]{3,2,1,0:T(8,128)S(1)}, f32[2,2,16,512]{3,2,1,0:T(8,128)S(1)}, u32[]{:S(2)}, u32[]{:S(2)}) collective-permute-start(f32[2,2,16,512]{3,2,1,0:T(8,128)S(1)} %get-tuple-element.40), channel_id=1, source_target_pairs={{0,1},{1,0},{2,3},{3,2},{4,5},{5,4},{6,7},{7,6},{8,9},{9,8},{10,11... | collective-permute-start | bytes 393224 | tf_op jit(solution)/shard_map/ppermute | solution.py:293
  49.0 4.7 %collective-permute-done.11.refs_1_ = f32[2,2,32,512]{3,2,1,0:T(8,128)S(1)} collective-permute-done((f32[2,2,32,512]{3,2,1,0:T(8,128)S(1)}, f32[2,2,32,512]{3,2,1,0:T(8,128)S(1)}, u32[]{:S(2)}, u32[]{:S(2)}) %collective-permute-start.11) | collective-permute-done | bytes 262176 | tf_op jit(solution)/shard_map/ppermute | solution.py:293
  53.8 1.7 %collective-permute-start.13 = (f32[2,32,512]{2,1,0:T(8,128)S(1)}, f32[2,32,512]{2,1,0:T(8,128)S(1)}, u32[]{:S(2)}, u32[]{:S(2)}) collective-permute-start(f32[2,32,512]{2,1,0:T(8,128)S(1)} %shard_map.50.refs_3_), channel_id=1, source_target_pairs={{0,3},{1,2},{2,1},{3,0},{4,7},{5,6},{6,5},{7,4},{8,11},{9,10},{10,... | collective-permute-start | bytes 393224 | tf_op jit(solution)/shard_map/ppermute | solution.py:285
  55.5 0.1 shard_map.51
  55.6 0.3 collective-permute-start.17
  55.8 2.1 %collective-permute-done.14.refs_1_ = f32[2,2,16,512]{3,2,1,0:T(8,128)S(1)} collective-permute-done((f32[2,2,16,512]{3,2,1,0:T(8,128)S(1)}, f32[2,2,16,512]{3,2,1,0:T(8,128)S(1)}, u32[]{:S(2)}, u32[]{:S(2)}) %collective-permute-start.14) | collective-permute-done | bytes 131104 | tf_op jit(solution)/shard_map/ppermute | solution.py:293
  57.9 0.9 %collective-permute-start.16 = (f32[2,16,512]{2,1,0:T(8,128)S(1)}, f32[2,16,512]{2,1,0:T(8,128)S(1)}, u32[]{:S(2)}, u32[]{:S(2)}) collective-permute-start(f32[2,16,512]{2,1,0:T(8,128)S(1)} %shard_map.52.refs_3_), channel_id=1, source_target_pairs={{0,3},{1,2},{2,1},{3,0},{4,7},{5,6},{6,5},{7,4},{8,11},{9,10},{10,... | collective-permute-start | bytes 196616 | tf_op jit(solution)/shard_map/ppermute | solution.py:285
  58.8 2.0 %collective-permute-done.13.refs_2_ = f32[2,32,512]{2,1,0:T(8,128)S(1)} collective-permute-done((f32[2,32,512]{2,1,0:T(8,128)S(1)}, f32[2,32,512]{2,1,0:T(8,128)S(1)}, u32[]{:S(2)}, u32[]{:S(2)}) %collective-permute-start.13) | collective-permute-done | bytes 131104 | tf_op jit(solution)/shard_map/ppermute | solution.py:285
  60.8 1.2 %collective-permute-done.17.refs_1_.refs_5_ = f32[2,2,16,512]{3,2,1,0:T(8,128)S(1)} collective-permute-done((f32[2,2,16,512]{3,2,1,0:T(8,128)S(1)}, f32[2,2,16,512]{3,2,1,0:T(8,128)S(1)}, u32[]{:S(2)}, u32[]{:S(2)}) %collective-permute-start.17) | collective-permute-done | bytes 131104 | tf_op jit(solution)/shard_map/ppermute | solution.py:293
  62.0 1.8 %collective-permute-start.18 = (f32[2,16,512]{2,1,0:T(8,128)S(1)}, f32[2,16,512]{2,1,0:T(8,128)S(1)}, u32[]{:S(2)}, u32[]{:S(2)}) collective-permute-start(f32[2,16,512]{2,1,0:T(8,128)S(1)} %shard_map.54.refs_3_), channel_id=1, source_target_pairs={{0,3},{1,2},{2,1},{3,0},{4,7},{5,6},{6,5},{7,4},{8,11},{9,10},{10,... | collective-permute-start | bytes 196616 | tf_op jit(solution)/shard_map/ppermute | solution.py:285
  63.8 0.3 collective-permute-done.16.refs_2_
  64.1 4.1 %collective-permute-done.18.refs_6_ = f32[2,16,512]{2,1,0:T(8,128)S(1)} collective-permute-done((f32[2,16,512]{2,1,0:T(8,128)S(1)}, f32[2,16,512]{2,1,0:T(8,128)S(1)}, u32[]{:S(2)}, u32[]{:S(2)}) %collective-permute-start.18) | collective-permute-done | bytes 65568 | tf_op jit(solution)/shard_map/ppermute | solution.py:285
  68.1 0.8 %shard_map.56 = f32[4,64,512]{2,1,0:T(8,128)} custom-call(f32[2,32,512]{2,1,0:T(8,128)S(1)} %shard_map.45.refs_7_.refs_0_, f32[2,32,512]{2,1,0:T(8,128)S(1)} %shard_map.47.refs_3_.refs_1_, f32[2,32,512]{2,1,0:T(8,128)S(1)} %shard_map.53.refs_2_, f32[2,16,512]{2,1,0:T(8,128)S(1)} %shard_map.55.refs_3_.refs_7_, ...), custom_call_target="tpu_custom_call" | custom-call | bytes 1310720 | tf_op jit(solution)/shard_map/pallas_call | solution.py:241
  (18 shorter events, 0.2 us)
Async XLA Ops:
  0.0 8.4 %collective-permute-start = (f32[4,256,512]{2,1,0:T(8,128)}, f32[4,256,512]{2,1,0:T(8,128)S(1)}, u32[]{:S(2)}, u32[]{:S(2)}) collective-permute-start(f32[4,256,512]{2,1,0:T(8,128)} %bitcast.5), channel_id=1, source_target_pairs={{0,4},{4,0},{8,12},{12,8},{16,20},{20,16},{24,28},{28,24},{1,5},{5... | collective-permute-start | bytes 6291464 | tf_op jit(solution)/shard_map/ppermute | solution.py:318
  0.5 8.0 %collective-permute-start.1 = (f32[4,256,512]{2,1,0:T(8,128)}, f32[4,256,512]{2,1,0:T(8,128)S(1)}, u32[]{:S(2)}, u32[]{:S(2)}) collective-permute-start(f32[4,256,512]{2,1,0:T(8,128)} %refs_2_.3), channel_id=1, source_target_pairs={{0,4},{4,0},{8,12},{12,8},{16,20},{20,16},{24,28},{28,24},{1,5},{5... | collective-permute-start | bytes 6291464 | tf_op jit(solution)/shard_map/ppermute | solution.py:319
  0.5 1.6 %copy-start = (f32[1,4,256,512]{3,2,1,0:T(8,128)S(1)}, f32[1,4,256,512]{3,2,1,0:T(8,128)}, u32[]{:S(2)}) copy-start(f32[1,4,256,512]{3,2,1,0:T(8,128)} %param.3) | copy-start | bytes 6291460
  2.2 3.7 %copy-start.2 = (f32[4,256,512]{2,1,0:T(8,128)S(1)}, f32[4,256,512]{2,1,0:T(8,128)}, u32[]{:S(2)}) copy-start(f32[4,256,512]{2,1,0:T(8,128)} %refs_2_.3) | copy-start | bytes 6291460
  2.2 15.9 %collective-permute-start.2 = (f32[2,4,32,512]{3,2,1,0:T(8,128)S(1)}, f32[2,4,32,512]{3,2,1,0:T(8,128)S(1)}, u32[]{:S(2)}, u32[]{:S(2)}) collective-permute-start(f32[2,4,32,512]{3,2,1,0:T(8,128)S(1)} %shard_map.37.refs_1_), channel_id=1, source_target_pairs={{0,28},{4,8},{8,4},{12,16},{16,12},{20,24},{24,20},{28,0},{1,29},{... | collective-permute-start | bytes 1572872 | tf_op jit(solution)/shard_map/ppermute | solution.py:329
  5.8 2.6 %copy-start.3 = (f32[3]{0:T(128)S(1)}, f32[3]{0:T(128)}, u32[]{:S(2)}) copy-start(f32[3]{0:T(128)} %refs_0_.3) | copy-start | bytes 40
  5.8 23.5 %collective-permute-start.6 = (f32[2,4,32,512]{3,2,1,0:T(8,128)S(1)}, f32[2,4,32,512]{3,2,1,0:T(8,128)S(1)}, u32[]{:S(2)}, u32[]{:S(2)}) collective-permute-start(f32[2,4,32,512]{3,2,1,0:T(8,128)S(1)} %shard_map.38.refs_2_), channel_id=1, source_target_pairs={{0,28},{4,8},{8,4},{12,16},{16,12},{20,24},{24,20},{28,0},{1,29},{... | collective-permute-start | bytes 1572872 | tf_op jit(solution)/shard_map/ppermute | solution.py:329
  18.2 26.7 %collective-permute-start.10 = (f32[2,4,32,512]{3,2,1,0:T(8,128)S(1)}, f32[2,4,32,512]{3,2,1,0:T(8,128)S(1)}, u32[]{:S(2)}, u32[]{:S(2)}) collective-permute-start(f32[2,4,32,512]{3,2,1,0:T(8,128)S(1)} %shard_map.41.refs_3_.refs_4_), channel_id=1, source_target_pairs={{0,28},{4,8},{8,4},{12,16},{16,12},{20,24},{24,20},{28,0},{1,29},{... | collective-permute-start | bytes 1572872 | tf_op jit(solution)/shard_map/ppermute | solution.py:316
  21.2 11.2 %collective-permute-start.3 = (f32[2,32,512]{2,1,0:T(8,128)S(1)}, f32[2,32,512]{2,1,0:T(8,128)S(1)}, u32[]{:S(2)}, u32[]{:S(2)}) collective-permute-start(f32[2,32,512]{2,1,0:T(8,128)S(1)} %get-tuple-element.28), channel_id=1, source_target_pairs={{0,3},{1,2},{2,1},{3,0},{4,7},{5,6},{6,5},{7,4},{8,11},{9,10},{10,... | collective-permute-start | bytes 393224 | tf_op jit(solution)/shard_map/ppermute | solution.py:302
  24.8 11.3 %collective-permute-start.4 = (f32[2,32,512]{2,1,0:T(8,128)S(1)}, f32[2,32,512]{2,1,0:T(8,128)S(1)}, u32[]{:S(2)}, u32[]{:S(2)}) collective-permute-start(f32[2,32,512]{2,1,0:T(8,128)S(1)} %get-tuple-element.29), channel_id=1, source_target_pairs={{0,2},{1,3},{2,0},{3,1},{4,6},{5,7},{6,4},{7,5},{8,10},{9,11},{10,... | collective-permute-start | bytes 393224 | tf_op jit(solution)/shard_map/ppermute | solution.py:302
  24.8 11.3 %collective-permute-start.5 = (f32[2,32,512]{2,1,0:T(8,128)S(1)}, f32[2,32,512]{2,1,0:T(8,128)S(1)}, u32[]{:S(2)}, u32[]{:S(2)}) collective-permute-start(f32[2,32,512]{2,1,0:T(8,128)S(1)} %get-tuple-element.30), channel_id=1, source_target_pairs={{0,1},{1,0},{2,3},{3,2},{4,5},{5,4},{6,7},{7,6},{8,9},{9,8},{10,11... | collective-permute-start | bytes 393224 | tf_op jit(solution)/shard_map/ppermute | solution.py:302
  29.3 7.6 %copy-start.1 = (f32[1,4,256,512]{3,2,1,0:T(8,128)S(1)}, f32[1,4,256,512]{3,2,1,0:T(8,128)}, u32[]{:S(2)}) copy-start(f32[1,4,256,512]{3,2,1,0:T(8,128)} %param.3) | copy-start | bytes 6291460
  29.4 18.1 %collective-permute-start.12 = (f32[2,4,16,512]{3,2,1,0:T(8,128)S(1)}, f32[2,4,16,512]{3,2,1,0:T(8,128)S(1)}, u32[]{:S(2)}, u32[]{:S(2)}) collective-permute-start(f32[2,4,16,512]{3,2,1,0:T(8,128)S(1)} %get-tuple-element.31.refs_3_.refs_5_), channel_id=1, source_target_pairs={{0,28},{4,8},{8,4},{12,16},{16,12},{20,24},{24,20},{28,0},{1,29},{... | collective-permute-start | bytes 786440 | tf_op jit(solution)/shard_map/ppermute | solution.py:316
  32.4 8.1 %collective-permute-start.7 = (f32[2,32,512]{2,1,0:T(8,128)S(1)}, f32[2,32,512]{2,1,0:T(8,128)S(1)}, u32[]{:S(2)}, u32[]{:S(2)}) collective-permute-start(f32[2,32,512]{2,1,0:T(8,128)S(1)} %get-tuple-element.33), channel_id=1, source_target_pairs={{0,3},{1,2},{2,1},{3,0},{4,7},{5,6},{6,5},{7,4},{8,11},{9,10},{10,... | collective-permute-start | bytes 393224 | tf_op jit(solution)/shard_map/ppermute | solution.py:302
  36.1 8.7 %collective-permute-start.8 = (f32[2,32,512]{2,1,0:T(8,128)S(1)}, f32[2,32,512]{2,1,0:T(8,128)S(1)}, u32[]{:S(2)}, u32[]{:S(2)}) collective-permute-start(f32[2,32,512]{2,1,0:T(8,128)S(1)} %get-tuple-element.34), channel_id=1, source_target_pairs={{0,2},{1,3},{2,0},{3,1},{4,6},{5,7},{6,4},{7,5},{8,10},{9,11},{10,... | collective-permute-start | bytes 393224 | tf_op jit(solution)/shard_map/ppermute | solution.py:302
  36.1 8.7 %collective-permute-start.9 = (f32[2,32,512]{2,1,0:T(8,128)S(1)}, f32[2,32,512]{2,1,0:T(8,128)S(1)}, u32[]{:S(2)}, u32[]{:S(2)}) collective-permute-start(f32[2,32,512]{2,1,0:T(8,128)S(1)} %get-tuple-element.35), channel_id=1, source_target_pairs={{0,1},{1,0},{2,3},{3,2},{4,5},{5,4},{6,7},{7,6},{8,9},{9,8},{10,11... | collective-permute-start | bytes 393224 | tf_op jit(solution)/shard_map/ppermute | solution.py:302
  45.0 8.8 %collective-permute-start.11 = (f32[2,2,32,512]{3,2,1,0:T(8,128)S(1)}, f32[2,2,32,512]{3,2,1,0:T(8,128)S(1)}, u32[]{:S(2)}, u32[]{:S(2)}) collective-permute-start(f32[2,2,32,512]{3,2,1,0:T(8,128)S(1)} %get-tuple-element.38), channel_id=1, source_target_pairs={{0,1},{1,0},{2,3},{3,2},{4,5},{5,4},{6,7},{7,6},{8,9},{9,8},{10,11... | collective-permute-start | bytes 786440 | tf_op jit(solution)/shard_map/ppermute | solution.py:293
  45.1 10.4 %collective-permute-start.15 = (f32[2,4,16,512]{3,2,1,0:T(8,128)S(1)}, f32[2,4,16,512]{3,2,1,0:T(8,128)S(1)}, u32[]{:S(2)}, u32[]{:S(2)}) collective-permute-start(f32[2,4,16,512]{3,2,1,0:T(8,128)S(1)} %get-tuple-element.36.refs_6_), channel_id=1, source_target_pairs={{0,28},{4,8},{8,4},{12,16},{16,12},{20,24},{24,20},{28,0},{1,29},{... | collective-permute-start | bytes 786440 | tf_op jit(solution)/shard_map/ppermute | solution.py:316
  47.5 10.4 %collective-permute-start.14 = (f32[2,2,16,512]{3,2,1,0:T(8,128)S(1)}, f32[2,2,16,512]{3,2,1,0:T(8,128)S(1)}, u32[]{:S(2)}, u32[]{:S(2)}) collective-permute-start(f32[2,2,16,512]{3,2,1,0:T(8,128)S(1)} %get-tuple-element.40), channel_id=1, source_target_pairs={{0,1},{1,0},{2,3},{3,2},{4,5},{5,4},{6,7},{7,6},{8,9},{9,8},{10,11... | collective-permute-start | bytes 393224 | tf_op jit(solution)/shard_map/ppermute | solution.py:293
  53.8 7.0 %collective-permute-start.13 = (f32[2,32,512]{2,1,0:T(8,128)S(1)}, f32[2,32,512]{2,1,0:T(8,128)S(1)}, u32[]{:S(2)}, u32[]{:S(2)}) collective-permute-start(f32[2,32,512]{2,1,0:T(8,128)S(1)} %shard_map.50.refs_3_), channel_id=1, source_target_pairs={{0,3},{1,2},{2,1},{3,0},{4,7},{5,6},{6,5},{7,4},{8,11},{9,10},{10,... | collective-permute-start | bytes 393224 | tf_op jit(solution)/shard_map/ppermute | solution.py:285
  55.6 6.4 %collective-permute-start.17 = (f32[2,2,16,512]{3,2,1,0:T(8,128)S(1)}, f32[2,2,16,512]{3,2,1,0:T(8,128)S(1)}, u32[]{:S(2)}, u32[]{:S(2)}) collective-permute-start(f32[2,2,16,512]{3,2,1,0:T(8,128)S(1)} %get-tuple-element.42), channel_id=1, source_target_pairs={{0,1},{1,0},{2,3},{3,2},{4,5},{5,4},{6,7},{7,6},{8,9},{9,8},{10,11... | collective-permute-start | bytes 393224 | tf_op jit(solution)/shard_map/ppermute | solution.py:293
  57.9 6.1 %collective-permute-start.16 = (f32[2,16,512]{2,1,0:T(8,128)S(1)}, f32[2,16,512]{2,1,0:T(8,128)S(1)}, u32[]{:S(2)}, u32[]{:S(2)}) collective-permute-start(f32[2,16,512]{2,1,0:T(8,128)S(1)} %shard_map.52.refs_3_), channel_id=1, source_target_pairs={{0,3},{1,2},{2,1},{3,0},{4,7},{5,6},{6,5},{7,4},{8,11},{9,10},{10,... | collective-permute-start | bytes 196616 | tf_op jit(solution)/shard_map/ppermute | solution.py:285
  62.0 6.1 %collective-permute-start.18 = (f32[2,16,512]{2,1,0:T(8,128)S(1)}, f32[2,16,512]{2,1,0:T(8,128)S(1)}, u32[]{:S(2)}, u32[]{:S(2)}) collective-permute-start(f32[2,16,512]{2,1,0:T(8,128)S(1)} %shard_map.54.refs_3_), channel_id=1, source_target_pairs={{0,3},{1,2},{2,1},{3,0},{4,7},{5,6},{6,5},{7,4},{8,11},{9,10},{10,... | collective-permute-start | bytes 196616 | tf_op jit(solution)/shard_map/ppermute | solution.py:285

commit v8 on v7

--- a/solution.py
+++ b/solution.py
@@ -340,10 +340,10 @@
         return call(sum_kernel, from_far.shape, (keep, came, from_far), weight=weight)
 
     cut_a, cut_b, cut_c = cuts
+    back0 = back_squares(chunks[0], halos[0])
     f0, (face_a,) = faces(chunks[0], halos[0], [cut_a])
-    back0 = back_squares(chunks[0], halos[0])
+    back1 = back_squares(chunks[1], halos[1])
     f1, (face_b, face_c) = faces(chunks[1], halos[1], [cut_b, cut_c])
-    back1 = back_squares(chunks[1], halos[1])
     back0 = sum_all(*back0)
     h_front = call(
         functools.partial(front_kernel, cuts),
@@ -352,7 +352,7 @@
         scalars=1,
         scratch=[pltpu.VMEM(plane2, jnp.float32)],
         flops=40 * cells,
-        weight=3_000_000_000,
+        weight=6_000_000_000,
     )
     back1 = sum_all(*back1)
     front_a = squares(cut_a, face_a)

time: 70.1 us -> 69.4 us (0.990)
  the two profiles are of different devices: /device:TPU:0 before, /device:TPU:6 now
where the time goes in v8:
time: 69.4 us; the launch traced here: 69.3 us
  waiting for transfers between devices  34.3 us (49%)
  starting transfers between devices  18.7 us (27%)
  Pallas kernels  14.4 us (21%)
  local copies, waits for them, and re-layouts  1.61 us (2%)
    pallas_call x20, Pallas kernels, __call__(): pl.pallas_call(body, out_shape=shapes, in_specs=[smem] * scalars + [pl.Bl...  14.4 us
    ppermute x6, waiting for transfers between devices, back_squares(): lax.ppermute(x, 'orb', [(i, i ^ d) for i in range(bands)])  8.68 us
    ppermute x2, waiting for transfers between devices, shards(): halos.append(lax.ppermute(piece, 'slab', face))  8.41 us
    ppermute x6, starting transfers between devices, back_squares(): lax.ppermute(x, 'orb', [(i, i ^ d) for i in range(bands)])  8.25 us
    ppermute x3, waiting for transfers between devices, squares(): return (keep, lax.ppermute(send, 'orb', near))  8.12 us
    ppermute x3, waiting for transfers between devices, add_far(): return (keep, came, lax.ppermute(total, 'orb', far))  7.75 us
    ppermute x3, starting transfers between devices, add_far(): return (keep, came, lax.ppermute(total, 'orb', far))  6.17 us
    ppermute x2, starting transfers between devices, shards(): halos.append(lax.ppermute(piece, 'slab', face))  1.88 us
  transfers between devices with their start and end apart: 19, of which 11 were waited for; matrix products, arithmetic and copies ran while one was open for 0% of the time, Pallas kernels for 20%

profile of v8, /device:TPU:6, one launch (start us, length us, event | category | flops | bytes accessed | tf_op | source)
XLA Modules:
  0.0 69.3 jit_solution(7193112014715886538)
XLA Ops:
  0.0 0.0 collective-permute-start
  0.0 0.5 collective-permute-start.1
  0.5 1.6 %copy-done = f32[1,4,256,512]{3,2,1,0:T(8,128)S(1)} copy-done((f32[1,4,256,512]{3,2,1,0:T(8,128)S(1)}, f32[1,4,256,512]{3,2,1,0:T(8,128)}, u32[]{:S(2)}) %copy-start) | copy-done | bytes 2097176
  2.2 0.0 copy-start.2
  2.2 0.2 collective-permute-start.2
  2.4 0.0 copy-start.3
  2.4 1.7 %collective-permute-start.6 = (f32[2,4,32,512]{3,2,1,0:T(8,128)S(1)}, f32[2,4,32,512]{3,2,1,0:T(8,128)S(1)}, u32[]{:S(2)}, u32[]{:S(2)}) collective-permute-start(f32[2,4,32,512]{3,2,1,0:T(8,128)S(1)} %shard_map.38.refs_2_), channel_id=1, source_target_pairs={{0,28},{4,8},{8,4},{12,16},{16,12},{20,24},{24,20},{28,0},{1,29},{... | collective-permute-start | bytes 1572872 | tf_op jit(solution)/shard_map/ppermute | solution.py:329
  4.1 2.5 %shard_map.39.refs_5_.refs_6_ = f32[2,256,512]{2,1,0:T(8,128)S(1)} custom-call(f32[4,256,512]{2,1,0:T(8,128)S(1)} %bitcast.8, f32[4,256,512]{2,1,0:T(8,128)S(1)} %copy-done.2, f32[2,4,32,512]{3,2,1,0:T(8,128)S(1)} %shard_map.38.refs_2_), custom_call_target="tpu_custom_call" | custom-call | flops 6291456 | bytes 5242880 | tf_op jit(solution)/shard_map/pallas_call | solution.py:241
  6.6 0.0 collective-permute-done.refs_3_
  6.6 0.7 %collective-permute-done.1.refs_4_ = f32[4,256,512]{2,1,0:T(8,128)S(1)} collective-permute-done((f32[4,256,512]{2,1,0:T(8,128)}, f32[4,256,512]{2,1,0:T(8,128)S(1)}, u32[]{:S(2)}, u32[]{:S(2)}) %collective-permute-start.1) | collective-permute-done | bytes 2097184 | tf_op jit(solution)/shard_map/ppermute | solution.py:319
  7.4 7.0 %shard_map.40 = (f32[2,256,512]{2,1,0:T(8,128)S(1)}, f32[2,256,512]{2,1,0:T(8,128)S(1)}, f32[8,512]{1,0:T(8,128)S(1)}) custom-call(f32[3]{0:T(128)S(1)} %copy-done.3, f32[4,256,512]{2,1,0:T(8,128)S(1)} %bitcast.9, f32[4,256,512]{2,1,0:T(8,128)S(1)} %copy-done.2, f32[4,256,512]{2,1,0:T(8,128)S(1)} %collective-permute-done.refs_3_, ...), custom_call_target="tpu_custom_call" | custom-call | flops 20971520 | bytes 11550732 | tf_op jit(solution)/shard_map/pallas_call | solution.py:241
  14.4 2.0 %collective-permute-done.2.refs_1_.refs_0_ = f32[2,4,32,512]{3,2,1,0:T(8,128)S(1)} collective-permute-done((f32[2,4,32,512]{3,2,1,0:T(8,128)S(1)}, f32[2,4,32,512]{3,2,1,0:T(8,128)S(1)}, u32[]{:S(2)}, u32[]{:S(2)}) %collective-permute-start.2) | collective-permute-done | bytes 524320 | tf_op jit(solution)/shard_map/ppermute | solution.py:329
  16.3 0.1 shard_map.41
  16.5 3.7 %collective-permute-start.3 = (f32[2,32,512]{2,1,0:T(8,128)S(1)}, f32[2,32,512]{2,1,0:T(8,128)S(1)}, u32[]{:S(2)}, u32[]{:S(2)}) collective-permute-start(f32[2,32,512]{2,1,0:T(8,128)S(1)} %get-tuple-element.28), channel_id=1, source_target_pairs={{0,3},{1,2},{2,1},{3,0},{4,7},{5,6},{6,5},{7,4},{8,11},{9,10},{10,... | collective-permute-start | bytes 393224 | tf_op jit(solution)/shard_map/ppermute | solution.py:302
  20.2 0.0 collective-permute-start.4
  20.2 0.8 %collective-permute-start.5 = (f32[2,32,512]{2,1,0:T(8,128)S(1)}, f32[2,32,512]{2,1,0:T(8,128)S(1)}, u32[]{:S(2)}, u32[]{:S(2)}) collective-permute-start(f32[2,32,512]{2,1,0:T(8,128)S(1)} %get-tuple-element.30), channel_id=1, source_target_pairs={{0,1},{1,0},{2,3},{3,2},{4,5},{5,4},{6,7},{7,6},{8,9},{9,8},{10,11... | collective-permute-start | bytes 393224 | tf_op jit(solution)/shard_map/ppermute | solution.py:302
  20.9 0.1 shard_map.42.refs_3_.refs_4_
  21.0 0.0 copy-start.1
  21.0 0.1 collective-permute-start.10
  21.1 6.5 %collective-permute-done.6.refs_1_.refs_0_ = f32[2,4,32,512]{3,2,1,0:T(8,128)S(1)} collective-permute-done((f32[2,4,32,512]{3,2,1,0:T(8,128)S(1)}, f32[2,4,32,512]{3,2,1,0:T(8,128)S(1)}, u32[]{:S(2)}, u32[]{:S(2)}) %collective-permute-start.6) | collective-permute-done | bytes 524320 | tf_op jit(solution)/shard_map/ppermute | solution.py:329
  27.6 0.1 shard_map.43
  27.7 3.7 %collective-permute-start.7 = (f32[2,32,512]{2,1,0:T(8,128)S(1)}, f32[2,32,512]{2,1,0:T(8,128)S(1)}, u32[]{:S(2)}, u32[]{:S(2)}) collective-permute-start(f32[2,32,512]{2,1,0:T(8,128)S(1)} %get-tuple-element.33), channel_id=1, source_target_pairs={{0,3},{1,2},{2,1},{3,0},{4,7},{5,6},{6,5},{7,4},{8,11},{9,10},{10,... | collective-permute-start | bytes 393224 | tf_op jit(solution)/shard_map/ppermute | solution.py:302
  31.4 0.1 shard_map.44
  31.5 0.0 collective-permute-done.3.refs_1_
  31.5 0.1 collective-permute-start.8
  31.6 0.7 %collective-permute-done.4.refs_2_ = f32[2,32,512]{2,1,0:T(8,128)S(1)} collective-permute-done((f32[2,32,512]{2,1,0:T(8,128)S(1)}, f32[2,32,512]{2,1,0:T(8,128)S(1)}, u32[]{:S(2)}, u32[]{:S(2)}) %collective-permute-start.4) | collective-permute-done | bytes 131104 | tf_op jit(solution)/shard_map/ppermute | solution.py:302
  32.3 0.1 collective-permute-start.9
  32.3 0.0 collective-permute-done.5.refs_3_
  32.3 0.0 collective-permute-start.12
  32.4 3.2 %shard_map.46.refs_4_ = f32[2,256,512]{2,1,0:T(8,128)S(1)} custom-call(f32[3]{0:T(128)S(1)} %copy-done.3, f32[4,256,512]{2,1,0:T(8,128)S(1)} %bitcast.10, f32[4,256,512]{2,1,0:T(8,128)S(1)} %copy-done.2, f32[2,256,512]{2,1,0:T(8,128)S(1)} %get-tuple-element.26.refs_3_, f32[2,4,32,512]{3,2,1,0:T(8,128)S(1)} %shard_map.42.refs_3_.refs_4_, ...), custom_call_target="tpu_custom_call" | custom-call | flops 6010485760 | bytes 7340044 | tf_op jit(solution)/shard_map/pallas_call | solution.py:241
  35.6 0.2 collective-permute-done.7.refs_1_
  35.7 7.8 %collective-permute-done.8.refs_2_ = f32[2,32,512]{2,1,0:T(8,128)S(1)} collective-permute-done((f32[2,32,512]{2,1,0:T(8,128)S(1)}, f32[2,32,512]{2,1,0:T(8,128)S(1)}, u32[]{:S(2)}, u32[]{:S(2)}) %collective-permute-start.8) | collective-permute-done | bytes 131104 | tf_op jit(solution)/shard_map/ppermute | solution.py:302
  43.6 0.1 shard_map.48
  43.7 0.1 collective-permute-start.11
  43.8 0.1 collective-permute-start.15
  43.9 0.6 collective-permute-done.12.refs_1_
  44.4 0.1 shard_map.49
  44.5 1.6 %collective-permute-start.14 = (f32[2,2,16,512]{3,2,1,0:T(8,128)S(1)}, f32[2,2,16,512]{3,2,1,0:T(8,128)S(1)}, u32[]{:S(2)}, u32[]{:S(2)}) collective-permute-start(f32[2,2,16,512]{3,2,1,0:T(8,128)S(1)} %get-tuple-element.40), channel_id=1, source_target_pairs={{0,1},{1,0},{2,3},{3,2},{4,5},{5,4},{6,7},{7,6},{8,9},{9,8},{10,11... | collective-permute-start | bytes 393224 | tf_op jit(solution)/shard_map/ppermute | solution.py:293
  46.1 6.8 %collective-permute-done.11.refs_1_ = f32[2,2,32,512]{3,2,1,0:T(8,128)S(1)} collective-permute-done((f32[2,2,32,512]{3,2,1,0:T(8,128)S(1)}, f32[2,2,32,512]{3,2,1,0:T(8,128)S(1)}, u32[]{:S(2)}, u32[]{:S(2)}) %collective-permute-start.11) | collective-permute-done | bytes 262176 | tf_op jit(solution)/shard_map/ppermute | solution.py:293
  52.9 2.5 %collective-permute-start.13 = (f32[2,32,512]{2,1,0:T(8,128)S(1)}, f32[2,32,512]{2,1,0:T(8,128)S(1)}, u32[]{:S(2)}, u32[]{:S(2)}) collective-permute-start(f32[2,32,512]{2,1,0:T(8,128)S(1)} %shard_map.50.refs_3_), channel_id=1, source_target_pairs={{0,3},{1,2},{2,1},{3,0},{4,7},{5,6},{6,5},{7,4},{8,11},{9,10},{10,... | collective-permute-start | bytes 393224 | tf_op jit(solution)/shard_map/ppermute | solution.py:285
  55.5 0.1 shard_map.51
  55.5 0.1 collective-permute-start.17
  55.7 1.8 %collective-permute-start.16 = (f32[2,16,512]{2,1,0:T(8,128)S(1)}, f32[2,16,512]{2,1,0:T(8,128)S(1)}, u32[]{:S(2)}, u32[]{:S(2)}) collective-permute-start(f32[2,16,512]{2,1,0:T(8,128)S(1)} %shard_map.52.refs_3_), channel_id=1, source_target_pairs={{0,3},{1,2},{2,1},{3,0},{4,7},{5,6},{6,5},{7,4},{8,11},{9,10},{10,... | collective-permute-start | bytes 196616 | tf_op jit(solution)/shard_map/ppermute | solution.py:285
  57.5 3.5 %collective-permute-done.13.refs_2_ = f32[2,32,512]{2,1,0:T(8,128)S(1)} collective-permute-done((f32[2,32,512]{2,1,0:T(8,128)S(1)}, f32[2,32,512]{2,1,0:T(8,128)S(1)}, u32[]{:S(2)}, u32[]{:S(2)}) %collective-permute-start.13) | collective-permute-done | bytes 131104 | tf_op jit(solution)/shard_map/ppermute | solution.py:285
  61.0 1.3 %collective-permute-done.17.refs_1_.refs_5_ = f32[2,2,16,512]{3,2,1,0:T(8,128)S(1)} collective-permute-done((f32[2,2,16,512]{3,2,1,0:T(8,128)S(1)}, f32[2,2,16,512]{3,2,1,0:T(8,128)S(1)}, u32[]{:S(2)}, u32[]{:S(2)}) %collective-permute-start.17) | collective-permute-done | bytes 131104 | tf_op jit(solution)/shard_map/ppermute | solution.py:293
  62.3 1.8 %collective-permute-start.18 = (f32[2,16,512]{2,1,0:T(8,128)S(1)}, f32[2,16,512]{2,1,0:T(8,128)S(1)}, u32[]{:S(2)}, u32[]{:S(2)}) collective-permute-start(f32[2,16,512]{2,1,0:T(8,128)S(1)} %shard_map.54.refs_3_), channel_id=1, source_target_pairs={{0,3},{1,2},{2,1},{3,0},{4,7},{5,6},{6,5},{7,4},{8,11},{9,10},{10,... | collective-permute-start | bytes 196616 | tf_op jit(solution)/shard_map/ppermute | solution.py:285
  64.1 4.3 %collective-permute-done.18.refs_6_ = f32[2,16,512]{2,1,0:T(8,128)S(1)} collective-permute-done((f32[2,16,512]{2,1,0:T(8,128)S(1)}, f32[2,16,512]{2,1,0:T(8,128)S(1)}, u32[]{:S(2)}, u32[]{:S(2)}) %collective-permute-start.18) | collective-permute-done | bytes 65568 | tf_op jit(solution)/shard_map/ppermute | solution.py:285
  68.4 0.8 %shard_map.56 = f32[4,64,512]{2,1,0:T(8,128)} custom-call(f32[2,32,512]{2,1,0:T(8,128)S(1)} %shard_map.45.refs_7_.refs_0_, f32[2,32,512]{2,1,0:T(8,128)S(1)} %shard_map.47.refs_3_.refs_1_, f32[2,32,512]{2,1,0:T(8,128)S(1)} %shard_map.53.refs_2_, f32[2,16,512]{2,1,0:T(8,128)S(1)} %shard_map.55.refs_3_.refs_7_, ...), custom_call_target="tpu_custom_call" | custom-call | bytes 1310720 | tf_op jit(solution)/shard_map/pallas_call | solution.py:241
  (18 shorter events, 0.2 us)
Async XLA Ops:
  0.0 6.6 %collective-permute-start = (f32[4,256,512]{2,1,0:T(8,128)}, f32[4,256,512]{2,1,0:T(8,128)S(1)}, u32[]{:S(2)}, u32[]{:S(2)}) collective-permute-start(f32[4,256,512]{2,1,0:T(8,128)} %bitcast.5), channel_id=1, source_target_pairs={{0,4},{4,0},{8,12},{12,8},{16,20},{20,16},{24,28},{28,24},{1,5},{5... | collective-permute-start | bytes 6291464 | tf_op jit(solution)/shard_map/ppermute | solution.py:318
  0.0 7.4 %collective-permute-start.1 = (f32[4,256,512]{2,1,0:T(8,128)}, f32[4,256,512]{2,1,0:T(8,128)S(1)}, u32[]{:S(2)}, u32[]{:S(2)}) collective-permute-start(f32[4,256,512]{2,1,0:T(8,128)} %refs_2_.3), channel_id=1, source_target_pairs={{0,4},{4,0},{8,12},{12,8},{16,20},{20,16},{24,28},{28,24},{1,5},{5... | collective-permute-start | bytes 6291464 | tf_op jit(solution)/shard_map/ppermute | solution.py:319
  0.5 1.6 %copy-start = (f32[1,4,256,512]{3,2,1,0:T(8,128)S(1)}, f32[1,4,256,512]{3,2,1,0:T(8,128)}, u32[]{:S(2)}) copy-start(f32[1,4,256,512]{3,2,1,0:T(8,128)} %param.3) | copy-start | bytes 6291460
  2.2 2.0 %copy-start.2 = (f32[4,256,512]{2,1,0:T(8,128)S(1)}, f32[4,256,512]{2,1,0:T(8,128)}, u32[]{:S(2)}) copy-start(f32[4,256,512]{2,1,0:T(8,128)} %refs_2_.3) | copy-start | bytes 6291460
  2.2 14.2 %collective-permute-start.2 = (f32[2,4,32,512]{3,2,1,0:T(8,128)S(1)}, f32[2,4,32,512]{3,2,1,0:T(8,128)S(1)}, u32[]{:S(2)}, u32[]{:S(2)}) collective-permute-start(f32[2,4,32,512]{3,2,1,0:T(8,128)S(1)} %shard_map.37.refs_1_), channel_id=1, source_target_pairs={{0,28},{4,8},{8,4},{12,16},{16,12},{20,24},{24,20},{28,0},{1,29},{... | collective-permute-start | bytes 1572872 | tf_op jit(solution)/shard_map/ppermute | solution.py:329
  2.4 4.9 %copy-start.3 = (f32[3]{0:T(128)S(1)}, f32[3]{0:T(128)}, u32[]{:S(2)}) copy-start(f32[3]{0:T(128)} %refs_0_.3) | copy-start | bytes 40
  2.4 25.1 %collective-permute-start.6 = (f32[2,4,32,512]{3,2,1,0:T(8,128)S(1)}, f32[2,4,32,512]{3,2,1,0:T(8,128)S(1)}, u32[]{:S(2)}, u32[]{:S(2)}) collective-permute-start(f32[2,4,32,512]{3,2,1,0:T(8,128)S(1)} %shard_map.38.refs_2_), channel_id=1, source_target_pairs={{0,28},{4,8},{8,4},{12,16},{16,12},{20,24},{24,20},{28,0},{1,29},{... | collective-permute-start | bytes 1572872 | tf_op jit(solution)/shard_map/ppermute | solution.py:329
  16.5 15.0 %collective-permute-start.3 = (f32[2,32,512]{2,1,0:T(8,128)S(1)}, f32[2,32,512]{2,1,0:T(8,128)S(1)}, u32[]{:S(2)}, u32[]{:S(2)}) collective-permute-start(f32[2,32,512]{2,1,0:T(8,128)S(1)} %get-tuple-element.28), channel_id=1, source_target_pairs={{0,3},{1,2},{2,1},{3,0},{4,7},{5,6},{6,5},{7,4},{8,11},{9,10},{10,... | collective-permute-start | bytes 393224 | tf_op jit(solution)/shard_map/ppermute | solution.py:302
  20.2 12.1 %collective-permute-start.4 = (f32[2,32,512]{2,1,0:T(8,128)S(1)}, f32[2,32,512]{2,1,0:T(8,128)S(1)}, u32[]{:S(2)}, u32[]{:S(2)}) collective-permute-start(f32[2,32,512]{2,1,0:T(8,128)S(1)} %get-tuple-element.29), channel_id=1, source_target_pairs={{0,2},{1,3},{2,0},{3,1},{4,6},{5,7},{6,4},{7,5},{8,10},{9,11},{10,... | collective-permute-start | bytes 393224 | tf_op jit(solution)/shard_map/ppermute | solution.py:302
  20.2 12.2 %collective-permute-start.5 = (f32[2,32,512]{2,1,0:T(8,128)S(1)}, f32[2,32,512]{2,1,0:T(8,128)S(1)}, u32[]{:S(2)}, u32[]{:S(2)}) collective-permute-start(f32[2,32,512]{2,1,0:T(8,128)S(1)} %get-tuple-element.30), channel_id=1, source_target_pairs={{0,1},{1,0},{2,3},{3,2},{4,5},{5,4},{6,7},{7,6},{8,9},{9,8},{10,11... | collective-permute-start | bytes 393224 | tf_op jit(solution)/shard_map/ppermute | solution.py:302
  21.0 11.4 %copy-start.1 = (f32[1,4,256,512]{3,2,1,0:T(8,128)S(1)}, f32[1,4,256,512]{3,2,1,0:T(8,128)}, u32[]{:S(2)}) copy-start(f32[1,4,256,512]{3,2,1,0:T(8,128)} %param.3) | copy-start | bytes 6291460
  21.0 22.5 %collective-permute-start.10 = (f32[2,4,32,512]{3,2,1,0:T(8,128)S(1)}, f32[2,4,32,512]{3,2,1,0:T(8,128)S(1)}, u32[]{:S(2)}, u32[]{:S(2)}) collective-permute-start(f32[2,4,32,512]{3,2,1,0:T(8,128)S(1)} %shard_map.42.refs_3_.refs_4_), channel_id=1, source_target_pairs={{0,28},{4,8},{8,4},{12,16},{16,12},{20,24},{24,20},{28,0},{1,29},{... | collective-permute-start | bytes 1572872 | tf_op jit(solution)/shard_map/ppermute | solution.py:316
  27.7 8.0 %collective-permute-start.7 = (f32[2,32,512]{2,1,0:T(8,128)S(1)}, f32[2,32,512]{2,1,0:T(8,128)S(1)}, u32[]{:S(2)}, u32[]{:S(2)}) collective-permute-start(f32[2,32,512]{2,1,0:T(8,128)S(1)} %get-tuple-element.33), channel_id=1, source_target_pairs={{0,3},{1,2},{2,1},{3,0},{4,7},{5,6},{6,5},{7,4},{8,11},{9,10},{10,... | collective-permute-start | bytes 393224 | tf_op jit(solution)/shard_map/ppermute | solution.py:302
  31.5 12.0 %collective-permute-start.8 = (f32[2,32,512]{2,1,0:T(8,128)S(1)}, f32[2,32,512]{2,1,0:T(8,128)S(1)}, u32[]{:S(2)}, u32[]{:S(2)}) collective-permute-start(f32[2,32,512]{2,1,0:T(8,128)S(1)} %get-tuple-element.34), channel_id=1, source_target_pairs={{0,2},{1,3},{2,0},{3,1},{4,6},{5,7},{6,4},{7,5},{8,10},{9,11},{10,... | collective-permute-start | bytes 393224 | tf_op jit(solution)/shard_map/ppermute | solution.py:302
  32.3 11.2 %collective-permute-start.9 = (f32[2,32,512]{2,1,0:T(8,128)S(1)}, f32[2,32,512]{2,1,0:T(8,128)S(1)}, u32[]{:S(2)}, u32[]{:S(2)}) collective-permute-start(f32[2,32,512]{2,1,0:T(8,128)S(1)} %get-tuple-element.35), channel_id=1, source_target_pairs={{0,1},{1,0},{2,3},{3,2},{4,5},{5,4},{6,7},{7,6},{8,9},{9,8},{10,11... | collective-permute-start | bytes 393224 | tf_op jit(solution)/shard_map/ppermute | solution.py:302
  32.3 12.1 %collective-permute-start.12 = (f32[2,4,16,512]{3,2,1,0:T(8,128)S(1)}, f32[2,4,16,512]{3,2,1,0:T(8,128)S(1)}, u32[]{:S(2)}, u32[]{:S(2)}) collective-permute-start(f32[2,4,16,512]{3,2,1,0:T(8,128)S(1)} %get-tuple-element.32.refs_4_.refs_5_), channel_id=1, source_target_pairs={{0,28},{4,8},{8,4},{12,16},{16,12},{20,24},{24,20},{28,0},{1,29},{... | collective-permute-start | bytes 786440 | tf_op jit(solution)/shard_map/ppermute | solution.py:316
  43.7 9.2 %collective-permute-start.11 = (f32[2,2,32,512]{3,2,1,0:T(8,128)S(1)}, f32[2,2,32,512]{3,2,1,0:T(8,128)S(1)}, u32[]{:S(2)}, u32[]{:S(2)}) collective-permute-start(f32[2,2,32,512]{3,2,1,0:T(8,128)S(1)} %get-tuple-element.38), channel_id=1, source_target_pairs={{0,1},{1,0},{2,3},{3,2},{4,5},{5,4},{6,7},{7,6},{8,9},{9,8},{10,11... | collective-permute-start | bytes 786440 | tf_op jit(solution)/shard_map/ppermute | solution.py:293
  43.8 11.7 %collective-permute-start.15 = (f32[2,4,16,512]{3,2,1,0:T(8,128)S(1)}, f32[2,4,16,512]{3,2,1,0:T(8,128)S(1)}, u32[]{:S(2)}, u32[]{:S(2)}) collective-permute-start(f32[2,4,16,512]{3,2,1,0:T(8,128)S(1)} %get-tuple-element.36.refs_6_), channel_id=1, source_target_pairs={{0,28},{4,8},{8,4},{12,16},{16,12},{20,24},{24,20},{28,0},{1,29},{... | collective-permute-start | bytes 786440 | tf_op jit(solution)/shard_map/ppermute | solution.py:316
  44.5 11.1 %collective-permute-start.14 = (f32[2,2,16,512]{3,2,1,0:T(8,128)S(1)}, f32[2,2,16,512]{3,2,1,0:T(8,128)S(1)}, u32[]{:S(2)}, u32[]{:S(2)}) collective-permute-start(f32[2,2,16,512]{3,2,1,0:T(8,128)S(1)} %get-tuple-element.40), channel_id=1, source_target_pairs={{0,1},{1,0},{2,3},{3,2},{4,5},{5,4},{6,7},{7,6},{8,9},{9,8},{10,11... | collective-permute-start | bytes 393224 | tf_op jit(solution)/shard_map/ppermute | solution.py:293
  52.9 8.0 %collective-permute-start.13 = (f32[2,32,512]{2,1,0:T(8,128)S(1)}, f32[2,32,512]{2,1,0:T(8,128)S(1)}, u32[]{:S(2)}, u32[]{:S(2)}) collective-permute-start(f32[2,32,512]{2,1,0:T(8,128)S(1)} %shard_map.50.refs_3_), channel_id=1, source_target_pairs={{0,3},{1,2},{2,1},{3,0},{4,7},{5,6},{6,5},{7,4},{8,11},{9,10},{10,... | collective-permute-start | bytes 393224 | tf_op jit(solution)/shard_map/ppermute | solution.py:285
  55.5 6.7 %collective-permute-start.17 = (f32[2,2,16,512]{3,2,1,0:T(8,128)S(1)}, f32[2,2,16,512]{3,2,1,0:T(8,128)S(1)}, u32[]{:S(2)}, u32[]{:S(2)}) collective-permute-start(f32[2,2,16,512]{3,2,1,0:T(8,128)S(1)} %get-tuple-element.42), channel_id=1, source_target_pairs={{0,1},{1,0},{2,3},{3,2},{4,5},{5,4},{6,7},{7,6},{8,9},{9,8},{10,11... | collective-permute-start | bytes 393224 | tf_op jit(solution)/shard_map/ppermute | solution.py:293
  55.7 8.5 %collective-permute-start.16 = (f32[2,16,512]{2,1,0:T(8,128)S(1)}, f32[2,16,512]{2,1,0:T(8,128)S(1)}, u32[]{:S(2)}, u32[]{:S(2)}) collective-permute-start(f32[2,16,512]{2,1,0:T(8,128)S(1)} %shard_map.52.refs_3_), channel_id=1, source_target_pairs={{0,3},{1,2},{2,1},{3,0},{4,7},{5,6},{6,5},{7,4},{8,11},{9,10},{10,... | collective-permute-start | bytes 196616 | tf_op jit(solution)/shard_map/ppermute | solution.py:285
  62.3 6.1 %collective-permute-start.18 = (f32[2,16,512]{2,1,0:T(8,128)S(1)}, f32[2,16,512]{2,1,0:T(8,128)S(1)}, u32[]{:S(2)}, u32[]{:S(2)}) collective-permute-start(f32[2,16,512]{2,1,0:T(8,128)S(1)} %shard_map.54.refs_3_), channel_id=1, source_target_pairs={{0,3},{1,2},{2,1},{3,0},{4,7},{5,6},{6,5},{7,4},{8,11},{9,10},{10,... | collective-permute-start | bytes 196616 | tf_op jit(solution)/shard_map/ppermute | solution.py:285

commit v9 on v8

--- a/solution.py
+++ b/solution.py
@@ -49,6 +49,16 @@
     return mid, (
         mid * (0.2 * pot - 0.05) + NEAR * (near + near_z) + FAR * (far + far_z)
     )
+
+
+def apply_rows(e, pot, near_z, far_z):
+    count, lanes = e.shape[0] - 4, e.shape[1]
+    mid = e[2 : 2 + count]
+    near = e[1 : 1 + count] + e[3 : 3 + count]
+    near = near + (pltpu.roll(mid, 1, 1) + pltpu.roll(mid, lanes - 1, 1))
+    far = e[0:count] + e[4 : 4 + count]
+    far = far + (pltpu.roll(mid, 2, 1) + pltpu.roll(mid, lanes - 2, 1))
+    return mid * (0.2 * pot - 0.05) + NEAR * (near + near_z) + FAR * (far + far_z)
 
 
 def blocks(rows, body):
@@ -138,19 +148,127 @@
     return [0, *range(bands - 1, 0, -1)]
 
 
-def back_kernel(chunk, row, halo, h, *outs):
-    odd = parity()
-    lo, hi = chunk
+def back_kernel(chunk, part, row, halo, h, *outs):
+    odd = parity()
+    lo, hi = part
+    in_halo = slice(lo - chunk[0], hi - chunk[0])
     two = row[0:1, :]
     me = lax.axis_index("orb")
     bands = halo.shape[1]
     for d, out in zip(offsets(bands), outs):
         band = me ^ d
-        d0, d1 = halo_terms(halo, band, odd)
+        d0, d1 = halo_terms(halo, band, odd, in_halo)
         v2 = h[0, band, lo:hi, :] + two * (NEAR * d1 + FAR * d0)
         v3 = h[1, band, lo:hi, :] + two * (FAR * d1)
         out[0] = square(v2, bands)
         out[1] = square(v3, bands)
+
+
+def tail_rows(ref, plane, band, start, more):
+    after = lax.rem(band + 1, ref.shape[1])
+    return jnp.concatenate(
+        [ref[plane, band, start:, :], ref[plane, after, :more, :]], axis=0
+    )
+
+
+def send_rows_kernel(part, psi, *outs):
+    me = lax.axis_index("orb")
+    for d, out in zip(offsets(psi.shape[1]), outs):
+        for plane in range(psi.shape[0]):
+            out[plane] = tail_rows(psi, plane, me ^ d, part[0] - 4, 4)
+
+
+def gather_kernel(*refs):
+    every, halo = refs[-2:]
+    odd = parity()
+    count = halo.shape[0] // (2 * (len(refs) - 3))
+    for k, ref in enumerate(refs[:-2]):
+        every[k] = ref[...]
+        for q in range(2):
+            if k:
+                first = (2 * (k - 1) + q) * count
+                halo[first : first + count, :] = ref[own(q, odd), 2 : 2 + count, :]
+
+
+def rows_kernel(part, c, x, x_in, pot, pot_in, g, t, h):
+    odd = parity()
+    me = lax.axis_index("orb")
+    at = [own(q, odd) for q in range(4)]
+    base, one, two = c[0] - c[2], c[1], 2.0 * c[2]
+    v = [tail_rows(pot, at[q], me, part[0] - 2, 2) for q in range(4)]
+    v += [tail_rows(pot_in, at[q], me, part[0] - 2, 2) for q in range(2)]
+    n = g.shape[2]
+
+    def step(k, carry):
+        e = [x[k, at[q]] for q in range(4)] + [x_in[k, at[q]] for q in range(4)]
+        m = [y[2 : 2 + n] for y in e]
+        g0 = apply_rows(e[0], v[0], m[1], m[2])
+        g1 = apply_rows(e[1], v[1], m[0] + m[2], m[3])
+        g[k, 0], g[k, 1] = g0, g1
+        full = [apply_rows(e[q], v[q], m[q - 1] + m[q + 1], m[q - 2] + m[q + 2])
+                for q in range(2, 6)]
+        f = [y[2 : n - 2] for y in [g0, g1, *full]]
+        for j in range(2):
+            t[k, j] = f[2 + j]
+            q = 2 + j
+            s = apply_rows(full[j], v[q][2 : n - 2], f[q - 1] + f[q + 1], f[q - 2] + f[q + 2])
+            h[k, j] = base * e[q][4 : n] + one * f[q] + two * s
+        return carry
+
+    lax.fori_loop(0, x.shape[0], step, 0)
+
+
+def rows_halo(part, k, halo, first, second, n):
+    if k:
+        at = [(2 * (k - 1) + q) * n for q in range(2)]
+        near, far = [halo[a : a + n, :] for a in at]
+    else:
+        odd = parity()
+        me = lax.axis_index("orb")
+        after = lax.rem(me + 1, first.shape[1])
+        near, far = [
+            jnp.concatenate(
+                [second[q, me, second.shape[2] - (n - 2) :, :], first[q, after, :2, :]],
+                axis=0,
+            )
+            for q in (1 - odd, odd)
+        ]
+    return NEAR * near + FAR * far, FAR * near
+
+
+def rows_face_kernel(part, halo, first, second, g, f, send):
+    n = g.shape[2]
+    for k in range(g.shape[0]):
+        terms = rows_halo(part, k, halo, first, second, n)
+        for q in range(2):
+            value = g[k, q] + terms[q]
+            f[k, q] = value
+            send[k, q] = value[2 : n - 2]
+
+
+def rows_front_kernel(part, c, x, pot, halo, first, second, f, t, h, back, front):
+    odd = parity()
+    me = lax.axis_index("orb")
+    base, one, two = c[0] - c[2], c[1], 2.0 * c[2]
+    n = f.shape[2]
+    v = [
+        tail_rows(pot, own(q, odd), me, part[0] - 2, 2)[2 : n - 2] for q in range(2)
+    ]
+    total = [0.0, 0.0]
+    count = f.shape[0]
+    for k in range(count):
+        d0, d1 = [y[2 : n - 2] for y in rows_halo(part, k, halo, first, second, n)]
+        v2 = h[k, 0] + two * (NEAR * d1 + FAR * d0)
+        v3 = h[k, 1] + two * (FAR * d1)
+        total = [total[0] + square(v2, count), total[1] + square(v3, count)]
+        f0, f1 = f[k, 0], f[k, 1]
+        t2, t3 = t[k, 0], t[k, 1]
+        m0, m1 = f0[2 : n - 2], f1[2 : n - 2]
+        s0 = apply_rows(f0, v[0], m1, t2)
+        s1 = apply_rows(f1, v[1], m0 + t2, t3)
+        front[k, 0] = base * x[k, own(0, odd)][4:n] + one * m0 + two * s0
+        front[k, 1] = base * x[k, own(1, odd)][4:n] + one * m1 + two * s1
+    back[0], back[1] = total
 
 
 def front_kernel(chunks, c, psi, pot, t, *rest):
@@ -212,15 +330,22 @@
     refs[-1][...] = total
 
 
-def join_kernel(places, *refs):
-    out = refs[-1]
-    odd = parity()
-    for (q, (lo, hi)), ref in zip(places[:-1], refs):
+def join_kernel(places, part, *refs):
+    row, halo, h, out = refs[-4:]
+    odd = parity()
+    for (q, (lo, hi)), ref in zip(places, refs):
         for j in range(2):
             out[own(q + j, odd), lo:hi, :] = ref[j]
-    (q, (lo, hi)), (keep, came, far) = places[-1], refs[-4:-1]
+    two = row[0:1, :]
+    count = h.shape[0]
+    total = [0.0, 0.0]
+    for k in range(count):
+        near, far = halo[k, 0], halo[k, 1]
+        v0 = h[k, 0] + two * (NEAR * near + FAR * far)
+        v1 = h[k, 1] + two * (FAR * near)
+        total = [total[0] + square(v0, count), total[1] + square(v1, count)]
     for j in range(2):
-        out[own(q + j, odd), lo:hi, :] = keep[0, j] + came[0, j] + far[j]
+        out[own(j, odd), part[0] : part[1], :] = total[j]
 
 
 class Line:
@@ -263,6 +388,8 @@
     half, part = wide // 2, wide // 4
     chunks = [(0, half), (half, wide)]
     cuts = [(0, half), (half, wide - part), (wide - part, wide)]
+    cut_a, cut_b, cut_c = cuts
+    padded, inner = (part + 8, part + 4)
     face = [(s, (s - 1 if s % 2 == 0 else s + 1) % slabs) for s in range(slabs)]
     partner = [(s, s ^ 1) for s in range(slabs)]
     near = [(i, i ^ 1) for i in range(bands)]
@@ -292,17 +419,16 @@
         )
         return keep, lax.ppermute(send, "orb", near)
 
-    def back_squares(chunk, halo):
+    def over_orb(x, d):
+        return lax.ppermute(x, "orb", [(i, i ^ d) for i in range(bands)])
+
+    def back_squares(chunk, rows, halo):
         keep, *sends = call(
-            functools.partial(back_kernel, chunk),
-            [pair_shape(chunk)[1:]] * bands,
+            functools.partial(back_kernel, chunk, rows),
+            [pair_shape(rows)[1:]] * bands,
             (row, halo, as_bands(h_back)),
         )
-        came = [
-            lax.ppermute(x, "orb", [(i, i ^ d) for i in range(bands)])
-            for d, x in zip(offsets(bands)[1:], sends)
-        ]
-        return keep, *came
+        return keep, *[over_orb(x, d) for d, x in zip(offsets(bands)[1:], sends)]
 
     def sum_all(keep, *came, weight=0):
         return call(sum_all_kernel, keep.shape, (keep, *came), weight=weight)
@@ -313,7 +439,7 @@
             [slab_shape(cut) for cut in parts],
             (halo, as_bands(g)),
         )
-        return fs, [lax.ppermute(x, "slab", face) for x in fs]
+        return fs, lax.ppermute(fs[0], "slab", face)
 
     psi_in = lax.ppermute(psi, "slab", partner)
     pot_in = lax.ppermute(potential, "slab", partner)
@@ -327,6 +453,12 @@
             hbm=True,
         )
         halos.append(lax.ppermute(piece, "slab", face))
+    keep, *sends = call(
+        functools.partial(send_rows_kernel, cut_c),
+        [(planes, padded, lanes)] * bands,
+        (as_bands(psi),),
+    )
+    x_parts = [keep, *[over_orb(x, d) for d, x in zip(offsets(bands)[1:], sends)]]
     g = call(start_kernel, plane2, (psi, potential), flops=24 * cells)
     t, h_back, row = call(
         inner_kernel,
@@ -339,12 +471,24 @@
     def summed(keep, came, from_far, weight=0):
         return call(sum_kernel, from_far.shape, (keep, came, from_far), weight=weight)
 
-    cut_a, cut_b, cut_c = cuts
-    back0 = back_squares(chunks[0], halos[0])
-    f0, (face_a,) = faces(chunks[0], halos[0], [cut_a])
-    back1 = back_squares(chunks[1], halos[1])
-    f1, (face_b, face_c) = faces(chunks[1], halos[1], [cut_b, cut_c])
-    back0 = sum_all(*back0)
+    back0 = back_squares(chunks[0], cut_a, halos[0])
+    f0, face_a = faces(chunks[0], halos[0], [cut_a])
+    x, piece = call(
+        gather_kernel,
+        [(bands, planes, padded, lanes), (2 * (bands - 1) * inner, lanes)],
+        x_parts,
+    )
+    x_halo = lax.ppermute(piece, "slab", face)
+    x_in = lax.ppermute(x, "slab", partner)
+    back1 = back_squares(chunks[1], cut_b, halos[1])
+    f1, face_b = faces(chunks[1], halos[1], [cut_b, cut_c])
+    x_first, x_t, x_back = call(
+        functools.partial(rows_kernel, cut_c),
+        [(bands, 2, inner, lanes)] + [(bands, 2, part, lanes)] * 2,
+        (coeffs, x, x_in, as_bands(potential), as_bands(pot_in)),
+        scalars=1,
+    )
+    back0 = sum_all(*back0, weight=0)
     h_front = call(
         functools.partial(front_kernel, cuts),
         plane2,
@@ -354,20 +498,30 @@
         flops=40 * cells,
         weight=6_000_000_000,
     )
-    back1 = sum_all(*back1)
+    back1 = sum_all(*back1, weight=0)
     front_a = squares(cut_a, face_a)
+    x_f, piece = call(
+        functools.partial(rows_face_kernel, cut_c),
+        [(bands, 2, inner, lanes), (bands, 2, part, lanes)],
+        (x_halo, *halos, x_first),
+    )
+    x_face = lax.ppermute(piece, "slab", face)
+    front_a = add_far(*front_a)
+    back2, x_front = call(
+        functools.partial(rows_front_kernel, cut_c),
+        [(2, part, lanes), (bands, 2, part, lanes)],
+        (coeffs, x, as_bands(potential), x_halo, *halos, x_f, x_t, x_back),
+        scalars=1,
+    )
     front_b = squares(cut_b, face_b)
-    front_a = add_far(*front_a)
-    front_c = squares(cut_c, face_c)
+    front_a = summed(*front_a)
     front_b = add_far(*front_b)
-    front_a = summed(*front_a)
-    front_c = add_far(*front_c)
     front_b = summed(*front_b)
-    places = [(2, chunk) for chunk in chunks] + [(0, cut) for cut in cuts]
+    places = [(2, cut) for cut in cuts] + [(0, cut_a), (0, cut_b)]
     return call(
-        functools.partial(join_kernel, places),
+        functools.partial(join_kernel, places, cut_c),
         (planes, wide, lanes),
-        (back0, back1, front_a, front_b, *front_c),
+        (back0, back1, back2, front_a, front_b, row, x_face, x_front),
     )
 
 

time: 69.4 us -> 79.4 us (1.14)
  the two profiles are of different devices: /device:TPU:6 before, /device:TPU:0 now
where the time goes in v9:
time: 79.4 us; the launch traced here: 79.3 us
  waiting for transfers between devices  29.5 us (37%)
  starting transfers between devices  29.3 us (37%)
  Pallas kernels  18.6 us (23%)
  local copies, waits for them, and re-layouts  1.6 us (2%)
    pallas_call x23, Pallas kernels, __call__(): pl.pallas_call(body, out_shape=shapes, in_specs=[smem] * scalars + [pl.Bl...  18.6 us
    ppermute x9, starting transfers between devices, over_orb(): return lax.ppermute(x, 'orb', [(i, i ^ d) for i in range(bands)])  13.3 us
    ppermute x2, waiting for transfers between devices, shards(): halos.append(lax.ppermute(piece, 'slab', face))  8.65 us
    ppermute x2, waiting for transfers between devices, add_far(): return (keep, came, lax.ppermute(total, 'orb', far))  6.55 us
    ppermute x9, waiting for transfers between devices, over_orb(): return lax.ppermute(x, 'orb', [(i, i ^ d) for i in range(bands)])  5.83 us
    ppermute x2, starting transfers between devices, shards(): halos.append(lax.ppermute(piece, 'slab', face))  5.1 us
    ppermute x2, starting transfers between devices, add_far(): return (keep, came, lax.ppermute(total, 'orb', far))  5.08 us
    ppermute x1, waiting for transfers between devices, shards(): x_halo = lax.ppermute(piece, 'slab', face)  3.85 us
  transfers between devices with their start and end apart: 22, of which 9 were waited for; matrix products, arithmetic and copies ran while one was open for 0% of the time, Pallas kernels for 22%

profile of v9, /device:TPU:0, one launch (start us, length us, event | category | flops | bytes accessed | tf_op | source)
XLA Modules:
  0.0 79.3 jit_solution(12614296213558681091)
XLA Ops:
  0.0 0.5 collective-permute-start
  0.5 0.1 collective-permute-start.1
  0.5 1.6 %copy-done = f32[1,4,256,512]{3,2,1,0:T(8,128)S(1)} copy-done((f32[1,4,256,512]{3,2,1,0:T(8,128)S(1)}, f32[1,4,256,512]{3,2,1,0:T(8,128)}, u32[]{:S(2)}) %copy-start) | copy-done | bytes 2097176
  2.2 3.6 %collective-permute-start.2 = (f32[2,4,32,512]{3,2,1,0:T(8,128)S(1)}, f32[2,4,32,512]{3,2,1,0:T(8,128)S(1)}, u32[]{:S(2)}, u32[]{:S(2)}) collective-permute-start(f32[2,4,32,512]{3,2,1,0:T(8,128)S(1)} %shard_map.37.refs_1_), channel_id=1, source_target_pairs={{0,28},{4,8},{8,4},{12,16},{16,12},{20,24},{24,20},{28,0},{1,29},{... | collective-permute-start | bytes 1572872 | tf_op jit(solution)/shard_map/ppermute | solution.py:455
  5.8 0.0 copy-start.2
  5.8 0.1 shard_map.39
  5.9 3.7 %collective-permute-start.6 = (f32[4,24,512]{2,1,0:T(8,128)S(1)}, f32[4,24,512]{2,1,0:T(8,128)S(1)}, u32[]{:S(2)}, u32[]{:S(2)}) collective-permute-start(f32[4,24,512]{2,1,0:T(8,128)S(1)} %get-tuple-element.43), channel_id=1, source_target_pairs={{0,3},{1,2},{2,1},{3,0},{4,7},{5,6},{6,5},{7,4},{8,11},{9,10},{10,... | collective-permute-start | bytes 589832 | tf_op jit(solution)/shard_map/ppermute | solution.py:423
  9.6 0.0 collective-permute-start.7
  9.6 0.0 collective-permute-done.refs_3_
  9.6 0.8 collective-permute-start.8
  10.3 2.5 %shard_map.40.refs_5_.refs_6_ = f32[2,256,512]{2,1,0:T(8,128)S(1)} custom-call(f32[4,256,512]{2,1,0:T(8,128)S(1)} %bitcast.11, f32[4,256,512]{2,1,0:T(8,128)S(1)} %copy-done.2, f32[4,24,512]{2,1,0:T(8,128)S(1)} %get-tuple-element.35.refs_2_.refs_0_), custom_call_target="tpu_custom_call" | custom-call | flops 6291456 | bytes 5242880 | tf_op jit(solution)/shard_map/pallas_call | solution.py:366
  12.9 7.0 %shard_map.41 = (f32[2,256,512]{2,1,0:T(8,128)S(1)}, f32[2,256,512]{2,1,0:T(8,128)S(1)}, f32[8,512]{1,0:T(8,128)S(1)}) custom-call(f32[3]{0:T(128)S(1)} %copy-done.3, f32[4,256,512]{2,1,0:T(8,128)S(1)} %bitcast.12, f32[4,256,512]{2,1,0:T(8,128)S(1)} %copy-done.2, f32[4,256,512]{2,1,0:T(8,128)S(1)} %collective-permute-done.refs_3_, ...), custom_call_target="tpu_custom_call" | custom-call | flops 20971520 | bytes 11550732 | tf_op jit(solution)/shard_map/pallas_call | solution.py:366
  19.9 0.2 shard_map.42
  20.0 0.1 shard_map.43.refs_4_
  20.2 5.8 %collective-permute-done.7.refs_2_ = f32[4,24,512]{2,1,0:T(8,128)S(1)} collective-permute-done((f32[4,24,512]{2,1,0:T(8,128)S(1)}, f32[4,24,512]{2,1,0:T(8,128)S(1)}, u32[]{:S(2)}, u32[]{:S(2)}) %collective-permute-start.7) | collective-permute-done | bytes 196640 | tf_op jit(solution)/shard_map/ppermute | solution.py:423
  26.0 0.1 shard_map.44
  26.0 0.1 collective-permute-start.9
  26.1 1.5 %collective-permute-start.10 = (f32[2,4,32,512]{3,2,1,0:T(8,128)S(1)}, f32[2,4,32,512]{3,2,1,0:T(8,128)S(1)}, u32[]{:S(2)}, u32[]{:S(2)}) collective-permute-start(f32[2,4,32,512]{3,2,1,0:T(8,128)S(1)} %shard_map.38.refs_1_), channel_id=1, source_target_pairs={{0,28},{4,8},{8,4},{12,16},{16,12},{20,24},{24,20},{28,0},{1,29},{... | collective-permute-start | bytes 1572872 | tf_op jit(solution)/shard_map/ppermute | solution.py:455
  27.7 2.5 %collective-permute-start.3 = (f32[2,32,512]{2,1,0:T(8,128)S(1)}, f32[2,32,512]{2,1,0:T(8,128)S(1)}, u32[]{:S(2)}, u32[]{:S(2)}) collective-permute-start(f32[2,32,512]{2,1,0:T(8,128)S(1)} %get-tuple-element.40), channel_id=1, source_target_pairs={{0,3},{1,2},{2,1},{3,0},{4,7},{5,6},{6,5},{7,4},{8,11},{9,10},{10,... | collective-permute-start | bytes 393224 | tf_op jit(solution)/shard_map/ppermute | solution.py:423
  30.1 1.9 %collective-permute-start.5 = (f32[2,32,512]{2,1,0:T(8,128)S(1)}, f32[2,32,512]{2,1,0:T(8,128)S(1)}, u32[]{:S(2)}, u32[]{:S(2)}) collective-permute-start(f32[2,32,512]{2,1,0:T(8,128)S(1)} %get-tuple-element.42), channel_id=1, source_target_pairs={{0,1},{1,0},{2,3},{3,2},{4,5},{5,4},{6,7},{7,6},{8,9},{9,8},{10,11... | collective-permute-start | bytes 393224 | tf_op jit(solution)/shard_map/ppermute | solution.py:423
  32.1 8.6 %collective-permute-done.10.refs_1_.refs_0_.refs_2_.refs_5_ = f32[2,4,32,512]{3,2,1,0:T(8,128)S(1)} collective-permute-done((f32[2,4,32,512]{3,2,1,0:T(8,128)S(1)}, f32[2,4,32,512]{3,2,1,0:T(8,128)S(1)}, u32[]{:S(2)}, u32[]{:S(2)}) %collective-permute-start.10) | collective-permute-done | bytes 524320 | tf_op jit(solution)/shard_map/ppermute | solution.py:455
  40.7 1.1 %collective-permute-start.15 = (f32[2,4,32,512]{3,2,1,0:T(8,128)S(1)}, f32[2,4,32,512]{3,2,1,0:T(8,128)S(1)}, u32[]{:S(2)}, u32[]{:S(2)}) collective-permute-start(f32[2,4,32,512]{3,2,1,0:T(8,128)S(1)} %shard_map.43.refs_4_), channel_id=1, source_target_pairs={{0,28},{4,8},{8,4},{12,16},{16,12},{20,24},{24,20},{28,0},{1,29},{... | collective-permute-start | bytes 1572872 | tf_op jit(solution)/shard_map/ppermute | solution.py:442
  41.8 0.1 shard_map.45
  41.9 0.1 shard_map.46
  42.0 2.5 %collective-permute-start.11 = (f32[2,16,512]{2,1,0:T(8,128)S(1)}, f32[2,16,512]{2,1,0:T(8,128)S(1)}, u32[]{:S(2)}, u32[]{:S(2)}) collective-permute-start(f32[2,16,512]{2,1,0:T(8,128)S(1)} %get-tuple-element.50), channel_id=1, source_target_pairs={{0,3},{1,2},{2,1},{3,0},{4,7},{5,6},{6,5},{7,4},{8,11},{9,10},{10,... | collective-permute-start | bytes 196616 | tf_op jit(solution)/shard_map/ppermute | solution.py:423
  44.5 2.8 %shard_map.47 = (f32[4,2,20,512]{3,2,1,0:T(8,128)S(1)}, f32[4,2,16,512]{3,2,1,0:T(8,128)S(1)}, f32[4,2,16,512]{3,2,1,0:T(8,128)S(1)}) custom-call(f32[3]{0:T(128)S(1)} %copy-done.3, f32[4,4,24,512]{3,2,1,0:T(8,128)S(1)} %get-tuple-element.46.refs_3_.refs_1_, f32[4,4,24,512]{3,2,1,0:T(8,128)S(1)} %collective-permute-done.9.refs_2_, ...), custom_call_target="tpu_custom_call" | custom-call | bytes 6619148 | tf_op jit(solution)/shard_map/pallas_call | solution.py:366
  47.3 0.1 collective-permute-start.12
  47.4 1.9 %collective-permute-start.13 = (f32[2,16,512]{2,1,0:T(8,128)S(1)}, f32[2,16,512]{2,1,0:T(8,128)S(1)}, u32[]{:S(2)}, u32[]{:S(2)}) collective-permute-start(f32[2,16,512]{2,1,0:T(8,128)S(1)} %get-tuple-element.52), channel_id=1, source_target_pairs={{0,1},{1,0},{2,3},{3,2},{4,5},{5,4},{6,7},{7,6},{8,9},{9,8},{10,11... | collective-permute-start | bytes 196616 | tf_op jit(solution)/shard_map/ppermute | solution.py:423
  49.3 0.7 collective-permute-start.14
  50.1 3.2 %shard_map.49.refs_4_ = f32[2,256,512]{2,1,0:T(8,128)S(1)} custom-call(f32[3]{0:T(128)S(1)} %copy-done.3, f32[4,256,512]{2,1,0:T(8,128)S(1)} %bitcast.13, f32[4,256,512]{2,1,0:T(8,128)S(1)} %copy-done.2, f32[2,256,512]{2,1,0:T(8,128)S(1)} %get-tuple-element.38.refs_3_, f32[2,4,32,512]{3,2,1,0:T(8,128)S(1)} %shard_map.43.refs_4_, ...), custom_call_target="tpu_custom_call" | custom-call | flops 6010485760 | bytes 7340044 | tf_op jit(solution)/shard_map/pallas_call | solution.py:366
  53.3 2.5 %collective-permute-done.15.refs_1_ = f32[2,4,32,512]{3,2,1,0:T(8,128)S(1)} collective-permute-done((f32[2,4,32,512]{3,2,1,0:T(8,128)S(1)}, f32[2,4,32,512]{3,2,1,0:T(8,128)S(1)}, u32[]{:S(2)}, u32[]{:S(2)}) %collective-permute-start.15) | collective-permute-done | bytes 524320 | tf_op jit(solution)/shard_map/ppermute | solution.py:442
  55.8 0.1 shard_map.51
  55.9 0.1 collective-permute-start.16
  56.0 1.2 %collective-permute-start.18 = (f32[2,4,16,512]{3,2,1,0:T(8,128)S(1)}, f32[2,4,16,512]{3,2,1,0:T(8,128)S(1)}, u32[]{:S(2)}, u32[]{:S(2)}) collective-permute-start(f32[2,4,16,512]{3,2,1,0:T(8,128)S(1)} %get-tuple-element.48.refs_5_), channel_id=1, source_target_pairs={{0,28},{4,8},{8,4},{12,16},{16,12},{20,24},{24,20},{28,0},{1,29},{... | collective-permute-start | bytes 786440 | tf_op jit(solution)/shard_map/ppermute | solution.py:442
  57.2 3.9 %collective-permute-done.14.refs_0_.refs_3_ = f32[120,512]{1,0:T(8,128)S(1)} collective-permute-done((f32[120,512]{1,0:T(8,128)S(1)}, f32[120,512]{1,0:T(8,128)S(1)}, u32[]{:S(2)}, u32[]{:S(2)}) %collective-permute-start.14) | collective-permute-done | bytes 245792 | tf_op jit(solution)/shard_map/ppermute | solution.py:481
  61.1 0.1 shard_map.52
  61.2 1.2 %collective-permute-start.21 = (f32[4,2,16,512]{3,2,1,0:T(8,128)S(1)}, f32[4,2,16,512]{3,2,1,0:T(8,128)S(1)}, u32[]{:S(2)}, u32[]{:S(2)}) collective-permute-start(f32[4,2,16,512]{3,2,1,0:T(8,128)S(1)} %get-tuple-element.63), channel_id=1, source_target_pairs={{0,28},{4,8},{8,4},{12,16},{16,12},{20,24},{24,20},{28,0},{1,29},{... | collective-permute-start | bytes 786440 | tf_op jit(solution)/shard_map/ppermute | solution.py:508
  62.4 0.4 collective-permute-done.16.refs_1_
  62.8 2.5 %collective-permute-start.17 = (f32[2,32,512]{2,1,0:T(8,128)S(1)}, f32[2,32,512]{2,1,0:T(8,128)S(1)}, u32[]{:S(2)}, u32[]{:S(2)}) collective-permute-start(f32[2,32,512]{2,1,0:T(8,128)S(1)} %shard_map.53.refs_9_), channel_id=1, source_target_pairs={{0,3},{1,2},{2,1},{3,0},{4,7},{5,6},{6,5},{7,4},{8,11},{9,10},{10,... | collective-permute-start | bytes 393224 | tf_op jit(solution)/shard_map/ppermute | solution.py:412
  65.3 1.2 %shard_map.54 = (f32[2,16,512]{2,1,0:T(8,128)S(1)}, f32[4,2,16,512]{3,2,1,0:T(8,128)S(1)}) custom-call(f32[3]{0:T(128)S(1)} %copy-done.3, f32[4,4,24,512]{3,2,1,0:T(8,128)S(1)} %get-tuple-element.46.refs_3_.refs_1_, f32[4,4,64,512]{3,2,1,0:T(8,128)S(1)} %bitcast.15, f32[120,512]{1,0:T(8,128)S(1)} %collective-permute-done.14.refs_0_.refs_3_, ...), custom_call_target="tpu_custom_call" | custom-call | bytes 5357580 | tf_op jit(solution)/shard_map/pallas_call | solution.py:366
  66.5 0.2 collective-permute-done.18.refs_1_
  66.7 0.1 shard_map.55
  66.8 0.9 %collective-permute-start.19 = (f32[2,2,16,512]{3,2,1,0:T(8,128)S(1)}, f32[2,2,16,512]{3,2,1,0:T(8,128)S(1)}, u32[]{:S(2)}, u32[]{:S(2)}) collective-permute-start(f32[2,2,16,512]{3,2,1,0:T(8,128)S(1)} %get-tuple-element.62), channel_id=1, source_target_pairs={{0,1},{1,0},{2,3},{3,2},{4,5},{5,4},{6,7},{7,6},{8,9},{9,8},{10,11... | collective-permute-start | bytes 393224 | tf_op jit(solution)/shard_map/ppermute | solution.py:420
  67.6 3.0 %collective-permute-done.17.refs_2_ = f32[2,32,512]{2,1,0:T(8,128)S(1)} collective-permute-done((f32[2,32,512]{2,1,0:T(8,128)S(1)}, f32[2,32,512]{2,1,0:T(8,128)S(1)}, u32[]{:S(2)}, u32[]{:S(2)}) %collective-permute-start.17) | collective-permute-done | bytes 131104 | tf_op jit(solution)/shard_map/ppermute | solution.py:412
  70.6 1.6 %collective-permute-done.19.refs_1_ = f32[2,2,16,512]{3,2,1,0:T(8,128)S(1)} collective-permute-done((f32[2,2,16,512]{3,2,1,0:T(8,128)S(1)}, f32[2,2,16,512]{3,2,1,0:T(8,128)S(1)}, u32[]{:S(2)}, u32[]{:S(2)}) %collective-permute-start.19) | collective-permute-done | bytes 131104 | tf_op jit(solution)/shard_map/ppermute | solution.py:420
  72.2 2.5 %collective-permute-start.20 = (f32[2,16,512]{2,1,0:T(8,128)S(1)}, f32[2,16,512]{2,1,0:T(8,128)S(1)}, u32[]{:S(2)}, u32[]{:S(2)}) collective-permute-start(f32[2,16,512]{2,1,0:T(8,128)S(1)} %shard_map.57.refs_3_), channel_id=1, source_target_pairs={{0,3},{1,2},{2,1},{3,0},{4,7},{5,6},{6,5},{7,4},{8,11},{9,10},{10,... | collective-permute-start | bytes 196616 | tf_op jit(solution)/shard_map/ppermute | solution.py:412
  74.7 3.6 %collective-permute-done.20.refs_2_ = f32[2,16,512]{2,1,0:T(8,128)S(1)} collective-permute-done((f32[2,16,512]{2,1,0:T(8,128)S(1)}, f32[2,16,512]{2,1,0:T(8,128)S(1)}, u32[]{:S(2)}, u32[]{:S(2)}) %collective-permute-start.20) | collective-permute-done | bytes 65568 | tf_op jit(solution)/shard_map/ppermute | solution.py:412
  78.4 0.9 %shard_map.59 = f32[4,64,512]{2,1,0:T(8,128)} custom-call(f32[2,32,512]{2,1,0:T(8,128)S(1)} %shard_map.48.refs_7_.refs_0_, f32[2,16,512]{2,1,0:T(8,128)S(1)} %shard_map.50.refs_3_.refs_1_, f32[2,16,512]{2,1,0:T(8,128)S(1)} %get-tuple-element.60.refs_3_.refs_2_, f32[2,32,512]{2,1,0:T(8,128)S(1)} %shard_map.56.refs_2_.refs_3_, ...), custom_call_target="tpu_custom_call" | custom-call | bytes 1523712 | tf_op jit(solution)/shard_map/pallas_call | solution.py:366
  (27 shorter events, 0.2 us)
Async XLA Ops:
  0.0 9.6 %collective-permute-start = (f32[4,256,512]{2,1,0:T(8,128)}, f32[4,256,512]{2,1,0:T(8,128)S(1)}, u32[]{:S(2)}, u32[]{:S(2)}) collective-permute-start(f32[4,256,512]{2,1,0:T(8,128)} %bitcast.7), channel_id=1, source_target_pairs={{0,4},{4,0},{8,12},{12,8},{16,20},{20,16},{24,28},{28,24},{1,5},{5... | collective-permute-start | bytes 6291464 | tf_op jit(solution)/shard_map/ppermute | solution.py:444
  0.5 12.4 %collective-permute-start.1 = (f32[4,256,512]{2,1,0:T(8,128)}, f32[4,256,512]{2,1,0:T(8,128)S(1)}, u32[]{:S(2)}, u32[]{:S(2)}) collective-permute-start(f32[4,256,512]{2,1,0:T(8,128)} %refs_2_.3), channel_id=1, source_target_pairs={{0,4},{4,0},{8,12},{12,8},{16,20},{20,16},{24,28},{28,24},{1,5},{5... | collective-permute-start | bytes 6291464 | tf_op jit(solution)/shard_map/ppermute | solution.py:445
  0.5 1.6 %copy-start = (f32[1,4,256,512]{3,2,1,0:T(8,128)S(1)}, f32[1,4,256,512]{3,2,1,0:T(8,128)}, u32[]{:S(2)}) copy-start(f32[1,4,256,512]{3,2,1,0:T(8,128)} %param.3) | copy-start | bytes 6291460
  2.2 17.7 %collective-permute-start.2 = (f32[2,4,32,512]{3,2,1,0:T(8,128)S(1)}, f32[2,4,32,512]{3,2,1,0:T(8,128)S(1)}, u32[]{:S(2)}, u32[]{:S(2)}) collective-permute-start(f32[2,4,32,512]{3,2,1,0:T(8,128)S(1)} %shard_map.37.refs_1_), channel_id=1, source_target_pairs={{0,28},{4,8},{8,4},{12,16},{16,12},{20,24},{24,20},{28,0},{1,29},{... | collective-permute-start | bytes 1572872 | tf_op jit(solution)/shard_map/ppermute | solution.py:455
  5.8 4.6 %copy-start.2 = (f32[4,256,512]{2,1,0:T(8,128)S(1)}, f32[4,256,512]{2,1,0:T(8,128)}, u32[]{:S(2)}) copy-start(f32[4,256,512]{2,1,0:T(8,128)} %refs_2_.3) | copy-start | bytes 6291460
  5.9 14.3 %collective-permute-start.6 = (f32[4,24,512]{2,1,0:T(8,128)S(1)}, f32[4,24,512]{2,1,0:T(8,128)S(1)}, u32[]{:S(2)}, u32[]{:S(2)}) collective-permute-start(f32[4,24,512]{2,1,0:T(8,128)S(1)} %get-tuple-element.43), channel_id=1, source_target_pairs={{0,3},{1,2},{2,1},{3,0},{4,7},{5,6},{6,5},{7,4},{8,11},{9,10},{10,... | collective-permute-start | bytes 589832 | tf_op jit(solution)/shard_map/ppermute | solution.py:423
  9.6 16.4 %collective-permute-start.7 = (f32[4,24,512]{2,1,0:T(8,128)S(1)}, f32[4,24,512]{2,1,0:T(8,128)S(1)}, u32[]{:S(2)}, u32[]{:S(2)}) collective-permute-start(f32[4,24,512]{2,1,0:T(8,128)S(1)} %get-tuple-element.44), channel_id=1, source_target_pairs={{0,2},{1,3},{2,0},{3,1},{4,6},{5,7},{6,4},{7,5},{8,10},{9,11},{10,... | collective-permute-start | bytes 589832 | tf_op jit(solution)/shard_map/ppermute | solution.py:423
  9.6 16.4 %collective-permute-start.8 = (f32[4,24,512]{2,1,0:T(8,128)S(1)}, f32[4,24,512]{2,1,0:T(8,128)S(1)}, u32[]{:S(2)}, u32[]{:S(2)}) collective-permute-start(f32[4,24,512]{2,1,0:T(8,128)S(1)} %get-tuple-element.45), channel_id=1, source_target_pairs={{0,1},{1,0},{2,3},{3,2},{4,5},{5,4},{6,7},{7,6},{8,9},{9,8},{10,11... | collective-permute-start | bytes 589832 | tf_op jit(solution)/shard_map/ppermute | solution.py:423
  10.3 2.5 %copy-start.3 = (f32[3]{0:T(128)S(1)}, f32[3]{0:T(128)}, u32[]{:S(2)}) copy-start(f32[3]{0:T(128)} %refs_0_.7) | copy-start | bytes 40
  26.0 15.9 %collective-permute-start.9 = (f32[4,4,24,512]{3,2,1,0:T(8,128)S(1)}, f32[4,4,24,512]{3,2,1,0:T(8,128)S(1)}, u32[]{:S(2)}, u32[]{:S(2)}) collective-permute-start(f32[4,4,24,512]{3,2,1,0:T(8,128)S(1)} %get-tuple-element.46.refs_3_.refs_1_), channel_id=1, source_target_pairs={{0,4},{4,0},{8,12},{12,8},{16,20},{20,16},{24,28},{28,24},{1,5},{5... | collective-permute-start | bytes 2359304 | tf_op jit(solution)/shard_map/ppermute | solution.py:482
  26.1 14.6 %collective-permute-start.10 = (f32[2,4,32,512]{3,2,1,0:T(8,128)S(1)}, f32[2,4,32,512]{3,2,1,0:T(8,128)S(1)}, u32[]{:S(2)}, u32[]{:S(2)}) collective-permute-start(f32[2,4,32,512]{3,2,1,0:T(8,128)S(1)} %shard_map.38.refs_1_), channel_id=1, source_target_pairs={{0,28},{4,8},{8,4},{12,16},{16,12},{20,24},{24,20},{28,0},{1,29},{... | collective-permute-start | bytes 1572872 | tf_op jit(solution)/shard_map/ppermute | solution.py:455
  27.7 19.6 %collective-permute-start.3 = (f32[2,32,512]{2,1,0:T(8,128)S(1)}, f32[2,32,512]{2,1,0:T(8,128)S(1)}, u32[]{:S(2)}, u32[]{:S(2)}) collective-permute-start(f32[2,32,512]{2,1,0:T(8,128)S(1)} %get-tuple-element.40), channel_id=1, source_target_pairs={{0,3},{1,2},{2,1},{3,0},{4,7},{5,6},{6,5},{7,4},{8,11},{9,10},{10,... | collective-permute-start | bytes 393224 | tf_op jit(solution)/shard_map/ppermute | solution.py:423
  30.1 17.3 %collective-permute-start.4 = (f32[2,32,512]{2,1,0:T(8,128)S(1)}, f32[2,32,512]{2,1,0:T(8,128)S(1)}, u32[]{:S(2)}, u32[]{:S(2)}) collective-permute-start(f32[2,32,512]{2,1,0:T(8,128)S(1)} %get-tuple-element.41), channel_id=1, source_target_pairs={{0,2},{1,3},{2,0},{3,1},{4,6},{5,7},{6,4},{7,5},{8,10},{9,11},{10,... | collective-permute-start | bytes 393224 | tf_op jit(solution)/shard_map/ppermute | solution.py:423
  30.1 19.2 %collective-permute-start.5 = (f32[2,32,512]{2,1,0:T(8,128)S(1)}, f32[2,32,512]{2,1,0:T(8,128)S(1)}, u32[]{:S(2)}, u32[]{:S(2)}) collective-permute-start(f32[2,32,512]{2,1,0:T(8,128)S(1)} %get-tuple-element.42), channel_id=1, source_target_pairs={{0,1},{1,0},{2,3},{3,2},{4,5},{5,4},{6,7},{7,6},{8,9},{9,8},{10,11... | collective-permute-start | bytes 393224 | tf_op jit(solution)/shard_map/ppermute | solution.py:423
  40.7 15.1 %collective-permute-start.15 = (f32[2,4,32,512]{3,2,1,0:T(8,128)S(1)}, f32[2,4,32,512]{3,2,1,0:T(8,128)S(1)}, u32[]{:S(2)}, u32[]{:S(2)}) collective-permute-start(f32[2,4,32,512]{3,2,1,0:T(8,128)S(1)} %shard_map.43.refs_4_), channel_id=1, source_target_pairs={{0,28},{4,8},{8,4},{12,16},{16,12},{20,24},{24,20},{28,0},{1,29},{... | collective-permute-start | bytes 1572872 | tf_op jit(solution)/shard_map/ppermute | solution.py:442
  42.0 11.3 %collective-permute-start.11 = (f32[2,16,512]{2,1,0:T(8,128)S(1)}, f32[2,16,512]{2,1,0:T(8,128)S(1)}, u32[]{:S(2)}, u32[]{:S(2)}) collective-permute-start(f32[2,16,512]{2,1,0:T(8,128)S(1)} %get-tuple-element.50), channel_id=1, source_target_pairs={{0,3},{1,2},{2,1},{3,0},{4,7},{5,6},{6,5},{7,4},{8,11},{9,10},{10,... | collective-permute-start | bytes 196616 | tf_op jit(solution)/shard_map/ppermute | solution.py:423
  44.5 5.5 %copy-start.1 = (f32[1,4,256,512]{3,2,1,0:T(8,128)S(1)}, f32[1,4,256,512]{3,2,1,0:T(8,128)}, u32[]{:S(2)}) copy-start(f32[1,4,256,512]{3,2,1,0:T(8,128)} %param.3) | copy-start | bytes 6291460
  47.3 5.9 %collective-permute-start.12 = (f32[2,16,512]{2,1,0:T(8,128)S(1)}, f32[2,16,512]{2,1,0:T(8,128)S(1)}, u32[]{:S(2)}, u32[]{:S(2)}) collective-permute-start(f32[2,16,512]{2,1,0:T(8,128)S(1)} %get-tuple-element.51), channel_id=1, source_target_pairs={{0,2},{1,3},{2,0},{3,1},{4,6},{5,7},{6,4},{7,5},{8,10},{9,11},{10,... | collective-permute-start | bytes 196616 | tf_op jit(solution)/shard_map/ppermute | solution.py:423
  47.4 5.9 %collective-permute-start.13 = (f32[2,16,512]{2,1,0:T(8,128)S(1)}, f32[2,16,512]{2,1,0:T(8,128)S(1)}, u32[]{:S(2)}, u32[]{:S(2)}) collective-permute-start(f32[2,16,512]{2,1,0:T(8,128)S(1)} %get-tuple-element.52), channel_id=1, source_target_pairs={{0,1},{1,0},{2,3},{3,2},{4,5},{5,4},{6,7},{7,6},{8,9},{9,8},{10,11... | collective-permute-start | bytes 196616 | tf_op jit(solution)/shard_map/ppermute | solution.py:423
  49.3 11.8 %collective-permute-start.14 = (f32[120,512]{1,0:T(8,128)S(1)}, f32[120,512]{1,0:T(8,128)S(1)}, u32[]{:S(2)}, u32[]{:S(2)}) collective-permute-start(f32[120,512]{1,0:T(8,128)S(1)} %get-tuple-element.54), channel_id=1, source_target_pairs={{0,28},{4,8},{8,4},{12,16},{16,12},{20,24},{24,20},{28,0},{1,29},{... | collective-permute-start | bytes 737288 | tf_op jit(solution)/shard_map/ppermute | solution.py:481
  55.9 6.8 %collective-permute-start.16 = (f32[2,2,32,512]{3,2,1,0:T(8,128)S(1)}, f32[2,2,32,512]{3,2,1,0:T(8,128)S(1)}, u32[]{:S(2)}, u32[]{:S(2)}) collective-permute-start(f32[2,2,32,512]{3,2,1,0:T(8,128)S(1)} %get-tuple-element.59), channel_id=1, source_target_pairs={{0,1},{1,0},{2,3},{3,2},{4,5},{5,4},{6,7},{7,6},{8,9},{9,8},{10,11... | collective-permute-start | bytes 786440 | tf_op jit(solution)/shard_map/ppermute | solution.py:420
  56.0 10.7 %collective-permute-start.18 = (f32[2,4,16,512]{3,2,1,0:T(8,128)S(1)}, f32[2,4,16,512]{3,2,1,0:T(8,128)S(1)}, u32[]{:S(2)}, u32[]{:S(2)}) collective-permute-start(f32[2,4,16,512]{3,2,1,0:T(8,128)S(1)} %get-tuple-element.48.refs_5_), channel_id=1, source_target_pairs={{0,28},{4,8},{8,4},{12,16},{16,12},{20,24},{24,20},{28,0},{1,29},{... | collective-permute-start | bytes 786440 | tf_op jit(solution)/shard_map/ppermute | solution.py:442
  61.2 17.2 %collective-permute-start.21 = (f32[4,2,16,512]{3,2,1,0:T(8,128)S(1)}, f32[4,2,16,512]{3,2,1,0:T(8,128)S(1)}, u32[]{:S(2)}, u32[]{:S(2)}) collective-permute-start(f32[4,2,16,512]{3,2,1,0:T(8,128)S(1)} %get-tuple-element.63), channel_id=1, source_target_pairs={{0,28},{4,8},{8,4},{12,16},{16,12},{20,24},{24,20},{28,0},{1,29},{... | collective-permute-start | bytes 786440 | tf_op jit(solution)/shard_map/ppermute | solution.py:508
  62.8 7.8 %collective-permute-start.17 = (f32[2,32,512]{2,1,0:T(8,128)S(1)}, f32[2,32,512]{2,1,0:T(8,128)S(1)}, u32[]{:S(2)}, u32[]{:S(2)}) collective-permute-start(f32[2,32,512]{2,1,0:T(8,128)S(1)} %shard_map.53.refs_9_), channel_id=1, source_target_pairs={{0,3},{1,2},{2,1},{3,0},{4,7},{5,6},{6,5},{7,4},{8,11},{9,10},{10,... | collective-permute-start | bytes 393224 | tf_op jit(solution)/shard_map/ppermute | solution.py:412
  66.8 5.4 %collective-permute-start.19 = (f32[2,2,16,512]{3,2,1,0:T(8,128)S(1)}, f32[2,2,16,512]{3,2,1,0:T(8,128)S(1)}, u32[]{:S(2)}, u32[]{:S(2)}) collective-permute-start(f32[2,2,16,512]{3,2,1,0:T(8,128)S(1)} %get-tuple-element.62), channel_id=1, source_target_pairs={{0,1},{1,0},{2,3},{3,2},{4,5},{5,4},{6,7},{7,6},{8,9},{9,8},{10,11... | collective-permute-start | bytes 393224 | tf_op jit(solution)/shard_map/ppermute | solution.py:420
  72.2 6.1 %collective-permute-start.20 = (f32[2,16,512]{2,1,0:T(8,128)S(1)}, f32[2,16,512]{2,1,0:T(8,128)S(1)}, u32[]{:S(2)}, u32[]{:S(2)}) collective-permute-start(f32[2,16,512]{2,1,0:T(8,128)S(1)} %shard_map.57.refs_3_), channel_id=1, source_target_pairs={{0,3},{1,2},{2,1},{3,0},{4,7},{5,6},{6,5},{7,4},{8,11},{9,10},{10,... | collective-permute-start | bytes 196616 | tf_op jit(solution)/shard_map/ppermute | solution.py:412

commit v10 on v9

--- a/solution.py
+++ b/solution.py
@@ -148,16 +148,15 @@
     return [0, *range(bands - 1, 0, -1)]
 
 
-def back_kernel(chunk, part, row, halo, h, *outs):
+def back_kernel(part, row, halo, h, *outs):
     odd = parity()
     lo, hi = part
-    in_halo = slice(lo - chunk[0], hi - chunk[0])
     two = row[0:1, :]
     me = lax.axis_index("orb")
     bands = halo.shape[1]
     for d, out in zip(offsets(bands), outs):
         band = me ^ d
-        d0, d1 = halo_terms(halo, band, odd, in_halo)
+        d0, d1 = halo_terms(halo, band, odd, slice(lo, hi))
         v2 = h[0, band, lo:hi, :] + two * (NEAR * d1 + FAR * d0)
         v3 = h[1, band, lo:hi, :] + two * (FAR * d1)
         out[0] = square(v2, bands)
@@ -386,7 +385,7 @@
     planes, rows, lanes = psi.shape
     wide = rows // bands
     half, part = wide // 2, wide // 4
-    chunks = [(0, half), (half, wide)]
+    chunk = (0, wide)
     cuts = [(0, half), (half, wide - part), (wide - part, wide)]
     cut_a, cut_b, cut_c = cuts
     padded, inner = (part + 8, part + 4)
@@ -422,9 +421,9 @@
     def over_orb(x, d):
         return lax.ppermute(x, "orb", [(i, i ^ d) for i in range(bands)])
 
-    def back_squares(chunk, rows, halo):
+    def back_squares(rows):
         keep, *sends = call(
-            functools.partial(back_kernel, chunk, rows),
+            functools.partial(back_kernel, rows),
             [pair_shape(rows)[1:]] * bands,
             (row, halo, as_bands(h_back)),
         )
@@ -433,26 +432,16 @@
     def sum_all(keep, *came, weight=0):
         return call(sum_all_kernel, keep.shape, (keep, *came), weight=weight)
 
-    def faces(chunk, halo, parts):
-        fs = call(
-            functools.partial(face_kernel, chunk, parts),
-            [slab_shape(cut) for cut in parts],
-            (halo, as_bands(g)),
-        )
-        return fs, lax.ppermute(fs[0], "slab", face)
-
     psi_in = lax.ppermute(psi, "slab", partner)
     pot_in = lax.ppermute(potential, "slab", partner)
-    halos = []
-    for chunk in chunks:
-        piece = call(
-            functools.partial(pack_kernel, chunk),
-            slab_shape(chunk),
-            (as_bands(psi),),
-            scratch=[pltpu.SemaphoreType.DMA],
-            hbm=True,
-        )
-        halos.append(lax.ppermute(piece, "slab", face))
+    piece = call(
+        functools.partial(pack_kernel, chunk),
+        slab_shape(chunk),
+        (as_bands(psi),),
+        scratch=[pltpu.SemaphoreType.DMA],
+        hbm=True,
+    )
+    halo = lax.ppermute(piece, "slab", face)
     keep, *sends = call(
         functools.partial(send_rows_kernel, cut_c),
         [(planes, padded, lanes)] * bands,
@@ -471,57 +460,59 @@
     def summed(keep, came, from_far, weight=0):
         return call(sum_kernel, from_far.shape, (keep, came, from_far), weight=weight)
 
-    back0 = back_squares(chunks[0], cut_a, halos[0])
-    f0, face_a = faces(chunks[0], halos[0], [cut_a])
     x, piece = call(
         gather_kernel,
         [(bands, planes, padded, lanes), (2 * (bands - 1) * inner, lanes)],
         x_parts,
     )
+    x_in = lax.ppermute(x, "slab", partner)
     x_halo = lax.ppermute(piece, "slab", face)
-    x_in = lax.ppermute(x, "slab", partner)
-    back1 = back_squares(chunks[1], cut_b, halos[1])
-    f1, face_b = faces(chunks[1], halos[1], [cut_b, cut_c])
     x_first, x_t, x_back = call(
         functools.partial(rows_kernel, cut_c),
         [(bands, 2, inner, lanes)] + [(bands, 2, part, lanes)] * 2,
         (coeffs, x, x_in, as_bands(potential), as_bands(pot_in)),
         scalars=1,
     )
-    back0 = sum_all(*back0, weight=0)
+    fs = call(
+        functools.partial(face_kernel, chunk, cuts),
+        [slab_shape(cut) for cut in cuts],
+        (halo, as_bands(g)),
+    )
+    face_a, face_b = [lax.ppermute(f, "slab", face) for f in fs[:2]]
+    back0 = back_squares((0, wide - part))
+    x_f, piece = call(
+        functools.partial(rows_face_kernel, cut_c),
+        [(bands, 2, inner, lanes), (bands, 2, part, lanes)],
+        (x_halo, halo, halo, x_first),
+    )
+    x_face = lax.ppermute(piece, "slab", face)
     h_front = call(
         functools.partial(front_kernel, cuts),
         plane2,
-        (coeffs, psi, potential, t, *f0, *f1),
+        (coeffs, psi, potential, t, *fs),
         scalars=1,
         scratch=[pltpu.VMEM(plane2, jnp.float32)],
         flops=40 * cells,
-        weight=6_000_000_000,
-    )
-    back1 = sum_all(*back1, weight=0)
-    front_a = squares(cut_a, face_a)
-    x_f, piece = call(
-        functools.partial(rows_face_kernel, cut_c),
-        [(bands, 2, inner, lanes), (bands, 2, part, lanes)],
-        (x_halo, *halos, x_first),
-    )
-    x_face = lax.ppermute(piece, "slab", face)
-    front_a = add_far(*front_a)
+        weight=4_000_000_000,
+    )
     back2, x_front = call(
         functools.partial(rows_front_kernel, cut_c),
         [(2, part, lanes), (bands, 2, part, lanes)],
-        (coeffs, x, as_bands(potential), x_halo, *halos, x_f, x_t, x_back),
+        (coeffs, x, as_bands(potential), x_halo, halo, halo, x_f, x_t, x_back),
         scalars=1,
     )
+    front_a = squares(cut_a, face_a)
+    back0 = sum_all(*back0, weight=1_000_000_000)
     front_b = squares(cut_b, face_b)
+    front_a = add_far(*front_a)
+    front_b = add_far(*front_b)
     front_a = summed(*front_a)
-    front_b = add_far(*front_b)
     front_b = summed(*front_b)
-    places = [(2, cut) for cut in cuts] + [(0, cut_a), (0, cut_b)]
+    places = [(2, (0, wide - part)), (2, cut_c), (0, cut_a), (0, cut_b)]
     return call(
         functools.partial(join_kernel, places, cut_c),
         (planes, wide, lanes),
-        (back0, back1, back2, front_a, front_b, row, x_face, x_front),
+        (back0, back2, front_a, front_b, row, x_face, x_front),
     )
 
 

time: 79.4 us -> 67 us (0.84)
  waiting for transfers between devices: 29.5 us -> 19.5 us
  starting transfers between devices: 29.3 us -> 27.1 us
    ppermute x4 -> x3, waiting for transfers between devices: 11.3 us -> 4.12 us  [the longest x2 4.12 us: shards(): face_a, face_b = [lax.ppermute(f, 'slab', face) for f in fs[:2]]]
    ppermute x9 -> x6, starting transfers between devices: 13.3 us -> 8.91 us  [over_orb(): return lax.ppermute(x, 'orb', [(i, i ^ d) for i in range(bands)])]
    ppermute x1, waiting for transfers between devices: 3.85 us -> 0.01 us  [shards(): x_halo = lax.ppermute(piece, 'slab', face)]
    ppermute x2, waiting for transfers between devices: 6.55 us -> 3.53 us  [add_far(): return (keep, came, lax.ppermute(total, 'orb', far))]
    ppermute x2, starting transfers between devices: 0.94 us -> 3.48 us  [squares(): return (keep, lax.ppermute(send, 'orb', near))]
    ppermute x4 -> x3, starting transfers between devices: 7.41 us -> 5.44 us  [the longest x1 3.57 us: shards(): halo = lax.ppermute(piece, 'slab', face)]
    ppermute x9 -> x6, waiting for transfers between devices: 5.83 us -> 7.55 us  [over_orb(): return lax.ppermute(x, 'orb', [(i, i ^ d) for i in range(bands)])]
    ppermute x2, waiting for transfers between devices: 1.96 us -> 3.57 us  [squares(): return (keep, lax.ppermute(send, 'orb', near))]
  transfers between devices with their start and end apart: 22 -> 18, of which waited for: 9 -> 8; matrix products, arithmetic and copies ran while one was open for 0% -> 0% of each run, Pallas kernels for 22% -> 26%
where the time goes in v10:
time: 67 us; the launch traced here: 66.9 us
  starting transfers between devices  27.1 us (40%)
  waiting for transfers between devices  19.5 us (29%)
  Pallas kernels  18.5 us (28%)
  local copies, waits for them, and re-layouts  1.61 us (2%)
    pallas_call x19, Pallas kernels, __call__(): pl.pallas_call(body, out_shape=shapes, in_specs=[smem] * scalars + [pl.Bl...  18.5 us
    ppermute x6, starting transfers between devices, over_orb(): return lax.ppermute(x, 'orb', [(i, i ^ d) for i in range(bands)])  8.91 us
    ppermute x6, waiting for transfers between devices, over_orb(): return lax.ppermute(x, 'orb', [(i, i ^ d) for i in range(bands)])  7.55 us
    ppermute x2, starting transfers between devices, add_far(): return (keep, came, lax.ppermute(total, 'orb', far))  5.11 us
    ppermute x2, waiting for transfers between devices, shards(): face_a, face_b = [lax.ppermute(f, 'slab', face) for f in fs[:2]]  4.12 us
    ppermute x1, starting transfers between devices, shards(): halo = lax.ppermute(piece, 'slab', face)  3.57 us
    ppermute x2, waiting for transfers between devices, squares(): return (keep, lax.ppermute(send, 'orb', near))  3.57 us
    ppermute x2, waiting for transfers between devices, add_far(): return (keep, came, lax.ppermute(total, 'orb', far))  3.53 us
  transfers between devices with their start and end apart: 18, of which 8 were waited for; matrix products, arithmetic and copies ran while one was open for 0% of the time, Pallas kernels for 26%

profile of v10, /device:TPU:0, one launch (start us, length us, event | category | flops | bytes accessed | tf_op | source)
XLA Modules:
  0.0 66.9 jit_solution(12324334101789627339)
XLA Ops:
  0.0 0.5 collective-permute-start
  0.5 0.1 collective-permute-start.1
  0.5 1.6 %copy-done.1 = f32[1,4,256,512]{3,2,1,0:T(8,128)S(1)} copy-done((f32[1,4,256,512]{3,2,1,0:T(8,128)S(1)}, f32[1,4,256,512]{3,2,1,0:T(8,128)}, u32[]{:S(2)}) %copy-start.1) | copy-done | bytes 2097176
  2.1 0.1 shard_map.37.refs_1_
  2.2 0.0 copy-start
  2.2 3.6 %collective-permute-start.2 = (f32[2,4,64,512]{3,2,1,0:T(8,128)S(1)}, f32[2,4,64,512]{3,2,1,0:T(8,128)S(1)}, u32[]{:S(2)}, u32[]{:S(2)}) collective-permute-start(f32[2,4,64,512]{3,2,1,0:T(8,128)S(1)} %shard_map.37.refs_1_), channel_id=1, source_target_pairs={{0,28},{4,8},{8,4},{12,16},{16,12},{20,24},{24,20},{28,0},{1,29},{... | collective-permute-start | bytes 3145736 | tf_op jit(solution)/shard_map/ppermute | solution.py:444
  5.8 0.1 shard_map.38
  5.9 3.7 %collective-permute-start.3 = (f32[4,24,512]{2,1,0:T(8,128)S(1)}, f32[4,24,512]{2,1,0:T(8,128)S(1)}, u32[]{:S(2)}, u32[]{:S(2)}) collective-permute-start(f32[4,24,512]{2,1,0:T(8,128)S(1)} %get-tuple-element.35), channel_id=1, source_target_pairs={{0,3},{1,2},{2,1},{3,0},{4,7},{5,6},{6,5},{7,4},{8,11},{9,10},{10,... | collective-permute-start | bytes 589832 | tf_op jit(solution)/shard_map/ppermute | solution.py:422
  9.5 0.0 collective-permute-start.4
  9.5 0.8 %collective-permute-start.5 = (f32[4,24,512]{2,1,0:T(8,128)S(1)}, f32[4,24,512]{2,1,0:T(8,128)S(1)}, u32[]{:S(2)}, u32[]{:S(2)}) collective-permute-start(f32[4,24,512]{2,1,0:T(8,128)S(1)} %get-tuple-element.37), channel_id=1, source_target_pairs={{0,1},{1,0},{2,3},{3,2},{4,5},{5,4},{6,7},{7,6},{8,9},{9,8},{10,11... | collective-permute-start | bytes 589832 | tf_op jit(solution)/shard_map/ppermute | solution.py:422
  10.3 2.5 %shard_map.39.refs_5_.refs_6_ = f32[2,256,512]{2,1,0:T(8,128)S(1)} custom-call(f32[4,256,512]{2,1,0:T(8,128)S(1)} %bitcast.12, f32[4,256,512]{2,1,0:T(8,128)S(1)} %copy-done, f32[4,24,512]{2,1,0:T(8,128)S(1)} %get-tuple-element.32.refs_2_.refs_0_), custom_call_target="tpu_custom_call" | custom-call | flops 6291456 | bytes 5242880 | tf_op jit(solution)/shard_map/pallas_call | solution.py:365
  12.8 7.0 %shard_map.40 = (f32[2,256,512]{2,1,0:T(8,128)S(1)}, f32[2,256,512]{2,1,0:T(8,128)S(1)}, f32[8,512]{1,0:T(8,128)S(1)}) custom-call(f32[3]{0:T(128)S(1)} %copy-done.3, f32[4,256,512]{2,1,0:T(8,128)S(1)} %bitcast.13, f32[4,256,512]{2,1,0:T(8,128)S(1)} %copy-done, f32[4,256,512]{2,1,0:T(8,128)S(1)} %collective-permute-done.refs_3_, ...), custom_call_target="tpu_custom_call" | custom-call | flops 20971520 | bytes 11550732 | tf_op jit(solution)/shard_map/pallas_call | solution.py:365
  19.8 0.0 collective-permute-done.3.refs_1_
  19.9 6.1 %collective-permute-done.4.refs_2_ = f32[4,24,512]{2,1,0:T(8,128)S(1)} collective-permute-done((f32[4,24,512]{2,1,0:T(8,128)S(1)}, f32[4,24,512]{2,1,0:T(8,128)S(1)}, u32[]{:S(2)}, u32[]{:S(2)}) %collective-permute-start.4) | collective-permute-done | bytes 196640 | tf_op jit(solution)/shard_map/ppermute | solution.py:422
  25.9 0.0 collective-permute-done.5.refs_3_
  25.9 0.1 shard_map.41
  26.0 0.1 collective-permute-start.6
  26.1 1.5 %collective-permute-start.11 = (f32[120,512]{1,0:T(8,128)S(1)}, f32[120,512]{1,0:T(8,128)S(1)}, u32[]{:S(2)}, u32[]{:S(2)}) collective-permute-start(f32[120,512]{1,0:T(8,128)S(1)} %get-tuple-element.48), channel_id=1, source_target_pairs={{0,28},{4,8},{8,4},{12,16},{16,12},{20,24},{24,20},{28,0},{1,29},{... | collective-permute-start | bytes 737288 | tf_op jit(solution)/shard_map/ppermute | solution.py:469
  27.6 0.7 %collective-permute-done.6.refs_2_ = f32[4,4,24,512]{3,2,1,0:T(8,128)S(1)} collective-permute-done((f32[4,4,24,512]{3,2,1,0:T(8,128)S(1)}, f32[4,4,24,512]{3,2,1,0:T(8,128)S(1)}, u32[]{:S(2)}, u32[]{:S(2)}) %collective-permute-start.6) | collective-permute-done | bytes 786464 | tf_op jit(solution)/shard_map/ppermute | solution.py:468
  28.4 2.8 %shard_map.42 = (f32[4,2,20,512]{3,2,1,0:T(8,128)S(1)}, f32[4,2,16,512]{3,2,1,0:T(8,128)S(1)}, f32[4,2,16,512]{3,2,1,0:T(8,128)S(1)}) custom-call(f32[3]{0:T(128)S(1)} %copy-done.3, f32[4,4,24,512]{3,2,1,0:T(8,128)S(1)} %get-tuple-element.39.refs_1_.refs_5_, f32[4,4,24,512]{3,2,1,0:T(8,128)S(1)} %collective-permute-done.6.refs_2_, ...), custom_call_target="tpu_custom_call" | custom-call | bytes 6619148 | tf_op jit(solution)/shard_map/pallas_call | solution.py:365
  31.1 0.2 shard_map.43
  31.3 1.2 %collective-permute-start.10 = (f32[2,4,32,512]{3,2,1,0:T(8,128)S(1)}, f32[2,4,32,512]{3,2,1,0:T(8,128)S(1)}, u32[]{:S(2)}, u32[]{:S(2)}) collective-permute-start(f32[2,4,32,512]{3,2,1,0:T(8,128)S(1)} %get-tuple-element.41.refs_3_.refs_4_), channel_id=1, source_target_pairs={{0,28},{4,8},{8,4},{12,16},{16,12},{20,24},{24,20},{28,0},{1,29},{... | collective-permute-start | bytes 1572872 | tf_op jit(solution)/shard_map/ppermute | solution.py:481
  32.5 0.2 shard_map.44
  32.8 0.0 copy-start.2
  32.8 3.5 %collective-permute-start.7 = (f32[2,48,512]{2,1,0:T(8,128)S(1)}, f32[2,48,512]{2,1,0:T(8,128)S(1)}, u32[]{:S(2)}, u32[]{:S(2)}) collective-permute-start(f32[2,48,512]{2,1,0:T(8,128)S(1)} %get-tuple-element.43), channel_id=1, source_target_pairs={{0,3},{1,2},{2,1},{3,0},{4,7},{5,6},{6,5},{7,4},{8,11},{9,10},{10,... | collective-permute-start | bytes 589832 | tf_op jit(solution)/shard_map/ppermute | solution.py:422
  36.3 0.0 collective-permute-start.8
  36.3 1.0 %collective-permute-start.9 = (f32[2,48,512]{2,1,0:T(8,128)S(1)}, f32[2,48,512]{2,1,0:T(8,128)S(1)}, u32[]{:S(2)}, u32[]{:S(2)}) collective-permute-start(f32[2,48,512]{2,1,0:T(8,128)S(1)} %get-tuple-element.45), channel_id=1, source_target_pairs={{0,1},{1,0},{2,3},{3,2},{4,5},{5,4},{6,7},{7,6},{8,9},{9,8},{10,11... | collective-permute-start | bytes 589832 | tf_op jit(solution)/shard_map/ppermute | solution.py:422
  37.2 0.0 collective-permute-done.11.refs_0_.refs_3_
  37.2 0.6 collective-permute-start.13
  37.9 0.1 shard_map.45
  38.0 3.2 %shard_map.46.refs_9_ = f32[2,256,512]{2,1,0:T(8,128)S(1)} custom-call(f32[3]{0:T(128)S(1)} %copy-done.3, f32[4,256,512]{2,1,0:T(8,128)S(1)} %bitcast.14, f32[4,256,512]{2,1,0:T(8,128)S(1)} %copy-done, f32[2,256,512]{2,1,0:T(8,128)S(1)} %get-tuple-element.38.refs_4_.refs_3_, f32[2,4,32,512]{3,2,1,0:T(8,128)S(1)} %get-tuple-element.41.refs_3_.refs_4_, ...), custom_call_target="tpu_custom_call" | custom-call | flops 4010485760 | bytes 7340044 | tf_op jit(solution)/shard_map/pallas_call | solution.py:365
  41.1 1.2 %shard_map.47 = (f32[2,16,512]{2,1,0:T(8,128)S(1)}, f32[4,2,16,512]{3,2,1,0:T(8,128)S(1)}) custom-call(f32[3]{0:T(128)S(1)} %copy-done.3, f32[4,4,24,512]{3,2,1,0:T(8,128)S(1)} %get-tuple-element.39.refs_1_.refs_5_, f32[4,4,64,512]{3,2,1,0:T(8,128)S(1)} %bitcast.8, f32[120,512]{1,0:T(8,128)S(1)} %collective-permute-done.11.refs_0_.refs_3_, ...), custom_call_target="tpu_custom_call" | custom-call | bytes 6406156 | tf_op jit(solution)/shard_map/pallas_call | solution.py:365
  42.3 3.9 %collective-permute-done.10.refs_1_ = f32[2,4,32,512]{3,2,1,0:T(8,128)S(1)} collective-permute-done((f32[2,4,32,512]{3,2,1,0:T(8,128)S(1)}, f32[2,4,32,512]{3,2,1,0:T(8,128)S(1)}, u32[]{:S(2)}, u32[]{:S(2)}) %collective-permute-start.10) | collective-permute-done | bytes 524320 | tf_op jit(solution)/shard_map/ppermute | solution.py:481
  46.2 0.1 shard_map.48
  46.3 1.7 %collective-permute-start.12 = (f32[2,2,32,512]{3,2,1,0:T(8,128)S(1)}, f32[2,2,32,512]{3,2,1,0:T(8,128)S(1)}, u32[]{:S(2)}, u32[]{:S(2)}) collective-permute-start(f32[2,2,32,512]{3,2,1,0:T(8,128)S(1)} %get-tuple-element.54), channel_id=1, source_target_pairs={{0,1},{1,0},{2,3},{3,2},{4,5},{5,4},{6,7},{7,6},{8,9},{9,8},{10,11... | collective-permute-start | bytes 786440 | tf_op jit(solution)/shard_map/ppermute | solution.py:419
  48.1 0.0 collective-permute-done.7.refs_1_
  48.1 2.0 %collective-permute-start.17 = (f32[4,2,16,512]{3,2,1,0:T(8,128)S(1)}, f32[4,2,16,512]{3,2,1,0:T(8,128)S(1)}, u32[]{:S(2)}, u32[]{:S(2)}) collective-permute-start(f32[4,2,16,512]{3,2,1,0:T(8,128)S(1)} %get-tuple-element.57), channel_id=1, source_target_pairs={{0,28},{4,8},{8,4},{12,16},{16,12},{20,24},{24,20},{28,0},{1,29},{... | collective-permute-start | bytes 786440 | tf_op jit(solution)/shard_map/ppermute | solution.py:488
  50.1 1.5 %collective-permute-done.8.refs_2_ = f32[2,48,512]{2,1,0:T(8,128)S(1)} collective-permute-done((f32[2,48,512]{2,1,0:T(8,128)S(1)}, f32[2,48,512]{2,1,0:T(8,128)S(1)}, u32[]{:S(2)}, u32[]{:S(2)}) %collective-permute-start.8) | collective-permute-done | bytes 196640 | tf_op jit(solution)/shard_map/ppermute | solution.py:422
  51.6 0.2 collective-permute-done.13.refs_1_
  51.9 0.1 shard_map.50
  51.9 1.7 %collective-permute-start.15 = (f32[2,2,16,512]{3,2,1,0:T(8,128)S(1)}, f32[2,2,16,512]{3,2,1,0:T(8,128)S(1)}, u32[]{:S(2)}, u32[]{:S(2)}) collective-permute-start(f32[2,2,16,512]{3,2,1,0:T(8,128)S(1)} %get-tuple-element.56), channel_id=1, source_target_pairs={{0,1},{1,0},{2,3},{3,2},{4,5},{5,4},{6,7},{7,6},{8,9},{9,8},{10,11... | collective-permute-start | bytes 393224 | tf_op jit(solution)/shard_map/ppermute | solution.py:419
  53.7 3.6 %collective-permute-done.12.refs_1_ = f32[2,2,32,512]{3,2,1,0:T(8,128)S(1)} collective-permute-done((f32[2,2,32,512]{3,2,1,0:T(8,128)S(1)}, f32[2,2,32,512]{3,2,1,0:T(8,128)S(1)}, u32[]{:S(2)}, u32[]{:S(2)}) %collective-permute-start.12) | collective-permute-done | bytes 262176 | tf_op jit(solution)/shard_map/ppermute | solution.py:419
  57.2 2.5 %collective-permute-start.14 = (f32[2,32,512]{2,1,0:T(8,128)S(1)}, f32[2,32,512]{2,1,0:T(8,128)S(1)}, u32[]{:S(2)}, u32[]{:S(2)}) collective-permute-start(f32[2,32,512]{2,1,0:T(8,128)S(1)} %shard_map.51.refs_2_), channel_id=1, source_target_pairs={{0,3},{1,2},{2,1},{3,0},{4,7},{5,6},{6,5},{7,4},{8,11},{9,10},{10,... | collective-permute-start | bytes 393224 | tf_op jit(solution)/shard_map/ppermute | solution.py:411
  59.7 0.0 collective-permute-done.15.refs_1_
  59.7 2.6 %collective-permute-start.16 = (f32[2,16,512]{2,1,0:T(8,128)S(1)}, f32[2,16,512]{2,1,0:T(8,128)S(1)}, u32[]{:S(2)}, u32[]{:S(2)}) collective-permute-start(f32[2,16,512]{2,1,0:T(8,128)S(1)} %shard_map.52.refs_3_), channel_id=1, source_target_pairs={{0,3},{1,2},{2,1},{3,0},{4,7},{5,6},{6,5},{7,4},{8,11},{9,10},{10,... | collective-permute-start | bytes 196616 | tf_op jit(solution)/shard_map/ppermute | solution.py:411
  62.4 1.9 %collective-permute-done.14.refs_2_ = f32[2,32,512]{2,1,0:T(8,128)S(1)} collective-permute-done((f32[2,32,512]{2,1,0:T(8,128)S(1)}, f32[2,32,512]{2,1,0:T(8,128)S(1)}, u32[]{:S(2)}, u32[]{:S(2)}) %collective-permute-start.14) | collective-permute-done | bytes 131104 | tf_op jit(solution)/shard_map/ppermute | solution.py:411
  64.3 1.6 %collective-permute-done.16.refs_2_ = f32[2,16,512]{2,1,0:T(8,128)S(1)} collective-permute-done((f32[2,16,512]{2,1,0:T(8,128)S(1)}, f32[2,16,512]{2,1,0:T(8,128)S(1)}, u32[]{:S(2)}, u32[]{:S(2)}) %collective-permute-start.16) | collective-permute-done | bytes 65568 | tf_op jit(solution)/shard_map/ppermute | solution.py:411
  66.0 0.9 %shard_map.55 = f32[4,64,512]{2,1,0:T(8,128)} custom-call(f32[2,48,512]{2,1,0:T(8,128)S(1)} %shard_map.49.refs_3_.refs_0_, f32[2,16,512]{2,1,0:T(8,128)S(1)} %get-tuple-element.52.refs_3_.refs_1_, f32[2,32,512]{2,1,0:T(8,128)S(1)} %shard_map.53.refs_3_.refs_2_, f32[2,16,512]{2,1,0:T(8,128)S(1)} %shard_map.54.refs_3_.refs_7_, ...), custom_call_target="tpu_custom_call" | custom-call | bytes 1523712 | tf_op jit(solution)/shard_map/pallas_call | solution.py:365
  (15 shorter events, 0.1 us)
Async XLA Ops:
  0.0 9.5 %collective-permute-start = (f32[4,256,512]{2,1,0:T(8,128)}, f32[4,256,512]{2,1,0:T(8,128)S(1)}, u32[]{:S(2)}, u32[]{:S(2)}) collective-permute-start(f32[4,256,512]{2,1,0:T(8,128)} %bitcast.9), channel_id=1, source_target_pairs={{0,4},{4,0},{8,12},{12,8},{16,20},{20,16},{24,28},{28,24},{1,5},{5... | collective-permute-start | bytes 6291464 | tf_op jit(solution)/shard_map/ppermute | solution.py:435
  0.5 12.4 %collective-permute-start.1 = (f32[4,256,512]{2,1,0:T(8,128)}, f32[4,256,512]{2,1,0:T(8,128)S(1)}, u32[]{:S(2)}, u32[]{:S(2)}) collective-permute-start(f32[4,256,512]{2,1,0:T(8,128)} %refs_2_.3), channel_id=1, source_target_pairs={{0,4},{4,0},{8,12},{12,8},{16,20},{20,16},{24,28},{28,24},{1,5},{5... | collective-permute-start | bytes 6291464 | tf_op jit(solution)/shard_map/ppermute | solution.py:436
  0.5 1.6 %copy-start.1 = (f32[1,4,256,512]{3,2,1,0:T(8,128)S(1)}, f32[1,4,256,512]{3,2,1,0:T(8,128)}, u32[]{:S(2)}) copy-start(f32[1,4,256,512]{3,2,1,0:T(8,128)} %param.3) | copy-start | bytes 6291460
  2.2 8.1 %copy-start = (f32[4,256,512]{2,1,0:T(8,128)S(1)}, f32[4,256,512]{2,1,0:T(8,128)}, u32[]{:S(2)}) copy-start(f32[4,256,512]{2,1,0:T(8,128)} %refs_2_.3) | copy-start | bytes 6291460
  2.2 28.9 %collective-permute-start.2 = (f32[2,4,64,512]{3,2,1,0:T(8,128)S(1)}, f32[2,4,64,512]{3,2,1,0:T(8,128)S(1)}, u32[]{:S(2)}, u32[]{:S(2)}) collective-permute-start(f32[2,4,64,512]{3,2,1,0:T(8,128)S(1)} %shard_map.37.refs_1_), channel_id=1, source_target_pairs={{0,28},{4,8},{8,4},{12,16},{16,12},{20,24},{24,20},{28,0},{1,29},{... | collective-permute-start | bytes 3145736 | tf_op jit(solution)/shard_map/ppermute | solution.py:444
  5.9 14.0 %collective-permute-start.3 = (f32[4,24,512]{2,1,0:T(8,128)S(1)}, f32[4,24,512]{2,1,0:T(8,128)S(1)}, u32[]{:S(2)}, u32[]{:S(2)}) collective-permute-start(f32[4,24,512]{2,1,0:T(8,128)S(1)} %get-tuple-element.35), channel_id=1, source_target_pairs={{0,3},{1,2},{2,1},{3,0},{4,7},{5,6},{6,5},{7,4},{8,11},{9,10},{10,... | collective-permute-start | bytes 589832 | tf_op jit(solution)/shard_map/ppermute | solution.py:422
  9.5 16.4 %collective-permute-start.4 = (f32[4,24,512]{2,1,0:T(8,128)S(1)}, f32[4,24,512]{2,1,0:T(8,128)S(1)}, u32[]{:S(2)}, u32[]{:S(2)}) collective-permute-start(f32[4,24,512]{2,1,0:T(8,128)S(1)} %get-tuple-element.36), channel_id=1, source_target_pairs={{0,2},{1,3},{2,0},{3,1},{4,6},{5,7},{6,4},{7,5},{8,10},{9,11},{10,... | collective-permute-start | bytes 589832 | tf_op jit(solution)/shard_map/ppermute | solution.py:422
  9.5 16.4 %collective-permute-start.5 = (f32[4,24,512]{2,1,0:T(8,128)S(1)}, f32[4,24,512]{2,1,0:T(8,128)S(1)}, u32[]{:S(2)}, u32[]{:S(2)}) collective-permute-start(f32[4,24,512]{2,1,0:T(8,128)S(1)} %get-tuple-element.37), channel_id=1, source_target_pairs={{0,1},{1,0},{2,3},{3,2},{4,5},{5,4},{6,7},{7,6},{8,9},{9,8},{10,11... | collective-permute-start | bytes 589832 | tf_op jit(solution)/shard_map/ppermute | solution.py:422
  10.3 2.5 %copy-start.3 = (f32[3]{0:T(128)S(1)}, f32[3]{0:T(128)}, u32[]{:S(2)}) copy-start(f32[3]{0:T(128)} %refs_0_.7) | copy-start | bytes 40
  26.0 2.4 %collective-permute-start.6 = (f32[4,4,24,512]{3,2,1,0:T(8,128)S(1)}, f32[4,4,24,512]{3,2,1,0:T(8,128)S(1)}, u32[]{:S(2)}, u32[]{:S(2)}) collective-permute-start(f32[4,4,24,512]{3,2,1,0:T(8,128)S(1)} %get-tuple-element.39.refs_1_.refs_5_), channel_id=1, source_target_pairs={{0,4},{4,0},{8,12},{12,8},{16,20},{20,16},{24,28},{28,24},{1,5},{5... | collective-permute-start | bytes 2359304 | tf_op jit(solution)/shard_map/ppermute | solution.py:468
  26.1 11.1 %collective-permute-start.11 = (f32[120,512]{1,0:T(8,128)S(1)}, f32[120,512]{1,0:T(8,128)S(1)}, u32[]{:S(2)}, u32[]{:S(2)}) collective-permute-start(f32[120,512]{1,0:T(8,128)S(1)} %get-tuple-element.48), channel_id=1, source_target_pairs={{0,28},{4,8},{8,4},{12,16},{16,12},{20,24},{24,20},{28,0},{1,29},{... | collective-permute-start | bytes 737288 | tf_op jit(solution)/shard_map/ppermute | solution.py:469
  31.3 14.9 %collective-permute-start.10 = (f32[2,4,32,512]{3,2,1,0:T(8,128)S(1)}, f32[2,4,32,512]{3,2,1,0:T(8,128)S(1)}, u32[]{:S(2)}, u32[]{:S(2)}) collective-permute-start(f32[2,4,32,512]{3,2,1,0:T(8,128)S(1)} %get-tuple-element.41.refs_3_.refs_4_), channel_id=1, source_target_pairs={{0,28},{4,8},{8,4},{12,16},{16,12},{20,24},{24,20},{28,0},{1,29},{... | collective-permute-start | bytes 1572872 | tf_op jit(solution)/shard_map/ppermute | solution.py:481
  32.8 5.2 %copy-start.2 = (f32[1,4,256,512]{3,2,1,0:T(8,128)S(1)}, f32[1,4,256,512]{3,2,1,0:T(8,128)}, u32[]{:S(2)}) copy-start(f32[1,4,256,512]{3,2,1,0:T(8,128)} %param.3) | copy-start | bytes 6291460
  32.8 15.3 %collective-permute-start.7 = (f32[2,48,512]{2,1,0:T(8,128)S(1)}, f32[2,48,512]{2,1,0:T(8,128)S(1)}, u32[]{:S(2)}, u32[]{:S(2)}) collective-permute-start(f32[2,48,512]{2,1,0:T(8,128)S(1)} %get-tuple-element.43), channel_id=1, source_target_pairs={{0,3},{1,2},{2,1},{3,0},{4,7},{5,6},{6,5},{7,4},{8,11},{9,10},{10,... | collective-permute-start | bytes 589832 | tf_op jit(solution)/shard_map/ppermute | solution.py:422
  36.3 15.3 %collective-permute-start.8 = (f32[2,48,512]{2,1,0:T(8,128)S(1)}, f32[2,48,512]{2,1,0:T(8,128)S(1)}, u32[]{:S(2)}, u32[]{:S(2)}) collective-permute-start(f32[2,48,512]{2,1,0:T(8,128)S(1)} %get-tuple-element.44), channel_id=1, source_target_pairs={{0,2},{1,3},{2,0},{3,1},{4,6},{5,7},{6,4},{7,5},{8,10},{9,11},{10,... | collective-permute-start | bytes 589832 | tf_op jit(solution)/shard_map/ppermute | solution.py:422
  36.3 15.3 %collective-permute-start.9 = (f32[2,48,512]{2,1,0:T(8,128)S(1)}, f32[2,48,512]{2,1,0:T(8,128)S(1)}, u32[]{:S(2)}, u32[]{:S(2)}) collective-permute-start(f32[2,48,512]{2,1,0:T(8,128)S(1)} %get-tuple-element.45), channel_id=1, source_target_pairs={{0,1},{1,0},{2,3},{3,2},{4,5},{5,4},{6,7},{7,6},{8,9},{9,8},{10,11... | collective-permute-start | bytes 589832 | tf_op jit(solution)/shard_map/ppermute | solution.py:422
  37.2 14.6 %collective-permute-start.13 = (f32[2,4,16,512]{3,2,1,0:T(8,128)S(1)}, f32[2,4,16,512]{3,2,1,0:T(8,128)S(1)}, u32[]{:S(2)}, u32[]{:S(2)}) collective-permute-start(f32[2,4,16,512]{3,2,1,0:T(8,128)S(1)} %get-tuple-element.46.refs_5_), channel_id=1, source_target_pairs={{0,28},{4,8},{8,4},{12,16},{16,12},{20,24},{24,20},{28,0},{1,29},{... | collective-permute-start | bytes 786440 | tf_op jit(solution)/shard_map/ppermute | solution.py:481
  46.3 10.9 %collective-permute-start.12 = (f32[2,2,32,512]{3,2,1,0:T(8,128)S(1)}, f32[2,2,32,512]{3,2,1,0:T(8,128)S(1)}, u32[]{:S(2)}, u32[]{:S(2)}) collective-permute-start(f32[2,2,32,512]{3,2,1,0:T(8,128)S(1)} %get-tuple-element.54), channel_id=1, source_target_pairs={{0,1},{1,0},{2,3},{3,2},{4,5},{5,4},{6,7},{7,6},{8,9},{9,8},{10,11... | collective-permute-start | bytes 786440 | tf_op jit(solution)/shard_map/ppermute | solution.py:419
  48.1 17.8 %collective-permute-start.17 = (f32[4,2,16,512]{3,2,1,0:T(8,128)S(1)}, f32[4,2,16,512]{3,2,1,0:T(8,128)S(1)}, u32[]{:S(2)}, u32[]{:S(2)}) collective-permute-start(f32[4,2,16,512]{3,2,1,0:T(8,128)S(1)} %get-tuple-element.57), channel_id=1, source_target_pairs={{0,28},{4,8},{8,4},{12,16},{16,12},{20,24},{24,20},{28,0},{1,29},{... | collective-permute-start | bytes 786440 | tf_op jit(solution)/shard_map/ppermute | solution.py:488
  51.9 7.8 %collective-permute-start.15 = (f32[2,2,16,512]{3,2,1,0:T(8,128)S(1)}, f32[2,2,16,512]{3,2,1,0:T(8,128)S(1)}, u32[]{:S(2)}, u32[]{:S(2)}) collective-permute-start(f32[2,2,16,512]{3,2,1,0:T(8,128)S(1)} %get-tuple-element.56), channel_id=1, source_target_pairs={{0,1},{1,0},{2,3},{3,2},{4,5},{5,4},{6,7},{7,6},{8,9},{9,8},{10,11... | collective-permute-start | bytes 393224 | tf_op jit(solution)/shard_map/ppermute | solution.py:419
  57.2 7.0 %collective-permute-start.14 = (f32[2,32,512]{2,1,0:T(8,128)S(1)}, f32[2,32,512]{2,1,0:T(8,128)S(1)}, u32[]{:S(2)}, u32[]{:S(2)}) collective-permute-start(f32[2,32,512]{2,1,0:T(8,128)S(1)} %shard_map.51.refs_2_), channel_id=1, source_target_pairs={{0,3},{1,2},{2,1},{3,0},{4,7},{5,6},{6,5},{7,4},{8,11},{9,10},{10,... | collective-permute-start | bytes 393224 | tf_op jit(solution)/shard_map/ppermute | solution.py:411
  59.7 6.2 %collective-permute-start.16 = (f32[2,16,512]{2,1,0:T(8,128)S(1)}, f32[2,16,512]{2,1,0:T(8,128)S(1)}, u32[]{:S(2)}, u32[]{:S(2)}) collective-permute-start(f32[2,16,512]{2,1,0:T(8,128)S(1)} %shard_map.52.refs_3_), channel_id=1, source_target_pairs={{0,3},{1,2},{2,1},{3,0},{4,7},{5,6},{6,5},{7,4},{8,11},{9,10},{10,... | collective-permute-start | bytes 196616 | tf_op jit(solution)/shard_map/ppermute | solution.py:411

commit v11 on v10

--- a/solution.py
+++ b/solution.py
@@ -467,19 +467,19 @@
     )
     x_in = lax.ppermute(x, "slab", partner)
     x_halo = lax.ppermute(piece, "slab", face)
+    fs = call(
+        functools.partial(face_kernel, chunk, cuts),
+        [slab_shape(cut) for cut in cuts],
+        (halo, as_bands(g)),
+    )
+    face_a, face_b = [lax.ppermute(f, "slab", face) for f in fs[:2]]
+    back0 = back_squares((0, wide - part))
     x_first, x_t, x_back = call(
         functools.partial(rows_kernel, cut_c),
         [(bands, 2, inner, lanes)] + [(bands, 2, part, lanes)] * 2,
         (coeffs, x, x_in, as_bands(potential), as_bands(pot_in)),
         scalars=1,
     )
-    fs = call(
-        functools.partial(face_kernel, chunk, cuts),
-        [slab_shape(cut) for cut in cuts],
-        (halo, as_bands(g)),
-    )
-    face_a, face_b = [lax.ppermute(f, "slab", face) for f in fs[:2]]
-    back0 = back_squares((0, wide - part))
     x_f, piece = call(
         functools.partial(rows_face_kernel, cut_c),
         [(bands, 2, inner, lanes), (bands, 2, part, lanes)],

time: 67 us -> 66.8 us (level)
  waiting for transfers between devices: 19.5 us -> 15.8 us
  starting transfers between devices: 27.1 us -> 29.2 us
  local copies, waits for them, and re-layouts: 1.61 us -> 2.99 us
    ppermute x2, waiting for transfers between devices: 4.12 us -> 1.12 us  [shards(): face_a, face_b = [lax.ppermute(f, 'slab', face) for f in fs[:2]]]
    unnamed x8, local copies, waits for them, and re-layouts: 1.61 us -> 2.99 us
    ppermute x1, waiting for transfers between devices: 0.01 us -> 1.27 us  [shards(): halo = lax.ppermute(piece, 'slab', face)]
    ppermute x2, starting transfers between devices: 1.87 us -> 2.94 us  [shards(): face_a, face_b = [lax.ppermute(f, 'slab', face) for f in fs[:2]]]
    ppermute x2, waiting for transfers between devices: 3.57 us -> 2.63 us  [squares(): return (keep, lax.ppermute(send, 'orb', near))]
    ppermute x6, waiting for transfers between devices: 7.55 us -> 6.66 us  [over_orb(): return lax.ppermute(x, 'orb', [(i, i ^ d) for i in range(bands)])]
    ppermute x1, waiting for transfers between devices: 0.74 us -> 0.01 us  [shards(): x_in = lax.ppermute(x, 'slab', partner)]
where the time goes in v11:
time: 66.8 us; the launch traced here: 66.6 us
  starting transfers between devices  29.2 us (44%)
  Pallas kernels  18.4 us (28%)
  waiting for transfers between devices  15.8 us (24%)
  local copies, waits for them, and re-layouts  2.99 us (4%)
    pallas_call x19, Pallas kernels, __call__(): pl.pallas_call(body, out_shape=shapes, in_specs=[smem] * scalars + [pl.Bl...  18.4 us
    ppermute x6, starting transfers between devices, over_orb(): return lax.ppermute(x, 'orb', [(i, i ^ d) for i in range(bands)])  9.2 us
    ppermute x6, waiting for transfers between devices, over_orb(): return lax.ppermute(x, 'orb', [(i, i ^ d) for i in range(bands)])  6.66 us
    ppermute x2, starting transfers between devices, add_far(): return (keep, came, lax.ppermute(total, 'orb', far))  5.25 us
    ppermute x2, waiting for transfers between devices, add_far(): return (keep, came, lax.ppermute(total, 'orb', far))  4.1 us
    ppermute x2, starting transfers between devices, squares(): return (keep, lax.ppermute(send, 'orb', near))  4.1 us
    ppermute x1, starting transfers between devices, shards(): halo = lax.ppermute(piece, 'slab', face)  3.57 us
    unnamed x8, local copies, waits for them, and re-layouts  2.99 us
  transfers between devices with their start and end apart: 18, of which 8 were waited for; matrix products, arithmetic and copies ran while one was open for 0% of the time, Pallas kernels for 26%

profile of v11, /device:TPU:0, one launch (start us, length us, event | category | flops | bytes accessed | tf_op | source)
XLA Modules:
  0.0 66.6 jit_solution(14965317604939623279)
XLA Ops:
  0.0 0.5 collective-permute-start
  0.5 0.1 collective-permute-start.1
  0.5 1.6 %copy-done.1 = f32[1,4,256,512]{3,2,1,0:T(8,128)S(1)} copy-done((f32[1,4,256,512]{3,2,1,0:T(8,128)S(1)}, f32[1,4,256,512]{3,2,1,0:T(8,128)}, u32[]{:S(2)}) %copy-start.1) | copy-done | bytes 2097176
  2.1 0.1 shard_map.37.refs_1_
  2.2 0.0 copy-start
  2.2 3.6 %collective-permute-start.2 = (f32[2,4,64,512]{3,2,1,0:T(8,128)S(1)}, f32[2,4,64,512]{3,2,1,0:T(8,128)S(1)}, u32[]{:S(2)}, u32[]{:S(2)}) collective-permute-start(f32[2,4,64,512]{3,2,1,0:T(8,128)S(1)} %shard_map.37.refs_1_), channel_id=1, source_target_pairs={{0,28},{4,8},{8,4},{12,16},{16,12},{20,24},{24,20},{28,0},{1,29},{... | collective-permute-start | bytes 3145736 | tf_op jit(solution)/shard_map/ppermute | solution.py:444
  5.8 0.1 shard_map.38
  5.9 3.7 %collective-permute-start.3 = (f32[4,24,512]{2,1,0:T(8,128)S(1)}, f32[4,24,512]{2,1,0:T(8,128)S(1)}, u32[]{:S(2)}, u32[]{:S(2)}) collective-permute-start(f32[4,24,512]{2,1,0:T(8,128)S(1)} %get-tuple-element.35), channel_id=1, source_target_pairs={{0,3},{1,2},{2,1},{3,0},{4,7},{5,6},{6,5},{7,4},{8,11},{9,10},{10,... | collective-permute-start | bytes 589832 | tf_op jit(solution)/shard_map/ppermute | solution.py:422
  9.5 0.0 collective-permute-start.4
  9.5 0.0 collective-permute-done.refs_3_
  9.5 0.8 %collective-permute-start.5 = (f32[4,24,512]{2,1,0:T(8,128)S(1)}, f32[4,24,512]{2,1,0:T(8,128)S(1)}, u32[]{:S(2)}, u32[]{:S(2)}) collective-permute-start(f32[4,24,512]{2,1,0:T(8,128)S(1)} %get-tuple-element.37), channel_id=1, source_target_pairs={{0,1},{1,0},{2,3},{3,2},{4,5},{5,4},{6,7},{7,6},{8,9},{9,8},{10,11... | collective-permute-start | bytes 589832 | tf_op jit(solution)/shard_map/ppermute | solution.py:422
  10.3 2.5 %shard_map.39.refs_5_.refs_6_ = f32[2,256,512]{2,1,0:T(8,128)S(1)} custom-call(f32[4,256,512]{2,1,0:T(8,128)S(1)} %bitcast.12, f32[4,256,512]{2,1,0:T(8,128)S(1)} %copy-done, f32[4,24,512]{2,1,0:T(8,128)S(1)} %get-tuple-element.32.refs_2_.refs_0_), custom_call_target="tpu_custom_call" | custom-call | flops 6291456 | bytes 5242880 | tf_op jit(solution)/shard_map/pallas_call | solution.py:365
  12.8 0.0 collective-permute-done.1.refs_4_
  12.8 7.0 %shard_map.40 = (f32[2,256,512]{2,1,0:T(8,128)S(1)}, f32[2,256,512]{2,1,0:T(8,128)S(1)}, f32[8,512]{1,0:T(8,128)S(1)}) custom-call(f32[3]{0:T(128)S(1)} %copy-done.3, f32[4,256,512]{2,1,0:T(8,128)S(1)} %bitcast.13, f32[4,256,512]{2,1,0:T(8,128)S(1)} %copy-done, f32[4,256,512]{2,1,0:T(8,128)S(1)} %collective-permute-done.refs_3_, ...), custom_call_target="tpu_custom_call" | custom-call | flops 20971520 | bytes 11550732 | tf_op jit(solution)/shard_map/pallas_call | solution.py:365
  19.8 0.0 collective-permute-done.3.refs_1_
  19.8 6.1 %collective-permute-done.4.refs_2_ = f32[4,24,512]{2,1,0:T(8,128)S(1)} collective-permute-done((f32[4,24,512]{2,1,0:T(8,128)S(1)}, f32[4,24,512]{2,1,0:T(8,128)S(1)}, u32[]{:S(2)}, u32[]{:S(2)}) %collective-permute-start.4) | collective-permute-done | bytes 196640 | tf_op jit(solution)/shard_map/ppermute | solution.py:422
  25.9 0.1 shard_map.41
  26.0 0.1 collective-permute-start.11
  26.1 1.5 %collective-permute-start.10 = (f32[120,512]{1,0:T(8,128)S(1)}, f32[120,512]{1,0:T(8,128)S(1)}, u32[]{:S(2)}, u32[]{:S(2)}) collective-permute-start(f32[120,512]{1,0:T(8,128)S(1)} %get-tuple-element.47), channel_id=1, source_target_pairs={{0,28},{4,8},{8,4},{12,16},{16,12},{20,24},{24,20},{28,0},{1,29},{... | collective-permute-start | bytes 737288 | tf_op jit(solution)/shard_map/ppermute | solution.py:469
  27.6 1.3 %collective-permute-done.2.refs_0_.refs_1_.refs_2_.refs_4_.refs_5_ = f32[2,4,64,512]{3,2,1,0:T(8,128)S(1)} collective-permute-done((f32[2,4,64,512]{3,2,1,0:T(8,128)S(1)}, f32[2,4,64,512]{3,2,1,0:T(8,128)S(1)}, u32[]{:S(2)}, u32[]{:S(2)}) %collective-permute-start.2) | collective-permute-done | bytes 1048608 | tf_op jit(solution)/shard_map/ppermute | solution.py:444
  28.9 0.1 shard_map.42
  29.1 2.9 %collective-permute-start.9 = (f32[2,4,32,512]{3,2,1,0:T(8,128)S(1)}, f32[2,4,32,512]{3,2,1,0:T(8,128)S(1)}, u32[]{:S(2)}, u32[]{:S(2)}) collective-permute-start(f32[2,4,32,512]{3,2,1,0:T(8,128)S(1)} %get-tuple-element.40.refs_3_.refs_4_), channel_id=1, source_target_pairs={{0,28},{4,8},{8,4},{12,16},{16,12},{20,24},{24,20},{28,0},{1,29},{... | collective-permute-start | bytes 1572872 | tf_op jit(solution)/shard_map/ppermute | solution.py:475
  31.9 0.2 shard_map.43
  32.1 4.1 %collective-permute-start.6 = (f32[2,48,512]{2,1,0:T(8,128)S(1)}, f32[2,48,512]{2,1,0:T(8,128)S(1)}, u32[]{:S(2)}, u32[]{:S(2)}) collective-permute-start(f32[2,48,512]{2,1,0:T(8,128)S(1)} %get-tuple-element.42), channel_id=1, source_target_pairs={{0,3},{1,2},{2,1},{3,0},{4,7},{5,6},{6,5},{7,4},{8,11},{9,10},{10,... | collective-permute-start | bytes 589832 | tf_op jit(solution)/shard_map/ppermute | solution.py:422
  36.3 0.6 collective-permute-start.8
  36.9 2.8 %shard_map.44 = (f32[4,2,20,512]{3,2,1,0:T(8,128)S(1)}, f32[4,2,16,512]{3,2,1,0:T(8,128)S(1)}, f32[4,2,16,512]{3,2,1,0:T(8,128)S(1)}) custom-call(f32[3]{0:T(128)S(1)} %copy-done.3, f32[4,4,24,512]{3,2,1,0:T(8,128)S(1)} %get-tuple-element.39.refs_2_.refs_1_, f32[4,4,24,512]{3,2,1,0:T(8,128)S(1)} %collective-permute-done.11.refs_2_, ...), custom_call_target="tpu_custom_call" | custom-call | bytes 6619148 | tf_op jit(solution)/shard_map/pallas_call | solution.py:365
  39.7 0.0 copy-start.2
  39.7 0.1 collective-permute-start.13
  39.8 0.1 shard_map.45
  39.9 1.4 %copy-done.2 = f32[1,4,256,512]{3,2,1,0:T(8,128)S(1)} copy-done((f32[1,4,256,512]{3,2,1,0:T(8,128)S(1)}, f32[1,4,256,512]{3,2,1,0:T(8,128)}, u32[]{:S(2)}) %copy-start.2) | copy-done | bytes 2097176
  41.3 3.2 %shard_map.46.refs_9_ = f32[2,256,512]{2,1,0:T(8,128)S(1)} custom-call(f32[3]{0:T(128)S(1)} %copy-done.3, f32[4,256,512]{2,1,0:T(8,128)S(1)} %bitcast.14, f32[4,256,512]{2,1,0:T(8,128)S(1)} %copy-done, f32[2,256,512]{2,1,0:T(8,128)S(1)} %get-tuple-element.38.refs_4_.refs_3_, f32[2,4,32,512]{3,2,1,0:T(8,128)S(1)} %get-tuple-element.40.refs_3_.refs_4_, ...), custom_call_target="tpu_custom_call" | custom-call | flops 4010485760 | bytes 7340044 | tf_op jit(solution)/shard_map/pallas_call | solution.py:365
  44.4 1.2 %shard_map.47 = (f32[2,16,512]{2,1,0:T(8,128)S(1)}, f32[4,2,16,512]{3,2,1,0:T(8,128)S(1)}) custom-call(f32[3]{0:T(128)S(1)} %copy-done.3, f32[4,4,24,512]{3,2,1,0:T(8,128)S(1)} %get-tuple-element.39.refs_2_.refs_1_, f32[4,4,64,512]{3,2,1,0:T(8,128)S(1)} %bitcast.8, f32[120,512]{1,0:T(8,128)S(1)} %collective-permute-done.10.refs_0_.refs_3_, ...), custom_call_target="tpu_custom_call" | custom-call | bytes 6406156 | tf_op jit(solution)/shard_map/pallas_call | solution.py:365
  45.6 0.3 collective-permute-done.9.refs_1_
  45.9 0.1 shard_map.48
  46.0 2.0 %collective-permute-start.12 = (f32[2,2,32,512]{3,2,1,0:T(8,128)S(1)}, f32[2,2,32,512]{3,2,1,0:T(8,128)S(1)}, u32[]{:S(2)}, u32[]{:S(2)}) collective-permute-start(f32[2,2,32,512]{3,2,1,0:T(8,128)S(1)} %get-tuple-element.54), channel_id=1, source_target_pairs={{0,1},{1,0},{2,3},{3,2},{4,5},{5,4},{6,7},{7,6},{8,9},{9,8},{10,11... | collective-permute-start | bytes 786440 | tf_op jit(solution)/shard_map/ppermute | solution.py:419
  48.1 2.0 %collective-permute-start.17 = (f32[4,2,16,512]{3,2,1,0:T(8,128)S(1)}, f32[4,2,16,512]{3,2,1,0:T(8,128)S(1)}, u32[]{:S(2)}, u32[]{:S(2)}) collective-permute-start(f32[4,2,16,512]{3,2,1,0:T(8,128)S(1)} %get-tuple-element.57), channel_id=1, source_target_pairs={{0,28},{4,8},{8,4},{12,16},{16,12},{20,24},{24,20},{28,0},{1,29},{... | collective-permute-start | bytes 786440 | tf_op jit(solution)/shard_map/ppermute | solution.py:488
  50.1 0.6 collective-permute-done.7.refs_2_
  50.7 0.8 %collective-permute-done.13.refs_1_ = f32[2,4,16,512]{3,2,1,0:T(8,128)S(1)} collective-permute-done((f32[2,4,16,512]{3,2,1,0:T(8,128)S(1)}, f32[2,4,16,512]{3,2,1,0:T(8,128)S(1)}, u32[]{:S(2)}, u32[]{:S(2)}) %collective-permute-start.13) | collective-permute-done | bytes 262176 | tf_op jit(solution)/shard_map/ppermute | solution.py:475
  51.5 0.1 shard_map.50
  51.6 2.0 %collective-permute-start.15 = (f32[2,2,16,512]{3,2,1,0:T(8,128)S(1)}, f32[2,2,16,512]{3,2,1,0:T(8,128)S(1)}, u32[]{:S(2)}, u32[]{:S(2)}) collective-permute-start(f32[2,2,16,512]{3,2,1,0:T(8,128)S(1)} %get-tuple-element.56), channel_id=1, source_target_pairs={{0,1},{1,0},{2,3},{3,2},{4,5},{5,4},{6,7},{7,6},{8,9},{9,8},{10,11... | collective-permute-start | bytes 393224 | tf_op jit(solution)/shard_map/ppermute | solution.py:419
  53.7 2.6 %collective-permute-done.12.refs_1_ = f32[2,2,32,512]{3,2,1,0:T(8,128)S(1)} collective-permute-done((f32[2,2,32,512]{3,2,1,0:T(8,128)S(1)}, f32[2,2,32,512]{3,2,1,0:T(8,128)S(1)}, u32[]{:S(2)}, u32[]{:S(2)}) %collective-permute-start.12) | collective-permute-done | bytes 262176 | tf_op jit(solution)/shard_map/ppermute | solution.py:419
  56.3 3.1 %collective-permute-start.14 = (f32[2,32,512]{2,1,0:T(8,128)S(1)}, f32[2,32,512]{2,1,0:T(8,128)S(1)}, u32[]{:S(2)}, u32[]{:S(2)}) collective-permute-start(f32[2,32,512]{2,1,0:T(8,128)S(1)} %shard_map.51.refs_2_), channel_id=1, source_target_pairs={{0,3},{1,2},{2,1},{3,0},{4,7},{5,6},{6,5},{7,4},{8,11},{9,10},{10,... | collective-permute-start | bytes 393224 | tf_op jit(solution)/shard_map/ppermute | solution.py:411
  59.4 0.0 collective-permute-done.15.refs_1_
  59.5 2.1 %collective-permute-start.16 = (f32[2,16,512]{2,1,0:T(8,128)S(1)}, f32[2,16,512]{2,1,0:T(8,128)S(1)}, u32[]{:S(2)}, u32[]{:S(2)}) collective-permute-start(f32[2,16,512]{2,1,0:T(8,128)S(1)} %shard_map.52.refs_3_), channel_id=1, source_target_pairs={{0,3},{1,2},{2,1},{3,0},{4,7},{5,6},{6,5},{7,4},{8,11},{9,10},{10,... | collective-permute-start | bytes 196616 | tf_op jit(solution)/shard_map/ppermute | solution.py:411
  61.6 2.1 %collective-permute-done.14.refs_2_ = f32[2,32,512]{2,1,0:T(8,128)S(1)} collective-permute-done((f32[2,32,512]{2,1,0:T(8,128)S(1)}, f32[2,32,512]{2,1,0:T(8,128)S(1)}, u32[]{:S(2)}, u32[]{:S(2)}) %collective-permute-start.14) | collective-permute-done | bytes 131104 | tf_op jit(solution)/shard_map/ppermute | solution.py:411
  63.7 2.0 %collective-permute-done.16.refs_2_ = f32[2,16,512]{2,1,0:T(8,128)S(1)} collective-permute-done((f32[2,16,512]{2,1,0:T(8,128)S(1)}, f32[2,16,512]{2,1,0:T(8,128)S(1)}, u32[]{:S(2)}, u32[]{:S(2)}) %collective-permute-start.16) | collective-permute-done | bytes 65568 | tf_op jit(solution)/shard_map/ppermute | solution.py:411
  65.7 0.0 collective-permute-done.17.refs_5_
  65.7 0.9 %shard_map.55 = f32[4,64,512]{2,1,0:T(8,128)} custom-call(f32[2,48,512]{2,1,0:T(8,128)S(1)} %shard_map.49.refs_3_.refs_0_, f32[2,16,512]{2,1,0:T(8,128)S(1)} %get-tuple-element.52.refs_3_.refs_1_, f32[2,32,512]{2,1,0:T(8,128)S(1)} %shard_map.53.refs_3_.refs_2_, f32[2,16,512]{2,1,0:T(8,128)S(1)} %shard_map.54.refs_3_.refs_7_, ...), custom_call_target="tpu_custom_call" | custom-call | bytes 1523712 | tf_op jit(solution)/shard_map/pallas_call | solution.py:365
  (15 shorter events, 0.1 us)
Async XLA Ops:
  0.0 9.5 %collective-permute-start = (f32[4,256,512]{2,1,0:T(8,128)}, f32[4,256,512]{2,1,0:T(8,128)S(1)}, u32[]{:S(2)}, u32[]{:S(2)}) collective-permute-start(f32[4,256,512]{2,1,0:T(8,128)} %bitcast.9), channel_id=1, source_target_pairs={{0,4},{4,0},{8,12},{12,8},{16,20},{20,16},{24,28},{28,24},{1,5},{5... | collective-permute-start | bytes 6291464 | tf_op jit(solution)/shard_map/ppermute | solution.py:435
  0.5 12.4 %collective-permute-start.1 = (f32[4,256,512]{2,1,0:T(8,128)}, f32[4,256,512]{2,1,0:T(8,128)S(1)}, u32[]{:S(2)}, u32[]{:S(2)}) collective-permute-start(f32[4,256,512]{2,1,0:T(8,128)} %refs_2_.3), channel_id=1, source_target_pairs={{0,4},{4,0},{8,12},{12,8},{16,20},{20,16},{24,28},{28,24},{1,5},{5... | collective-permute-start | bytes 6291464 | tf_op jit(solution)/shard_map/ppermute | solution.py:436
  0.5 1.6 %copy-start.1 = (f32[1,4,256,512]{3,2,1,0:T(8,128)S(1)}, f32[1,4,256,512]{3,2,1,0:T(8,128)}, u32[]{:S(2)}) copy-start(f32[1,4,256,512]{3,2,1,0:T(8,128)} %param.3) | copy-start | bytes 6291460
  2.2 8.1 %copy-start = (f32[4,256,512]{2,1,0:T(8,128)S(1)}, f32[4,256,512]{2,1,0:T(8,128)}, u32[]{:S(2)}) copy-start(f32[4,256,512]{2,1,0:T(8,128)} %refs_2_.3) | copy-start | bytes 6291460
  2.2 26.7 %collective-permute-start.2 = (f32[2,4,64,512]{3,2,1,0:T(8,128)S(1)}, f32[2,4,64,512]{3,2,1,0:T(8,128)S(1)}, u32[]{:S(2)}, u32[]{:S(2)}) collective-permute-start(f32[2,4,64,512]{3,2,1,0:T(8,128)S(1)} %shard_map.37.refs_1_), channel_id=1, source_target_pairs={{0,28},{4,8},{8,4},{12,16},{16,12},{20,24},{24,20},{28,0},{1,29},{... | collective-permute-start | bytes 3145736 | tf_op jit(solution)/shard_map/ppermute | solution.py:444
  5.9 14.0 %collective-permute-start.3 = (f32[4,24,512]{2,1,0:T(8,128)S(1)}, f32[4,24,512]{2,1,0:T(8,128)S(1)}, u32[]{:S(2)}, u32[]{:S(2)}) collective-permute-start(f32[4,24,512]{2,1,0:T(8,128)S(1)} %get-tuple-element.35), channel_id=1, source_target_pairs={{0,3},{1,2},{2,1},{3,0},{4,7},{5,6},{6,5},{7,4},{8,11},{9,10},{10,... | collective-permute-start | bytes 589832 | tf_op jit(solution)/shard_map/ppermute | solution.py:422
  9.5 16.4 %collective-permute-start.4 = (f32[4,24,512]{2,1,0:T(8,128)S(1)}, f32[4,24,512]{2,1,0:T(8,128)S(1)}, u32[]{:S(2)}, u32[]{:S(2)}) collective-permute-start(f32[4,24,512]{2,1,0:T(8,128)S(1)} %get-tuple-element.36), channel_id=1, source_target_pairs={{0,2},{1,3},{2,0},{3,1},{4,6},{5,7},{6,4},{7,5},{8,10},{9,11},{10,... | collective-permute-start | bytes 589832 | tf_op jit(solution)/shard_map/ppermute | solution.py:422
  9.5 16.4 %collective-permute-start.5 = (f32[4,24,512]{2,1,0:T(8,128)S(1)}, f32[4,24,512]{2,1,0:T(8,128)S(1)}, u32[]{:S(2)}, u32[]{:S(2)}) collective-permute-start(f32[4,24,512]{2,1,0:T(8,128)S(1)} %get-tuple-element.37), channel_id=1, source_target_pairs={{0,1},{1,0},{2,3},{3,2},{4,5},{5,4},{6,7},{7,6},{8,9},{9,8},{10,11... | collective-permute-start | bytes 589832 | tf_op jit(solution)/shard_map/ppermute | solution.py:422
  10.3 2.5 %copy-start.3 = (f32[3]{0:T(128)S(1)}, f32[3]{0:T(128)}, u32[]{:S(2)}) copy-start(f32[3]{0:T(128)} %refs_0_.7) | copy-start | bytes 40
  26.0 10.2 %collective-permute-start.11 = (f32[4,4,24,512]{3,2,1,0:T(8,128)S(1)}, f32[4,4,24,512]{3,2,1,0:T(8,128)S(1)}, u32[]{:S(2)}, u32[]{:S(2)}) collective-permute-start(f32[4,4,24,512]{3,2,1,0:T(8,128)S(1)} %get-tuple-element.39.refs_2_.refs_1_), channel_id=1, source_target_pairs={{0,4},{4,0},{8,12},{12,8},{16,20},{20,16},{24,28},{28,24},{1,5},{5... | collective-permute-start | bytes 2359304 | tf_op jit(solution)/shard_map/ppermute | solution.py:468
  26.1 13.6 %collective-permute-start.10 = (f32[120,512]{1,0:T(8,128)S(1)}, f32[120,512]{1,0:T(8,128)S(1)}, u32[]{:S(2)}, u32[]{:S(2)}) collective-permute-start(f32[120,512]{1,0:T(8,128)S(1)} %get-tuple-element.47), channel_id=1, source_target_pairs={{0,28},{4,8},{8,4},{12,16},{16,12},{20,24},{24,20},{28,0},{1,29},{... | collective-permute-start | bytes 737288 | tf_op jit(solution)/shard_map/ppermute | solution.py:469
  29.1 16.9 %collective-permute-start.9 = (f32[2,4,32,512]{3,2,1,0:T(8,128)S(1)}, f32[2,4,32,512]{3,2,1,0:T(8,128)S(1)}, u32[]{:S(2)}, u32[]{:S(2)}) collective-permute-start(f32[2,4,32,512]{3,2,1,0:T(8,128)S(1)} %get-tuple-element.40.refs_3_.refs_4_), channel_id=1, source_target_pairs={{0,28},{4,8},{8,4},{12,16},{16,12},{20,24},{24,20},{28,0},{1,29},{... | collective-permute-start | bytes 1572872 | tf_op jit(solution)/shard_map/ppermute | solution.py:475
  32.1 15.9 %collective-permute-start.6 = (f32[2,48,512]{2,1,0:T(8,128)S(1)}, f32[2,48,512]{2,1,0:T(8,128)S(1)}, u32[]{:S(2)}, u32[]{:S(2)}) collective-permute-start(f32[2,48,512]{2,1,0:T(8,128)S(1)} %get-tuple-element.42), channel_id=1, source_target_pairs={{0,3},{1,2},{2,1},{3,0},{4,7},{5,6},{6,5},{7,4},{8,11},{9,10},{10,... | collective-permute-start | bytes 589832 | tf_op jit(solution)/shard_map/ppermute | solution.py:422
  36.3 14.4 %collective-permute-start.7 = (f32[2,48,512]{2,1,0:T(8,128)S(1)}, f32[2,48,512]{2,1,0:T(8,128)S(1)}, u32[]{:S(2)}, u32[]{:S(2)}) collective-permute-start(f32[2,48,512]{2,1,0:T(8,128)S(1)} %get-tuple-element.43), channel_id=1, source_target_pairs={{0,2},{1,3},{2,0},{3,1},{4,6},{5,7},{6,4},{7,5},{8,10},{9,11},{10,... | collective-permute-start | bytes 589832 | tf_op jit(solution)/shard_map/ppermute | solution.py:422
  36.3 14.4 %collective-permute-start.8 = (f32[2,48,512]{2,1,0:T(8,128)S(1)}, f32[2,48,512]{2,1,0:T(8,128)S(1)}, u32[]{:S(2)}, u32[]{:S(2)}) collective-permute-start(f32[2,48,512]{2,1,0:T(8,128)S(1)} %get-tuple-element.44), channel_id=1, source_target_pairs={{0,1},{1,0},{2,3},{3,2},{4,5},{5,4},{6,7},{7,6},{8,9},{9,8},{10,11... | collective-permute-start | bytes 589832 | tf_op jit(solution)/shard_map/ppermute | solution.py:422
  39.7 1.6 %copy-start.2 = (f32[1,4,256,512]{3,2,1,0:T(8,128)S(1)}, f32[1,4,256,512]{3,2,1,0:T(8,128)}, u32[]{:S(2)}) copy-start(f32[1,4,256,512]{3,2,1,0:T(8,128)} %param.3) | copy-start | bytes 6291460
  39.7 11.9 %collective-permute-start.13 = (f32[2,4,16,512]{3,2,1,0:T(8,128)S(1)}, f32[2,4,16,512]{3,2,1,0:T(8,128)S(1)}, u32[]{:S(2)}, u32[]{:S(2)}) collective-permute-start(f32[2,4,16,512]{3,2,1,0:T(8,128)S(1)} %get-tuple-element.45.refs_5_), channel_id=1, source_target_pairs={{0,28},{4,8},{8,4},{12,16},{16,12},{20,24},{24,20},{28,0},{1,29},{... | collective-permute-start | bytes 786440 | tf_op jit(solution)/shard_map/ppermute | solution.py:475
  46.0 10.2 %collective-permute-start.12 = (f32[2,2,32,512]{3,2,1,0:T(8,128)S(1)}, f32[2,2,32,512]{3,2,1,0:T(8,128)S(1)}, u32[]{:S(2)}, u32[]{:S(2)}) collective-permute-start(f32[2,2,32,512]{3,2,1,0:T(8,128)S(1)} %get-tuple-element.54), channel_id=1, source_target_pairs={{0,1},{1,0},{2,3},{3,2},{4,5},{5,4},{6,7},{7,6},{8,9},{9,8},{10,11... | collective-permute-start | bytes 786440 | tf_op jit(solution)/shard_map/ppermute | solution.py:419
  48.1 17.6 %collective-permute-start.17 = (f32[4,2,16,512]{3,2,1,0:T(8,128)S(1)}, f32[4,2,16,512]{3,2,1,0:T(8,128)S(1)}, u32[]{:S(2)}, u32[]{:S(2)}) collective-permute-start(f32[4,2,16,512]{3,2,1,0:T(8,128)S(1)} %get-tuple-element.57), channel_id=1, source_target_pairs={{0,28},{4,8},{8,4},{12,16},{16,12},{20,24},{24,20},{28,0},{1,29},{... | collective-permute-start | bytes 786440 | tf_op jit(solution)/shard_map/ppermute | solution.py:488
  51.6 7.8 %collective-permute-start.15 = (f32[2,2,16,512]{3,2,1,0:T(8,128)S(1)}, f32[2,2,16,512]{3,2,1,0:T(8,128)S(1)}, u32[]{:S(2)}, u32[]{:S(2)}) collective-permute-start(f32[2,2,16,512]{3,2,1,0:T(8,128)S(1)} %get-tuple-element.56), channel_id=1, source_target_pairs={{0,1},{1,0},{2,3},{3,2},{4,5},{5,4},{6,7},{7,6},{8,9},{9,8},{10,11... | collective-permute-start | bytes 393224 | tf_op jit(solution)/shard_map/ppermute | solution.py:419
  56.3 7.3 %collective-permute-start.14 = (f32[2,32,512]{2,1,0:T(8,128)S(1)}, f32[2,32,512]{2,1,0:T(8,128)S(1)}, u32[]{:S(2)}, u32[]{:S(2)}) collective-permute-start(f32[2,32,512]{2,1,0:T(8,128)S(1)} %shard_map.51.refs_2_), channel_id=1, source_target_pairs={{0,3},{1,2},{2,1},{3,0},{4,7},{5,6},{6,5},{7,4},{8,11},{9,10},{10,... | collective-permute-start | bytes 393224 | tf_op jit(solution)/shard_map/ppermute | solution.py:411
  59.5 6.2 %collective-permute-start.16 = (f32[2,16,512]{2,1,0:T(8,128)S(1)}, f32[2,16,512]{2,1,0:T(8,128)S(1)}, u32[]{:S(2)}, u32[]{:S(2)}) collective-permute-start(f32[2,16,512]{2,1,0:T(8,128)S(1)} %shard_map.52.refs_3_), channel_id=1, source_target_pairs={{0,3},{1,2},{2,1},{3,0},{4,7},{5,6},{6,5},{7,4},{8,11},{9,10},{10,... | collective-permute-start | bytes 196616 | tf_op jit(solution)/shard_map/ppermute | solution.py:411

commit v12 on v11

--- a/solution.py
+++ b/solution.py
@@ -467,13 +467,13 @@
     )
     x_in = lax.ppermute(x, "slab", partner)
     x_halo = lax.ppermute(piece, "slab", face)
+    back0 = back_squares((0, wide - part))
     fs = call(
         functools.partial(face_kernel, chunk, cuts),
         [slab_shape(cut) for cut in cuts],
         (halo, as_bands(g)),
     )
     face_a, face_b = [lax.ppermute(f, "slab", face) for f in fs[:2]]
-    back0 = back_squares((0, wide - part))
     x_first, x_t, x_back = call(
         functools.partial(rows_kernel, cut_c),
         [(bands, 2, inner, lanes)] + [(bands, 2, part, lanes)] * 2,
@@ -501,8 +501,8 @@
         (coeffs, x, as_bands(potential), x_halo, halo, halo, x_f, x_t, x_back),
         scalars=1,
     )
+    back0 = sum_all(*back0, weight=3_000_000_000)
     front_a = squares(cut_a, face_a)
-    back0 = sum_all(*back0, weight=1_000_000_000)
     front_b = squares(cut_b, face_b)
     front_a = add_far(*front_a)
     front_b = add_far(*front_b)

time: 66.8 us -> 68.7 us (1.028)
  waiting for transfers between devices: 15.8 us -> 18.6 us
  local copies, waits for them, and re-layouts: 2.99 us -> 2.12 us
    ppermute x6, waiting for transfers between devices: 6.66 us -> 10.5 us  [over_orb(): return lax.ppermute(x, 'orb', [(i, i ^ d) for i in range(bands)])]
    ppermute x2, waiting for transfers between devices: 4.1 us -> 2.44 us  [add_far(): return (keep, came, lax.ppermute(total, 'orb', far))]
    ppermute x2, starting transfers between devices: 4.1 us -> 2.78 us  [squares(): return (keep, lax.ppermute(send, 'orb', near))]
    unnamed x8, local copies, waits for them, and re-layouts: 2.99 us -> 2.12 us
    ppermute x2, starting transfers between devices: 5.25 us -> 6.07 us  [add_far(): return (keep, came, lax.ppermute(total, 'orb', far))]
  transfers between devices with their start and end apart: 18 -> 18, of which waited for: 8 -> 9; matrix products, arithmetic and copies ran while one was open for 0% -> 0% of each run, Pallas kernels for 26% -> 26%
where the time goes in v12:
time: 68.7 us; the launch traced here: 68.4 us
  starting transfers between devices  29 us (42%)
  waiting for transfers between devices  18.6 us (27%)
  Pallas kernels  18.5 us (27%)
  local copies, waits for them, and re-layouts  2.12 us (3%)
    pallas_call x19, Pallas kernels, __call__(): pl.pallas_call(body, out_shape=shapes, in_specs=[smem] * scalars + [pl.Bl...  18.5 us
    ppermute x6, waiting for transfers between devices, over_orb(): return lax.ppermute(x, 'orb', [(i, i ^ d) for i in range(bands)])  10.5 us
    ppermute x6, starting transfers between devices, over_orb(): return lax.ppermute(x, 'orb', [(i, i ^ d) for i in range(bands)])  9.7 us
    ppermute x2, starting transfers between devices, add_far(): return (keep, came, lax.ppermute(total, 'orb', far))  6.07 us
    ppermute x1, starting transfers between devices, shards(): halo = lax.ppermute(piece, 'slab', face)  3.57 us
    ppermute x2, starting transfers between devices, squares(): return (keep, lax.ppermute(send, 'orb', near))  2.78 us
    ppermute x2, starting transfers between devices, shards(): face_a, face_b = [lax.ppermute(f, 'slab', face) for f in fs[:2]]  2.78 us
    ppermute x2, waiting for transfers between devices, squares(): return (keep, lax.ppermute(send, 'orb', near))  2.7 us
  transfers between devices with their start and end apart: 18, of which 9 were waited for; matrix products, arithmetic and copies ran while one was open for 0% of the time, Pallas kernels for 26%

profile of v12, /device:TPU:0, one launch (start us, length us, event | category | flops | bytes accessed | tf_op | source)
XLA Modules:
  0.0 68.4 jit_solution(12075082319092362791)
XLA Ops:
  0.0 0.5 collective-permute-start
  0.5 0.1 collective-permute-start.1
  0.5 1.6 %copy-done.1 = f32[1,4,256,512]{3,2,1,0:T(8,128)S(1)} copy-done((f32[1,4,256,512]{3,2,1,0:T(8,128)S(1)}, f32[1,4,256,512]{3,2,1,0:T(8,128)}, u32[]{:S(2)}) %copy-start.1) | copy-done | bytes 2097176
  2.1 0.1 shard_map.37.refs_1_
  2.2 0.0 copy-start
  2.2 3.6 %collective-permute-start.2 = (f32[2,4,64,512]{3,2,1,0:T(8,128)S(1)}, f32[2,4,64,512]{3,2,1,0:T(8,128)S(1)}, u32[]{:S(2)}, u32[]{:S(2)}) collective-permute-start(f32[2,4,64,512]{3,2,1,0:T(8,128)S(1)} %shard_map.37.refs_1_), channel_id=1, source_target_pairs={{0,28},{4,8},{8,4},{12,16},{16,12},{20,24},{24,20},{28,0},{1,29},{... | collective-permute-start | bytes 3145736 | tf_op jit(solution)/shard_map/ppermute | solution.py:444
  5.8 0.1 shard_map.38
  5.9 3.7 %collective-permute-start.3 = (f32[4,24,512]{2,1,0:T(8,128)S(1)}, f32[4,24,512]{2,1,0:T(8,128)S(1)}, u32[]{:S(2)}, u32[]{:S(2)}) collective-permute-start(f32[4,24,512]{2,1,0:T(8,128)S(1)} %get-tuple-element.35), channel_id=1, source_target_pairs={{0,3},{1,2},{2,1},{3,0},{4,7},{5,6},{6,5},{7,4},{8,11},{9,10},{10,... | collective-permute-start | bytes 589832 | tf_op jit(solution)/shard_map/ppermute | solution.py:422
  9.5 0.8 %collective-permute-start.5 = (f32[4,24,512]{2,1,0:T(8,128)S(1)}, f32[4,24,512]{2,1,0:T(8,128)S(1)}, u32[]{:S(2)}, u32[]{:S(2)}) collective-permute-start(f32[4,24,512]{2,1,0:T(8,128)S(1)} %get-tuple-element.37), channel_id=1, source_target_pairs={{0,1},{1,0},{2,3},{3,2},{4,5},{5,4},{6,7},{7,6},{8,9},{9,8},{10,11... | collective-permute-start | bytes 589832 | tf_op jit(solution)/shard_map/ppermute | solution.py:422
  10.3 2.5 %shard_map.39.refs_5_.refs_6_ = f32[2,256,512]{2,1,0:T(8,128)S(1)} custom-call(f32[4,256,512]{2,1,0:T(8,128)S(1)} %bitcast.12, f32[4,256,512]{2,1,0:T(8,128)S(1)} %copy-done, f32[4,24,512]{2,1,0:T(8,128)S(1)} %get-tuple-element.32.refs_2_.refs_0_), custom_call_target="tpu_custom_call" | custom-call | flops 6291456 | bytes 5242880 | tf_op jit(solution)/shard_map/pallas_call | solution.py:365
  12.8 0.0 collective-permute-done.1.refs_4_
  12.8 7.0 %shard_map.40 = (f32[2,256,512]{2,1,0:T(8,128)S(1)}, f32[2,256,512]{2,1,0:T(8,128)S(1)}, f32[8,512]{1,0:T(8,128)S(1)}) custom-call(f32[3]{0:T(128)S(1)} %copy-done.3, f32[4,256,512]{2,1,0:T(8,128)S(1)} %bitcast.13, f32[4,256,512]{2,1,0:T(8,128)S(1)} %copy-done, f32[4,256,512]{2,1,0:T(8,128)S(1)} %collective-permute-done.refs_3_, ...), custom_call_target="tpu_custom_call" | custom-call | flops 20971520 | bytes 11550732 | tf_op jit(solution)/shard_map/pallas_call | solution.py:365
  19.8 6.1 %collective-permute-done.4.refs_2_ = f32[4,24,512]{2,1,0:T(8,128)S(1)} collective-permute-done((f32[4,24,512]{2,1,0:T(8,128)S(1)}, f32[4,24,512]{2,1,0:T(8,128)S(1)}, u32[]{:S(2)}, u32[]{:S(2)}) %collective-permute-start.4) | collective-permute-done | bytes 196640 | tf_op jit(solution)/shard_map/ppermute | solution.py:422
  25.9 0.0 collective-permute-done.5.refs_3_
  25.9 0.1 shard_map.41
  26.0 0.1 collective-permute-start.10
  26.1 1.5 %collective-permute-start.9 = (f32[120,512]{1,0:T(8,128)S(1)}, f32[120,512]{1,0:T(8,128)S(1)}, u32[]{:S(2)}, u32[]{:S(2)}) collective-permute-start(f32[120,512]{1,0:T(8,128)S(1)} %get-tuple-element.44), channel_id=1, source_target_pairs={{0,28},{4,8},{8,4},{12,16},{16,12},{20,24},{24,20},{28,0},{1,29},{... | collective-permute-start | bytes 737288 | tf_op jit(solution)/shard_map/ppermute | solution.py:469
  27.6 1.3 %collective-permute-done.2.refs_1_.refs_0_.refs_2_.refs_4_.refs_5_ = f32[2,4,64,512]{3,2,1,0:T(8,128)S(1)} collective-permute-done((f32[2,4,64,512]{3,2,1,0:T(8,128)S(1)}, f32[2,4,64,512]{3,2,1,0:T(8,128)S(1)}, u32[]{:S(2)}, u32[]{:S(2)}) %collective-permute-start.2) | collective-permute-done | bytes 1048608 | tf_op jit(solution)/shard_map/ppermute | solution.py:444
  28.9 0.2 shard_map.42
  29.1 4.6 %collective-permute-start.6 = (f32[2,48,512]{2,1,0:T(8,128)S(1)}, f32[2,48,512]{2,1,0:T(8,128)S(1)}, u32[]{:S(2)}, u32[]{:S(2)}) collective-permute-start(f32[2,48,512]{2,1,0:T(8,128)S(1)} %get-tuple-element.41), channel_id=1, source_target_pairs={{0,3},{1,2},{2,1},{3,0},{4,7},{5,6},{6,5},{7,4},{8,11},{9,10},{10,... | collective-permute-start | bytes 589832 | tf_op jit(solution)/shard_map/ppermute | solution.py:422
  33.7 0.6 collective-permute-start.8
  34.4 0.1 shard_map.43
  34.5 0.0 collective-permute-done.10.refs_2_
  34.5 1.8 %collective-permute-start.11 = (f32[2,4,32,512]{3,2,1,0:T(8,128)S(1)}, f32[2,4,32,512]{3,2,1,0:T(8,128)S(1)}, u32[]{:S(2)}, u32[]{:S(2)}) collective-permute-start(f32[2,4,32,512]{3,2,1,0:T(8,128)S(1)} %get-tuple-element.45.refs_5_.refs_4_), channel_id=1, source_target_pairs={{0,28},{4,8},{8,4},{12,16},{16,12},{20,24},{24,20},{28,0},{1,29},{... | collective-permute-start | bytes 1572872 | tf_op jit(solution)/shard_map/ppermute | solution.py:476
  36.3 2.8 %shard_map.44 = (f32[4,2,20,512]{3,2,1,0:T(8,128)S(1)}, f32[4,2,16,512]{3,2,1,0:T(8,128)S(1)}, f32[4,2,16,512]{3,2,1,0:T(8,128)S(1)}) custom-call(f32[3]{0:T(128)S(1)} %copy-done.3, f32[4,4,24,512]{3,2,1,0:T(8,128)S(1)} %get-tuple-element.39.refs_3_.refs_1_, f32[4,4,24,512]{3,2,1,0:T(8,128)S(1)} %collective-permute-done.10.refs_2_, ...), custom_call_target="tpu_custom_call" | custom-call | bytes 6619148 | tf_op jit(solution)/shard_map/pallas_call | solution.py:365
  39.1 0.0 copy-start.2
  39.1 0.0 collective-permute-done.9.refs_0_.refs_3_
  39.1 1.0 %collective-permute-start.13 = (f32[2,4,16,512]{3,2,1,0:T(8,128)S(1)}, f32[2,4,16,512]{3,2,1,0:T(8,128)S(1)}, u32[]{:S(2)}, u32[]{:S(2)}) collective-permute-start(f32[2,4,16,512]{3,2,1,0:T(8,128)S(1)} %get-tuple-element.50.refs_5_), channel_id=1, source_target_pairs={{0,28},{4,8},{8,4},{12,16},{16,12},{20,24},{24,20},{28,0},{1,29},{... | collective-permute-start | bytes 786440 | tf_op jit(solution)/shard_map/ppermute | solution.py:476
  40.1 0.1 shard_map.45
  40.2 0.5 copy-done.2
  40.7 3.2 %shard_map.46.refs_9_ = f32[2,256,512]{2,1,0:T(8,128)S(1)} custom-call(f32[3]{0:T(128)S(1)} %copy-done.3, f32[4,256,512]{2,1,0:T(8,128)S(1)} %bitcast.14, f32[4,256,512]{2,1,0:T(8,128)S(1)} %copy-done, f32[2,256,512]{2,1,0:T(8,128)S(1)} %get-tuple-element.38.refs_4_.refs_3_, f32[2,4,32,512]{3,2,1,0:T(8,128)S(1)} %get-tuple-element.45.refs_5_.refs_4_, ...), custom_call_target="tpu_custom_call" | custom-call | flops 4010485760 | bytes 7340044 | tf_op jit(solution)/shard_map/pallas_call | solution.py:365
  43.9 1.2 %shard_map.47 = (f32[2,16,512]{2,1,0:T(8,128)S(1)}, f32[4,2,16,512]{3,2,1,0:T(8,128)S(1)}) custom-call(f32[3]{0:T(128)S(1)} %copy-done.3, f32[4,4,24,512]{3,2,1,0:T(8,128)S(1)} %get-tuple-element.39.refs_3_.refs_1_, f32[4,4,64,512]{3,2,1,0:T(8,128)S(1)} %bitcast.8, f32[120,512]{1,0:T(8,128)S(1)} %collective-permute-done.9.refs_0_.refs_3_, ...), custom_call_target="tpu_custom_call" | custom-call | bytes 6406156 | tf_op jit(solution)/shard_map/pallas_call | solution.py:365
  45.1 0.0 collective-permute-done.6.refs_1_
  45.1 4.4 %collective-permute-done.7.refs_2_ = f32[2,48,512]{2,1,0:T(8,128)S(1)} collective-permute-done((f32[2,48,512]{2,1,0:T(8,128)S(1)}, f32[2,48,512]{2,1,0:T(8,128)S(1)}, u32[]{:S(2)}, u32[]{:S(2)}) %collective-permute-start.7) | collective-permute-done | bytes 196640 | tf_op jit(solution)/shard_map/ppermute | solution.py:422
  49.5 0.1 collective-permute-done.11.refs_1_
  49.6 0.1 shard_map.49
  49.8 1.5 %collective-permute-start.12 = (f32[2,2,32,512]{3,2,1,0:T(8,128)S(1)}, f32[2,2,32,512]{3,2,1,0:T(8,128)S(1)}, u32[]{:S(2)}, u32[]{:S(2)}) collective-permute-start(f32[2,2,32,512]{3,2,1,0:T(8,128)S(1)} %get-tuple-element.54), channel_id=1, source_target_pairs={{0,1},{1,0},{2,3},{3,2},{4,5},{5,4},{6,7},{7,6},{8,9},{9,8},{10,11... | collective-permute-start | bytes 786440 | tf_op jit(solution)/shard_map/ppermute | solution.py:419
  51.2 2.0 %collective-permute-start.17 = (f32[4,2,16,512]{3,2,1,0:T(8,128)S(1)}, f32[4,2,16,512]{3,2,1,0:T(8,128)S(1)}, u32[]{:S(2)}, u32[]{:S(2)}) collective-permute-start(f32[4,2,16,512]{3,2,1,0:T(8,128)S(1)} %get-tuple-element.57), channel_id=1, source_target_pairs={{0,28},{4,8},{8,4},{12,16},{16,12},{20,24},{24,20},{28,0},{1,29},{... | collective-permute-start | bytes 786440 | tf_op jit(solution)/shard_map/ppermute | solution.py:488
  53.2 1.6 %collective-permute-done.13.refs_1_ = f32[2,4,16,512]{3,2,1,0:T(8,128)S(1)} collective-permute-done((f32[2,4,16,512]{3,2,1,0:T(8,128)S(1)}, f32[2,4,16,512]{3,2,1,0:T(8,128)S(1)}, u32[]{:S(2)}, u32[]{:S(2)}) %collective-permute-start.13) | collective-permute-done | bytes 262176 | tf_op jit(solution)/shard_map/ppermute | solution.py:476
  54.8 0.1 shard_map.50
  54.9 1.3 %collective-permute-start.15 = (f32[2,2,16,512]{3,2,1,0:T(8,128)S(1)}, f32[2,2,16,512]{3,2,1,0:T(8,128)S(1)}, u32[]{:S(2)}, u32[]{:S(2)}) collective-permute-start(f32[2,2,16,512]{3,2,1,0:T(8,128)S(1)} %get-tuple-element.56), channel_id=1, source_target_pairs={{0,1},{1,0},{2,3},{3,2},{4,5},{5,4},{6,7},{7,6},{8,9},{9,8},{10,11... | collective-permute-start | bytes 393224 | tf_op jit(solution)/shard_map/ppermute | solution.py:419
  56.2 2.3 %collective-permute-done.12.refs_1_ = f32[2,2,32,512]{3,2,1,0:T(8,128)S(1)} collective-permute-done((f32[2,2,32,512]{3,2,1,0:T(8,128)S(1)}, f32[2,2,32,512]{3,2,1,0:T(8,128)S(1)}, u32[]{:S(2)}, u32[]{:S(2)}) %collective-permute-start.12) | collective-permute-done | bytes 262176 | tf_op jit(solution)/shard_map/ppermute | solution.py:419
  58.5 2.4 %collective-permute-start.14 = (f32[2,32,512]{2,1,0:T(8,128)S(1)}, f32[2,32,512]{2,1,0:T(8,128)S(1)}, u32[]{:S(2)}, u32[]{:S(2)}) collective-permute-start(f32[2,32,512]{2,1,0:T(8,128)S(1)} %shard_map.51.refs_2_), channel_id=1, source_target_pairs={{0,3},{1,2},{2,1},{3,0},{4,7},{5,6},{6,5},{7,4},{8,11},{9,10},{10,... | collective-permute-start | bytes 393224 | tf_op jit(solution)/shard_map/ppermute | solution.py:411
  60.9 0.4 collective-permute-done.15.refs_1_
  61.3 3.7 %collective-permute-start.16 = (f32[2,16,512]{2,1,0:T(8,128)S(1)}, f32[2,16,512]{2,1,0:T(8,128)S(1)}, u32[]{:S(2)}, u32[]{:S(2)}) collective-permute-start(f32[2,16,512]{2,1,0:T(8,128)S(1)} %shard_map.52.refs_3_), channel_id=1, source_target_pairs={{0,3},{1,2},{2,1},{3,0},{4,7},{5,6},{6,5},{7,4},{8,11},{9,10},{10,... | collective-permute-start | bytes 196616 | tf_op jit(solution)/shard_map/ppermute | solution.py:411
  65.0 0.4 collective-permute-done.14.refs_2_
  65.4 2.0 %collective-permute-done.16.refs_2_ = f32[2,16,512]{2,1,0:T(8,128)S(1)} collective-permute-done((f32[2,16,512]{2,1,0:T(8,128)S(1)}, f32[2,16,512]{2,1,0:T(8,128)S(1)}, u32[]{:S(2)}, u32[]{:S(2)}) %collective-permute-start.16) | collective-permute-done | bytes 65568 | tf_op jit(solution)/shard_map/ppermute | solution.py:411
  67.5 0.9 %shard_map.55 = f32[4,64,512]{2,1,0:T(8,128)} custom-call(f32[2,48,512]{2,1,0:T(8,128)S(1)} %shard_map.48.refs_3_.refs_0_, f32[2,16,512]{2,1,0:T(8,128)S(1)} %get-tuple-element.52.refs_4_.refs_1_, f32[2,32,512]{2,1,0:T(8,128)S(1)} %shard_map.53.refs_3_.refs_2_, f32[2,16,512]{2,1,0:T(8,128)S(1)} %shard_map.54.refs_3_.refs_7_, ...), custom_call_target="tpu_custom_call" | custom-call | bytes 1523712 | tf_op jit(solution)/shard_map/pallas_call | solution.py:365
  (15 shorter events, 0.1 us)
Async XLA Ops:
  0.0 9.5 %collective-permute-start = (f32[4,256,512]{2,1,0:T(8,128)}, f32[4,256,512]{2,1,0:T(8,128)S(1)}, u32[]{:S(2)}, u32[]{:S(2)}) collective-permute-start(f32[4,256,512]{2,1,0:T(8,128)} %bitcast.9), channel_id=1, source_target_pairs={{0,4},{4,0},{8,12},{12,8},{16,20},{20,16},{24,28},{28,24},{1,5},{5... | collective-permute-start | bytes 6291464 | tf_op jit(solution)/shard_map/ppermute | solution.py:435
  0.5 12.4 %collective-permute-start.1 = (f32[4,256,512]{2,1,0:T(8,128)}, f32[4,256,512]{2,1,0:T(8,128)S(1)}, u32[]{:S(2)}, u32[]{:S(2)}) collective-permute-start(f32[4,256,512]{2,1,0:T(8,128)} %refs_2_.3), channel_id=1, source_target_pairs={{0,4},{4,0},{8,12},{12,8},{16,20},{20,16},{24,28},{28,24},{1,5},{5... | collective-permute-start | bytes 6291464 | tf_op jit(solution)/shard_map/ppermute | solution.py:436
  0.5 1.6 %copy-start.1 = (f32[1,4,256,512]{3,2,1,0:T(8,128)S(1)}, f32[1,4,256,512]{3,2,1,0:T(8,128)}, u32[]{:S(2)}) copy-start(f32[1,4,256,512]{3,2,1,0:T(8,128)} %param.3) | copy-start | bytes 6291460
  2.2 8.1 %copy-start = (f32[4,256,512]{2,1,0:T(8,128)S(1)}, f32[4,256,512]{2,1,0:T(8,128)}, u32[]{:S(2)}) copy-start(f32[4,256,512]{2,1,0:T(8,128)} %refs_2_.3) | copy-start | bytes 6291460
  2.2 26.7 %collective-permute-start.2 = (f32[2,4,64,512]{3,2,1,0:T(8,128)S(1)}, f32[2,4,64,512]{3,2,1,0:T(8,128)S(1)}, u32[]{:S(2)}, u32[]{:S(2)}) collective-permute-start(f32[2,4,64,512]{3,2,1,0:T(8,128)S(1)} %shard_map.37.refs_1_), channel_id=1, source_target_pairs={{0,28},{4,8},{8,4},{12,16},{16,12},{20,24},{24,20},{28,0},{1,29},{... | collective-permute-start | bytes 3145736 | tf_op jit(solution)/shard_map/ppermute | solution.py:444
  5.9 14.0 %collective-permute-start.3 = (f32[4,24,512]{2,1,0:T(8,128)S(1)}, f32[4,24,512]{2,1,0:T(8,128)S(1)}, u32[]{:S(2)}, u32[]{:S(2)}) collective-permute-start(f32[4,24,512]{2,1,0:T(8,128)S(1)} %get-tuple-element.35), channel_id=1, source_target_pairs={{0,3},{1,2},{2,1},{3,0},{4,7},{5,6},{6,5},{7,4},{8,11},{9,10},{10,... | collective-permute-start | bytes 589832 | tf_op jit(solution)/shard_map/ppermute | solution.py:422
  9.5 16.4 %collective-permute-start.4 = (f32[4,24,512]{2,1,0:T(8,128)S(1)}, f32[4,24,512]{2,1,0:T(8,128)S(1)}, u32[]{:S(2)}, u32[]{:S(2)}) collective-permute-start(f32[4,24,512]{2,1,0:T(8,128)S(1)} %get-tuple-element.36), channel_id=1, source_target_pairs={{0,2},{1,3},{2,0},{3,1},{4,6},{5,7},{6,4},{7,5},{8,10},{9,11},{10,... | collective-permute-start | bytes 589832 | tf_op jit(solution)/shard_map/ppermute | solution.py:422
  9.5 16.4 %collective-permute-start.5 = (f32[4,24,512]{2,1,0:T(8,128)S(1)}, f32[4,24,512]{2,1,0:T(8,128)S(1)}, u32[]{:S(2)}, u32[]{:S(2)}) collective-permute-start(f32[4,24,512]{2,1,0:T(8,128)S(1)} %get-tuple-element.37), channel_id=1, source_target_pairs={{0,1},{1,0},{2,3},{3,2},{4,5},{5,4},{6,7},{7,6},{8,9},{9,8},{10,11... | collective-permute-start | bytes 589832 | tf_op jit(solution)/shard_map/ppermute | solution.py:422
  10.3 2.5 %copy-start.3 = (f32[3]{0:T(128)S(1)}, f32[3]{0:T(128)}, u32[]{:S(2)}) copy-start(f32[3]{0:T(128)} %refs_0_.7) | copy-start | bytes 40
  26.0 8.5 %collective-permute-start.10 = (f32[4,4,24,512]{3,2,1,0:T(8,128)S(1)}, f32[4,4,24,512]{3,2,1,0:T(8,128)S(1)}, u32[]{:S(2)}, u32[]{:S(2)}) collective-permute-start(f32[4,4,24,512]{3,2,1,0:T(8,128)S(1)} %get-tuple-element.39.refs_3_.refs_1_), channel_id=1, source_target_pairs={{0,4},{4,0},{8,12},{12,8},{16,20},{20,16},{24,28},{28,24},{1,5},{5... | collective-permute-start | bytes 2359304 | tf_op jit(solution)/shard_map/ppermute | solution.py:468
  26.1 13.0 %collective-permute-start.9 = (f32[120,512]{1,0:T(8,128)S(1)}, f32[120,512]{1,0:T(8,128)S(1)}, u32[]{:S(2)}, u32[]{:S(2)}) collective-permute-start(f32[120,512]{1,0:T(8,128)S(1)} %get-tuple-element.44), channel_id=1, source_target_pairs={{0,28},{4,8},{8,4},{12,16},{16,12},{20,24},{24,20},{28,0},{1,29},{... | collective-permute-start | bytes 737288 | tf_op jit(solution)/shard_map/ppermute | solution.py:469
  29.1 15.9 %collective-permute-start.6 = (f32[2,48,512]{2,1,0:T(8,128)S(1)}, f32[2,48,512]{2,1,0:T(8,128)S(1)}, u32[]{:S(2)}, u32[]{:S(2)}) collective-permute-start(f32[2,48,512]{2,1,0:T(8,128)S(1)} %get-tuple-element.41), channel_id=1, source_target_pairs={{0,3},{1,2},{2,1},{3,0},{4,7},{5,6},{6,5},{7,4},{8,11},{9,10},{10,... | collective-permute-start | bytes 589832 | tf_op jit(solution)/shard_map/ppermute | solution.py:422
  33.7 15.8 %collective-permute-start.7 = (f32[2,48,512]{2,1,0:T(8,128)S(1)}, f32[2,48,512]{2,1,0:T(8,128)S(1)}, u32[]{:S(2)}, u32[]{:S(2)}) collective-permute-start(f32[2,48,512]{2,1,0:T(8,128)S(1)} %get-tuple-element.42), channel_id=1, source_target_pairs={{0,2},{1,3},{2,0},{3,1},{4,6},{5,7},{6,4},{7,5},{8,10},{9,11},{10,... | collective-permute-start | bytes 589832 | tf_op jit(solution)/shard_map/ppermute | solution.py:422
  33.7 15.8 %collective-permute-start.8 = (f32[2,48,512]{2,1,0:T(8,128)S(1)}, f32[2,48,512]{2,1,0:T(8,128)S(1)}, u32[]{:S(2)}, u32[]{:S(2)}) collective-permute-start(f32[2,48,512]{2,1,0:T(8,128)S(1)} %get-tuple-element.43), channel_id=1, source_target_pairs={{0,1},{1,0},{2,3},{3,2},{4,5},{5,4},{6,7},{7,6},{8,9},{9,8},{10,11... | collective-permute-start | bytes 589832 | tf_op jit(solution)/shard_map/ppermute | solution.py:422
  34.5 15.1 %collective-permute-start.11 = (f32[2,4,32,512]{3,2,1,0:T(8,128)S(1)}, f32[2,4,32,512]{3,2,1,0:T(8,128)S(1)}, u32[]{:S(2)}, u32[]{:S(2)}) collective-permute-start(f32[2,4,32,512]{3,2,1,0:T(8,128)S(1)} %get-tuple-element.45.refs_5_.refs_4_), channel_id=1, source_target_pairs={{0,28},{4,8},{8,4},{12,16},{16,12},{20,24},{24,20},{28,0},{1,29},{... | collective-permute-start | bytes 1572872 | tf_op jit(solution)/shard_map/ppermute | solution.py:476
  39.1 1.6 %copy-start.2 = (f32[1,4,256,512]{3,2,1,0:T(8,128)S(1)}, f32[1,4,256,512]{3,2,1,0:T(8,128)}, u32[]{:S(2)}) copy-start(f32[1,4,256,512]{3,2,1,0:T(8,128)} %param.3) | copy-start | bytes 6291460
  39.1 15.7 %collective-permute-start.13 = (f32[2,4,16,512]{3,2,1,0:T(8,128)S(1)}, f32[2,4,16,512]{3,2,1,0:T(8,128)S(1)}, u32[]{:S(2)}, u32[]{:S(2)}) collective-permute-start(f32[2,4,16,512]{3,2,1,0:T(8,128)S(1)} %get-tuple-element.50.refs_5_), channel_id=1, source_target_pairs={{0,28},{4,8},{8,4},{12,16},{16,12},{20,24},{24,20},{28,0},{1,29},{... | collective-permute-start | bytes 786440 | tf_op jit(solution)/shard_map/ppermute | solution.py:476
  49.8 8.7 %collective-permute-start.12 = (f32[2,2,32,512]{3,2,1,0:T(8,128)S(1)}, f32[2,2,32,512]{3,2,1,0:T(8,128)S(1)}, u32[]{:S(2)}, u32[]{:S(2)}) collective-permute-start(f32[2,2,32,512]{3,2,1,0:T(8,128)S(1)} %get-tuple-element.54), channel_id=1, source_target_pairs={{0,1},{1,0},{2,3},{3,2},{4,5},{5,4},{6,7},{7,6},{8,9},{9,8},{10,11... | collective-permute-start | bytes 786440 | tf_op jit(solution)/shard_map/ppermute | solution.py:419
  51.2 16.2 %collective-permute-start.17 = (f32[4,2,16,512]{3,2,1,0:T(8,128)S(1)}, f32[4,2,16,512]{3,2,1,0:T(8,128)S(1)}, u32[]{:S(2)}, u32[]{:S(2)}) collective-permute-start(f32[4,2,16,512]{3,2,1,0:T(8,128)S(1)} %get-tuple-element.57), channel_id=1, source_target_pairs={{0,28},{4,8},{8,4},{12,16},{16,12},{20,24},{24,20},{28,0},{1,29},{... | collective-permute-start | bytes 786440 | tf_op jit(solution)/shard_map/ppermute | solution.py:488
  54.9 6.4 %collective-permute-start.15 = (f32[2,2,16,512]{3,2,1,0:T(8,128)S(1)}, f32[2,2,16,512]{3,2,1,0:T(8,128)S(1)}, u32[]{:S(2)}, u32[]{:S(2)}) collective-permute-start(f32[2,2,16,512]{3,2,1,0:T(8,128)S(1)} %get-tuple-element.56), channel_id=1, source_target_pairs={{0,1},{1,0},{2,3},{3,2},{4,5},{5,4},{6,7},{7,6},{8,9},{9,8},{10,11... | collective-permute-start | bytes 393224 | tf_op jit(solution)/shard_map/ppermute | solution.py:419
  58.5 6.9 %collective-permute-start.14 = (f32[2,32,512]{2,1,0:T(8,128)S(1)}, f32[2,32,512]{2,1,0:T(8,128)S(1)}, u32[]{:S(2)}, u32[]{:S(2)}) collective-permute-start(f32[2,32,512]{2,1,0:T(8,128)S(1)} %shard_map.51.refs_2_), channel_id=1, source_target_pairs={{0,3},{1,2},{2,1},{3,0},{4,7},{5,6},{6,5},{7,4},{8,11},{9,10},{10,... | collective-permute-start | bytes 393224 | tf_op jit(solution)/shard_map/ppermute | solution.py:411
  61.3 6.1 %collective-permute-start.16 = (f32[2,16,512]{2,1,0:T(8,128)S(1)}, f32[2,16,512]{2,1,0:T(8,128)S(1)}, u32[]{:S(2)}, u32[]{:S(2)}) collective-permute-start(f32[2,16,512]{2,1,0:T(8,128)S(1)} %shard_map.52.refs_3_), channel_id=1, source_target_pairs={{0,3},{1,2},{2,1},{3,0},{4,7},{5,6},{6,5},{7,4},{8,11},{9,10},{10,... | collective-permute-start | bytes 196616 | tf_op jit(solution)/shard_map/ppermute | solution.py:411

commit v13 on v9

--- a/solution.py
+++ b/solution.py
@@ -148,20 +148,25 @@
     return [0, *range(bands - 1, 0, -1)]
 
 
-def back_kernel(chunk, part, row, halo, h, *outs):
+def back_kernel(chunk, part, row, halo, h, keep, send):
     odd = parity()
     lo, hi = part
     in_halo = slice(lo - chunk[0], hi - chunk[0])
     two = row[0:1, :]
     me = lax.axis_index("orb")
     bands = halo.shape[1]
-    for d, out in zip(offsets(bands), outs):
-        band = me ^ d
+
+    def put(band, out, slot):
         d0, d1 = halo_terms(halo, band, odd, in_halo)
         v2 = h[0, band, lo:hi, :] + two * (NEAR * d1 + FAR * d0)
         v3 = h[1, band, lo:hi, :] + two * (FAR * d1)
-        out[0] = square(v2, bands)
-        out[1] = square(v3, bands)
+        out[slot, 0] = square(v2, bands)
+        out[slot, 1] = square(v3, bands)
+
+    put(me ^ 1, send, 0)
+    put(me ^ 2, send, 1)
+    put(me, keep, 0)
+    put(me ^ 3, keep, 1)
 
 
 def tail_rows(ref, plane, band, start, more):
@@ -323,13 +328,6 @@
     out[...] = keep[0] + came[0] + far[...]
 
 
-def sum_all_kernel(*refs):
-    total = refs[0][...]
-    for ref in refs[1:-1]:
-        total = total + ref[...]
-    refs[-1][...] = total
-
-
 def join_kernel(places, part, *refs):
     row, halo, h, out = refs[-4:]
     odd = parity()
@@ -422,16 +420,14 @@
     def over_orb(x, d):
         return lax.ppermute(x, "orb", [(i, i ^ d) for i in range(bands)])
 
-    def back_squares(chunk, rows, halo):
-        keep, *sends = call(
+    def back_squares(chunk, rows, halo, weight=0):
+        keep, send = call(
             functools.partial(back_kernel, chunk, rows),
-            [pair_shape(rows)[1:]] * bands,
+            [pair_shape(rows)] * 2,
             (row, halo, as_bands(h_back)),
+            weight=weight,
         )
-        return keep, *[over_orb(x, d) for d, x in zip(offsets(bands)[1:], sends)]
-
-    def sum_all(keep, *came, weight=0):
-        return call(sum_all_kernel, keep.shape, (keep, *came), weight=weight)
+        return keep, lax.ppermute(send, "orb", near)
 
     def faces(chunk, halo, parts):
         fs = call(
@@ -471,24 +467,24 @@
     def summed(keep, came, from_far, weight=0):
         return call(sum_kernel, from_far.shape, (keep, came, from_far), weight=weight)
 
-    back0 = back_squares(chunks[0], cut_a, halos[0])
-    f0, face_a = faces(chunks[0], halos[0], [cut_a])
     x, piece = call(
         gather_kernel,
         [(bands, planes, padded, lanes), (2 * (bands - 1) * inner, lanes)],
         x_parts,
     )
+    x_in = lax.ppermute(x, "slab", partner)
     x_halo = lax.ppermute(piece, "slab", face)
-    x_in = lax.ppermute(x, "slab", partner)
-    back1 = back_squares(chunks[1], cut_b, halos[1])
+    back0 = back_squares(chunks[0], cut_a, halos[0])
+    f0, face_a = faces(chunks[0], halos[0], [cut_a])
     f1, face_b = faces(chunks[1], halos[1], [cut_b, cut_c])
+    back1 = back_squares(chunks[1], cut_b, halos[1], weight=8_000_000_000)
     x_first, x_t, x_back = call(
         functools.partial(rows_kernel, cut_c),
         [(bands, 2, inner, lanes)] + [(bands, 2, part, lanes)] * 2,
         (coeffs, x, x_in, as_bands(potential), as_bands(pot_in)),
         scalars=1,
     )
-    back0 = sum_all(*back0, weight=0)
+    back0 = add_far(*back0)
     h_front = call(
         functools.partial(front_kernel, cuts),
         plane2,
@@ -496,17 +492,17 @@
         scalars=1,
         scratch=[pltpu.VMEM(plane2, jnp.float32)],
         flops=40 * cells,
-        weight=6_000_000_000,
-    )
-    back1 = sum_all(*back1, weight=0)
+    )
+    back1 = add_far(*back1)
     front_a = squares(cut_a, face_a)
+    back0 = summed(*back0)
+    back1 = summed(*back1)
     x_f, piece = call(
         functools.partial(rows_face_kernel, cut_c),
         [(bands, 2, inner, lanes), (bands, 2, part, lanes)],
         (x_halo, *halos, x_first),
     )
     x_face = lax.ppermute(piece, "slab", face)
-    front_a = add_far(*front_a)
     back2, x_front = call(
         functools.partial(rows_front_kernel, cut_c),
         [(2, part, lanes), (bands, 2, part, lanes)],
@@ -514,8 +510,9 @@
         scalars=1,
     )
     front_b = squares(cut_b, face_b)
+    front_a = add_far(*front_a)
+    front_b = add_far(*front_b)
     front_a = summed(*front_a)
-    front_b = add_far(*front_b)
     front_b = summed(*front_b)
     places = [(2, cut) for cut in cuts] + [(0, cut_a), (0, cut_b)]
     return call(

time: 79.4 us -> 70.7 us (0.89)
  waiting for transfers between devices: 29.5 us -> 21.2 us
  starting transfers between devices: 29.3 us -> 28.5 us
    ppermute x2, waiting for transfers between devices: 8.65 us -> 0.01 us  [shards(): halos.append(lax.ppermute(piece, 'slab', face))]
    ppermute x9 -> x3, starting transfers between devices: 13.3 us -> 4.88 us  [over_orb(): return lax.ppermute(x, 'orb', [(i, i ^ d) for i in range(bands)])]
    ppermute x2 -> x4, waiting for transfers between devices: 6.55 us -> 11.9 us  [add_far(): return (keep, came, lax.ppermute(total, 'orb', far))]
    ppermute x1, waiting for transfers between devices: 3.85 us -> 0.01 us  [shards(): x_halo = lax.ppermute(piece, 'slab', face)]
    ppermute x2, starting transfers between devices: 2.3 us -> 5.78 us  [faces(): return (fs, lax.ppermute(fs[0], 'slab', face))]
    ppermute x2 -> x4, starting transfers between devices: 5.08 us -> 7.98 us  [add_far(): return (keep, came, lax.ppermute(total, 'orb', far))]
    ppermute x2, waiting for transfers between devices: 2.69 us -> 0.01 us  [faces(): return (fs, lax.ppermute(fs[0], 'slab', face))]
    ppermute x0 -> x2, starting transfers between devices: none -> 1.86 us  [back_squares(): return (keep, lax.ppermute(send, 'orb', near))]
  transfers between devices with their start and end apart: 22 -> 20, of which waited for: 9 -> 5; matrix products, arithmetic and copies ran while one was open for 0% -> 0% of each run, Pallas kernels for 22% -> 25%
where the time goes in v13:
time: 70.7 us; the launch traced here: 70.2 us
  starting transfers between devices  28.5 us (40%)
  waiting for transfers between devices  21.2 us (30%)
  Pallas kernels  18.6 us (26%)
  local copies, waits for them, and re-layouts  1.6 us (2%)
    pallas_call x25, Pallas kernels, __call__(): pl.pallas_call(body, out_shape=shapes, in_specs=[smem] * scalars + [pl.Bl...  18.6 us
    ppermute x4, waiting for transfers between devices, add_far(): return (keep, came, lax.ppermute(total, 'orb', far))  11.9 us
    ppermute x4, starting transfers between devices, add_far(): return (keep, came, lax.ppermute(total, 'orb', far))  7.98 us
    ppermute x3, waiting for transfers between devices, over_orb(): return lax.ppermute(x, 'orb', [(i, i ^ d) for i in range(bands)])  5.78 us
    ppermute x2, starting transfers between devices, faces(): return (fs, lax.ppermute(fs[0], 'slab', face))  5.78 us
    ppermute x3, starting transfers between devices, over_orb(): return lax.ppermute(x, 'orb', [(i, i ^ d) for i in range(bands)])  4.88 us
    ppermute x2, starting transfers between devices, shards(): halos.append(lax.ppermute(piece, 'slab', face))  3.66 us
    ppermute x2, waiting for transfers between devices, squares(): return (keep, lax.ppermute(send, 'orb', near))  3.51 us
  transfers between devices with their start and end apart: 20, of which 5 were waited for; matrix products, arithmetic and copies ran while one was open for 0% of the time, Pallas kernels for 25%

profile of v13, /device:TPU:0, one launch (start us, length us, event | category | flops | bytes accessed | tf_op | source)
XLA Modules:
  0.0 70.2 jit_solution(422312469958352700)
XLA Ops:
  0.0 0.5 collective-permute-start
  0.5 0.1 collective-permute-start.1
  0.5 1.6 %copy-done = f32[1,4,256,512]{3,2,1,0:T(8,128)S(1)} copy-done((f32[1,4,256,512]{3,2,1,0:T(8,128)S(1)}, f32[1,4,256,512]{3,2,1,0:T(8,128)}, u32[]{:S(2)}) %copy-start) | copy-done | bytes 2097176
  2.2 3.6 %collective-permute-start.2 = (f32[2,4,32,512]{3,2,1,0:T(8,128)S(1)}, f32[2,4,32,512]{3,2,1,0:T(8,128)S(1)}, u32[]{:S(2)}, u32[]{:S(2)}) collective-permute-start(f32[2,4,32,512]{3,2,1,0:T(8,128)S(1)} %shard_map.37.refs_1_), channel_id=1, source_target_pairs={{0,28},{4,8},{8,4},{12,16},{16,12},{20,24},{24,20},{28,0},{1,29},{... | collective-permute-start | bytes 1572872 | tf_op jit(solution)/shard_map/ppermute | solution.py:451
  5.8 0.0 copy-start.2
  5.8 0.1 collective-permute-start.8
  5.9 0.1 shard_map.39
  6.0 4.2 %collective-permute-start.3 = (f32[4,24,512]{2,1,0:T(8,128)S(1)}, f32[4,24,512]{2,1,0:T(8,128)S(1)}, u32[]{:S(2)}, u32[]{:S(2)}) collective-permute-start(f32[4,24,512]{2,1,0:T(8,128)S(1)} %get-tuple-element.34), channel_id=1, source_target_pairs={{0,3},{1,2},{2,1},{3,0},{4,7},{5,6},{6,5},{7,4},{8,11},{9,10},{10,... | collective-permute-start | bytes 589832 | tf_op jit(solution)/shard_map/ppermute | solution.py:421
  10.2 0.6 collective-permute-start.5
  10.9 2.5 %shard_map.40.refs_5_.refs_6_ = f32[2,256,512]{2,1,0:T(8,128)S(1)} custom-call(f32[4,256,512]{2,1,0:T(8,128)S(1)} %bitcast.11, f32[4,256,512]{2,1,0:T(8,128)S(1)} %copy-done.2, f32[4,24,512]{2,1,0:T(8,128)S(1)} %get-tuple-element.31.refs_2_.refs_0_), custom_call_target="tpu_custom_call" | custom-call | flops 6291456 | bytes 5242880 | tf_op jit(solution)/shard_map/pallas_call | solution.py:364
  13.4 7.0 %shard_map.41 = (f32[2,256,512]{2,1,0:T(8,128)S(1)}, f32[2,256,512]{2,1,0:T(8,128)S(1)}, f32[8,512]{1,0:T(8,128)S(1)}) custom-call(f32[3]{0:T(128)S(1)} %copy-done.3, f32[4,256,512]{2,1,0:T(8,128)S(1)} %bitcast.12, f32[4,256,512]{2,1,0:T(8,128)S(1)} %copy-done.2, f32[4,256,512]{2,1,0:T(8,128)S(1)} %collective-permute-done.refs_3_, ...), custom_call_target="tpu_custom_call" | custom-call | flops 20971520 | bytes 11550732 | tf_op jit(solution)/shard_map/pallas_call | solution.py:364
  20.4 5.8 %collective-permute-done.4.refs_2_ = f32[4,24,512]{2,1,0:T(8,128)S(1)} collective-permute-done((f32[4,24,512]{2,1,0:T(8,128)S(1)}, f32[4,24,512]{2,1,0:T(8,128)S(1)}, u32[]{:S(2)}, u32[]{:S(2)}) %collective-permute-start.4) | collective-permute-done | bytes 196640 | tf_op jit(solution)/shard_map/ppermute | solution.py:421
  26.2 0.1 shard_map.42
  26.2 0.1 collective-permute-start.7
  26.3 0.0 collective-permute-done.2.refs_1_.refs_0_.refs_4_
  26.3 0.2 shard_map.43
  26.5 0.1 collective-permute-start.6
  26.6 0.1 shard_map.44.refs_2_.refs_4_
  26.7 3.5 %collective-permute-start.10 = (f32[2,4,32,512]{3,2,1,0:T(8,128)S(1)}, f32[2,4,32,512]{3,2,1,0:T(8,128)S(1)}, u32[]{:S(2)}, u32[]{:S(2)}) collective-permute-start(f32[2,4,32,512]{3,2,1,0:T(8,128)S(1)} %shard_map.44.refs_2_.refs_4_), channel_id=1, source_target_pairs={{0,28},{4,8},{8,4},{12,16},{16,12},{20,24},{24,20},{28,0},{1,29},{... | collective-permute-start | bytes 1572872 | tf_op jit(solution)/shard_map/ppermute | solution.py:438
  30.2 0.0 collective-permute-done.8.refs_0_.refs_1_.refs_2_.refs_5_
  30.2 0.1 shard_map.45
  30.2 0.1 shard_map.46
  30.3 1.8 %collective-permute-start.11 = (f32[2,2,16,512]{3,2,1,0:T(8,128)S(1)}, f32[2,2,16,512]{3,2,1,0:T(8,128)S(1)}, u32[]{:S(2)}, u32[]{:S(2)}) collective-permute-start(f32[2,2,16,512]{3,2,1,0:T(8,128)S(1)} %get-tuple-element.45), channel_id=1, source_target_pairs={{0,1},{1,0},{2,3},{3,2},{4,5},{5,4},{6,7},{7,6},{8,9},{9,8},{10,11... | collective-permute-start | bytes 393224 | tf_op jit(solution)/shard_map/ppermute | solution.py:430
  32.1 0.4 collective-permute-start.13
  32.5 0.0 collective-permute-done.7.refs_2_
  32.5 2.3 %collective-permute-start.15 = (f32[2,4,16,512]{3,2,1,0:T(8,128)S(1)}, f32[2,4,16,512]{3,2,1,0:T(8,128)S(1)}, u32[]{:S(2)}, u32[]{:S(2)}) collective-permute-start(f32[2,4,16,512]{3,2,1,0:T(8,128)S(1)} %get-tuple-element.41.refs_3_.refs_5_), channel_id=1, source_target_pairs={{0,28},{4,8},{8,4},{12,16},{16,12},{20,24},{24,20},{28,0},{1,29},{... | collective-permute-start | bytes 786440 | tf_op jit(solution)/shard_map/ppermute | solution.py:438
  34.8 2.8 %shard_map.47 = (f32[4,2,20,512]{3,2,1,0:T(8,128)S(1)}, f32[4,2,16,512]{3,2,1,0:T(8,128)S(1)}, f32[4,2,16,512]{3,2,1,0:T(8,128)S(1)}) custom-call(f32[3]{0:T(128)S(1)} %copy-done.3, f32[4,4,24,512]{3,2,1,0:T(8,128)S(1)} %get-tuple-element.38.refs_3_.refs_1_, f32[4,4,24,512]{3,2,1,0:T(8,128)S(1)} %collective-permute-done.7.refs_2_, ...), custom_call_target="tpu_custom_call" | custom-call | bytes 6619148 | tf_op jit(solution)/shard_map/pallas_call | solution.py:364
  37.6 0.0 collective-permute-done.6.refs_1_
  37.6 2.5 %collective-permute-start.9 = (f32[2,32,512]{2,1,0:T(8,128)S(1)}, f32[2,32,512]{2,1,0:T(8,128)S(1)}, u32[]{:S(2)}, u32[]{:S(2)}) collective-permute-start(f32[2,32,512]{2,1,0:T(8,128)S(1)} %shard_map.48.refs_7_), channel_id=1, source_target_pairs={{0,3},{1,2},{2,1},{3,0},{4,7},{5,6},{6,5},{7,4},{8,11},{9,10},{10,... | collective-permute-start | bytes 393224 | tf_op jit(solution)/shard_map/ppermute | solution.py:410
  40.2 3.2 %shard_map.49.refs_2_ = f32[2,256,512]{2,1,0:T(8,128)S(1)} custom-call(f32[3]{0:T(128)S(1)} %copy-done.3, f32[4,256,512]{2,1,0:T(8,128)S(1)} %bitcast.13, f32[4,256,512]{2,1,0:T(8,128)S(1)} %copy-done.2, f32[2,256,512]{2,1,0:T(8,128)S(1)} %get-tuple-element.37.refs_4_.refs_3_, f32[2,4,32,512]{3,2,1,0:T(8,128)S(1)} %shard_map.44.refs_2_.refs_4_, ...), custom_call_target="tpu_custom_call" | custom-call | flops 10485760 | bytes 7340044 | tf_op jit(solution)/shard_map/pallas_call | solution.py:364
  43.3 0.0 collective-permute-done.11.refs_1_
  43.4 0.0 collective-permute-done.10.refs_1_
  43.4 0.1 shard_map.51
  43.5 0.9 %collective-permute-start.14 = (f32[2,2,32,512]{3,2,1,0:T(8,128)S(1)}, f32[2,2,32,512]{3,2,1,0:T(8,128)S(1)}, u32[]{:S(2)}, u32[]{:S(2)}) collective-permute-start(f32[2,2,32,512]{3,2,1,0:T(8,128)S(1)} %get-tuple-element.52), channel_id=1, source_target_pairs={{0,1},{1,0},{2,3},{3,2},{4,5},{5,4},{6,7},{7,6},{8,9},{9,8},{10,11... | collective-permute-start | bytes 786440 | tf_op jit(solution)/shard_map/ppermute | solution.py:418
  44.4 2.5 %collective-permute-start.12 = (f32[2,16,512]{2,1,0:T(8,128)S(1)}, f32[2,16,512]{2,1,0:T(8,128)S(1)}, u32[]{:S(2)}, u32[]{:S(2)}) collective-permute-start(f32[2,16,512]{2,1,0:T(8,128)S(1)} %shard_map.50.refs_3_), channel_id=1, source_target_pairs={{0,3},{1,2},{2,1},{3,0},{4,7},{5,6},{6,5},{7,4},{8,11},{9,10},{10,... | collective-permute-start | bytes 196616 | tf_op jit(solution)/shard_map/ppermute | solution.py:410
  46.9 7.3 %collective-permute-done.12.refs_2_ = f32[2,16,512]{2,1,0:T(8,128)S(1)} collective-permute-done((f32[2,16,512]{2,1,0:T(8,128)S(1)}, f32[2,16,512]{2,1,0:T(8,128)S(1)}, u32[]{:S(2)}, u32[]{:S(2)}) %collective-permute-start.12) | collective-permute-done | bytes 65568 | tf_op jit(solution)/shard_map/ppermute | solution.py:410
  54.3 0.1 shard_map.54
  54.4 2.4 %collective-permute-start.19 = (f32[4,2,16,512]{3,2,1,0:T(8,128)S(1)}, f32[4,2,16,512]{3,2,1,0:T(8,128)S(1)}, u32[]{:S(2)}, u32[]{:S(2)}) collective-permute-start(f32[4,2,16,512]{3,2,1,0:T(8,128)S(1)} %get-tuple-element.55), channel_id=1, source_target_pairs={{0,28},{4,8},{8,4},{12,16},{16,12},{20,24},{24,20},{28,0},{1,29},{... | collective-permute-start | bytes 786440 | tf_op jit(solution)/shard_map/ppermute | solution.py:505
  56.8 1.2 %shard_map.55 = (f32[2,16,512]{2,1,0:T(8,128)S(1)}, f32[4,2,16,512]{3,2,1,0:T(8,128)S(1)}) custom-call(f32[3]{0:T(128)S(1)} %copy-done.3, f32[4,4,24,512]{3,2,1,0:T(8,128)S(1)} %get-tuple-element.38.refs_3_.refs_1_, f32[4,4,64,512]{3,2,1,0:T(8,128)S(1)} %bitcast.15, f32[120,512]{1,0:T(8,128)S(1)} %collective-permute-done.13.refs_0_.refs_3_, ...), custom_call_target="tpu_custom_call" | custom-call | bytes 5357580 | tf_op jit(solution)/shard_map/pallas_call | solution.py:364
  58.0 0.1 shard_map.56
  58.1 0.1 collective-permute-start.17
  58.2 0.0 collective-permute-done.14.refs_1_
  58.2 1.4 %collective-permute-start.16 = (f32[2,32,512]{2,1,0:T(8,128)S(1)}, f32[2,32,512]{2,1,0:T(8,128)S(1)}, u32[]{:S(2)}, u32[]{:S(2)}) collective-permute-start(f32[2,32,512]{2,1,0:T(8,128)S(1)} %shard_map.57.refs_2_), channel_id=1, source_target_pairs={{0,3},{1,2},{2,1},{3,0},{4,7},{5,6},{6,5},{7,4},{8,11},{9,10},{10,... | collective-permute-start | bytes 393224 | tf_op jit(solution)/shard_map/ppermute | solution.py:410
  59.6 3.5 %collective-permute-done.17.refs_1_ = f32[2,2,16,512]{3,2,1,0:T(8,128)S(1)} collective-permute-done((f32[2,2,16,512]{3,2,1,0:T(8,128)S(1)}, f32[2,2,16,512]{3,2,1,0:T(8,128)S(1)}, u32[]{:S(2)}, u32[]{:S(2)}) %collective-permute-start.17) | collective-permute-done | bytes 131104 | tf_op jit(solution)/shard_map/ppermute | solution.py:418
  63.2 1.5 %collective-permute-start.18 = (f32[2,16,512]{2,1,0:T(8,128)S(1)}, f32[2,16,512]{2,1,0:T(8,128)S(1)}, u32[]{:S(2)}, u32[]{:S(2)}) collective-permute-start(f32[2,16,512]{2,1,0:T(8,128)S(1)} %shard_map.58.refs_3_), channel_id=1, source_target_pairs={{0,3},{1,2},{2,1},{3,0},{4,7},{5,6},{6,5},{7,4},{8,11},{9,10},{10,... | collective-permute-start | bytes 196616 | tf_op jit(solution)/shard_map/ppermute | solution.py:410
  64.7 1.2 %collective-permute-done.16.refs_2_ = f32[2,32,512]{2,1,0:T(8,128)S(1)} collective-permute-done((f32[2,32,512]{2,1,0:T(8,128)S(1)}, f32[2,32,512]{2,1,0:T(8,128)S(1)}, u32[]{:S(2)}, u32[]{:S(2)}) %collective-permute-start.16) | collective-permute-done | bytes 131104 | tf_op jit(solution)/shard_map/ppermute | solution.py:410
  65.9 3.4 %collective-permute-done.18.refs_2_ = f32[2,16,512]{2,1,0:T(8,128)S(1)} collective-permute-done((f32[2,16,512]{2,1,0:T(8,128)S(1)}, f32[2,16,512]{2,1,0:T(8,128)S(1)}, u32[]{:S(2)}, u32[]{:S(2)}) %collective-permute-start.18) | collective-permute-done | bytes 65568 | tf_op jit(solution)/shard_map/ppermute | solution.py:410
  69.3 0.9 %shard_map.61 = f32[4,64,512]{2,1,0:T(8,128)} custom-call(f32[2,32,512]{2,1,0:T(8,128)S(1)} %shard_map.52.refs_3_.refs_0_, f32[2,16,512]{2,1,0:T(8,128)S(1)} %shard_map.53.refs_4_.refs_1_, f32[2,16,512]{2,1,0:T(8,128)S(1)} %get-tuple-element.51.refs_3_.refs_2_, f32[2,32,512]{2,1,0:T(8,128)S(1)} %shard_map.59.refs_3_, ...), custom_call_target="tpu_custom_call" | custom-call | bytes 1523712 | tf_op jit(solution)/shard_map/pallas_call | solution.py:364
  (25 shorter events, 0.3 us)
Async XLA Ops:
  0.0 10.2 %collective-permute-start = (f32[4,256,512]{2,1,0:T(8,128)}, f32[4,256,512]{2,1,0:T(8,128)S(1)}, u32[]{:S(2)}, u32[]{:S(2)}) collective-permute-start(f32[4,256,512]{2,1,0:T(8,128)} %bitcast.7), channel_id=1, source_target_pairs={{0,4},{4,0},{8,12},{12,8},{16,20},{20,16},{24,28},{28,24},{1,5},{5... | collective-permute-start | bytes 6291464 | tf_op jit(solution)/shard_map/ppermute | solution.py:440
  0.5 9.8 %collective-permute-start.1 = (f32[4,256,512]{2,1,0:T(8,128)}, f32[4,256,512]{2,1,0:T(8,128)S(1)}, u32[]{:S(2)}, u32[]{:S(2)}) collective-permute-start(f32[4,256,512]{2,1,0:T(8,128)} %refs_2_.3), channel_id=1, source_target_pairs={{0,4},{4,0},{8,12},{12,8},{16,20},{20,16},{24,28},{28,24},{1,5},{5... | collective-permute-start | bytes 6291464 | tf_op jit(solution)/shard_map/ppermute | solution.py:441
  0.5 1.6 %copy-start = (f32[1,4,256,512]{3,2,1,0:T(8,128)S(1)}, f32[1,4,256,512]{3,2,1,0:T(8,128)}, u32[]{:S(2)}) copy-start(f32[1,4,256,512]{3,2,1,0:T(8,128)} %param.3) | copy-start | bytes 6291460
  2.2 24.2 %collective-permute-start.2 = (f32[2,4,32,512]{3,2,1,0:T(8,128)S(1)}, f32[2,4,32,512]{3,2,1,0:T(8,128)S(1)}, u32[]{:S(2)}, u32[]{:S(2)}) collective-permute-start(f32[2,4,32,512]{3,2,1,0:T(8,128)S(1)} %shard_map.37.refs_1_), channel_id=1, source_target_pairs={{0,28},{4,8},{8,4},{12,16},{16,12},{20,24},{24,20},{28,0},{1,29},{... | collective-permute-start | bytes 1572872 | tf_op jit(solution)/shard_map/ppermute | solution.py:451
  5.8 5.1 %copy-start.2 = (f32[4,256,512]{2,1,0:T(8,128)S(1)}, f32[4,256,512]{2,1,0:T(8,128)}, u32[]{:S(2)}) copy-start(f32[4,256,512]{2,1,0:T(8,128)} %refs_2_.3) | copy-start | bytes 6291460
  5.8 24.4 %collective-permute-start.8 = (f32[2,4,32,512]{3,2,1,0:T(8,128)S(1)}, f32[2,4,32,512]{3,2,1,0:T(8,128)S(1)}, u32[]{:S(2)}, u32[]{:S(2)}) collective-permute-start(f32[2,4,32,512]{3,2,1,0:T(8,128)S(1)} %shard_map.38.refs_1_), channel_id=1, source_target_pairs={{0,28},{4,8},{8,4},{12,16},{16,12},{20,24},{24,20},{28,0},{1,29},{... | collective-permute-start | bytes 1572872 | tf_op jit(solution)/shard_map/ppermute | solution.py:451
  6.0 14.4 %collective-permute-start.3 = (f32[4,24,512]{2,1,0:T(8,128)S(1)}, f32[4,24,512]{2,1,0:T(8,128)S(1)}, u32[]{:S(2)}, u32[]{:S(2)}) collective-permute-start(f32[4,24,512]{2,1,0:T(8,128)S(1)} %get-tuple-element.34), channel_id=1, source_target_pairs={{0,3},{1,2},{2,1},{3,0},{4,7},{5,6},{6,5},{7,4},{8,11},{9,10},{10,... | collective-permute-start | bytes 589832 | tf_op jit(solution)/shard_map/ppermute | solution.py:421
  10.2 16.0 %collective-permute-start.4 = (f32[4,24,512]{2,1,0:T(8,128)S(1)}, f32[4,24,512]{2,1,0:T(8,128)S(1)}, u32[]{:S(2)}, u32[]{:S(2)}) collective-permute-start(f32[4,24,512]{2,1,0:T(8,128)S(1)} %get-tuple-element.35), channel_id=1, source_target_pairs={{0,2},{1,3},{2,0},{3,1},{4,6},{5,7},{6,4},{7,5},{8,10},{9,11},{10,... | collective-permute-start | bytes 589832 | tf_op jit(solution)/shard_map/ppermute | solution.py:421
  10.2 16.0 %collective-permute-start.5 = (f32[4,24,512]{2,1,0:T(8,128)S(1)}, f32[4,24,512]{2,1,0:T(8,128)S(1)}, u32[]{:S(2)}, u32[]{:S(2)}) collective-permute-start(f32[4,24,512]{2,1,0:T(8,128)S(1)} %get-tuple-element.36), channel_id=1, source_target_pairs={{0,1},{1,0},{2,3},{3,2},{4,5},{5,4},{6,7},{7,6},{8,9},{9,8},{10,11... | collective-permute-start | bytes 589832 | tf_op jit(solution)/shard_map/ppermute | solution.py:421
  10.9 2.5 %copy-start.3 = (f32[3]{0:T(128)S(1)}, f32[3]{0:T(128)}, u32[]{:S(2)}) copy-start(f32[3]{0:T(128)} %refs_0_.7) | copy-start | bytes 40
  26.2 6.3 %collective-permute-start.7 = (f32[4,4,24,512]{3,2,1,0:T(8,128)S(1)}, f32[4,4,24,512]{3,2,1,0:T(8,128)S(1)}, u32[]{:S(2)}, u32[]{:S(2)}) collective-permute-start(f32[4,4,24,512]{3,2,1,0:T(8,128)S(1)} %get-tuple-element.38.refs_3_.refs_1_), channel_id=1, source_target_pairs={{0,4},{4,0},{8,12},{12,8},{16,20},{20,16},{24,28},{28,24},{1,5},{5... | collective-permute-start | bytes 2359304 | tf_op jit(solution)/shard_map/ppermute | solution.py:475
  26.5 11.1 %collective-permute-start.6 = (f32[2,2,32,512]{3,2,1,0:T(8,128)S(1)}, f32[2,2,32,512]{3,2,1,0:T(8,128)S(1)}, u32[]{:S(2)}, u32[]{:S(2)}) collective-permute-start(f32[2,2,32,512]{3,2,1,0:T(8,128)S(1)} %get-tuple-element.40), channel_id=1, source_target_pairs={{0,1},{1,0},{2,3},{3,2},{4,5},{5,4},{6,7},{7,6},{8,9},{9,8},{10,11... | collective-permute-start | bytes 786440 | tf_op jit(solution)/shard_map/ppermute | solution.py:430
  26.7 16.7 %collective-permute-start.10 = (f32[2,4,32,512]{3,2,1,0:T(8,128)S(1)}, f32[2,4,32,512]{3,2,1,0:T(8,128)S(1)}, u32[]{:S(2)}, u32[]{:S(2)}) collective-permute-start(f32[2,4,32,512]{3,2,1,0:T(8,128)S(1)} %shard_map.44.refs_2_.refs_4_), channel_id=1, source_target_pairs={{0,28},{4,8},{8,4},{12,16},{16,12},{20,24},{24,20},{28,0},{1,29},{... | collective-permute-start | bytes 1572872 | tf_op jit(solution)/shard_map/ppermute | solution.py:438
  30.3 13.0 %collective-permute-start.11 = (f32[2,2,16,512]{3,2,1,0:T(8,128)S(1)}, f32[2,2,16,512]{3,2,1,0:T(8,128)S(1)}, u32[]{:S(2)}, u32[]{:S(2)}) collective-permute-start(f32[2,2,16,512]{3,2,1,0:T(8,128)S(1)} %get-tuple-element.45), channel_id=1, source_target_pairs={{0,1},{1,0},{2,3},{3,2},{4,5},{5,4},{6,7},{7,6},{8,9},{9,8},{10,11... | collective-permute-start | bytes 393224 | tf_op jit(solution)/shard_map/ppermute | solution.py:430
  32.1 22.2 %collective-permute-start.13 = (f32[120,512]{1,0:T(8,128)S(1)}, f32[120,512]{1,0:T(8,128)S(1)}, u32[]{:S(2)}, u32[]{:S(2)}) collective-permute-start(f32[120,512]{1,0:T(8,128)S(1)} %get-tuple-element.47), channel_id=1, source_target_pairs={{0,28},{4,8},{8,4},{12,16},{16,12},{20,24},{24,20},{28,0},{1,29},{... | collective-permute-start | bytes 737288 | tf_op jit(solution)/shard_map/ppermute | solution.py:476
  32.5 25.5 %collective-permute-start.15 = (f32[2,4,16,512]{3,2,1,0:T(8,128)S(1)}, f32[2,4,16,512]{3,2,1,0:T(8,128)S(1)}, u32[]{:S(2)}, u32[]{:S(2)}) collective-permute-start(f32[2,4,16,512]{3,2,1,0:T(8,128)S(1)} %get-tuple-element.41.refs_3_.refs_5_), channel_id=1, source_target_pairs={{0,28},{4,8},{8,4},{12,16},{16,12},{20,24},{24,20},{28,0},{1,29},{... | collective-permute-start | bytes 786440 | tf_op jit(solution)/shard_map/ppermute | solution.py:438
  34.8 5.4 %copy-start.1 = (f32[1,4,256,512]{3,2,1,0:T(8,128)S(1)}, f32[1,4,256,512]{3,2,1,0:T(8,128)}, u32[]{:S(2)}) copy-start(f32[1,4,256,512]{3,2,1,0:T(8,128)} %param.3) | copy-start | bytes 6291460
  37.6 9.3 %collective-permute-start.9 = (f32[2,32,512]{2,1,0:T(8,128)S(1)}, f32[2,32,512]{2,1,0:T(8,128)S(1)}, u32[]{:S(2)}, u32[]{:S(2)}) collective-permute-start(f32[2,32,512]{2,1,0:T(8,128)S(1)} %shard_map.48.refs_7_), channel_id=1, source_target_pairs={{0,3},{1,2},{2,1},{3,0},{4,7},{5,6},{6,5},{7,4},{8,11},{9,10},{10,... | collective-permute-start | bytes 393224 | tf_op jit(solution)/shard_map/ppermute | solution.py:410
  43.5 14.7 %collective-permute-start.14 = (f32[2,2,32,512]{3,2,1,0:T(8,128)S(1)}, f32[2,2,32,512]{3,2,1,0:T(8,128)S(1)}, u32[]{:S(2)}, u32[]{:S(2)}) collective-permute-start(f32[2,2,32,512]{3,2,1,0:T(8,128)S(1)} %get-tuple-element.52), channel_id=1, source_target_pairs={{0,1},{1,0},{2,3},{3,2},{4,5},{5,4},{6,7},{7,6},{8,9},{9,8},{10,11... | collective-permute-start | bytes 786440 | tf_op jit(solution)/shard_map/ppermute | solution.py:418
  44.4 9.8 %collective-permute-start.12 = (f32[2,16,512]{2,1,0:T(8,128)S(1)}, f32[2,16,512]{2,1,0:T(8,128)S(1)}, u32[]{:S(2)}, u32[]{:S(2)}) collective-permute-start(f32[2,16,512]{2,1,0:T(8,128)S(1)} %shard_map.50.refs_3_), channel_id=1, source_target_pairs={{0,3},{1,2},{2,1},{3,0},{4,7},{5,6},{6,5},{7,4},{8,11},{9,10},{10,... | collective-permute-start | bytes 196616 | tf_op jit(solution)/shard_map/ppermute | solution.py:410
  54.4 14.9 %collective-permute-start.19 = (f32[4,2,16,512]{3,2,1,0:T(8,128)S(1)}, f32[4,2,16,512]{3,2,1,0:T(8,128)S(1)}, u32[]{:S(2)}, u32[]{:S(2)}) collective-permute-start(f32[4,2,16,512]{3,2,1,0:T(8,128)S(1)} %get-tuple-element.55), channel_id=1, source_target_pairs={{0,28},{4,8},{8,4},{12,16},{16,12},{20,24},{24,20},{28,0},{1,29},{... | collective-permute-start | bytes 786440 | tf_op jit(solution)/shard_map/ppermute | solution.py:505
  58.1 5.0 %collective-permute-start.17 = (f32[2,2,16,512]{3,2,1,0:T(8,128)S(1)}, f32[2,2,16,512]{3,2,1,0:T(8,128)S(1)}, u32[]{:S(2)}, u32[]{:S(2)}) collective-permute-start(f32[2,2,16,512]{3,2,1,0:T(8,128)S(1)} %get-tuple-element.54), channel_id=1, source_target_pairs={{0,1},{1,0},{2,3},{3,2},{4,5},{5,4},{6,7},{7,6},{8,9},{9,8},{10,11... | collective-permute-start | bytes 393224 | tf_op jit(solution)/shard_map/ppermute | solution.py:418
  58.2 7.6 %collective-permute-start.16 = (f32[2,32,512]{2,1,0:T(8,128)S(1)}, f32[2,32,512]{2,1,0:T(8,128)S(1)}, u32[]{:S(2)}, u32[]{:S(2)}) collective-permute-start(f32[2,32,512]{2,1,0:T(8,128)S(1)} %shard_map.57.refs_2_), channel_id=1, source_target_pairs={{0,3},{1,2},{2,1},{3,0},{4,7},{5,6},{6,5},{7,4},{8,11},{9,10},{10,... | collective-permute-start | bytes 393224 | tf_op jit(solution)/shard_map/ppermute | solution.py:410
  63.2 6.1 %collective-permute-start.18 = (f32[2,16,512]{2,1,0:T(8,128)S(1)}, f32[2,16,512]{2,1,0:T(8,128)S(1)}, u32[]{:S(2)}, u32[]{:S(2)}) collective-permute-start(f32[2,16,512]{2,1,0:T(8,128)S(1)} %shard_map.58.refs_3_), channel_id=1, source_target_pairs={{0,3},{1,2},{2,1},{3,0},{4,7},{5,6},{6,5},{7,4},{8,11},{9,10},{10,... | collective-permute-start | bytes 196616 | tf_op jit(solution)/shard_map/ppermute | solution.py:410

commit v14 on v13

--- a/solution.py
+++ b/solution.py
@@ -478,12 +478,6 @@
     f0, face_a = faces(chunks[0], halos[0], [cut_a])
     f1, face_b = faces(chunks[1], halos[1], [cut_b, cut_c])
     back1 = back_squares(chunks[1], cut_b, halos[1], weight=8_000_000_000)
-    x_first, x_t, x_back = call(
-        functools.partial(rows_kernel, cut_c),
-        [(bands, 2, inner, lanes)] + [(bands, 2, part, lanes)] * 2,
-        (coeffs, x, x_in, as_bands(potential), as_bands(pot_in)),
-        scalars=1,
-    )
     back0 = add_far(*back0)
     h_front = call(
         functools.partial(front_kernel, cuts),
@@ -495,8 +489,16 @@
     )
     back1 = add_far(*back1)
     front_a = squares(cut_a, face_a)
+    x_first, x_t, x_back = call(
+        functools.partial(rows_kernel, cut_c),
+        [(bands, 2, inner, lanes)] + [(bands, 2, part, lanes)] * 2,
+        (coeffs, x, x_in, as_bands(potential), as_bands(pot_in)),
+        scalars=1,
+    )
     back0 = summed(*back0)
-    back1 = summed(*back1)
+    front_b = squares(cut_b, face_b)
+    back1 = summed(*back1, weight=4_000_000_000)
+    front_a = add_far(*front_a)
     x_f, piece = call(
         functools.partial(rows_face_kernel, cut_c),
         [(bands, 2, inner, lanes), (bands, 2, part, lanes)],
@@ -509,11 +511,9 @@
         (coeffs, x, as_bands(potential), x_halo, *halos, x_f, x_t, x_back),
         scalars=1,
     )
-    front_b = squares(cut_b, face_b)
-    front_a = add_far(*front_a)
     front_b = add_far(*front_b)
     front_a = summed(*front_a)
-    front_b = summed(*front_b)
+    front_b = summed(*front_b, weight=2_000_000_000)
     places = [(2, cut) for cut in cuts] + [(0, cut_a), (0, cut_b)]
     return call(
         functools.partial(join_kernel, places, cut_c),

time: 70.7 us -> 67 us (0.948)
  waiting for transfers between devices: 21.2 us -> 18.4 us
    ppermute x4, waiting for transfers between devices: 11.9 us -> 4.69 us  [add_far(): return (keep, came, lax.ppermute(total, 'orb', far))]
    ppermute x2, waiting for transfers between devices: 0.01 us -> 2.86 us  [back_squares(): return (keep, lax.ppermute(send, 'orb', near))]
    ppermute x1, starting transfers between devices: 0.36 us -> 2.74 us  [shards(): x_halo = lax.ppermute(piece, 'slab', face)]
    ppermute x1, starting transfers between devices: 2.44 us -> 0.07 us  [shards(): x_face = lax.ppermute(piece, 'slab', face)]
    ppermute x2, starting transfers between devices: 5.78 us -> 4.33 us  [faces(): return (fs, lax.ppermute(fs[0], 'slab', face))]
    ppermute x2, starting transfers between devices: 0.99 us -> 2.16 us  [squares(): return (keep, lax.ppermute(send, 'orb', near))]
    ppermute x1, waiting for transfers between devices: 0.01 us -> 0.85 us  [shards(): x_face = lax.ppermute(piece, 'slab', face)]
  transfers between devices with their start and end apart: 20 -> 20, of which waited for: 5 -> 6; matrix products, arithmetic and copies ran while one was open for 0% -> 0% of each run, Pallas kernels for 25% -> 26%
where the time goes in v14:
time: 67 us; the launch traced here: 66.8 us
  starting transfers between devices  28 us (42%)
  Pallas kernels  18.6 us (28%)
  waiting for transfers between devices  18.4 us (27%)
  local copies, waits for them, and re-layouts  1.6 us (2%)
    pallas_call x25, Pallas kernels, __call__(): pl.pallas_call(body, out_shape=shapes, in_specs=[smem] * scalars + [pl.Bl...  18.6 us
    ppermute x4, starting transfers between devices, add_far(): return (keep, came, lax.ppermute(total, 'orb', far))  7.91 us
    ppermute x3, waiting for transfers between devices, over_orb(): return lax.ppermute(x, 'orb', [(i, i ^ d) for i in range(bands)])  5.78 us
    ppermute x3, starting transfers between devices, over_orb(): return lax.ppermute(x, 'orb', [(i, i ^ d) for i in range(bands)])  4.88 us
    ppermute x4, waiting for transfers between devices, add_far(): return (keep, came, lax.ppermute(total, 'orb', far))  4.69 us
    ppermute x2, starting transfers between devices, faces(): return (fs, lax.ppermute(fs[0], 'slab', face))  4.33 us
    ppermute x2, waiting for transfers between devices, squares(): return (keep, lax.ppermute(send, 'orb', near))  4.17 us
    ppermute x2, starting transfers between devices, shards(): halos.append(lax.ppermute(piece, 'slab', face))  3.66 us
  transfers between devices with their start and end apart: 20, of which 6 were waited for; matrix products, arithmetic and copies ran while one was open for 0% of the time, Pallas kernels for 26%

profile of v14, /device:TPU:0, one launch (start us, length us, event | category | flops | bytes accessed | tf_op | source)
XLA Modules:
  0.0 66.8 jit_solution(14834751013774223449)
XLA Ops:
  0.0 0.5 collective-permute-start
  0.5 0.1 collective-permute-start.1
  0.5 1.6 %copy-done = f32[1,4,256,512]{3,2,1,0:T(8,128)S(1)} copy-done((f32[1,4,256,512]{3,2,1,0:T(8,128)S(1)}, f32[1,4,256,512]{3,2,1,0:T(8,128)}, u32[]{:S(2)}) %copy-start) | copy-done | bytes 2097176
  2.2 3.6 %collective-permute-start.2 = (f32[2,4,32,512]{3,2,1,0:T(8,128)S(1)}, f32[2,4,32,512]{3,2,1,0:T(8,128)S(1)}, u32[]{:S(2)}, u32[]{:S(2)}) collective-permute-start(f32[2,4,32,512]{3,2,1,0:T(8,128)S(1)} %shard_map.37.refs_1_), channel_id=1, source_target_pairs={{0,28},{4,8},{8,4},{12,16},{16,12},{20,24},{24,20},{28,0},{1,29},{... | collective-permute-start | bytes 1572872 | tf_op jit(solution)/shard_map/ppermute | solution.py:451
  5.8 0.0 copy-start.2
  5.8 0.1 collective-permute-start.7
  5.9 0.1 shard_map.39
  6.0 4.2 %collective-permute-start.3 = (f32[4,24,512]{2,1,0:T(8,128)S(1)}, f32[4,24,512]{2,1,0:T(8,128)S(1)}, u32[]{:S(2)}, u32[]{:S(2)}) collective-permute-start(f32[4,24,512]{2,1,0:T(8,128)S(1)} %get-tuple-element.34), channel_id=1, source_target_pairs={{0,3},{1,2},{2,1},{3,0},{4,7},{5,6},{6,5},{7,4},{8,11},{9,10},{10,... | collective-permute-start | bytes 589832 | tf_op jit(solution)/shard_map/ppermute | solution.py:421
  10.2 0.0 collective-permute-done.refs_3_
  10.2 0.0 collective-permute-start.4
  10.2 0.6 collective-permute-start.5
  10.9 2.5 %shard_map.40.refs_5_.refs_6_ = f32[2,256,512]{2,1,0:T(8,128)S(1)} custom-call(f32[4,256,512]{2,1,0:T(8,128)S(1)} %bitcast.11, f32[4,256,512]{2,1,0:T(8,128)S(1)} %copy-done.2, f32[4,24,512]{2,1,0:T(8,128)S(1)} %get-tuple-element.31.refs_2_.refs_0_), custom_call_target="tpu_custom_call" | custom-call | flops 6291456 | bytes 5242880 | tf_op jit(solution)/shard_map/pallas_call | solution.py:364
  13.4 7.0 %shard_map.41 = (f32[2,256,512]{2,1,0:T(8,128)S(1)}, f32[2,256,512]{2,1,0:T(8,128)S(1)}, f32[8,512]{1,0:T(8,128)S(1)}) custom-call(f32[3]{0:T(128)S(1)} %copy-done.3, f32[4,256,512]{2,1,0:T(8,128)S(1)} %bitcast.12, f32[4,256,512]{2,1,0:T(8,128)S(1)} %copy-done.2, f32[4,256,512]{2,1,0:T(8,128)S(1)} %collective-permute-done.refs_3_, ...), custom_call_target="tpu_custom_call" | custom-call | flops 20971520 | bytes 11550732 | tf_op jit(solution)/shard_map/pallas_call | solution.py:364
  20.4 0.0 collective-permute-done.3.refs_1_
  20.4 5.8 %collective-permute-done.4.refs_2_ = f32[4,24,512]{2,1,0:T(8,128)S(1)} collective-permute-done((f32[4,24,512]{2,1,0:T(8,128)S(1)}, f32[4,24,512]{2,1,0:T(8,128)S(1)}, u32[]{:S(2)}, u32[]{:S(2)}) %collective-permute-start.4) | collective-permute-done | bytes 196640 | tf_op jit(solution)/shard_map/ppermute | solution.py:421
  26.2 0.0 collective-permute-done.5.refs_3_
  26.2 0.1 shard_map.42
  26.2 0.1 collective-permute-start.9
  26.3 0.0 collective-permute-done.2.refs_1_.refs_0_.refs_4_
  26.3 0.2 shard_map.43
  26.5 0.1 collective-permute-start.6
  26.6 0.1 shard_map.44.refs_2_.refs_4_
  26.7 3.5 %collective-permute-start.10 = (f32[2,4,32,512]{3,2,1,0:T(8,128)S(1)}, f32[2,4,32,512]{3,2,1,0:T(8,128)S(1)}, u32[]{:S(2)}, u32[]{:S(2)}) collective-permute-start(f32[2,4,32,512]{3,2,1,0:T(8,128)S(1)} %shard_map.44.refs_2_.refs_4_), channel_id=1, source_target_pairs={{0,28},{4,8},{8,4},{12,16},{16,12},{20,24},{24,20},{28,0},{1,29},{... | collective-permute-start | bytes 1572872 | tf_op jit(solution)/shard_map/ppermute | solution.py:438
  30.2 0.0 collective-permute-done.7.refs_0_.refs_1_.refs_2_.refs_5_
  30.2 0.1 shard_map.45
  30.2 0.8 %collective-permute-start.13 = (f32[2,4,16,512]{3,2,1,0:T(8,128)S(1)}, f32[2,4,16,512]{3,2,1,0:T(8,128)S(1)}, u32[]{:S(2)}, u32[]{:S(2)}) collective-permute-start(f32[2,4,16,512]{3,2,1,0:T(8,128)S(1)} %get-tuple-element.41.refs_3_.refs_5_), channel_id=1, source_target_pairs={{0,28},{4,8},{8,4},{12,16},{16,12},{20,24},{24,20},{28,0},{1,29},{... | collective-permute-start | bytes 786440 | tf_op jit(solution)/shard_map/ppermute | solution.py:438
  31.1 0.1 shard_map.46
  31.2 1.6 %collective-permute-start.11 = (f32[2,2,16,512]{3,2,1,0:T(8,128)S(1)}, f32[2,2,16,512]{3,2,1,0:T(8,128)S(1)}, u32[]{:S(2)}, u32[]{:S(2)}) collective-permute-start(f32[2,2,16,512]{3,2,1,0:T(8,128)S(1)} %get-tuple-element.44), channel_id=1, source_target_pairs={{0,1},{1,0},{2,3},{3,2},{4,5},{5,4},{6,7},{7,6},{8,9},{9,8},{10,11... | collective-permute-start | bytes 393224 | tf_op jit(solution)/shard_map/ppermute | solution.py:430
  32.8 2.9 %collective-permute-done.6.refs_1_ = f32[2,2,32,512]{3,2,1,0:T(8,128)S(1)} collective-permute-done((f32[2,2,32,512]{3,2,1,0:T(8,128)S(1)}, f32[2,2,32,512]{3,2,1,0:T(8,128)S(1)}, u32[]{:S(2)}, u32[]{:S(2)}) %collective-permute-start.6) | collective-permute-done | bytes 262176 | tf_op jit(solution)/shard_map/ppermute | solution.py:430
  35.7 2.5 %collective-permute-start.8 = (f32[2,32,512]{2,1,0:T(8,128)S(1)}, f32[2,32,512]{2,1,0:T(8,128)S(1)}, u32[]{:S(2)}, u32[]{:S(2)}) collective-permute-start(f32[2,32,512]{2,1,0:T(8,128)S(1)} %shard_map.47.refs_7_), channel_id=1, source_target_pairs={{0,3},{1,2},{2,1},{3,0},{4,7},{5,6},{6,5},{7,4},{8,11},{9,10},{10,... | collective-permute-start | bytes 393224 | tf_op jit(solution)/shard_map/ppermute | solution.py:410
  38.2 3.2 %shard_map.48.refs_2_ = f32[2,256,512]{2,1,0:T(8,128)S(1)} custom-call(f32[3]{0:T(128)S(1)} %copy-done.3, f32[4,256,512]{2,1,0:T(8,128)S(1)} %bitcast.13, f32[4,256,512]{2,1,0:T(8,128)S(1)} %copy-done.2, f32[2,256,512]{2,1,0:T(8,128)S(1)} %get-tuple-element.37.refs_4_.refs_3_, f32[2,4,32,512]{3,2,1,0:T(8,128)S(1)} %shard_map.44.refs_2_.refs_4_, ...), custom_call_target="tpu_custom_call" | custom-call | flops 10485760 | bytes 7340044 | tf_op jit(solution)/shard_map/pallas_call | solution.py:364
  41.4 1.4 %collective-permute-start.12 = (f32[2,16,512]{2,1,0:T(8,128)S(1)}, f32[2,16,512]{2,1,0:T(8,128)S(1)}, u32[]{:S(2)}, u32[]{:S(2)}) collective-permute-start(f32[2,16,512]{2,1,0:T(8,128)S(1)} %shard_map.49.refs_3_), channel_id=1, source_target_pairs={{0,3},{1,2},{2,1},{3,0},{4,7},{5,6},{6,5},{7,4},{8,11},{9,10},{10,... | collective-permute-start | bytes 196616 | tf_op jit(solution)/shard_map/ppermute | solution.py:410
  42.9 2.7 %collective-permute-start.14 = (f32[120,512]{1,0:T(8,128)S(1)}, f32[120,512]{1,0:T(8,128)S(1)}, u32[]{:S(2)}, u32[]{:S(2)}) collective-permute-start(f32[120,512]{1,0:T(8,128)S(1)} %get-tuple-element.48), channel_id=1, source_target_pairs={{0,28},{4,8},{8,4},{12,16},{16,12},{20,24},{24,20},{28,0},{1,29},{... | collective-permute-start | bytes 737288 | tf_op jit(solution)/shard_map/ppermute | solution.py:476
  45.6 0.1 shard_map.50
  45.7 1.5 %collective-permute-start.15 = (f32[2,2,32,512]{3,2,1,0:T(8,128)S(1)}, f32[2,2,32,512]{3,2,1,0:T(8,128)S(1)}, u32[]{:S(2)}, u32[]{:S(2)}) collective-permute-start(f32[2,2,32,512]{3,2,1,0:T(8,128)S(1)} %get-tuple-element.49), channel_id=1, source_target_pairs={{0,1},{1,0},{2,3},{3,2},{4,5},{5,4},{6,7},{7,6},{8,9},{9,8},{10,11... | collective-permute-start | bytes 786440 | tf_op jit(solution)/shard_map/ppermute | solution.py:418
  47.2 2.8 %shard_map.51 = (f32[4,2,20,512]{3,2,1,0:T(8,128)S(1)}, f32[4,2,16,512]{3,2,1,0:T(8,128)S(1)}, f32[4,2,16,512]{3,2,1,0:T(8,128)S(1)}) custom-call(f32[3]{0:T(128)S(1)} %copy-done.3, f32[4,4,24,512]{3,2,1,0:T(8,128)S(1)} %get-tuple-element.38.refs_3_.refs_1_, f32[4,4,24,512]{3,2,1,0:T(8,128)S(1)} %collective-permute-done.9.refs_2_, ...), custom_call_target="tpu_custom_call" | custom-call | bytes 6619148 | tf_op jit(solution)/shard_map/pallas_call | solution.py:364
  50.1 0.1 shard_map.53
  50.2 0.6 collective-permute-start.17
  50.8 4.2 %collective-permute-done.15.refs_1_ = f32[2,2,32,512]{3,2,1,0:T(8,128)S(1)} collective-permute-done((f32[2,2,32,512]{3,2,1,0:T(8,128)S(1)}, f32[2,2,32,512]{3,2,1,0:T(8,128)S(1)}, u32[]{:S(2)}, u32[]{:S(2)}) %collective-permute-start.15) | collective-permute-done | bytes 262176 | tf_op jit(solution)/shard_map/ppermute | solution.py:418
  55.0 2.5 %collective-permute-start.16 = (f32[2,32,512]{2,1,0:T(8,128)S(1)}, f32[2,32,512]{2,1,0:T(8,128)S(1)}, u32[]{:S(2)}, u32[]{:S(2)}) collective-permute-start(f32[2,32,512]{2,1,0:T(8,128)S(1)} %shard_map.55.refs_4_), channel_id=1, source_target_pairs={{0,3},{1,2},{2,1},{3,0},{4,7},{5,6},{6,5},{7,4},{8,11},{9,10},{10,... | collective-permute-start | bytes 393224 | tf_op jit(solution)/shard_map/ppermute | solution.py:410
  57.6 0.1 shard_map.56
  57.7 0.1 collective-permute-start.19
  57.7 1.2 %shard_map.57 = (f32[2,16,512]{2,1,0:T(8,128)S(1)}, f32[4,2,16,512]{3,2,1,0:T(8,128)S(1)}) custom-call(f32[3]{0:T(128)S(1)} %copy-done.3, f32[4,4,24,512]{3,2,1,0:T(8,128)S(1)} %get-tuple-element.38.refs_3_.refs_1_, f32[4,4,64,512]{3,2,1,0:T(8,128)S(1)} %bitcast.15, f32[120,512]{1,0:T(8,128)S(1)} %collective-permute-done.14.refs_0_.refs_3_, ...), custom_call_target="tpu_custom_call" | custom-call | bytes 5357580 | tf_op jit(solution)/shard_map/pallas_call | solution.py:364
  59.0 1.4 %collective-permute-start.18 = (f32[2,16,512]{2,1,0:T(8,128)S(1)}, f32[2,16,512]{2,1,0:T(8,128)S(1)}, u32[]{:S(2)}, u32[]{:S(2)}) collective-permute-start(f32[2,16,512]{2,1,0:T(8,128)S(1)} %shard_map.58.refs_3_), channel_id=1, source_target_pairs={{0,3},{1,2},{2,1},{3,0},{4,7},{5,6},{6,5},{7,4},{8,11},{9,10},{10,... | collective-permute-start | bytes 196616 | tf_op jit(solution)/shard_map/ppermute | solution.py:410
  60.4 1.6 %collective-permute-done.16.refs_2_ = f32[2,32,512]{2,1,0:T(8,128)S(1)} collective-permute-done((f32[2,32,512]{2,1,0:T(8,128)S(1)}, f32[2,32,512]{2,1,0:T(8,128)S(1)}, u32[]{:S(2)}, u32[]{:S(2)}) %collective-permute-start.16) | collective-permute-done | bytes 131104 | tf_op jit(solution)/shard_map/ppermute | solution.py:410
  62.0 3.1 %collective-permute-done.18.refs_2_ = f32[2,16,512]{2,1,0:T(8,128)S(1)} collective-permute-done((f32[2,16,512]{2,1,0:T(8,128)S(1)}, f32[2,16,512]{2,1,0:T(8,128)S(1)}, u32[]{:S(2)}, u32[]{:S(2)}) %collective-permute-start.18) | collective-permute-done | bytes 65568 | tf_op jit(solution)/shard_map/ppermute | solution.py:410
  65.1 0.9 %collective-permute-done.19.refs_6_ = f32[4,2,16,512]{3,2,1,0:T(8,128)S(1)} collective-permute-done((f32[4,2,16,512]{3,2,1,0:T(8,128)S(1)}, f32[4,2,16,512]{3,2,1,0:T(8,128)S(1)}, u32[]{:S(2)}, u32[]{:S(2)}) %collective-permute-start.19) | collective-permute-done | bytes 262176 | tf_op jit(solution)/shard_map/ppermute | solution.py:507
  66.0 0.9 %shard_map.61 = f32[4,64,512]{2,1,0:T(8,128)} custom-call(f32[2,32,512]{2,1,0:T(8,128)S(1)} %shard_map.52.refs_3_.refs_0_, f32[2,16,512]{2,1,0:T(8,128)S(1)} %shard_map.54.refs_2_.refs_1_, f32[2,16,512]{2,1,0:T(8,128)S(1)} %get-tuple-element.53.refs_2_, f32[2,32,512]{2,1,0:T(8,128)S(1)} %shard_map.59.refs_3_, f32[2,16,512]{2,1,0:T(8,128)S(1)} %shard_map.60.refs_4_.refs_8_, ...), custom_call_target="tpu_custom_call" | custom-call | bytes 1523712 | tf_op jit(solution)/shard_map/pallas_call | solution.py:364
  (25 shorter events, 0.2 us)
Async XLA Ops:
  0.0 10.2 %collective-permute-start = (f32[4,256,512]{2,1,0:T(8,128)}, f32[4,256,512]{2,1,0:T(8,128)S(1)}, u32[]{:S(2)}, u32[]{:S(2)}) collective-permute-start(f32[4,256,512]{2,1,0:T(8,128)} %bitcast.7), channel_id=1, source_target_pairs={{0,4},{4,0},{8,12},{12,8},{16,20},{20,16},{24,28},{28,24},{1,5},{5... | collective-permute-start | bytes 6291464 | tf_op jit(solution)/shard_map/ppermute | solution.py:440
  0.5 9.8 %collective-permute-start.1 = (f32[4,256,512]{2,1,0:T(8,128)}, f32[4,256,512]{2,1,0:T(8,128)S(1)}, u32[]{:S(2)}, u32[]{:S(2)}) collective-permute-start(f32[4,256,512]{2,1,0:T(8,128)} %refs_2_.3), channel_id=1, source_target_pairs={{0,4},{4,0},{8,12},{12,8},{16,20},{20,16},{24,28},{28,24},{1,5},{5... | collective-permute-start | bytes 6291464 | tf_op jit(solution)/shard_map/ppermute | solution.py:441
  0.5 1.6 %copy-start = (f32[1,4,256,512]{3,2,1,0:T(8,128)S(1)}, f32[1,4,256,512]{3,2,1,0:T(8,128)}, u32[]{:S(2)}) copy-start(f32[1,4,256,512]{3,2,1,0:T(8,128)} %param.3) | copy-start | bytes 6291460
  2.2 24.2 %collective-permute-start.2 = (f32[2,4,32,512]{3,2,1,0:T(8,128)S(1)}, f32[2,4,32,512]{3,2,1,0:T(8,128)S(1)}, u32[]{:S(2)}, u32[]{:S(2)}) collective-permute-start(f32[2,4,32,512]{3,2,1,0:T(8,128)S(1)} %shard_map.37.refs_1_), channel_id=1, source_target_pairs={{0,28},{4,8},{8,4},{12,16},{16,12},{20,24},{24,20},{28,0},{1,29},{... | collective-permute-start | bytes 1572872 | tf_op jit(solution)/shard_map/ppermute | solution.py:451
  5.8 5.1 %copy-start.2 = (f32[4,256,512]{2,1,0:T(8,128)S(1)}, f32[4,256,512]{2,1,0:T(8,128)}, u32[]{:S(2)}) copy-start(f32[4,256,512]{2,1,0:T(8,128)} %refs_2_.3) | copy-start | bytes 6291460
  5.8 24.4 %collective-permute-start.7 = (f32[2,4,32,512]{3,2,1,0:T(8,128)S(1)}, f32[2,4,32,512]{3,2,1,0:T(8,128)S(1)}, u32[]{:S(2)}, u32[]{:S(2)}) collective-permute-start(f32[2,4,32,512]{3,2,1,0:T(8,128)S(1)} %shard_map.38.refs_1_), channel_id=1, source_target_pairs={{0,28},{4,8},{8,4},{12,16},{16,12},{20,24},{24,20},{28,0},{1,29},{... | collective-permute-start | bytes 1572872 | tf_op jit(solution)/shard_map/ppermute | solution.py:451
  6.0 14.4 %collective-permute-start.3 = (f32[4,24,512]{2,1,0:T(8,128)S(1)}, f32[4,24,512]{2,1,0:T(8,128)S(1)}, u32[]{:S(2)}, u32[]{:S(2)}) collective-permute-start(f32[4,24,512]{2,1,0:T(8,128)S(1)} %get-tuple-element.34), channel_id=1, source_target_pairs={{0,3},{1,2},{2,1},{3,0},{4,7},{5,6},{6,5},{7,4},{8,11},{9,10},{10,... | collective-permute-start | bytes 589832 | tf_op jit(solution)/shard_map/ppermute | solution.py:421
  10.2 16.0 %collective-permute-start.4 = (f32[4,24,512]{2,1,0:T(8,128)S(1)}, f32[4,24,512]{2,1,0:T(8,128)S(1)}, u32[]{:S(2)}, u32[]{:S(2)}) collective-permute-start(f32[4,24,512]{2,1,0:T(8,128)S(1)} %get-tuple-element.35), channel_id=1, source_target_pairs={{0,2},{1,3},{2,0},{3,1},{4,6},{5,7},{6,4},{7,5},{8,10},{9,11},{10,... | collective-permute-start | bytes 589832 | tf_op jit(solution)/shard_map/ppermute | solution.py:421
  10.2 16.0 %collective-permute-start.5 = (f32[4,24,512]{2,1,0:T(8,128)S(1)}, f32[4,24,512]{2,1,0:T(8,128)S(1)}, u32[]{:S(2)}, u32[]{:S(2)}) collective-permute-start(f32[4,24,512]{2,1,0:T(8,128)S(1)} %get-tuple-element.36), channel_id=1, source_target_pairs={{0,1},{1,0},{2,3},{3,2},{4,5},{5,4},{6,7},{7,6},{8,9},{9,8},{10,11... | collective-permute-start | bytes 589832 | tf_op jit(solution)/shard_map/ppermute | solution.py:421
  10.9 2.5 %copy-start.3 = (f32[3]{0:T(128)S(1)}, f32[3]{0:T(128)}, u32[]{:S(2)}) copy-start(f32[3]{0:T(128)} %refs_0_.7) | copy-start | bytes 40
  26.2 19.5 %collective-permute-start.9 = (f32[4,4,24,512]{3,2,1,0:T(8,128)S(1)}, f32[4,4,24,512]{3,2,1,0:T(8,128)S(1)}, u32[]{:S(2)}, u32[]{:S(2)}) collective-permute-start(f32[4,4,24,512]{3,2,1,0:T(8,128)S(1)} %get-tuple-element.38.refs_3_.refs_1_), channel_id=1, source_target_pairs={{0,4},{4,0},{8,12},{12,8},{16,20},{20,16},{24,28},{28,24},{1,5},{5... | collective-permute-start | bytes 2359304 | tf_op jit(solution)/shard_map/ppermute | solution.py:475
  26.5 9.2 %collective-permute-start.6 = (f32[2,2,32,512]{3,2,1,0:T(8,128)S(1)}, f32[2,2,32,512]{3,2,1,0:T(8,128)S(1)}, u32[]{:S(2)}, u32[]{:S(2)}) collective-permute-start(f32[2,2,32,512]{3,2,1,0:T(8,128)S(1)} %get-tuple-element.40), channel_id=1, source_target_pairs={{0,1},{1,0},{2,3},{3,2},{4,5},{5,4},{6,7},{7,6},{8,9},{9,8},{10,11... | collective-permute-start | bytes 786440 | tf_op jit(solution)/shard_map/ppermute | solution.py:430
  26.7 16.2 %collective-permute-start.10 = (f32[2,4,32,512]{3,2,1,0:T(8,128)S(1)}, f32[2,4,32,512]{3,2,1,0:T(8,128)S(1)}, u32[]{:S(2)}, u32[]{:S(2)}) collective-permute-start(f32[2,4,32,512]{3,2,1,0:T(8,128)S(1)} %shard_map.44.refs_2_.refs_4_), channel_id=1, source_target_pairs={{0,28},{4,8},{8,4},{12,16},{16,12},{20,24},{24,20},{28,0},{1,29},{... | collective-permute-start | bytes 1572872 | tf_op jit(solution)/shard_map/ppermute | solution.py:438
  30.2 19.8 %collective-permute-start.13 = (f32[2,4,16,512]{3,2,1,0:T(8,128)S(1)}, f32[2,4,16,512]{3,2,1,0:T(8,128)S(1)}, u32[]{:S(2)}, u32[]{:S(2)}) collective-permute-start(f32[2,4,16,512]{3,2,1,0:T(8,128)S(1)} %get-tuple-element.41.refs_3_.refs_5_), channel_id=1, source_target_pairs={{0,28},{4,8},{8,4},{12,16},{16,12},{20,24},{24,20},{28,0},{1,29},{... | collective-permute-start | bytes 786440 | tf_op jit(solution)/shard_map/ppermute | solution.py:438
  31.1 7.1 %copy-start.1 = (f32[1,4,256,512]{3,2,1,0:T(8,128)S(1)}, f32[1,4,256,512]{3,2,1,0:T(8,128)}, u32[]{:S(2)}) copy-start(f32[1,4,256,512]{3,2,1,0:T(8,128)} %param.3) | copy-start | bytes 6291460
  31.2 10.2 %collective-permute-start.11 = (f32[2,2,16,512]{3,2,1,0:T(8,128)S(1)}, f32[2,2,16,512]{3,2,1,0:T(8,128)S(1)}, u32[]{:S(2)}, u32[]{:S(2)}) collective-permute-start(f32[2,2,16,512]{3,2,1,0:T(8,128)S(1)} %get-tuple-element.44), channel_id=1, source_target_pairs={{0,1},{1,0},{2,3},{3,2},{4,5},{5,4},{6,7},{7,6},{8,9},{9,8},{10,11... | collective-permute-start | bytes 393224 | tf_op jit(solution)/shard_map/ppermute | solution.py:430
  35.7 14.4 %collective-permute-start.8 = (f32[2,32,512]{2,1,0:T(8,128)S(1)}, f32[2,32,512]{2,1,0:T(8,128)S(1)}, u32[]{:S(2)}, u32[]{:S(2)}) collective-permute-start(f32[2,32,512]{2,1,0:T(8,128)S(1)} %shard_map.47.refs_7_), channel_id=1, source_target_pairs={{0,3},{1,2},{2,1},{3,0},{4,7},{5,6},{6,5},{7,4},{8,11},{9,10},{10,... | collective-permute-start | bytes 393224 | tf_op jit(solution)/shard_map/ppermute | solution.py:410
  41.4 9.4 %collective-permute-start.12 = (f32[2,16,512]{2,1,0:T(8,128)S(1)}, f32[2,16,512]{2,1,0:T(8,128)S(1)}, u32[]{:S(2)}, u32[]{:S(2)}) collective-permute-start(f32[2,16,512]{2,1,0:T(8,128)S(1)} %shard_map.49.refs_3_), channel_id=1, source_target_pairs={{0,3},{1,2},{2,1},{3,0},{4,7},{5,6},{6,5},{7,4},{8,11},{9,10},{10,... | collective-permute-start | bytes 196616 | tf_op jit(solution)/shard_map/ppermute | solution.py:410
  42.9 14.7 %collective-permute-start.14 = (f32[120,512]{1,0:T(8,128)S(1)}, f32[120,512]{1,0:T(8,128)S(1)}, u32[]{:S(2)}, u32[]{:S(2)}) collective-permute-start(f32[120,512]{1,0:T(8,128)S(1)} %get-tuple-element.48), channel_id=1, source_target_pairs={{0,28},{4,8},{8,4},{12,16},{16,12},{20,24},{24,20},{28,0},{1,29},{... | collective-permute-start | bytes 737288 | tf_op jit(solution)/shard_map/ppermute | solution.py:476
  45.7 9.3 %collective-permute-start.15 = (f32[2,2,32,512]{3,2,1,0:T(8,128)S(1)}, f32[2,2,32,512]{3,2,1,0:T(8,128)S(1)}, u32[]{:S(2)}, u32[]{:S(2)}) collective-permute-start(f32[2,2,32,512]{3,2,1,0:T(8,128)S(1)} %get-tuple-element.49), channel_id=1, source_target_pairs={{0,1},{1,0},{2,3},{3,2},{4,5},{5,4},{6,7},{7,6},{8,9},{9,8},{10,11... | collective-permute-start | bytes 786440 | tf_op jit(solution)/shard_map/ppermute | solution.py:418
  50.2 8.8 %collective-permute-start.17 = (f32[2,2,16,512]{3,2,1,0:T(8,128)S(1)}, f32[2,2,16,512]{3,2,1,0:T(8,128)S(1)}, u32[]{:S(2)}, u32[]{:S(2)}) collective-permute-start(f32[2,2,16,512]{3,2,1,0:T(8,128)S(1)} %get-tuple-element.54), channel_id=1, source_target_pairs={{0,1},{1,0},{2,3},{3,2},{4,5},{5,4},{6,7},{7,6},{8,9},{9,8},{10,11... | collective-permute-start | bytes 393224 | tf_op jit(solution)/shard_map/ppermute | solution.py:418
  55.0 6.9 %collective-permute-start.16 = (f32[2,32,512]{2,1,0:T(8,128)S(1)}, f32[2,32,512]{2,1,0:T(8,128)S(1)}, u32[]{:S(2)}, u32[]{:S(2)}) collective-permute-start(f32[2,32,512]{2,1,0:T(8,128)S(1)} %shard_map.55.refs_4_), channel_id=1, source_target_pairs={{0,3},{1,2},{2,1},{3,0},{4,7},{5,6},{6,5},{7,4},{8,11},{9,10},{10,... | collective-permute-start | bytes 393224 | tf_op jit(solution)/shard_map/ppermute | solution.py:410
  57.7 8.3 %collective-permute-start.19 = (f32[4,2,16,512]{3,2,1,0:T(8,128)S(1)}, f32[4,2,16,512]{3,2,1,0:T(8,128)S(1)}, u32[]{:S(2)}, u32[]{:S(2)}) collective-permute-start(f32[4,2,16,512]{3,2,1,0:T(8,128)S(1)} %get-tuple-element.55), channel_id=1, source_target_pairs={{0,28},{4,8},{8,4},{12,16},{16,12},{20,24},{24,20},{28,0},{1,29},{... | collective-permute-start | bytes 786440 | tf_op jit(solution)/shard_map/ppermute | solution.py:507
  59.0 6.1 %collective-permute-start.18 = (f32[2,16,512]{2,1,0:T(8,128)S(1)}, f32[2,16,512]{2,1,0:T(8,128)S(1)}, u32[]{:S(2)}, u32[]{:S(2)}) collective-permute-start(f32[2,16,512]{2,1,0:T(8,128)S(1)} %shard_map.58.refs_3_), channel_id=1, source_target_pairs={{0,3},{1,2},{2,1},{3,0},{4,7},{5,6},{6,5},{7,4},{8,11},{9,10},{10,... | collective-permute-start | bytes 196616 | tf_op jit(solution)/shard_map/ppermute | solution.py:410

commit v15 on v13

--- a/solution.py
+++ b/solution.py
@@ -467,6 +467,7 @@
     def summed(keep, came, from_far, weight=0):
         return call(sum_kernel, from_far.shape, (keep, came, from_far), weight=weight)
 
+    f0, face_a = faces(chunks[0], halos[0], [cut_a])
     x, piece = call(
         gather_kernel,
         [(bands, planes, padded, lanes), (2 * (bands - 1) * inner, lanes)],
@@ -475,7 +476,6 @@
     x_in = lax.ppermute(x, "slab", partner)
     x_halo = lax.ppermute(piece, "slab", face)
     back0 = back_squares(chunks[0], cut_a, halos[0])
-    f0, face_a = faces(chunks[0], halos[0], [cut_a])
     f1, face_b = faces(chunks[1], halos[1], [cut_b, cut_c])
     back1 = back_squares(chunks[1], cut_b, halos[1], weight=8_000_000_000)
     x_first, x_t, x_back = call(
@@ -496,7 +496,8 @@
     back1 = add_far(*back1)
     front_a = squares(cut_a, face_a)
     back0 = summed(*back0)
-    back1 = summed(*back1)
+    front_b = squares(cut_b, face_b)
+    back1 = summed(*back1, weight=4_000_000_000)
     x_f, piece = call(
         functools.partial(rows_face_kernel, cut_c),
         [(bands, 2, inner, lanes), (bands, 2, part, lanes)],
@@ -509,11 +510,10 @@
         (coeffs, x, as_bands(potential), x_halo, *halos, x_f, x_t, x_back),
         scalars=1,
     )
-    front_b = squares(cut_b, face_b)
     front_a = add_far(*front_a)
     front_b = add_far(*front_b)
     front_a = summed(*front_a)
-    front_b = summed(*front_b)
+    front_b = summed(*front_b, weight=1_000_000_000)
     places = [(2, cut) for cut in cuts] + [(0, cut_a), (0, cut_b)]
     return call(
         functools.partial(join_kernel, places, cut_c),

time: 70.7 us -> 65.4 us (0.925)
  waiting for transfers between devices: 21.2 us -> 17.5 us
  starting transfers between devices: 28.5 us -> 27.4 us
    ppermute x4, waiting for transfers between devices: 11.9 us -> 5.59 us  [add_far(): return (keep, came, lax.ppermute(total, 'orb', far))]
    ppermute x1, waiting for transfers between devices: 0.01 us -> 4.29 us  [shards(): x_halo = lax.ppermute(piece, 'slab', face)]
    ppermute x2, waiting for transfers between devices: 3.51 us -> 0.01 us  [squares(): return (keep, lax.ppermute(send, 'orb', near))]
    ppermute x2, waiting for transfers between devices: 0.01 us -> 2.72 us  [shards(): halos.append(lax.ppermute(piece, 'slab', face))]
    ppermute x1, starting transfers between devices: 2.44 us -> 0.54 us  [shards(): x_face = lax.ppermute(piece, 'slab', face)]
    ppermute x2, starting transfers between devices: 0.99 us -> 2.86 us  [squares(): return (keep, lax.ppermute(send, 'orb', near))]
    ppermute x3, waiting for transfers between devices: 5.78 us -> 4.13 us  [over_orb(): return lax.ppermute(x, 'orb', [(i, i ^ d) for i in range(bands)])]
    ppermute x2, starting transfers between devices: 5.78 us -> 4.43 us  [faces(): return (fs, lax.ppermute(fs[0], 'slab', face))]
  transfers between devices with their start and end apart: 20 -> 20, of which waited for: 5 -> 7; matrix products, arithmetic and copies ran while one was open for 0% -> 0% of each run, Pallas kernels for 25% -> 27%
where the time goes in v15:
time: 65.4 us; the launch traced here: 65.3 us
  starting transfers between devices  27.4 us (42%)
  Pallas kernels  18.5 us (28%)
  waiting for transfers between devices  17.5 us (27%)
  local copies, waits for them, and re-layouts  1.6 us (2%)
    pallas_call x25, Pallas kernels, __call__(): pl.pallas_call(body, out_shape=shapes, in_specs=[smem] * scalars + [pl.Bl...  18.5 us
    ppermute x4, starting transfers between devices, add_far(): return (keep, came, lax.ppermute(total, 'orb', far))  8.19 us
    ppermute x4, waiting for transfers between devices, add_far(): return (keep, came, lax.ppermute(total, 'orb', far))  5.59 us
    ppermute x3, starting transfers between devices, over_orb(): return lax.ppermute(x, 'orb', [(i, i ^ d) for i in range(bands)])  4.88 us
    ppermute x2, starting transfers between devices, faces(): return (fs, lax.ppermute(fs[0], 'slab', face))  4.43 us
    ppermute x1, waiting for transfers between devices, shards(): x_halo = lax.ppermute(piece, 'slab', face)  4.29 us
    ppermute x3, waiting for transfers between devices, over_orb(): return lax.ppermute(x, 'orb', [(i, i ^ d) for i in range(bands)])  4.13 us
    ppermute x2, starting transfers between devices, shards(): halos.append(lax.ppermute(piece, 'slab', face))  3.66 us
  transfers between devices with their start and end apart: 20, of which 7 were waited for; matrix products, arithmetic and copies ran while one was open for 0% of the time, Pallas kernels for 27%

profile of v15, /device:TPU:0, one launch (start us, length us, event | category | flops | bytes accessed | tf_op | source)
XLA Modules:
  0.0 65.3 jit_solution(8698713299870726432)
XLA Ops:
  0.0 0.5 collective-permute-start
  0.5 0.1 collective-permute-start.1
  0.5 1.6 %copy-done = f32[1,4,256,512]{3,2,1,0:T(8,128)S(1)} copy-done((f32[1,4,256,512]{3,2,1,0:T(8,128)S(1)}, f32[1,4,256,512]{3,2,1,0:T(8,128)}, u32[]{:S(2)}) %copy-start) | copy-done | bytes 2097176
  2.2 3.6 %collective-permute-start.2 = (f32[2,4,32,512]{3,2,1,0:T(8,128)S(1)}, f32[2,4,32,512]{3,2,1,0:T(8,128)S(1)}, u32[]{:S(2)}, u32[]{:S(2)}) collective-permute-start(f32[2,4,32,512]{3,2,1,0:T(8,128)S(1)} %shard_map.37.refs_1_), channel_id=1, source_target_pairs={{0,28},{4,8},{8,4},{12,16},{16,12},{20,24},{24,20},{28,0},{1,29},{... | collective-permute-start | bytes 1572872 | tf_op jit(solution)/shard_map/ppermute | solution.py:451
  5.8 0.0 copy-start.2
  5.8 0.1 collective-permute-start.8
  5.9 0.1 shard_map.39
  6.0 4.2 %collective-permute-start.3 = (f32[4,24,512]{2,1,0:T(8,128)S(1)}, f32[4,24,512]{2,1,0:T(8,128)S(1)}, u32[]{:S(2)}, u32[]{:S(2)}) collective-permute-start(f32[4,24,512]{2,1,0:T(8,128)S(1)} %get-tuple-element.34), channel_id=1, source_target_pairs={{0,3},{1,2},{2,1},{3,0},{4,7},{5,6},{6,5},{7,4},{8,11},{9,10},{10,... | collective-permute-start | bytes 589832 | tf_op jit(solution)/shard_map/ppermute | solution.py:421
  10.2 0.0 collective-permute-done.refs_3_
  10.2 0.0 collective-permute-start.4
  10.2 0.0 collective-permute-done.1.refs_4_
  10.2 0.6 collective-permute-start.5
  10.9 2.5 %shard_map.40.refs_5_.refs_6_ = f32[2,256,512]{2,1,0:T(8,128)S(1)} custom-call(f32[4,256,512]{2,1,0:T(8,128)S(1)} %bitcast.11, f32[4,256,512]{2,1,0:T(8,128)S(1)} %copy-done.2, f32[4,24,512]{2,1,0:T(8,128)S(1)} %get-tuple-element.31.refs_2_.refs_0_), custom_call_target="tpu_custom_call" | custom-call | flops 6291456 | bytes 5242880 | tf_op jit(solution)/shard_map/pallas_call | solution.py:364
  13.4 7.0 %shard_map.41 = (f32[2,256,512]{2,1,0:T(8,128)S(1)}, f32[2,256,512]{2,1,0:T(8,128)S(1)}, f32[8,512]{1,0:T(8,128)S(1)}) custom-call(f32[3]{0:T(128)S(1)} %copy-done.3, f32[4,256,512]{2,1,0:T(8,128)S(1)} %bitcast.12, f32[4,256,512]{2,1,0:T(8,128)S(1)} %copy-done.2, f32[4,256,512]{2,1,0:T(8,128)S(1)} %collective-permute-done.refs_3_, ...), custom_call_target="tpu_custom_call" | custom-call | flops 20971520 | bytes 11550732 | tf_op jit(solution)/shard_map/pallas_call | solution.py:364
  20.4 0.0 collective-permute-done.2.refs_0_.refs_1_.refs_4_
  20.4 0.1 shard_map.42.refs_4_
  20.5 1.6 %collective-permute-start.10 = (f32[2,4,32,512]{3,2,1,0:T(8,128)S(1)}, f32[2,4,32,512]{3,2,1,0:T(8,128)S(1)}, u32[]{:S(2)}, u32[]{:S(2)}) collective-permute-start(f32[2,4,32,512]{3,2,1,0:T(8,128)S(1)} %shard_map.42.refs_4_), channel_id=1, source_target_pairs={{0,28},{4,8},{8,4},{12,16},{16,12},{20,24},{24,20},{28,0},{1,29},{... | collective-permute-start | bytes 1572872 | tf_op jit(solution)/shard_map/ppermute | solution.py:438
  22.0 4.1 %collective-permute-done.4.refs_2_ = f32[4,24,512]{2,1,0:T(8,128)S(1)} collective-permute-done((f32[4,24,512]{2,1,0:T(8,128)S(1)}, f32[4,24,512]{2,1,0:T(8,128)S(1)}, u32[]{:S(2)}, u32[]{:S(2)}) %collective-permute-start.4) | collective-permute-done | bytes 196640 | tf_op jit(solution)/shard_map/ppermute | solution.py:421
  26.2 0.0 collective-permute-done.5.refs_3_
  26.2 0.1 shard_map.43
  26.2 0.1 collective-permute-start.7
  26.3 0.2 shard_map.44
  26.5 0.1 collective-permute-start.6
  26.6 2.7 %collective-permute-done.8.refs_0_.refs_1_.refs_2_.refs_5_ = f32[2,4,32,512]{3,2,1,0:T(8,128)S(1)} collective-permute-done((f32[2,4,32,512]{3,2,1,0:T(8,128)S(1)}, f32[2,4,32,512]{3,2,1,0:T(8,128)S(1)}, u32[]{:S(2)}, u32[]{:S(2)}) %collective-permute-start.8) | collective-permute-done | bytes 524320 | tf_op jit(solution)/shard_map/ppermute | solution.py:451
  29.3 0.1 shard_map.45
  29.4 2.9 %collective-permute-start.13 = (f32[2,4,16,512]{3,2,1,0:T(8,128)S(1)}, f32[2,4,16,512]{3,2,1,0:T(8,128)S(1)}, u32[]{:S(2)}, u32[]{:S(2)}) collective-permute-start(f32[2,4,16,512]{3,2,1,0:T(8,128)S(1)} %get-tuple-element.41.refs_3_.refs_5_), channel_id=1, source_target_pairs={{0,28},{4,8},{8,4},{12,16},{16,12},{20,24},{24,20},{28,0},{1,29},{... | collective-permute-start | bytes 786440 | tf_op jit(solution)/shard_map/ppermute | solution.py:438
  32.2 0.1 shard_map.46
  32.3 1.6 %collective-permute-start.11 = (f32[2,2,16,512]{3,2,1,0:T(8,128)S(1)}, f32[2,2,16,512]{3,2,1,0:T(8,128)S(1)}, u32[]{:S(2)}, u32[]{:S(2)}) collective-permute-start(f32[2,2,16,512]{3,2,1,0:T(8,128)S(1)} %get-tuple-element.45), channel_id=1, source_target_pairs={{0,1},{1,0},{2,3},{3,2},{4,5},{5,4},{6,7},{7,6},{8,9},{9,8},{10,11... | collective-permute-start | bytes 393224 | tf_op jit(solution)/shard_map/ppermute | solution.py:430
  34.0 2.8 %shard_map.47 = (f32[4,2,20,512]{3,2,1,0:T(8,128)S(1)}, f32[4,2,16,512]{3,2,1,0:T(8,128)S(1)}, f32[4,2,16,512]{3,2,1,0:T(8,128)S(1)}) custom-call(f32[3]{0:T(128)S(1)} %copy-done.3, f32[4,4,24,512]{3,2,1,0:T(8,128)S(1)} %get-tuple-element.38.refs_3_.refs_1_, f32[4,4,24,512]{3,2,1,0:T(8,128)S(1)} %collective-permute-done.7.refs_2_, ...), custom_call_target="tpu_custom_call" | custom-call | bytes 6619148 | tf_op jit(solution)/shard_map/pallas_call | solution.py:364
  36.8 2.5 %collective-permute-start.9 = (f32[2,32,512]{2,1,0:T(8,128)S(1)}, f32[2,32,512]{2,1,0:T(8,128)S(1)}, u32[]{:S(2)}, u32[]{:S(2)}) collective-permute-start(f32[2,32,512]{2,1,0:T(8,128)S(1)} %shard_map.48.refs_7_), channel_id=1, source_target_pairs={{0,3},{1,2},{2,1},{3,0},{4,7},{5,6},{6,5},{7,4},{8,11},{9,10},{10,... | collective-permute-start | bytes 393224 | tf_op jit(solution)/shard_map/ppermute | solution.py:410
  39.3 3.2 %shard_map.49.refs_2_ = f32[2,256,512]{2,1,0:T(8,128)S(1)} custom-call(f32[3]{0:T(128)S(1)} %copy-done.3, f32[4,256,512]{2,1,0:T(8,128)S(1)} %bitcast.13, f32[4,256,512]{2,1,0:T(8,128)S(1)} %copy-done.2, f32[2,256,512]{2,1,0:T(8,128)S(1)} %get-tuple-element.37.refs_2_.refs_3_, f32[2,4,32,512]{3,2,1,0:T(8,128)S(1)} %shard_map.42.refs_4_, ...), custom_call_target="tpu_custom_call" | custom-call | flops 10485760 | bytes 7340044 | tf_op jit(solution)/shard_map/pallas_call | solution.py:364
  42.5 1.4 %collective-permute-start.12 = (f32[2,16,512]{2,1,0:T(8,128)S(1)}, f32[2,16,512]{2,1,0:T(8,128)S(1)}, u32[]{:S(2)}, u32[]{:S(2)}) collective-permute-start(f32[2,16,512]{2,1,0:T(8,128)S(1)} %shard_map.50.refs_3_), channel_id=1, source_target_pairs={{0,3},{1,2},{2,1},{3,0},{4,7},{5,6},{6,5},{7,4},{8,11},{9,10},{10,... | collective-permute-start | bytes 196616 | tf_op jit(solution)/shard_map/ppermute | solution.py:410
  43.9 0.6 collective-permute-start.14
  44.5 0.1 shard_map.51
  44.6 0.1 collective-permute-start.15
  44.7 0.8 %collective-permute-done.13.refs_1_ = f32[2,4,16,512]{3,2,1,0:T(8,128)S(1)} collective-permute-done((f32[2,4,16,512]{3,2,1,0:T(8,128)S(1)}, f32[2,4,16,512]{3,2,1,0:T(8,128)S(1)}, u32[]{:S(2)}, u32[]{:S(2)}) %collective-permute-start.13) | collective-permute-done | bytes 262176 | tf_op jit(solution)/shard_map/ppermute | solution.py:438
  45.5 0.1 shard_map.53
  45.6 2.8 %collective-permute-start.17 = (f32[2,2,16,512]{3,2,1,0:T(8,128)S(1)}, f32[2,2,16,512]{3,2,1,0:T(8,128)S(1)}, u32[]{:S(2)}, u32[]{:S(2)}) collective-permute-start(f32[2,2,16,512]{3,2,1,0:T(8,128)S(1)} %get-tuple-element.54), channel_id=1, source_target_pairs={{0,1},{1,0},{2,3},{3,2},{4,5},{5,4},{6,7},{7,6},{8,9},{9,8},{10,11... | collective-permute-start | bytes 393224 | tf_op jit(solution)/shard_map/ppermute | solution.py:418
  48.3 0.4 collective-permute-done.12.refs_2_
  48.7 4.3 %collective-permute-done.14.refs_0_.refs_3_ = f32[120,512]{1,0:T(8,128)S(1)} collective-permute-done((f32[120,512]{1,0:T(8,128)S(1)}, f32[120,512]{1,0:T(8,128)S(1)}, u32[]{:S(2)}, u32[]{:S(2)}) %collective-permute-start.14) | collective-permute-done | bytes 245792 | tf_op jit(solution)/shard_map/ppermute | solution.py:477
  53.0 0.1 shard_map.55
  53.1 0.5 collective-permute-start.19
  53.6 1.2 %shard_map.56 = (f32[2,16,512]{2,1,0:T(8,128)S(1)}, f32[4,2,16,512]{3,2,1,0:T(8,128)S(1)}) custom-call(f32[3]{0:T(128)S(1)} %copy-done.3, f32[4,4,24,512]{3,2,1,0:T(8,128)S(1)} %get-tuple-element.38.refs_3_.refs_1_, f32[4,4,64,512]{3,2,1,0:T(8,128)S(1)} %bitcast.15, f32[120,512]{1,0:T(8,128)S(1)} %collective-permute-done.14.refs_0_.refs_3_, ...), custom_call_target="tpu_custom_call" | custom-call | bytes 5357580 | tf_op jit(solution)/shard_map/pallas_call | solution.py:364
  54.9 3.3 %collective-permute-start.16 = (f32[2,32,512]{2,1,0:T(8,128)S(1)}, f32[2,32,512]{2,1,0:T(8,128)S(1)}, u32[]{:S(2)}, u32[]{:S(2)}) collective-permute-start(f32[2,32,512]{2,1,0:T(8,128)S(1)} %shard_map.57.refs_2_), channel_id=1, source_target_pairs={{0,3},{1,2},{2,1},{3,0},{4,7},{5,6},{6,5},{7,4},{8,11},{9,10},{10,... | collective-permute-start | bytes 393224 | tf_op jit(solution)/shard_map/ppermute | solution.py:410
  58.1 1.0 %collective-permute-start.18 = (f32[2,16,512]{2,1,0:T(8,128)S(1)}, f32[2,16,512]{2,1,0:T(8,128)S(1)}, u32[]{:S(2)}, u32[]{:S(2)}) collective-permute-start(f32[2,16,512]{2,1,0:T(8,128)S(1)} %shard_map.58.refs_3_), channel_id=1, source_target_pairs={{0,3},{1,2},{2,1},{3,0},{4,7},{5,6},{6,5},{7,4},{8,11},{9,10},{10,... | collective-permute-start | bytes 196616 | tf_op jit(solution)/shard_map/ppermute | solution.py:410
  59.1 3.4 %collective-permute-done.16.refs_2_ = f32[2,32,512]{2,1,0:T(8,128)S(1)} collective-permute-done((f32[2,32,512]{2,1,0:T(8,128)S(1)}, f32[2,32,512]{2,1,0:T(8,128)S(1)}, u32[]{:S(2)}, u32[]{:S(2)}) %collective-permute-start.16) | collective-permute-done | bytes 131104 | tf_op jit(solution)/shard_map/ppermute | solution.py:410
  62.5 1.9 %collective-permute-done.18.refs_2_ = f32[2,16,512]{2,1,0:T(8,128)S(1)} collective-permute-done((f32[2,16,512]{2,1,0:T(8,128)S(1)}, f32[2,16,512]{2,1,0:T(8,128)S(1)}, u32[]{:S(2)}, u32[]{:S(2)}) %collective-permute-start.18) | collective-permute-done | bytes 65568 | tf_op jit(solution)/shard_map/ppermute | solution.py:410
  64.4 0.9 %shard_map.61 = f32[4,64,512]{2,1,0:T(8,128)} custom-call(f32[2,32,512]{2,1,0:T(8,128)S(1)} %shard_map.52.refs_3_.refs_0_, f32[2,16,512]{2,1,0:T(8,128)S(1)} %shard_map.54.refs_4_.refs_1_, f32[2,16,512]{2,1,0:T(8,128)S(1)} %get-tuple-element.52.refs_2_, f32[2,32,512]{2,1,0:T(8,128)S(1)} %shard_map.59.refs_3_, f32[2,16,512]{2,1,0:T(8,128)S(1)} %shard_map.60.refs_4_.refs_8_, ...), custom_call_target="tpu_custom_call" | custom-call | bytes 1523712 | tf_op jit(solution)/shard_map/pallas_call | solution.py:364
  (25 shorter events, 0.3 us)
Async XLA Ops:
  0.0 10.2 %collective-permute-start = (f32[4,256,512]{2,1,0:T(8,128)}, f32[4,256,512]{2,1,0:T(8,128)S(1)}, u32[]{:S(2)}, u32[]{:S(2)}) collective-permute-start(f32[4,256,512]{2,1,0:T(8,128)} %bitcast.7), channel_id=1, source_target_pairs={{0,4},{4,0},{8,12},{12,8},{16,20},{20,16},{24,28},{28,24},{1,5},{5... | collective-permute-start | bytes 6291464 | tf_op jit(solution)/shard_map/ppermute | solution.py:440
  0.5 9.8 %collective-permute-start.1 = (f32[4,256,512]{2,1,0:T(8,128)}, f32[4,256,512]{2,1,0:T(8,128)S(1)}, u32[]{:S(2)}, u32[]{:S(2)}) collective-permute-start(f32[4,256,512]{2,1,0:T(8,128)} %refs_2_.3), channel_id=1, source_target_pairs={{0,4},{4,0},{8,12},{12,8},{16,20},{20,16},{24,28},{28,24},{1,5},{5... | collective-permute-start | bytes 6291464 | tf_op jit(solution)/shard_map/ppermute | solution.py:441
  0.5 1.6 %copy-start = (f32[1,4,256,512]{3,2,1,0:T(8,128)S(1)}, f32[1,4,256,512]{3,2,1,0:T(8,128)}, u32[]{:S(2)}) copy-start(f32[1,4,256,512]{3,2,1,0:T(8,128)} %param.3) | copy-start | bytes 6291460
  2.2 18.2 %collective-permute-start.2 = (f32[2,4,32,512]{3,2,1,0:T(8,128)S(1)}, f32[2,4,32,512]{3,2,1,0:T(8,128)S(1)}, u32[]{:S(2)}, u32[]{:S(2)}) collective-permute-start(f32[2,4,32,512]{3,2,1,0:T(8,128)S(1)} %shard_map.37.refs_1_), channel_id=1, source_target_pairs={{0,28},{4,8},{8,4},{12,16},{16,12},{20,24},{24,20},{28,0},{1,29},{... | collective-permute-start | bytes 1572872 | tf_op jit(solution)/shard_map/ppermute | solution.py:451
  5.8 5.1 %copy-start.2 = (f32[4,256,512]{2,1,0:T(8,128)S(1)}, f32[4,256,512]{2,1,0:T(8,128)}, u32[]{:S(2)}) copy-start(f32[4,256,512]{2,1,0:T(8,128)} %refs_2_.3) | copy-start | bytes 6291460
  5.8 23.5 %collective-permute-start.8 = (f32[2,4,32,512]{3,2,1,0:T(8,128)S(1)}, f32[2,4,32,512]{3,2,1,0:T(8,128)S(1)}, u32[]{:S(2)}, u32[]{:S(2)}) collective-permute-start(f32[2,4,32,512]{3,2,1,0:T(8,128)S(1)} %shard_map.38.refs_1_), channel_id=1, source_target_pairs={{0,28},{4,8},{8,4},{12,16},{16,12},{20,24},{24,20},{28,0},{1,29},{... | collective-permute-start | bytes 1572872 | tf_op jit(solution)/shard_map/ppermute | solution.py:451
  6.0 16.1 %collective-permute-start.3 = (f32[4,24,512]{2,1,0:T(8,128)S(1)}, f32[4,24,512]{2,1,0:T(8,128)S(1)}, u32[]{:S(2)}, u32[]{:S(2)}) collective-permute-start(f32[4,24,512]{2,1,0:T(8,128)S(1)} %get-tuple-element.34), channel_id=1, source_target_pairs={{0,3},{1,2},{2,1},{3,0},{4,7},{5,6},{6,5},{7,4},{8,11},{9,10},{10,... | collective-permute-start | bytes 589832 | tf_op jit(solution)/shard_map/ppermute | solution.py:421
  10.2 16.0 %collective-permute-start.4 = (f32[4,24,512]{2,1,0:T(8,128)S(1)}, f32[4,24,512]{2,1,0:T(8,128)S(1)}, u32[]{:S(2)}, u32[]{:S(2)}) collective-permute-start(f32[4,24,512]{2,1,0:T(8,128)S(1)} %get-tuple-element.35), channel_id=1, source_target_pairs={{0,2},{1,3},{2,0},{3,1},{4,6},{5,7},{6,4},{7,5},{8,10},{9,11},{10,... | collective-permute-start | bytes 589832 | tf_op jit(solution)/shard_map/ppermute | solution.py:421
  10.2 16.0 %collective-permute-start.5 = (f32[4,24,512]{2,1,0:T(8,128)S(1)}, f32[4,24,512]{2,1,0:T(8,128)S(1)}, u32[]{:S(2)}, u32[]{:S(2)}) collective-permute-start(f32[4,24,512]{2,1,0:T(8,128)S(1)} %get-tuple-element.36), channel_id=1, source_target_pairs={{0,1},{1,0},{2,3},{3,2},{4,5},{5,4},{6,7},{7,6},{8,9},{9,8},{10,11... | collective-permute-start | bytes 589832 | tf_op jit(solution)/shard_map/ppermute | solution.py:421
  10.9 2.5 %copy-start.3 = (f32[3]{0:T(128)S(1)}, f32[3]{0:T(128)}, u32[]{:S(2)}) copy-start(f32[3]{0:T(128)} %refs_0_.7) | copy-start | bytes 40
  20.5 24.0 %collective-permute-start.10 = (f32[2,4,32,512]{3,2,1,0:T(8,128)S(1)}, f32[2,4,32,512]{3,2,1,0:T(8,128)S(1)}, u32[]{:S(2)}, u32[]{:S(2)}) collective-permute-start(f32[2,4,32,512]{3,2,1,0:T(8,128)S(1)} %shard_map.42.refs_4_), channel_id=1, source_target_pairs={{0,28},{4,8},{8,4},{12,16},{16,12},{20,24},{24,20},{28,0},{1,29},{... | collective-permute-start | bytes 1572872 | tf_op jit(solution)/shard_map/ppermute | solution.py:438
  26.2 7.7 %collective-permute-start.7 = (f32[4,4,24,512]{3,2,1,0:T(8,128)S(1)}, f32[4,4,24,512]{3,2,1,0:T(8,128)S(1)}, u32[]{:S(2)}, u32[]{:S(2)}) collective-permute-start(f32[4,4,24,512]{3,2,1,0:T(8,128)S(1)} %get-tuple-element.38.refs_3_.refs_1_), channel_id=1, source_target_pairs={{0,4},{4,0},{8,12},{12,8},{16,20},{20,16},{24,28},{28,24},{1,5},{5... | collective-permute-start | bytes 2359304 | tf_op jit(solution)/shard_map/ppermute | solution.py:476
  26.5 10.2 %collective-permute-start.6 = (f32[2,2,32,512]{3,2,1,0:T(8,128)S(1)}, f32[2,2,32,512]{3,2,1,0:T(8,128)S(1)}, u32[]{:S(2)}, u32[]{:S(2)}) collective-permute-start(f32[2,2,32,512]{3,2,1,0:T(8,128)S(1)} %get-tuple-element.40), channel_id=1, source_target_pairs={{0,1},{1,0},{2,3},{3,2},{4,5},{5,4},{6,7},{7,6},{8,9},{9,8},{10,11... | collective-permute-start | bytes 786440 | tf_op jit(solution)/shard_map/ppermute | solution.py:430
  29.4 16.1 %collective-permute-start.13 = (f32[2,4,16,512]{3,2,1,0:T(8,128)S(1)}, f32[2,4,16,512]{3,2,1,0:T(8,128)S(1)}, u32[]{:S(2)}, u32[]{:S(2)}) collective-permute-start(f32[2,4,16,512]{3,2,1,0:T(8,128)S(1)} %get-tuple-element.41.refs_3_.refs_5_), channel_id=1, source_target_pairs={{0,28},{4,8},{8,4},{12,16},{16,12},{20,24},{24,20},{28,0},{1,29},{... | collective-permute-start | bytes 786440 | tf_op jit(solution)/shard_map/ppermute | solution.py:438
  32.3 10.2 %collective-permute-start.11 = (f32[2,2,16,512]{3,2,1,0:T(8,128)S(1)}, f32[2,2,16,512]{3,2,1,0:T(8,128)S(1)}, u32[]{:S(2)}, u32[]{:S(2)}) collective-permute-start(f32[2,2,16,512]{3,2,1,0:T(8,128)S(1)} %get-tuple-element.45), channel_id=1, source_target_pairs={{0,1},{1,0},{2,3},{3,2},{4,5},{5,4},{6,7},{7,6},{8,9},{9,8},{10,11... | collective-permute-start | bytes 393224 | tf_op jit(solution)/shard_map/ppermute | solution.py:430
  34.0 5.3 %copy-start.1 = (f32[1,4,256,512]{3,2,1,0:T(8,128)S(1)}, f32[1,4,256,512]{3,2,1,0:T(8,128)}, u32[]{:S(2)}) copy-start(f32[1,4,256,512]{3,2,1,0:T(8,128)} %param.3) | copy-start | bytes 6291460
  36.8 7.9 %collective-permute-start.9 = (f32[2,32,512]{2,1,0:T(8,128)S(1)}, f32[2,32,512]{2,1,0:T(8,128)S(1)}, u32[]{:S(2)}, u32[]{:S(2)}) collective-permute-start(f32[2,32,512]{2,1,0:T(8,128)S(1)} %shard_map.48.refs_7_), channel_id=1, source_target_pairs={{0,3},{1,2},{2,1},{3,0},{4,7},{5,6},{6,5},{7,4},{8,11},{9,10},{10,... | collective-permute-start | bytes 393224 | tf_op jit(solution)/shard_map/ppermute | solution.py:410
  42.5 6.2 %collective-permute-start.12 = (f32[2,16,512]{2,1,0:T(8,128)S(1)}, f32[2,16,512]{2,1,0:T(8,128)S(1)}, u32[]{:S(2)}, u32[]{:S(2)}) collective-permute-start(f32[2,16,512]{2,1,0:T(8,128)S(1)} %shard_map.50.refs_3_), channel_id=1, source_target_pairs={{0,3},{1,2},{2,1},{3,0},{4,7},{5,6},{6,5},{7,4},{8,11},{9,10},{10,... | collective-permute-start | bytes 196616 | tf_op jit(solution)/shard_map/ppermute | solution.py:410
  43.9 9.1 %collective-permute-start.14 = (f32[120,512]{1,0:T(8,128)S(1)}, f32[120,512]{1,0:T(8,128)S(1)}, u32[]{:S(2)}, u32[]{:S(2)}) collective-permute-start(f32[120,512]{1,0:T(8,128)S(1)} %get-tuple-element.48), channel_id=1, source_target_pairs={{0,28},{4,8},{8,4},{12,16},{16,12},{20,24},{24,20},{28,0},{1,29},{... | collective-permute-start | bytes 737288 | tf_op jit(solution)/shard_map/ppermute | solution.py:477
  44.6 10.2 %collective-permute-start.15 = (f32[2,2,32,512]{3,2,1,0:T(8,128)S(1)}, f32[2,2,32,512]{3,2,1,0:T(8,128)S(1)}, u32[]{:S(2)}, u32[]{:S(2)}) collective-permute-start(f32[2,2,32,512]{3,2,1,0:T(8,128)S(1)} %get-tuple-element.53), channel_id=1, source_target_pairs={{0,1},{1,0},{2,3},{3,2},{4,5},{5,4},{6,7},{7,6},{8,9},{9,8},{10,11... | collective-permute-start | bytes 786440 | tf_op jit(solution)/shard_map/ppermute | solution.py:418
  45.6 12.6 %collective-permute-start.17 = (f32[2,2,16,512]{3,2,1,0:T(8,128)S(1)}, f32[2,2,16,512]{3,2,1,0:T(8,128)S(1)}, u32[]{:S(2)}, u32[]{:S(2)}) collective-permute-start(f32[2,2,16,512]{3,2,1,0:T(8,128)S(1)} %get-tuple-element.54), channel_id=1, source_target_pairs={{0,1},{1,0},{2,3},{3,2},{4,5},{5,4},{6,7},{7,6},{8,9},{9,8},{10,11... | collective-permute-start | bytes 393224 | tf_op jit(solution)/shard_map/ppermute | solution.py:418
  53.1 11.3 %collective-permute-start.19 = (f32[4,2,16,512]{3,2,1,0:T(8,128)S(1)}, f32[4,2,16,512]{3,2,1,0:T(8,128)S(1)}, u32[]{:S(2)}, u32[]{:S(2)}) collective-permute-start(f32[4,2,16,512]{3,2,1,0:T(8,128)S(1)} %get-tuple-element.55), channel_id=1, source_target_pairs={{0,28},{4,8},{8,4},{12,16},{16,12},{20,24},{24,20},{28,0},{1,29},{... | collective-permute-start | bytes 786440 | tf_op jit(solution)/shard_map/ppermute | solution.py:506
  54.9 7.6 %collective-permute-start.16 = (f32[2,32,512]{2,1,0:T(8,128)S(1)}, f32[2,32,512]{2,1,0:T(8,128)S(1)}, u32[]{:S(2)}, u32[]{:S(2)}) collective-permute-start(f32[2,32,512]{2,1,0:T(8,128)S(1)} %shard_map.57.refs_2_), channel_id=1, source_target_pairs={{0,3},{1,2},{2,1},{3,0},{4,7},{5,6},{6,5},{7,4},{8,11},{9,10},{10,... | collective-permute-start | bytes 393224 | tf_op jit(solution)/shard_map/ppermute | solution.py:410
  58.1 6.2 %collective-permute-start.18 = (f32[2,16,512]{2,1,0:T(8,128)S(1)}, f32[2,16,512]{2,1,0:T(8,128)S(1)}, u32[]{:S(2)}, u32[]{:S(2)}) collective-permute-start(f32[2,16,512]{2,1,0:T(8,128)S(1)} %shard_map.58.refs_3_), channel_id=1, source_target_pairs={{0,3},{1,2},{2,1},{3,0},{4,7},{5,6},{6,5},{7,4},{8,11},{9,10},{10,... | collective-permute-start | bytes 196616 | tf_op jit(solution)/shard_map/ppermute | solution.py:410

commit v16 on v15

--- a/solution.py
+++ b/solution.py
@@ -66,7 +66,7 @@
         body(pl.multiple_of(i * BLOCK, BLOCK))
         return carry
 
-    lax.fori_loop(0, rows // BLOCK, step, 0)
+    lax.fori_loop(0, rows // BLOCK, step, 0, unroll=4)
 
 
 def pack_kernel(chunk, psi, out, sem):
@@ -220,7 +220,7 @@
             h[k, j] = base * e[q][4 : n] + one * f[q] + two * s
         return carry
 
-    lax.fori_loop(0, x.shape[0], step, 0)
+    lax.fori_loop(0, x.shape[0], step, 0, unroll=True)
 
 
 def rows_halo(part, k, halo, first, second, n):
@@ -498,22 +498,22 @@
     back0 = summed(*back0)
     front_b = squares(cut_b, face_b)
     back1 = summed(*back1, weight=4_000_000_000)
+    front_a = add_far(*front_a)
     x_f, piece = call(
         functools.partial(rows_face_kernel, cut_c),
         [(bands, 2, inner, lanes), (bands, 2, part, lanes)],
         (x_halo, *halos, x_first),
     )
     x_face = lax.ppermute(piece, "slab", face)
+    front_b = add_far(*front_b)
     back2, x_front = call(
         functools.partial(rows_front_kernel, cut_c),
         [(2, part, lanes), (bands, 2, part, lanes)],
         (coeffs, x, as_bands(potential), x_halo, *halos, x_f, x_t, x_back),
         scalars=1,
     )
-    front_a = add_far(*front_a)
-    front_b = add_far(*front_b)
     front_a = summed(*front_a)
-    front_b = summed(*front_b, weight=1_000_000_000)
+    front_b = summed(*front_b, weight=2_000_000_000)
     places = [(2, cut) for cut in cuts] + [(0, cut_a), (0, cut_b)]
     return call(
         functools.partial(join_kernel, places, cut_c),

time: 65.4 us -> 66 us (level)
  Pallas kernels: 18.5 us -> 15.2 us
  waiting for transfers between devices: 17.5 us -> 19.7 us
  starting transfers between devices: 27.4 us -> 29.2 us
    ppermute x2, waiting for transfers between devices: 0.01 us -> 4.84 us  [squares(): return (keep, lax.ppermute(send, 'orb', near))]
    ppermute x1, waiting for transfers between devices: 4.29 us -> 0.01 us  [shards(): x_halo = lax.ppermute(piece, 'slab', face)]
    pallas_call x25, Pallas kernels: 18.5 us -> 15.2 us  [__call__(): pl.pallas_call(body, out_shape=shapes, in_specs=[smem] * scalars + [pl.Bl...]
    ppermute x4, waiting for transfers between devices: 5.59 us -> 3.4 us  [add_far(): return (keep, came, lax.ppermute(total, 'orb', far))]
    ppermute x1, waiting for transfers between devices: 0.01 us -> 1.99 us  [shards(): x_face = lax.ppermute(piece, 'slab', face)]
    ppermute x2, starting transfers between devices: 4.43 us -> 5.69 us  [faces(): return (fs, lax.ppermute(fs[0], 'slab', face))]
    ppermute x3, waiting for transfers between devices: 4.13 us -> 5.15 us  [over_orb(): return lax.ppermute(x, 'orb', [(i, i ^ d) for i in range(bands)])]
    ppermute x2, waiting for transfers between devices: 0.76 us -> 1.54 us  [faces(): return (fs, lax.ppermute(fs[0], 'slab', face))]
  transfers between devices with their start and end apart: 20 -> 20, of which waited for: 7 -> 7; matrix products, arithmetic and copies ran while one was open for 0% -> 0% of each run, Pallas kernels for 27% -> 22%
where the time goes in v16:
time: 66 us; the launch traced here: 65.8 us
  starting transfers between devices  29.2 us (44%)
  waiting for transfers between devices  19.7 us (30%)
  Pallas kernels  15.2 us (23%)
  local copies, waits for them, and re-layouts  1.6 us (2%)
    pallas_call x25, Pallas kernels, __call__(): pl.pallas_call(body, out_shape=shapes, in_specs=[smem] * scalars + [pl.Bl...  15.2 us
    ppermute x4, starting transfers between devices, add_far(): return (keep, came, lax.ppermute(total, 'orb', far))  7.96 us
    ppermute x2, starting transfers between devices, faces(): return (fs, lax.ppermute(fs[0], 'slab', face))  5.69 us
    ppermute x3, waiting for transfers between devices, over_orb(): return lax.ppermute(x, 'orb', [(i, i ^ d) for i in range(bands)])  5.15 us
    ppermute x3, starting transfers between devices, over_orb(): return lax.ppermute(x, 'orb', [(i, i ^ d) for i in range(bands)])  4.88 us
    ppermute x2, waiting for transfers between devices, squares(): return (keep, lax.ppermute(send, 'orb', near))  4.84 us
    ppermute x2, starting transfers between devices, shards(): halos.append(lax.ppermute(piece, 'slab', face))  3.66 us
    ppermute x4, waiting for transfers between devices, add_far(): return (keep, came, lax.ppermute(total, 'orb', far))  3.4 us
  transfers between devices with their start and end apart: 20, of which 7 were waited for; matrix products, arithmetic and copies ran while one was open for 0% of the time, Pallas kernels for 22%

profile of v16, /device:TPU:0, one launch (start us, length us, event | category | flops | bytes accessed | tf_op | source)
XLA Modules:
  0.0 65.8 jit_solution(18411624738266576890)
XLA Ops:
  0.0 0.5 collective-permute-start
  0.5 0.1 collective-permute-start.1
  0.5 1.6 %copy-done = f32[1,4,256,512]{3,2,1,0:T(8,128)S(1)} copy-done((f32[1,4,256,512]{3,2,1,0:T(8,128)S(1)}, f32[1,4,256,512]{3,2,1,0:T(8,128)}, u32[]{:S(2)}) %copy-start) | copy-done | bytes 2097176
  2.2 3.6 %collective-permute-start.2 = (f32[2,4,32,512]{3,2,1,0:T(8,128)S(1)}, f32[2,4,32,512]{3,2,1,0:T(8,128)S(1)}, u32[]{:S(2)}, u32[]{:S(2)}) collective-permute-start(f32[2,4,32,512]{3,2,1,0:T(8,128)S(1)} %shard_map.37.refs_1_), channel_id=1, source_target_pairs={{0,28},{4,8},{8,4},{12,16},{16,12},{20,24},{24,20},{28,0},{1,29},{... | collective-permute-start | bytes 1572872 | tf_op jit(solution)/shard_map/ppermute | solution.py:451
  5.8 0.0 copy-start.2
  5.8 0.1 collective-permute-start.8
  5.9 0.1 shard_map.39
  6.0 4.2 %collective-permute-start.3 = (f32[4,24,512]{2,1,0:T(8,128)S(1)}, f32[4,24,512]{2,1,0:T(8,128)S(1)}, u32[]{:S(2)}, u32[]{:S(2)}) collective-permute-start(f32[4,24,512]{2,1,0:T(8,128)S(1)} %get-tuple-element.34), channel_id=1, source_target_pairs={{0,3},{1,2},{2,1},{3,0},{4,7},{5,6},{6,5},{7,4},{8,11},{9,10},{10,... | collective-permute-start | bytes 589832 | tf_op jit(solution)/shard_map/ppermute | solution.py:421
  10.2 0.0 collective-permute-done.refs_3_
  10.2 0.0 collective-permute-start.4
  10.2 0.6 collective-permute-start.5
  10.9 1.6 %shard_map.40.refs_5_.refs_6_ = f32[2,256,512]{2,1,0:T(8,128)S(1)} custom-call(f32[4,256,512]{2,1,0:T(8,128)S(1)} %bitcast.11, f32[4,256,512]{2,1,0:T(8,128)S(1)} %copy-done.2, f32[4,24,512]{2,1,0:T(8,128)S(1)} %get-tuple-element.31.refs_2_.refs_0_), custom_call_target="tpu_custom_call" | custom-call | flops 6291456 | bytes 5242880 | tf_op jit(solution)/shard_map/pallas_call | solution.py:364
  12.5 5.6 %shard_map.41 = (f32[2,256,512]{2,1,0:T(8,128)S(1)}, f32[2,256,512]{2,1,0:T(8,128)S(1)}, f32[8,512]{1,0:T(8,128)S(1)}) custom-call(f32[3]{0:T(128)S(1)} %copy-done.3, f32[4,256,512]{2,1,0:T(8,128)S(1)} %bitcast.12, f32[4,256,512]{2,1,0:T(8,128)S(1)} %copy-done.2, f32[4,256,512]{2,1,0:T(8,128)S(1)} %collective-permute-done.refs_3_, ...), custom_call_target="tpu_custom_call" | custom-call | flops 20971520 | bytes 11550732 | tf_op jit(solution)/shard_map/pallas_call | solution.py:364
  18.1 0.1 shard_map.42.refs_4_
  18.2 2.8 %collective-permute-start.10 = (f32[2,4,32,512]{3,2,1,0:T(8,128)S(1)}, f32[2,4,32,512]{3,2,1,0:T(8,128)S(1)}, u32[]{:S(2)}, u32[]{:S(2)}) collective-permute-start(f32[2,4,32,512]{3,2,1,0:T(8,128)S(1)} %shard_map.42.refs_4_), channel_id=1, source_target_pairs={{0,28},{4,8},{8,4},{12,16},{16,12},{20,24},{24,20},{28,0},{1,29},{... | collective-permute-start | bytes 1572872 | tf_op jit(solution)/shard_map/ppermute | solution.py:438
  21.0 0.0 collective-permute-done.3.refs_1_
  21.0 5.1 %collective-permute-done.4.refs_2_ = f32[4,24,512]{2,1,0:T(8,128)S(1)} collective-permute-done((f32[4,24,512]{2,1,0:T(8,128)S(1)}, f32[4,24,512]{2,1,0:T(8,128)S(1)}, u32[]{:S(2)}, u32[]{:S(2)}) %collective-permute-start.4) | collective-permute-done | bytes 196640 | tf_op jit(solution)/shard_map/ppermute | solution.py:421
  26.2 0.0 collective-permute-done.5.refs_3_
  26.2 0.1 shard_map.43
  26.2 0.1 collective-permute-start.7
  26.3 0.2 shard_map.44
  26.5 0.1 collective-permute-start.6
  26.6 2.7 %collective-permute-done.8.refs_0_.refs_1_.refs_2_.refs_5_ = f32[2,4,32,512]{3,2,1,0:T(8,128)S(1)} collective-permute-done((f32[2,4,32,512]{3,2,1,0:T(8,128)S(1)}, f32[2,4,32,512]{3,2,1,0:T(8,128)S(1)}, u32[]{:S(2)}, u32[]{:S(2)}) %collective-permute-start.8) | collective-permute-done | bytes 524320 | tf_op jit(solution)/shard_map/ppermute | solution.py:451
  29.3 0.1 shard_map.45
  29.4 2.9 %collective-permute-start.13 = (f32[2,4,16,512]{3,2,1,0:T(8,128)S(1)}, f32[2,4,16,512]{3,2,1,0:T(8,128)S(1)}, u32[]{:S(2)}, u32[]{:S(2)}) collective-permute-start(f32[2,4,16,512]{3,2,1,0:T(8,128)S(1)} %get-tuple-element.41.refs_3_.refs_5_), channel_id=1, source_target_pairs={{0,28},{4,8},{8,4},{12,16},{16,12},{20,24},{24,20},{28,0},{1,29},{... | collective-permute-start | bytes 786440 | tf_op jit(solution)/shard_map/ppermute | solution.py:438
  32.2 0.1 shard_map.46
  32.3 1.6 %collective-permute-start.11 = (f32[2,2,16,512]{3,2,1,0:T(8,128)S(1)}, f32[2,2,16,512]{3,2,1,0:T(8,128)S(1)}, u32[]{:S(2)}, u32[]{:S(2)}) collective-permute-start(f32[2,2,16,512]{3,2,1,0:T(8,128)S(1)} %get-tuple-element.45), channel_id=1, source_target_pairs={{0,1},{1,0},{2,3},{3,2},{4,5},{5,4},{6,7},{7,6},{8,9},{9,8},{10,11... | collective-permute-start | bytes 393224 | tf_op jit(solution)/shard_map/ppermute | solution.py:430
  34.0 0.0 collective-permute-done.7.refs_2_
  34.0 2.5 %shard_map.47 = (f32[4,2,20,512]{3,2,1,0:T(8,128)S(1)}, f32[4,2,16,512]{3,2,1,0:T(8,128)S(1)}, f32[4,2,16,512]{3,2,1,0:T(8,128)S(1)}) custom-call(f32[3]{0:T(128)S(1)} %copy-done.3, f32[4,4,24,512]{3,2,1,0:T(8,128)S(1)} %get-tuple-element.38.refs_3_.refs_1_, f32[4,4,24,512]{3,2,1,0:T(8,128)S(1)} %collective-permute-done.7.refs_2_, ...), custom_call_target="tpu_custom_call" | custom-call | bytes 6619148 | tf_op jit(solution)/shard_map/pallas_call | solution.py:364
  36.5 2.5 %collective-permute-start.9 = (f32[2,32,512]{2,1,0:T(8,128)S(1)}, f32[2,32,512]{2,1,0:T(8,128)S(1)}, u32[]{:S(2)}, u32[]{:S(2)}) collective-permute-start(f32[2,32,512]{2,1,0:T(8,128)S(1)} %shard_map.48.refs_7_), channel_id=1, source_target_pairs={{0,3},{1,2},{2,1},{3,0},{4,7},{5,6},{6,5},{7,4},{8,11},{9,10},{10,... | collective-permute-start | bytes 393224 | tf_op jit(solution)/shard_map/ppermute | solution.py:410
  39.0 2.4 %shard_map.49.refs_2_ = f32[2,256,512]{2,1,0:T(8,128)S(1)} custom-call(f32[3]{0:T(128)S(1)} %copy-done.3, f32[4,256,512]{2,1,0:T(8,128)S(1)} %bitcast.13, f32[4,256,512]{2,1,0:T(8,128)S(1)} %copy-done.2, f32[2,256,512]{2,1,0:T(8,128)S(1)} %get-tuple-element.37.refs_2_.refs_3_, f32[2,4,32,512]{3,2,1,0:T(8,128)S(1)} %shard_map.42.refs_4_, ...), custom_call_target="tpu_custom_call" | custom-call | flops 10485760 | bytes 7340044 | tf_op jit(solution)/shard_map/pallas_call | solution.py:364
  41.5 1.4 %collective-permute-start.12 = (f32[2,16,512]{2,1,0:T(8,128)S(1)}, f32[2,16,512]{2,1,0:T(8,128)S(1)}, u32[]{:S(2)}, u32[]{:S(2)}) collective-permute-start(f32[2,16,512]{2,1,0:T(8,128)S(1)} %shard_map.50.refs_3_), channel_id=1, source_target_pairs={{0,3},{1,2},{2,1},{3,0},{4,7},{5,6},{6,5},{7,4},{8,11},{9,10},{10,... | collective-permute-start | bytes 196616 | tf_op jit(solution)/shard_map/ppermute | solution.py:410
  42.9 0.9 %collective-permute-start.14 = (f32[120,512]{1,0:T(8,128)S(1)}, f32[120,512]{1,0:T(8,128)S(1)}, u32[]{:S(2)}, u32[]{:S(2)}) collective-permute-start(f32[120,512]{1,0:T(8,128)S(1)} %get-tuple-element.48), channel_id=1, source_target_pairs={{0,28},{4,8},{8,4},{12,16},{16,12},{20,24},{24,20},{28,0},{1,29},{... | collective-permute-start | bytes 737288 | tf_op jit(solution)/shard_map/ppermute | solution.py:477
  43.7 0.1 shard_map.51
  43.8 0.1 collective-permute-start.15
  44.0 1.5 %collective-permute-done.13.refs_1_ = f32[2,4,16,512]{3,2,1,0:T(8,128)S(1)} collective-permute-done((f32[2,4,16,512]{3,2,1,0:T(8,128)S(1)}, f32[2,4,16,512]{3,2,1,0:T(8,128)S(1)}, u32[]{:S(2)}, u32[]{:S(2)}) %collective-permute-start.13) | collective-permute-done | bytes 262176 | tf_op jit(solution)/shard_map/ppermute | solution.py:438
  45.5 0.1 shard_map.53
  45.6 2.8 %collective-permute-start.16 = (f32[2,2,16,512]{3,2,1,0:T(8,128)S(1)}, f32[2,2,16,512]{3,2,1,0:T(8,128)S(1)}, u32[]{:S(2)}, u32[]{:S(2)}) collective-permute-start(f32[2,2,16,512]{3,2,1,0:T(8,128)S(1)} %get-tuple-element.53), channel_id=1, source_target_pairs={{0,1},{1,0},{2,3},{3,2},{4,5},{5,4},{6,7},{7,6},{8,9},{9,8},{10,11... | collective-permute-start | bytes 393224 | tf_op jit(solution)/shard_map/ppermute | solution.py:418
  48.4 4.8 %collective-permute-done.15.refs_1_ = f32[2,2,32,512]{3,2,1,0:T(8,128)S(1)} collective-permute-done((f32[2,2,32,512]{3,2,1,0:T(8,128)S(1)}, f32[2,2,32,512]{3,2,1,0:T(8,128)S(1)}, u32[]{:S(2)}, u32[]{:S(2)}) %collective-permute-start.15) | collective-permute-done | bytes 262176 | tf_op jit(solution)/shard_map/ppermute | solution.py:418
  53.2 2.4 %collective-permute-start.17 = (f32[2,32,512]{2,1,0:T(8,128)S(1)}, f32[2,32,512]{2,1,0:T(8,128)S(1)}, u32[]{:S(2)}, u32[]{:S(2)}) collective-permute-start(f32[2,32,512]{2,1,0:T(8,128)S(1)} %shard_map.55.refs_4_), channel_id=1, source_target_pairs={{0,3},{1,2},{2,1},{3,0},{4,7},{5,6},{6,5},{7,4},{8,11},{9,10},{10,... | collective-permute-start | bytes 393224 | tf_op jit(solution)/shard_map/ppermute | solution.py:410
  55.6 0.1 shard_map.56
  55.7 1.0 %collective-permute-start.19 = (f32[4,2,16,512]{3,2,1,0:T(8,128)S(1)}, f32[4,2,16,512]{3,2,1,0:T(8,128)S(1)}, u32[]{:S(2)}, u32[]{:S(2)}) collective-permute-start(f32[4,2,16,512]{3,2,1,0:T(8,128)S(1)} %get-tuple-element.55), channel_id=1, source_target_pairs={{0,28},{4,8},{8,4},{12,16},{16,12},{20,24},{24,20},{28,0},{1,29},{... | collective-permute-start | bytes 786440 | tf_op jit(solution)/shard_map/ppermute | solution.py:507
  56.8 1.6 %collective-permute-start.18 = (f32[2,16,512]{2,1,0:T(8,128)S(1)}, f32[2,16,512]{2,1,0:T(8,128)S(1)}, u32[]{:S(2)}, u32[]{:S(2)}) collective-permute-start(f32[2,16,512]{2,1,0:T(8,128)S(1)} %shard_map.57.refs_9_), channel_id=1, source_target_pairs={{0,3},{1,2},{2,1},{3,0},{4,7},{5,6},{6,5},{7,4},{8,11},{9,10},{10,... | collective-permute-start | bytes 196616 | tf_op jit(solution)/shard_map/ppermute | solution.py:410
  58.3 1.2 %shard_map.58 = (f32[2,16,512]{2,1,0:T(8,128)S(1)}, f32[4,2,16,512]{3,2,1,0:T(8,128)S(1)}) custom-call(f32[3]{0:T(128)S(1)} %copy-done.3, f32[4,4,24,512]{3,2,1,0:T(8,128)S(1)} %get-tuple-element.38.refs_3_.refs_1_, f32[4,4,64,512]{3,2,1,0:T(8,128)S(1)} %bitcast.15, f32[120,512]{1,0:T(8,128)S(1)} %collective-permute-done.14.refs_0_.refs_3_, ...), custom_call_target="tpu_custom_call" | custom-call | bytes 5357580 | tf_op jit(solution)/shard_map/pallas_call | solution.py:364
  59.5 1.2 %collective-permute-done.17.refs_2_ = f32[2,32,512]{2,1,0:T(8,128)S(1)} collective-permute-done((f32[2,32,512]{2,1,0:T(8,128)S(1)}, f32[2,32,512]{2,1,0:T(8,128)S(1)}, u32[]{:S(2)}, u32[]{:S(2)}) %collective-permute-start.17) | collective-permute-done | bytes 131104 | tf_op jit(solution)/shard_map/ppermute | solution.py:410
  60.7 2.2 %collective-permute-done.18.refs_2_ = f32[2,16,512]{2,1,0:T(8,128)S(1)} collective-permute-done((f32[2,16,512]{2,1,0:T(8,128)S(1)}, f32[2,16,512]{2,1,0:T(8,128)S(1)}, u32[]{:S(2)}, u32[]{:S(2)}) %collective-permute-start.18) | collective-permute-done | bytes 65568 | tf_op jit(solution)/shard_map/ppermute | solution.py:410
  63.0 2.0 %collective-permute-done.19.refs_6_ = f32[4,2,16,512]{3,2,1,0:T(8,128)S(1)} collective-permute-done((f32[4,2,16,512]{3,2,1,0:T(8,128)S(1)}, f32[4,2,16,512]{3,2,1,0:T(8,128)S(1)}, u32[]{:S(2)}, u32[]{:S(2)}) %collective-permute-start.19) | collective-permute-done | bytes 262176 | tf_op jit(solution)/shard_map/ppermute | solution.py:507
  64.9 0.9 %shard_map.61 = f32[4,64,512]{2,1,0:T(8,128)} custom-call(f32[2,32,512]{2,1,0:T(8,128)S(1)} %shard_map.52.refs_3_.refs_0_, f32[2,16,512]{2,1,0:T(8,128)S(1)} %shard_map.54.refs_2_.refs_1_, f32[2,16,512]{2,1,0:T(8,128)S(1)} %get-tuple-element.54.refs_3_.refs_2_, f32[2,32,512]{2,1,0:T(8,128)S(1)} %shard_map.59.refs_3_, ...), custom_call_target="tpu_custom_call" | custom-call | bytes 1523712 | tf_op jit(solution)/shard_map/pallas_call | solution.py:364
  (25 shorter events, 0.3 us)
Async XLA Ops:
  0.0 10.2 %collective-permute-start = (f32[4,256,512]{2,1,0:T(8,128)}, f32[4,256,512]{2,1,0:T(8,128)S(1)}, u32[]{:S(2)}, u32[]{:S(2)}) collective-permute-start(f32[4,256,512]{2,1,0:T(8,128)} %bitcast.7), channel_id=1, source_target_pairs={{0,4},{4,0},{8,12},{12,8},{16,20},{20,16},{24,28},{28,24},{1,5},{5... | collective-permute-start | bytes 6291464 | tf_op jit(solution)/shard_map/ppermute | solution.py:440
  0.5 9.8 %collective-permute-start.1 = (f32[4,256,512]{2,1,0:T(8,128)}, f32[4,256,512]{2,1,0:T(8,128)S(1)}, u32[]{:S(2)}, u32[]{:S(2)}) collective-permute-start(f32[4,256,512]{2,1,0:T(8,128)} %refs_2_.3), channel_id=1, source_target_pairs={{0,4},{4,0},{8,12},{12,8},{16,20},{20,16},{24,28},{28,24},{1,5},{5... | collective-permute-start | bytes 6291464 | tf_op jit(solution)/shard_map/ppermute | solution.py:441
  0.5 1.6 %copy-start = (f32[1,4,256,512]{3,2,1,0:T(8,128)S(1)}, f32[1,4,256,512]{3,2,1,0:T(8,128)}, u32[]{:S(2)}) copy-start(f32[1,4,256,512]{3,2,1,0:T(8,128)} %param.3) | copy-start | bytes 6291460
  2.2 15.9 %collective-permute-start.2 = (f32[2,4,32,512]{3,2,1,0:T(8,128)S(1)}, f32[2,4,32,512]{3,2,1,0:T(8,128)S(1)}, u32[]{:S(2)}, u32[]{:S(2)}) collective-permute-start(f32[2,4,32,512]{3,2,1,0:T(8,128)S(1)} %shard_map.37.refs_1_), channel_id=1, source_target_pairs={{0,28},{4,8},{8,4},{12,16},{16,12},{20,24},{24,20},{28,0},{1,29},{... | collective-permute-start | bytes 1572872 | tf_op jit(solution)/shard_map/ppermute | solution.py:451
  5.8 5.1 %copy-start.2 = (f32[4,256,512]{2,1,0:T(8,128)S(1)}, f32[4,256,512]{2,1,0:T(8,128)}, u32[]{:S(2)}) copy-start(f32[4,256,512]{2,1,0:T(8,128)} %refs_2_.3) | copy-start | bytes 6291460
  5.8 23.5 %collective-permute-start.8 = (f32[2,4,32,512]{3,2,1,0:T(8,128)S(1)}, f32[2,4,32,512]{3,2,1,0:T(8,128)S(1)}, u32[]{:S(2)}, u32[]{:S(2)}) collective-permute-start(f32[2,4,32,512]{3,2,1,0:T(8,128)S(1)} %shard_map.38.refs_1_), channel_id=1, source_target_pairs={{0,28},{4,8},{8,4},{12,16},{16,12},{20,24},{24,20},{28,0},{1,29},{... | collective-permute-start | bytes 1572872 | tf_op jit(solution)/shard_map/ppermute | solution.py:451
  6.0 15.0 %collective-permute-start.3 = (f32[4,24,512]{2,1,0:T(8,128)S(1)}, f32[4,24,512]{2,1,0:T(8,128)S(1)}, u32[]{:S(2)}, u32[]{:S(2)}) collective-permute-start(f32[4,24,512]{2,1,0:T(8,128)S(1)} %get-tuple-element.34), channel_id=1, source_target_pairs={{0,3},{1,2},{2,1},{3,0},{4,7},{5,6},{6,5},{7,4},{8,11},{9,10},{10,... | collective-permute-start | bytes 589832 | tf_op jit(solution)/shard_map/ppermute | solution.py:421
  10.2 16.0 %collective-permute-start.4 = (f32[4,24,512]{2,1,0:T(8,128)S(1)}, f32[4,24,512]{2,1,0:T(8,128)S(1)}, u32[]{:S(2)}, u32[]{:S(2)}) collective-permute-start(f32[4,24,512]{2,1,0:T(8,128)S(1)} %get-tuple-element.35), channel_id=1, source_target_pairs={{0,2},{1,3},{2,0},{3,1},{4,6},{5,7},{6,4},{7,5},{8,10},{9,11},{10,... | collective-permute-start | bytes 589832 | tf_op jit(solution)/shard_map/ppermute | solution.py:421
  10.2 16.0 %collective-permute-start.5 = (f32[4,24,512]{2,1,0:T(8,128)S(1)}, f32[4,24,512]{2,1,0:T(8,128)S(1)}, u32[]{:S(2)}, u32[]{:S(2)}) collective-permute-start(f32[4,24,512]{2,1,0:T(8,128)S(1)} %get-tuple-element.36), channel_id=1, source_target_pairs={{0,1},{1,0},{2,3},{3,2},{4,5},{5,4},{6,7},{7,6},{8,9},{9,8},{10,11... | collective-permute-start | bytes 589832 | tf_op jit(solution)/shard_map/ppermute | solution.py:421
  10.9 1.6 %copy-start.3 = (f32[3]{0:T(128)S(1)}, f32[3]{0:T(128)}, u32[]{:S(2)}) copy-start(f32[3]{0:T(128)} %refs_0_.7) | copy-start | bytes 40
  18.2 25.5 %collective-permute-start.10 = (f32[2,4,32,512]{3,2,1,0:T(8,128)S(1)}, f32[2,4,32,512]{3,2,1,0:T(8,128)S(1)}, u32[]{:S(2)}, u32[]{:S(2)}) collective-permute-start(f32[2,4,32,512]{3,2,1,0:T(8,128)S(1)} %shard_map.42.refs_4_), channel_id=1, source_target_pairs={{0,28},{4,8},{8,4},{12,16},{16,12},{20,24},{24,20},{28,0},{1,29},{... | collective-permute-start | bytes 1572872 | tf_op jit(solution)/shard_map/ppermute | solution.py:438
  26.2 7.7 %collective-permute-start.7 = (f32[4,4,24,512]{3,2,1,0:T(8,128)S(1)}, f32[4,4,24,512]{3,2,1,0:T(8,128)S(1)}, u32[]{:S(2)}, u32[]{:S(2)}) collective-permute-start(f32[4,4,24,512]{3,2,1,0:T(8,128)S(1)} %get-tuple-element.38.refs_3_.refs_1_), channel_id=1, source_target_pairs={{0,4},{4,0},{8,12},{12,8},{16,20},{20,16},{24,28},{28,24},{1,5},{5... | collective-permute-start | bytes 2359304 | tf_op jit(solution)/shard_map/ppermute | solution.py:476
  26.5 10.0 %collective-permute-start.6 = (f32[2,2,32,512]{3,2,1,0:T(8,128)S(1)}, f32[2,2,32,512]{3,2,1,0:T(8,128)S(1)}, u32[]{:S(2)}, u32[]{:S(2)}) collective-permute-start(f32[2,2,32,512]{3,2,1,0:T(8,128)S(1)} %get-tuple-element.40), channel_id=1, source_target_pairs={{0,1},{1,0},{2,3},{3,2},{4,5},{5,4},{6,7},{7,6},{8,9},{9,8},{10,11... | collective-permute-start | bytes 786440 | tf_op jit(solution)/shard_map/ppermute | solution.py:430
  29.4 16.1 %collective-permute-start.13 = (f32[2,4,16,512]{3,2,1,0:T(8,128)S(1)}, f32[2,4,16,512]{3,2,1,0:T(8,128)S(1)}, u32[]{:S(2)}, u32[]{:S(2)}) collective-permute-start(f32[2,4,16,512]{3,2,1,0:T(8,128)S(1)} %get-tuple-element.41.refs_3_.refs_5_), channel_id=1, source_target_pairs={{0,28},{4,8},{8,4},{12,16},{16,12},{20,24},{24,20},{28,0},{1,29},{... | collective-permute-start | bytes 786440 | tf_op jit(solution)/shard_map/ppermute | solution.py:438
  32.3 9.1 %collective-permute-start.11 = (f32[2,2,16,512]{3,2,1,0:T(8,128)S(1)}, f32[2,2,16,512]{3,2,1,0:T(8,128)S(1)}, u32[]{:S(2)}, u32[]{:S(2)}) collective-permute-start(f32[2,2,16,512]{3,2,1,0:T(8,128)S(1)} %get-tuple-element.45), channel_id=1, source_target_pairs={{0,1},{1,0},{2,3},{3,2},{4,5},{5,4},{6,7},{7,6},{8,9},{9,8},{10,11... | collective-permute-start | bytes 393224 | tf_op jit(solution)/shard_map/ppermute | solution.py:430
  34.0 5.1 %copy-start.1 = (f32[1,4,256,512]{3,2,1,0:T(8,128)S(1)}, f32[1,4,256,512]{3,2,1,0:T(8,128)}, u32[]{:S(2)}) copy-start(f32[1,4,256,512]{3,2,1,0:T(8,128)} %param.3) | copy-start | bytes 6291460
  36.5 7.4 %collective-permute-start.9 = (f32[2,32,512]{2,1,0:T(8,128)S(1)}, f32[2,32,512]{2,1,0:T(8,128)S(1)}, u32[]{:S(2)}, u32[]{:S(2)}) collective-permute-start(f32[2,32,512]{2,1,0:T(8,128)S(1)} %shard_map.48.refs_7_), channel_id=1, source_target_pairs={{0,3},{1,2},{2,1},{3,0},{4,7},{5,6},{6,5},{7,4},{8,11},{9,10},{10,... | collective-permute-start | bytes 393224 | tf_op jit(solution)/shard_map/ppermute | solution.py:410
  41.5 6.9 %collective-permute-start.12 = (f32[2,16,512]{2,1,0:T(8,128)S(1)}, f32[2,16,512]{2,1,0:T(8,128)S(1)}, u32[]{:S(2)}, u32[]{:S(2)}) collective-permute-start(f32[2,16,512]{2,1,0:T(8,128)S(1)} %shard_map.50.refs_3_), channel_id=1, source_target_pairs={{0,3},{1,2},{2,1},{3,0},{4,7},{5,6},{6,5},{7,4},{8,11},{9,10},{10,... | collective-permute-start | bytes 196616 | tf_op jit(solution)/shard_map/ppermute | solution.py:410
  42.9 12.8 %collective-permute-start.14 = (f32[120,512]{1,0:T(8,128)S(1)}, f32[120,512]{1,0:T(8,128)S(1)}, u32[]{:S(2)}, u32[]{:S(2)}) collective-permute-start(f32[120,512]{1,0:T(8,128)S(1)} %get-tuple-element.48), channel_id=1, source_target_pairs={{0,28},{4,8},{8,4},{12,16},{16,12},{20,24},{24,20},{28,0},{1,29},{... | collective-permute-start | bytes 737288 | tf_op jit(solution)/shard_map/ppermute | solution.py:477
  43.8 9.4 %collective-permute-start.15 = (f32[2,2,32,512]{3,2,1,0:T(8,128)S(1)}, f32[2,2,32,512]{3,2,1,0:T(8,128)S(1)}, u32[]{:S(2)}, u32[]{:S(2)}) collective-permute-start(f32[2,2,32,512]{3,2,1,0:T(8,128)S(1)} %get-tuple-element.49), channel_id=1, source_target_pairs={{0,1},{1,0},{2,3},{3,2},{4,5},{5,4},{6,7},{7,6},{8,9},{9,8},{10,11... | collective-permute-start | bytes 786440 | tf_op jit(solution)/shard_map/ppermute | solution.py:418
  45.6 11.2 %collective-permute-start.16 = (f32[2,2,16,512]{3,2,1,0:T(8,128)S(1)}, f32[2,2,16,512]{3,2,1,0:T(8,128)S(1)}, u32[]{:S(2)}, u32[]{:S(2)}) collective-permute-start(f32[2,2,16,512]{3,2,1,0:T(8,128)S(1)} %get-tuple-element.53), channel_id=1, source_target_pairs={{0,1},{1,0},{2,3},{3,2},{4,5},{5,4},{6,7},{7,6},{8,9},{9,8},{10,11... | collective-permute-start | bytes 393224 | tf_op jit(solution)/shard_map/ppermute | solution.py:418
  53.2 7.5 %collective-permute-start.17 = (f32[2,32,512]{2,1,0:T(8,128)S(1)}, f32[2,32,512]{2,1,0:T(8,128)S(1)}, u32[]{:S(2)}, u32[]{:S(2)}) collective-permute-start(f32[2,32,512]{2,1,0:T(8,128)S(1)} %shard_map.55.refs_4_), channel_id=1, source_target_pairs={{0,3},{1,2},{2,1},{3,0},{4,7},{5,6},{6,5},{7,4},{8,11},{9,10},{10,... | collective-permute-start | bytes 393224 | tf_op jit(solution)/shard_map/ppermute | solution.py:410
  55.7 9.2 %collective-permute-start.19 = (f32[4,2,16,512]{3,2,1,0:T(8,128)S(1)}, f32[4,2,16,512]{3,2,1,0:T(8,128)S(1)}, u32[]{:S(2)}, u32[]{:S(2)}) collective-permute-start(f32[4,2,16,512]{3,2,1,0:T(8,128)S(1)} %get-tuple-element.55), channel_id=1, source_target_pairs={{0,28},{4,8},{8,4},{12,16},{16,12},{20,24},{24,20},{28,0},{1,29},{... | collective-permute-start | bytes 786440 | tf_op jit(solution)/shard_map/ppermute | solution.py:507
  56.8 6.2 %collective-permute-start.18 = (f32[2,16,512]{2,1,0:T(8,128)S(1)}, f32[2,16,512]{2,1,0:T(8,128)S(1)}, u32[]{:S(2)}, u32[]{:S(2)}) collective-permute-start(f32[2,16,512]{2,1,0:T(8,128)S(1)} %shard_map.57.refs_9_), channel_id=1, source_target_pairs={{0,3},{1,2},{2,1},{3,0},{4,7},{5,6},{6,5},{7,4},{8,11},{9,10},{10,... | collective-permute-start | bytes 196616 | tf_op jit(solution)/shard_map/ppermute | solution.py:410

commit v17 on v16

--- a/solution.py
+++ b/solution.py
@@ -498,13 +498,13 @@
     back0 = summed(*back0)
     front_b = squares(cut_b, face_b)
     back1 = summed(*back1, weight=4_000_000_000)
-    front_a = add_far(*front_a)
     x_f, piece = call(
         functools.partial(rows_face_kernel, cut_c),
         [(bands, 2, inner, lanes), (bands, 2, part, lanes)],
         (x_halo, *halos, x_first),
     )
     x_face = lax.ppermute(piece, "slab", face)
+    front_a = add_far(*front_a)
     front_b = add_far(*front_b)
     back2, x_front = call(
         functools.partial(rows_front_kernel, cut_c),
@@ -513,7 +513,7 @@
         scalars=1,
     )
     front_a = summed(*front_a)
-    front_b = summed(*front_b, weight=2_000_000_000)
+    front_b = summed(*front_b, weight=1_000_000_000)
     places = [(2, cut) for cut in cuts] + [(0, cut_a), (0, cut_b)]
     return call(
         functools.partial(join_kernel, places, cut_c),

time: 66 us -> 64.2 us (0.973)
  waiting for transfers between devices: 19.7 us -> 16.5 us
  starting transfers between devices: 29.2 us -> 30.5 us
    ppermute x2, waiting for transfers between devices: 4.84 us -> 0.02 us  [squares(): return (keep, lax.ppermute(send, 'orb', near))]
    ppermute x1, waiting for transfers between devices: 0.01 us -> 3.45 us  [shards(): x_halo = lax.ppermute(piece, 'slab', face)]
    ppermute x1, waiting for transfers between devices: 1.99 us -> 0.01 us  [shards(): x_face = lax.ppermute(piece, 'slab', face)]
    ppermute x4, starting transfers between devices: 7.96 us -> 9.06 us  [add_far(): return (keep, came, lax.ppermute(total, 'orb', far))]
  transfers between devices with their start and end apart: 20 -> 20, of which waited for: 7 -> 6; matrix products, arithmetic and copies ran while one was open for 0% -> 0% of each run, Pallas kernels for 22% -> 22%
where the time goes in v17:
time: 64.2 us; the launch traced here: 64.1 us
  starting transfers between devices  30.5 us (48%)
  waiting for transfers between devices  16.5 us (26%)
  Pallas kernels  15.2 us (24%)
  local copies, waits for them, and re-layouts  1.6 us (2%)
    pallas_call x25, Pallas kernels, __call__(): pl.pallas_call(body, out_shape=shapes, in_specs=[smem] * scalars + [pl.Bl...  15.2 us
    ppermute x4, starting transfers between devices, add_far(): return (keep, came, lax.ppermute(total, 'orb', far))  9.06 us
    ppermute x2, starting transfers between devices, faces(): return (fs, lax.ppermute(fs[0], 'slab', face))  5.69 us
    ppermute x3, waiting for transfers between devices, over_orb(): return lax.ppermute(x, 'orb', [(i, i ^ d) for i in range(bands)])  5.15 us
    ppermute x3, starting transfers between devices, over_orb(): return lax.ppermute(x, 'orb', [(i, i ^ d) for i in range(bands)])  4.88 us
    ppermute x2, starting transfers between devices, shards(): halos.append(lax.ppermute(piece, 'slab', face))  3.66 us
    ppermute x4, waiting for transfers between devices, add_far(): return (keep, came, lax.ppermute(total, 'orb', far))  3.63 us
    ppermute x1, waiting for transfers between devices, shards(): x_halo = lax.ppermute(piece, 'slab', face)  3.45 us
  transfers between devices with their start and end apart: 20, of which 6 were waited for; matrix products, arithmetic and copies ran while one was open for 0% of the time, Pallas kernels for 22%

profile of v17, /device:TPU:0, one launch (start us, length us, event | category | flops | bytes accessed | tf_op | source)
XLA Modules:
  0.0 64.1 jit_solution(11839616344433846845)
XLA Ops:
  0.0 0.5 collective-permute-start
  0.5 0.1 collective-permute-start.1
  0.5 1.6 %copy-done = f32[1,4,256,512]{3,2,1,0:T(8,128)S(1)} copy-done((f32[1,4,256,512]{3,2,1,0:T(8,128)S(1)}, f32[1,4,256,512]{3,2,1,0:T(8,128)}, u32[]{:S(2)}) %copy-start) | copy-done | bytes 2097176
  2.2 3.6 %collective-permute-start.2 = (f32[2,4,32,512]{3,2,1,0:T(8,128)S(1)}, f32[2,4,32,512]{3,2,1,0:T(8,128)S(1)}, u32[]{:S(2)}, u32[]{:S(2)}) collective-permute-start(f32[2,4,32,512]{3,2,1,0:T(8,128)S(1)} %shard_map.37.refs_1_), channel_id=1, source_target_pairs={{0,28},{4,8},{8,4},{12,16},{16,12},{20,24},{24,20},{28,0},{1,29},{... | collective-permute-start | bytes 1572872 | tf_op jit(solution)/shard_map/ppermute | solution.py:451
  5.8 0.0 copy-start.2
  5.8 0.1 collective-permute-start.8
  5.9 0.1 shard_map.39
  6.0 4.2 %collective-permute-start.3 = (f32[4,24,512]{2,1,0:T(8,128)S(1)}, f32[4,24,512]{2,1,0:T(8,128)S(1)}, u32[]{:S(2)}, u32[]{:S(2)}) collective-permute-start(f32[4,24,512]{2,1,0:T(8,128)S(1)} %get-tuple-element.34), channel_id=1, source_target_pairs={{0,3},{1,2},{2,1},{3,0},{4,7},{5,6},{6,5},{7,4},{8,11},{9,10},{10,... | collective-permute-start | bytes 589832 | tf_op jit(solution)/shard_map/ppermute | solution.py:421
  10.2 0.0 collective-permute-done.refs_3_
  10.2 0.0 collective-permute-start.4
  10.2 0.0 collective-permute-done.1.refs_4_
  10.2 0.6 %collective-permute-start.5 = (f32[4,24,512]{2,1,0:T(8,128)S(1)}, f32[4,24,512]{2,1,0:T(8,128)S(1)}, u32[]{:S(2)}, u32[]{:S(2)}) collective-permute-start(f32[4,24,512]{2,1,0:T(8,128)S(1)} %get-tuple-element.36), channel_id=1, source_target_pairs={{0,1},{1,0},{2,3},{3,2},{4,5},{5,4},{6,7},{7,6},{8,9},{9,8},{10,11... | collective-permute-start | bytes 589832 | tf_op jit(solution)/shard_map/ppermute | solution.py:421
  10.9 1.6 %shard_map.40.refs_5_.refs_6_ = f32[2,256,512]{2,1,0:T(8,128)S(1)} custom-call(f32[4,256,512]{2,1,0:T(8,128)S(1)} %bitcast.11, f32[4,256,512]{2,1,0:T(8,128)S(1)} %copy-done.2, f32[4,24,512]{2,1,0:T(8,128)S(1)} %get-tuple-element.31.refs_2_.refs_0_), custom_call_target="tpu_custom_call" | custom-call | flops 6291456 | bytes 5242880 | tf_op jit(solution)/shard_map/pallas_call | solution.py:364
  12.5 5.6 %shard_map.41 = (f32[2,256,512]{2,1,0:T(8,128)S(1)}, f32[2,256,512]{2,1,0:T(8,128)S(1)}, f32[8,512]{1,0:T(8,128)S(1)}) custom-call(f32[3]{0:T(128)S(1)} %copy-done.3, f32[4,256,512]{2,1,0:T(8,128)S(1)} %bitcast.12, f32[4,256,512]{2,1,0:T(8,128)S(1)} %copy-done.2, f32[4,256,512]{2,1,0:T(8,128)S(1)} %collective-permute-done.refs_3_, ...), custom_call_target="tpu_custom_call" | custom-call | flops 20971520 | bytes 11550732 | tf_op jit(solution)/shard_map/pallas_call | solution.py:364
  18.1 0.0 collective-permute-done.2.refs_0_.refs_1_.refs_4_
  18.1 0.1 shard_map.42.refs_4_
  18.2 2.8 %collective-permute-start.10 = (f32[2,4,32,512]{3,2,1,0:T(8,128)S(1)}, f32[2,4,32,512]{3,2,1,0:T(8,128)S(1)}, u32[]{:S(2)}, u32[]{:S(2)}) collective-permute-start(f32[2,4,32,512]{3,2,1,0:T(8,128)S(1)} %shard_map.42.refs_4_), channel_id=1, source_target_pairs={{0,28},{4,8},{8,4},{12,16},{16,12},{20,24},{24,20},{28,0},{1,29},{... | collective-permute-start | bytes 1572872 | tf_op jit(solution)/shard_map/ppermute | solution.py:438
  21.0 5.1 %collective-permute-done.4.refs_2_ = f32[4,24,512]{2,1,0:T(8,128)S(1)} collective-permute-done((f32[4,24,512]{2,1,0:T(8,128)S(1)}, f32[4,24,512]{2,1,0:T(8,128)S(1)}, u32[]{:S(2)}, u32[]{:S(2)}) %collective-permute-start.4) | collective-permute-done | bytes 196640 | tf_op jit(solution)/shard_map/ppermute | solution.py:421
  26.2 0.0 collective-permute-done.5.refs_3_
  26.2 0.1 shard_map.43
  26.2 0.1 collective-permute-start.7
  26.3 0.2 shard_map.44
  26.5 0.1 collective-permute-start.6
  26.6 2.7 %collective-permute-done.8.refs_0_.refs_1_.refs_2_.refs_5_ = f32[2,4,32,512]{3,2,1,0:T(8,128)S(1)} collective-permute-done((f32[2,4,32,512]{3,2,1,0:T(8,128)S(1)}, f32[2,4,32,512]{3,2,1,0:T(8,128)S(1)}, u32[]{:S(2)}, u32[]{:S(2)}) %collective-permute-start.8) | collective-permute-done | bytes 524320 | tf_op jit(solution)/shard_map/ppermute | solution.py:451
  29.3 0.1 shard_map.45
  29.4 2.9 %collective-permute-start.13 = (f32[2,4,16,512]{3,2,1,0:T(8,128)S(1)}, f32[2,4,16,512]{3,2,1,0:T(8,128)S(1)}, u32[]{:S(2)}, u32[]{:S(2)}) collective-permute-start(f32[2,4,16,512]{3,2,1,0:T(8,128)S(1)} %get-tuple-element.41.refs_3_.refs_5_), channel_id=1, source_target_pairs={{0,28},{4,8},{8,4},{12,16},{16,12},{20,24},{24,20},{28,0},{1,29},{... | collective-permute-start | bytes 786440 | tf_op jit(solution)/shard_map/ppermute | solution.py:438
  32.2 0.1 shard_map.46
  32.3 1.6 %collective-permute-start.11 = (f32[2,2,16,512]{3,2,1,0:T(8,128)S(1)}, f32[2,2,16,512]{3,2,1,0:T(8,128)S(1)}, u32[]{:S(2)}, u32[]{:S(2)}) collective-permute-start(f32[2,2,16,512]{3,2,1,0:T(8,128)S(1)} %get-tuple-element.45), channel_id=1, source_target_pairs={{0,1},{1,0},{2,3},{3,2},{4,5},{5,4},{6,7},{7,6},{8,9},{9,8},{10,11... | collective-permute-start | bytes 393224 | tf_op jit(solution)/shard_map/ppermute | solution.py:430
  34.0 2.5 %shard_map.47 = (f32[4,2,20,512]{3,2,1,0:T(8,128)S(1)}, f32[4,2,16,512]{3,2,1,0:T(8,128)S(1)}, f32[4,2,16,512]{3,2,1,0:T(8,128)S(1)}) custom-call(f32[3]{0:T(128)S(1)} %copy-done.3, f32[4,4,24,512]{3,2,1,0:T(8,128)S(1)} %get-tuple-element.38.refs_3_.refs_1_, f32[4,4,24,512]{3,2,1,0:T(8,128)S(1)} %collective-permute-done.7.refs_2_, ...), custom_call_target="tpu_custom_call" | custom-call | bytes 6619148 | tf_op jit(solution)/shard_map/pallas_call | solution.py:364
  36.5 2.5 %collective-permute-start.9 = (f32[2,32,512]{2,1,0:T(8,128)S(1)}, f32[2,32,512]{2,1,0:T(8,128)S(1)}, u32[]{:S(2)}, u32[]{:S(2)}) collective-permute-start(f32[2,32,512]{2,1,0:T(8,128)S(1)} %shard_map.48.refs_7_), channel_id=1, source_target_pairs={{0,3},{1,2},{2,1},{3,0},{4,7},{5,6},{6,5},{7,4},{8,11},{9,10},{10,... | collective-permute-start | bytes 393224 | tf_op jit(solution)/shard_map/ppermute | solution.py:410
  39.0 2.4 %shard_map.49.refs_2_ = f32[2,256,512]{2,1,0:T(8,128)S(1)} custom-call(f32[3]{0:T(128)S(1)} %copy-done.3, f32[4,256,512]{2,1,0:T(8,128)S(1)} %bitcast.13, f32[4,256,512]{2,1,0:T(8,128)S(1)} %copy-done.2, f32[2,256,512]{2,1,0:T(8,128)S(1)} %get-tuple-element.37.refs_2_.refs_3_, f32[2,4,32,512]{3,2,1,0:T(8,128)S(1)} %shard_map.42.refs_4_, ...), custom_call_target="tpu_custom_call" | custom-call | flops 10485760 | bytes 7340044 | tf_op jit(solution)/shard_map/pallas_call | solution.py:364
  41.5 1.4 %collective-permute-start.12 = (f32[2,16,512]{2,1,0:T(8,128)S(1)}, f32[2,16,512]{2,1,0:T(8,128)S(1)}, u32[]{:S(2)}, u32[]{:S(2)}) collective-permute-start(f32[2,16,512]{2,1,0:T(8,128)S(1)} %shard_map.50.refs_3_), channel_id=1, source_target_pairs={{0,3},{1,2},{2,1},{3,0},{4,7},{5,6},{6,5},{7,4},{8,11},{9,10},{10,... | collective-permute-start | bytes 196616 | tf_op jit(solution)/shard_map/ppermute | solution.py:410
  42.9 0.9 %collective-permute-start.14 = (f32[120,512]{1,0:T(8,128)S(1)}, f32[120,512]{1,0:T(8,128)S(1)}, u32[]{:S(2)}, u32[]{:S(2)}) collective-permute-start(f32[120,512]{1,0:T(8,128)S(1)} %get-tuple-element.48), channel_id=1, source_target_pairs={{0,28},{4,8},{8,4},{12,16},{16,12},{20,24},{24,20},{28,0},{1,29},{... | collective-permute-start | bytes 737288 | tf_op jit(solution)/shard_map/ppermute | solution.py:477
  43.7 0.1 shard_map.51
  43.8 0.1 collective-permute-start.16
  44.0 1.5 %collective-permute-done.13.refs_1_ = f32[2,4,16,512]{3,2,1,0:T(8,128)S(1)} collective-permute-done((f32[2,4,16,512]{3,2,1,0:T(8,128)S(1)}, f32[2,4,16,512]{3,2,1,0:T(8,128)S(1)}, u32[]{:S(2)}, u32[]{:S(2)}) %collective-permute-start.13) | collective-permute-done | bytes 262176 | tf_op jit(solution)/shard_map/ppermute | solution.py:438
  45.5 0.1 shard_map.53
  45.6 2.8 %collective-permute-start.15 = (f32[2,2,16,512]{3,2,1,0:T(8,128)S(1)}, f32[2,2,16,512]{3,2,1,0:T(8,128)S(1)}, u32[]{:S(2)}, u32[]{:S(2)}) collective-permute-start(f32[2,2,16,512]{3,2,1,0:T(8,128)S(1)} %get-tuple-element.52), channel_id=1, source_target_pairs={{0,1},{1,0},{2,3},{3,2},{4,5},{5,4},{6,7},{7,6},{8,9},{9,8},{10,11... | collective-permute-start | bytes 393224 | tf_op jit(solution)/shard_map/ppermute | solution.py:418
  48.4 3.4 %collective-permute-done.14.refs_0_.refs_3_ = f32[120,512]{1,0:T(8,128)S(1)} collective-permute-done((f32[120,512]{1,0:T(8,128)S(1)}, f32[120,512]{1,0:T(8,128)S(1)}, u32[]{:S(2)}, u32[]{:S(2)}) %collective-permute-start.14) | collective-permute-done | bytes 245792 | tf_op jit(solution)/shard_map/ppermute | solution.py:477
  51.8 0.1 shard_map.55
  51.9 1.3 %collective-permute-start.19 = (f32[4,2,16,512]{3,2,1,0:T(8,128)S(1)}, f32[4,2,16,512]{3,2,1,0:T(8,128)S(1)}, u32[]{:S(2)}, u32[]{:S(2)}) collective-permute-start(f32[4,2,16,512]{3,2,1,0:T(8,128)S(1)} %get-tuple-element.55), channel_id=1, source_target_pairs={{0,28},{4,8},{8,4},{12,16},{16,12},{20,24},{24,20},{28,0},{1,29},{... | collective-permute-start | bytes 786440 | tf_op jit(solution)/shard_map/ppermute | solution.py:506
  53.2 0.0 collective-permute-done.16.refs_1_
  53.2 3.7 %collective-permute-start.17 = (f32[2,32,512]{2,1,0:T(8,128)S(1)}, f32[2,32,512]{2,1,0:T(8,128)S(1)}, u32[]{:S(2)}, u32[]{:S(2)}) collective-permute-start(f32[2,32,512]{2,1,0:T(8,128)S(1)} %shard_map.56.refs_2_), channel_id=1, source_target_pairs={{0,3},{1,2},{2,1},{3,0},{4,7},{5,6},{6,5},{7,4},{8,11},{9,10},{10,... | collective-permute-start | bytes 393224 | tf_op jit(solution)/shard_map/ppermute | solution.py:410
  56.9 1.4 %collective-permute-start.18 = (f32[2,16,512]{2,1,0:T(8,128)S(1)}, f32[2,16,512]{2,1,0:T(8,128)S(1)}, u32[]{:S(2)}, u32[]{:S(2)}) collective-permute-start(f32[2,16,512]{2,1,0:T(8,128)S(1)} %shard_map.57.refs_9_), channel_id=1, source_target_pairs={{0,3},{1,2},{2,1},{3,0},{4,7},{5,6},{6,5},{7,4},{8,11},{9,10},{10,... | collective-permute-start | bytes 196616 | tf_op jit(solution)/shard_map/ppermute | solution.py:410
  58.3 1.2 %shard_map.58 = (f32[2,16,512]{2,1,0:T(8,128)S(1)}, f32[4,2,16,512]{3,2,1,0:T(8,128)S(1)}) custom-call(f32[3]{0:T(128)S(1)} %copy-done.3, f32[4,4,24,512]{3,2,1,0:T(8,128)S(1)} %get-tuple-element.38.refs_3_.refs_1_, f32[4,4,64,512]{3,2,1,0:T(8,128)S(1)} %bitcast.15, f32[120,512]{1,0:T(8,128)S(1)} %collective-permute-done.14.refs_0_.refs_3_, ...), custom_call_target="tpu_custom_call" | custom-call | bytes 5357580 | tf_op jit(solution)/shard_map/pallas_call | solution.py:364
  59.5 1.2 %collective-permute-done.17.refs_2_ = f32[2,32,512]{2,1,0:T(8,128)S(1)} collective-permute-done((f32[2,32,512]{2,1,0:T(8,128)S(1)}, f32[2,32,512]{2,1,0:T(8,128)S(1)}, u32[]{:S(2)}, u32[]{:S(2)}) %collective-permute-start.17) | collective-permute-done | bytes 131104 | tf_op jit(solution)/shard_map/ppermute | solution.py:410
  60.7 2.5 %collective-permute-done.18.refs_2_ = f32[2,16,512]{2,1,0:T(8,128)S(1)} collective-permute-done((f32[2,16,512]{2,1,0:T(8,128)S(1)}, f32[2,16,512]{2,1,0:T(8,128)S(1)}, u32[]{:S(2)}, u32[]{:S(2)}) %collective-permute-start.18) | collective-permute-done | bytes 65568 | tf_op jit(solution)/shard_map/ppermute | solution.py:410
  63.2 0.9 %shard_map.61 = f32[4,64,512]{2,1,0:T(8,128)} custom-call(f32[2,32,512]{2,1,0:T(8,128)S(1)} %shard_map.52.refs_3_.refs_0_, f32[2,16,512]{2,1,0:T(8,128)S(1)} %shard_map.54.refs_4_.refs_1_, f32[2,16,512]{2,1,0:T(8,128)S(1)} %get-tuple-element.54.refs_3_.refs_2_, f32[2,32,512]{2,1,0:T(8,128)S(1)} %shard_map.59.refs_3_, ...), custom_call_target="tpu_custom_call" | custom-call | bytes 1523712 | tf_op jit(solution)/shard_map/pallas_call | solution.py:364
  (25 shorter events, 0.2 us)
Async XLA Ops:
  0.0 10.2 %collective-permute-start = (f32[4,256,512]{2,1,0:T(8,128)}, f32[4,256,512]{2,1,0:T(8,128)S(1)}, u32[]{:S(2)}, u32[]{:S(2)}) collective-permute-start(f32[4,256,512]{2,1,0:T(8,128)} %bitcast.7), channel_id=1, source_target_pairs={{0,4},{4,0},{8,12},{12,8},{16,20},{20,16},{24,28},{28,24},{1,5},{5... | collective-permute-start | bytes 6291464 | tf_op jit(solution)/shard_map/ppermute | solution.py:440
  0.5 9.8 %collective-permute-start.1 = (f32[4,256,512]{2,1,0:T(8,128)}, f32[4,256,512]{2,1,0:T(8,128)S(1)}, u32[]{:S(2)}, u32[]{:S(2)}) collective-permute-start(f32[4,256,512]{2,1,0:T(8,128)} %refs_2_.3), channel_id=1, source_target_pairs={{0,4},{4,0},{8,12},{12,8},{16,20},{20,16},{24,28},{28,24},{1,5},{5... | collective-permute-start | bytes 6291464 | tf_op jit(solution)/shard_map/ppermute | solution.py:441
  0.5 1.6 %copy-start = (f32[1,4,256,512]{3,2,1,0:T(8,128)S(1)}, f32[1,4,256,512]{3,2,1,0:T(8,128)}, u32[]{:S(2)}) copy-start(f32[1,4,256,512]{3,2,1,0:T(8,128)} %param.3) | copy-start | bytes 6291460
  2.2 15.9 %collective-permute-start.2 = (f32[2,4,32,512]{3,2,1,0:T(8,128)S(1)}, f32[2,4,32,512]{3,2,1,0:T(8,128)S(1)}, u32[]{:S(2)}, u32[]{:S(2)}) collective-permute-start(f32[2,4,32,512]{3,2,1,0:T(8,128)S(1)} %shard_map.37.refs_1_), channel_id=1, source_target_pairs={{0,28},{4,8},{8,4},{12,16},{16,12},{20,24},{24,20},{28,0},{1,29},{... | collective-permute-start | bytes 1572872 | tf_op jit(solution)/shard_map/ppermute | solution.py:451
  5.8 5.1 %copy-start.2 = (f32[4,256,512]{2,1,0:T(8,128)S(1)}, f32[4,256,512]{2,1,0:T(8,128)}, u32[]{:S(2)}) copy-start(f32[4,256,512]{2,1,0:T(8,128)} %refs_2_.3) | copy-start | bytes 6291460
  5.8 23.5 %collective-permute-start.8 = (f32[2,4,32,512]{3,2,1,0:T(8,128)S(1)}, f32[2,4,32,512]{3,2,1,0:T(8,128)S(1)}, u32[]{:S(2)}, u32[]{:S(2)}) collective-permute-start(f32[2,4,32,512]{3,2,1,0:T(8,128)S(1)} %shard_map.38.refs_1_), channel_id=1, source_target_pairs={{0,28},{4,8},{8,4},{12,16},{16,12},{20,24},{24,20},{28,0},{1,29},{... | collective-permute-start | bytes 1572872 | tf_op jit(solution)/shard_map/ppermute | solution.py:451
  6.0 15.0 %collective-permute-start.3 = (f32[4,24,512]{2,1,0:T(8,128)S(1)}, f32[4,24,512]{2,1,0:T(8,128)S(1)}, u32[]{:S(2)}, u32[]{:S(2)}) collective-permute-start(f32[4,24,512]{2,1,0:T(8,128)S(1)} %get-tuple-element.34), channel_id=1, source_target_pairs={{0,3},{1,2},{2,1},{3,0},{4,7},{5,6},{6,5},{7,4},{8,11},{9,10},{10,... | collective-permute-start | bytes 589832 | tf_op jit(solution)/shard_map/ppermute | solution.py:421
  10.2 16.0 %collective-permute-start.4 = (f32[4,24,512]{2,1,0:T(8,128)S(1)}, f32[4,24,512]{2,1,0:T(8,128)S(1)}, u32[]{:S(2)}, u32[]{:S(2)}) collective-permute-start(f32[4,24,512]{2,1,0:T(8,128)S(1)} %get-tuple-element.35), channel_id=1, source_target_pairs={{0,2},{1,3},{2,0},{3,1},{4,6},{5,7},{6,4},{7,5},{8,10},{9,11},{10,... | collective-permute-start | bytes 589832 | tf_op jit(solution)/shard_map/ppermute | solution.py:421
  10.2 16.0 %collective-permute-start.5 = (f32[4,24,512]{2,1,0:T(8,128)S(1)}, f32[4,24,512]{2,1,0:T(8,128)S(1)}, u32[]{:S(2)}, u32[]{:S(2)}) collective-permute-start(f32[4,24,512]{2,1,0:T(8,128)S(1)} %get-tuple-element.36), channel_id=1, source_target_pairs={{0,1},{1,0},{2,3},{3,2},{4,5},{5,4},{6,7},{7,6},{8,9},{9,8},{10,11... | collective-permute-start | bytes 589832 | tf_op jit(solution)/shard_map/ppermute | solution.py:421
  10.9 1.6 %copy-start.3 = (f32[3]{0:T(128)S(1)}, f32[3]{0:T(128)}, u32[]{:S(2)}) copy-start(f32[3]{0:T(128)} %refs_0_.7) | copy-start | bytes 40
  18.2 25.5 %collective-permute-start.10 = (f32[2,4,32,512]{3,2,1,0:T(8,128)S(1)}, f32[2,4,32,512]{3,2,1,0:T(8,128)S(1)}, u32[]{:S(2)}, u32[]{:S(2)}) collective-permute-start(f32[2,4,32,512]{3,2,1,0:T(8,128)S(1)} %shard_map.42.refs_4_), channel_id=1, source_target_pairs={{0,28},{4,8},{8,4},{12,16},{16,12},{20,24},{24,20},{28,0},{1,29},{... | collective-permute-start | bytes 1572872 | tf_op jit(solution)/shard_map/ppermute | solution.py:438
  26.2 7.7 %collective-permute-start.7 = (f32[4,4,24,512]{3,2,1,0:T(8,128)S(1)}, f32[4,4,24,512]{3,2,1,0:T(8,128)S(1)}, u32[]{:S(2)}, u32[]{:S(2)}) collective-permute-start(f32[4,4,24,512]{3,2,1,0:T(8,128)S(1)} %get-tuple-element.38.refs_3_.refs_1_), channel_id=1, source_target_pairs={{0,4},{4,0},{8,12},{12,8},{16,20},{20,16},{24,28},{28,24},{1,5},{5... | collective-permute-start | bytes 2359304 | tf_op jit(solution)/shard_map/ppermute | solution.py:476
  26.5 10.0 %collective-permute-start.6 = (f32[2,2,32,512]{3,2,1,0:T(8,128)S(1)}, f32[2,2,32,512]{3,2,1,0:T(8,128)S(1)}, u32[]{:S(2)}, u32[]{:S(2)}) collective-permute-start(f32[2,2,32,512]{3,2,1,0:T(8,128)S(1)} %get-tuple-element.40), channel_id=1, source_target_pairs={{0,1},{1,0},{2,3},{3,2},{4,5},{5,4},{6,7},{7,6},{8,9},{9,8},{10,11... | collective-permute-start | bytes 786440 | tf_op jit(solution)/shard_map/ppermute | solution.py:430
  29.4 16.1 %collective-permute-start.13 = (f32[2,4,16,512]{3,2,1,0:T(8,128)S(1)}, f32[2,4,16,512]{3,2,1,0:T(8,128)S(1)}, u32[]{:S(2)}, u32[]{:S(2)}) collective-permute-start(f32[2,4,16,512]{3,2,1,0:T(8,128)S(1)} %get-tuple-element.41.refs_3_.refs_5_), channel_id=1, source_target_pairs={{0,28},{4,8},{8,4},{12,16},{16,12},{20,24},{24,20},{28,0},{1,29},{... | collective-permute-start | bytes 786440 | tf_op jit(solution)/shard_map/ppermute | solution.py:438
  32.3 9.1 %collective-permute-start.11 = (f32[2,2,16,512]{3,2,1,0:T(8,128)S(1)}, f32[2,2,16,512]{3,2,1,0:T(8,128)S(1)}, u32[]{:S(2)}, u32[]{:S(2)}) collective-permute-start(f32[2,2,16,512]{3,2,1,0:T(8,128)S(1)} %get-tuple-element.45), channel_id=1, source_target_pairs={{0,1},{1,0},{2,3},{3,2},{4,5},{5,4},{6,7},{7,6},{8,9},{9,8},{10,11... | collective-permute-start | bytes 393224 | tf_op jit(solution)/shard_map/ppermute | solution.py:430
  34.0 5.1 %copy-start.1 = (f32[1,4,256,512]{3,2,1,0:T(8,128)S(1)}, f32[1,4,256,512]{3,2,1,0:T(8,128)}, u32[]{:S(2)}) copy-start(f32[1,4,256,512]{3,2,1,0:T(8,128)} %param.3) | copy-start | bytes 6291460
  36.5 7.4 %collective-permute-start.9 = (f32[2,32,512]{2,1,0:T(8,128)S(1)}, f32[2,32,512]{2,1,0:T(8,128)S(1)}, u32[]{:S(2)}, u32[]{:S(2)}) collective-permute-start(f32[2,32,512]{2,1,0:T(8,128)S(1)} %shard_map.48.refs_7_), channel_id=1, source_target_pairs={{0,3},{1,2},{2,1},{3,0},{4,7},{5,6},{6,5},{7,4},{8,11},{9,10},{10,... | collective-permute-start | bytes 393224 | tf_op jit(solution)/shard_map/ppermute | solution.py:410
  41.5 6.9 %collective-permute-start.12 = (f32[2,16,512]{2,1,0:T(8,128)S(1)}, f32[2,16,512]{2,1,0:T(8,128)S(1)}, u32[]{:S(2)}, u32[]{:S(2)}) collective-permute-start(f32[2,16,512]{2,1,0:T(8,128)S(1)} %shard_map.50.refs_3_), channel_id=1, source_target_pairs={{0,3},{1,2},{2,1},{3,0},{4,7},{5,6},{6,5},{7,4},{8,11},{9,10},{10,... | collective-permute-start | bytes 196616 | tf_op jit(solution)/shard_map/ppermute | solution.py:410
  42.9 8.9 %collective-permute-start.14 = (f32[120,512]{1,0:T(8,128)S(1)}, f32[120,512]{1,0:T(8,128)S(1)}, u32[]{:S(2)}, u32[]{:S(2)}) collective-permute-start(f32[120,512]{1,0:T(8,128)S(1)} %get-tuple-element.48), channel_id=1, source_target_pairs={{0,28},{4,8},{8,4},{12,16},{16,12},{20,24},{24,20},{28,0},{1,29},{... | collective-permute-start | bytes 737288 | tf_op jit(solution)/shard_map/ppermute | solution.py:477
  43.8 9.4 %collective-permute-start.16 = (f32[2,2,32,512]{3,2,1,0:T(8,128)S(1)}, f32[2,2,32,512]{3,2,1,0:T(8,128)S(1)}, u32[]{:S(2)}, u32[]{:S(2)}) collective-permute-start(f32[2,2,32,512]{3,2,1,0:T(8,128)S(1)} %get-tuple-element.53), channel_id=1, source_target_pairs={{0,1},{1,0},{2,3},{3,2},{4,5},{5,4},{6,7},{7,6},{8,9},{9,8},{10,11... | collective-permute-start | bytes 786440 | tf_op jit(solution)/shard_map/ppermute | solution.py:418
  45.6 11.4 %collective-permute-start.15 = (f32[2,2,16,512]{3,2,1,0:T(8,128)S(1)}, f32[2,2,16,512]{3,2,1,0:T(8,128)S(1)}, u32[]{:S(2)}, u32[]{:S(2)}) collective-permute-start(f32[2,2,16,512]{3,2,1,0:T(8,128)S(1)} %get-tuple-element.52), channel_id=1, source_target_pairs={{0,1},{1,0},{2,3},{3,2},{4,5},{5,4},{6,7},{7,6},{8,9},{9,8},{10,11... | collective-permute-start | bytes 393224 | tf_op jit(solution)/shard_map/ppermute | solution.py:418
  51.9 11.3 %collective-permute-start.19 = (f32[4,2,16,512]{3,2,1,0:T(8,128)S(1)}, f32[4,2,16,512]{3,2,1,0:T(8,128)S(1)}, u32[]{:S(2)}, u32[]{:S(2)}) collective-permute-start(f32[4,2,16,512]{3,2,1,0:T(8,128)S(1)} %get-tuple-element.55), channel_id=1, source_target_pairs={{0,28},{4,8},{8,4},{12,16},{16,12},{20,24},{24,20},{28,0},{1,29},{... | collective-permute-start | bytes 786440 | tf_op jit(solution)/shard_map/ppermute | solution.py:506
  53.2 7.5 %collective-permute-start.17 = (f32[2,32,512]{2,1,0:T(8,128)S(1)}, f32[2,32,512]{2,1,0:T(8,128)S(1)}, u32[]{:S(2)}, u32[]{:S(2)}) collective-permute-start(f32[2,32,512]{2,1,0:T(8,128)S(1)} %shard_map.56.refs_2_), channel_id=1, source_target_pairs={{0,3},{1,2},{2,1},{3,0},{4,7},{5,6},{6,5},{7,4},{8,11},{9,10},{10,... | collective-permute-start | bytes 393224 | tf_op jit(solution)/shard_map/ppermute | solution.py:410
  56.9 6.2 %collective-permute-start.18 = (f32[2,16,512]{2,1,0:T(8,128)S(1)}, f32[2,16,512]{2,1,0:T(8,128)S(1)}, u32[]{:S(2)}, u32[]{:S(2)}) collective-permute-start(f32[2,16,512]{2,1,0:T(8,128)S(1)} %shard_map.57.refs_9_), channel_id=1, source_target_pairs={{0,3},{1,2},{2,1},{3,0},{4,7},{5,6},{6,5},{7,4},{8,11},{9,10},{10,... | collective-permute-start | bytes 196616 | tf_op jit(solution)/shard_map/ppermute | solution.py:410

commit v18 on v17

--- a/solution.py
+++ b/solution.py
@@ -477,13 +477,7 @@
     x_halo = lax.ppermute(piece, "slab", face)
     back0 = back_squares(chunks[0], cut_a, halos[0])
     f1, face_b = faces(chunks[1], halos[1], [cut_b, cut_c])
-    back1 = back_squares(chunks[1], cut_b, halos[1], weight=8_000_000_000)
-    x_first, x_t, x_back = call(
-        functools.partial(rows_kernel, cut_c),
-        [(bands, 2, inner, lanes)] + [(bands, 2, part, lanes)] * 2,
-        (coeffs, x, x_in, as_bands(potential), as_bands(pot_in)),
-        scalars=1,
-    )
+    back1 = back_squares(chunks[1], cut_b, halos[1])
     back0 = add_far(*back0)
     h_front = call(
         functools.partial(front_kernel, cuts),
@@ -497,7 +491,13 @@
     front_a = squares(cut_a, face_a)
     back0 = summed(*back0)
     front_b = squares(cut_b, face_b)
-    back1 = summed(*back1, weight=4_000_000_000)
+    back1 = summed(*back1, weight=2_000_000_000)
+    x_first, x_t, x_back = call(
+        functools.partial(rows_kernel, cut_c),
+        [(bands, 2, inner, lanes)] + [(bands, 2, part, lanes)] * 2,
+        (coeffs, x, x_in, as_bands(potential), as_bands(pot_in)),
+        scalars=1,
+    )
     x_f, piece = call(
         functools.partial(rows_face_kernel, cut_c),
         [(bands, 2, inner, lanes), (bands, 2, part, lanes)],

time: 64.2 us -> 64.2 us (level)
  waiting for transfers between devices: 16.5 us -> 19.2 us
  starting transfers between devices: 30.5 us -> 27.9 us
    ppermute x2, waiting for transfers between devices: 0.01 us -> 2.91 us  [back_squares(): return (keep, lax.ppermute(send, 'orb', near))]
    ppermute x3, waiting for transfers between devices: 5.15 us -> 7.61 us  [over_orb(): return lax.ppermute(x, 'orb', [(i, i ^ d) for i in range(bands)])]
    ppermute x1, waiting for transfers between devices: 3.45 us -> 1.28 us  [shards(): x_halo = lax.ppermute(piece, 'slab', face)]
    ppermute x2, waiting for transfers between devices: 2.72 us -> 0.87 us  [shards(): halos.append(lax.ppermute(piece, 'slab', face))]
    ppermute x4, waiting for transfers between devices: 3.63 us -> 5.02 us  [add_far(): return (keep, came, lax.ppermute(total, 'orb', far))]
    ppermute x2, starting transfers between devices: 5.69 us -> 4.41 us  [faces(): return (fs, lax.ppermute(fs[0], 'slab', face))]
    ppermute x4, starting transfers between devices: 9.06 us -> 8.12 us  [add_far(): return (keep, came, lax.ppermute(total, 'orb', far))]
    ppermute x1, starting transfers between devices: 0.85 us -> 0.01 us  [shards(): x_halo = lax.ppermute(piece, 'slab', face)]
  transfers between devices with their start and end apart: 20 -> 20, of which waited for: 6 -> 9; matrix products, arithmetic and copies ran while one was open for 0% -> 0% of each run, Pallas kernels for 22% -> 22%
where the time goes in v18:
time: 64.2 us; the launch traced here: 64.1 us
  starting transfers between devices  27.9 us (43%)
  waiting for transfers between devices  19.2 us (30%)
  Pallas kernels  15.2 us (24%)
  local copies, waits for them, and re-layouts  1.6 us (2%)
    pallas_call x25, Pallas kernels, __call__(): pl.pallas_call(body, out_shape=shapes, in_specs=[smem] * scalars + [pl.Bl...  15.2 us
    ppermute x4, starting transfers between devices, add_far(): return (keep, came, lax.ppermute(total, 'orb', far))  8.12 us
    ppermute x3, waiting for transfers between devices, over_orb(): return lax.ppermute(x, 'orb', [(i, i ^ d) for i in range(bands)])  7.61 us
    ppermute x4, waiting for transfers between devices, add_far(): return (keep, came, lax.ppermute(total, 'orb', far))  5.02 us
    ppermute x3, starting transfers between devices, over_orb(): return lax.ppermute(x, 'orb', [(i, i ^ d) for i in range(bands)])  4.45 us
    ppermute x2, starting transfers between devices, faces(): return (fs, lax.ppermute(fs[0], 'slab', face))  4.41 us
    ppermute x2, starting transfers between devices, shards(): halos.append(lax.ppermute(piece, 'slab', face))  4.23 us
    ppermute x2, starting transfers between devices, squares(): return (keep, lax.ppermute(send, 'orb', near))  2.92 us
  transfers between devices with their start and end apart: 20, of which 9 were waited for; matrix products, arithmetic and copies ran while one was open for 0% of the time, Pallas kernels for 22%

profile of v18, /device:TPU:0, one launch (start us, length us, event | category | flops | bytes accessed | tf_op | source)
XLA Modules:
  0.0 64.1 jit_solution(5567944875695421133)
XLA Ops:
  0.0 0.5 collective-permute-start
  0.5 0.1 collective-permute-start.1
  0.5 1.6 %copy-done = f32[1,4,256,512]{3,2,1,0:T(8,128)S(1)} copy-done((f32[1,4,256,512]{3,2,1,0:T(8,128)S(1)}, f32[1,4,256,512]{3,2,1,0:T(8,128)}, u32[]{:S(2)}) %copy-start) | copy-done | bytes 2097176
  2.2 3.6 %collective-permute-start.2 = (f32[2,4,32,512]{3,2,1,0:T(8,128)S(1)}, f32[2,4,32,512]{3,2,1,0:T(8,128)S(1)}, u32[]{:S(2)}, u32[]{:S(2)}) collective-permute-start(f32[2,4,32,512]{3,2,1,0:T(8,128)S(1)} %shard_map.37.refs_1_), channel_id=1, source_target_pairs={{0,28},{4,8},{8,4},{12,16},{16,12},{20,24},{24,20},{28,0},{1,29},{... | collective-permute-start | bytes 1572872 | tf_op jit(solution)/shard_map/ppermute | solution.py:451
  5.8 0.0 copy-start.2
  5.8 0.1 shard_map.39
  5.9 3.7 %collective-permute-start.3 = (f32[4,24,512]{2,1,0:T(8,128)S(1)}, f32[4,24,512]{2,1,0:T(8,128)S(1)}, u32[]{:S(2)}, u32[]{:S(2)}) collective-permute-start(f32[4,24,512]{2,1,0:T(8,128)S(1)} %get-tuple-element.34), channel_id=1, source_target_pairs={{0,3},{1,2},{2,1},{3,0},{4,7},{5,6},{6,5},{7,4},{8,11},{9,10},{10,... | collective-permute-start | bytes 589832 | tf_op jit(solution)/shard_map/ppermute | solution.py:421
  9.6 0.0 collective-permute-start.4
  9.6 0.0 collective-permute-done.refs_3_
  9.6 0.8 %collective-permute-start.5 = (f32[4,24,512]{2,1,0:T(8,128)S(1)}, f32[4,24,512]{2,1,0:T(8,128)S(1)}, u32[]{:S(2)}, u32[]{:S(2)}) collective-permute-start(f32[4,24,512]{2,1,0:T(8,128)S(1)} %get-tuple-element.36), channel_id=1, source_target_pairs={{0,1},{1,0},{2,3},{3,2},{4,5},{5,4},{6,7},{7,6},{8,9},{9,8},{10,11... | collective-permute-start | bytes 589832 | tf_op jit(solution)/shard_map/ppermute | solution.py:421
  10.3 0.7 %collective-permute-start.7 = (f32[2,4,32,512]{3,2,1,0:T(8,128)S(1)}, f32[2,4,32,512]{3,2,1,0:T(8,128)S(1)}, u32[]{:S(2)}, u32[]{:S(2)}) collective-permute-start(f32[2,4,32,512]{3,2,1,0:T(8,128)S(1)} %shard_map.38.refs_1_), channel_id=1, source_target_pairs={{0,28},{4,8},{8,4},{12,16},{16,12},{20,24},{24,20},{28,0},{1,29},{... | collective-permute-start | bytes 1572872 | tf_op jit(solution)/shard_map/ppermute | solution.py:451
  11.0 1.6 %shard_map.40.refs_5_.refs_6_ = f32[2,256,512]{2,1,0:T(8,128)S(1)} custom-call(f32[4,256,512]{2,1,0:T(8,128)S(1)} %bitcast.11, f32[4,256,512]{2,1,0:T(8,128)S(1)} %copy-done.2, f32[4,24,512]{2,1,0:T(8,128)S(1)} %get-tuple-element.31.refs_2_.refs_0_), custom_call_target="tpu_custom_call" | custom-call | flops 6291456 | bytes 5242880 | tf_op jit(solution)/shard_map/pallas_call | solution.py:364
  12.6 5.6 %shard_map.41 = (f32[2,256,512]{2,1,0:T(8,128)S(1)}, f32[2,256,512]{2,1,0:T(8,128)S(1)}, f32[8,512]{1,0:T(8,128)S(1)}) custom-call(f32[3]{0:T(128)S(1)} %copy-done.3, f32[4,256,512]{2,1,0:T(8,128)S(1)} %bitcast.12, f32[4,256,512]{2,1,0:T(8,128)S(1)} %copy-done.2, f32[4,256,512]{2,1,0:T(8,128)S(1)} %collective-permute-done.refs_3_, ...), custom_call_target="tpu_custom_call" | custom-call | flops 20971520 | bytes 11550732 | tf_op jit(solution)/shard_map/pallas_call | solution.py:364
  18.3 0.1 shard_map.42.refs_4_
  18.4 7.6 %collective-permute-done.4.refs_2_ = f32[4,24,512]{2,1,0:T(8,128)S(1)} collective-permute-done((f32[4,24,512]{2,1,0:T(8,128)S(1)}, f32[4,24,512]{2,1,0:T(8,128)S(1)}, u32[]{:S(2)}, u32[]{:S(2)}) %collective-permute-start.4) | collective-permute-done | bytes 196640 | tf_op jit(solution)/shard_map/ppermute | solution.py:421
  26.0 0.1 shard_map.43
  26.0 0.1 collective-permute-start.14
  26.1 1.5 %collective-permute-start.9 = (f32[2,4,32,512]{3,2,1,0:T(8,128)S(1)}, f32[2,4,32,512]{3,2,1,0:T(8,128)S(1)}, u32[]{:S(2)}, u32[]{:S(2)}) collective-permute-start(f32[2,4,32,512]{3,2,1,0:T(8,128)S(1)} %shard_map.42.refs_4_), channel_id=1, source_target_pairs={{0,28},{4,8},{8,4},{12,16},{16,12},{20,24},{24,20},{28,0},{1,29},{... | collective-permute-start | bytes 1572872 | tf_op jit(solution)/shard_map/ppermute | solution.py:438
  27.7 0.2 shard_map.44
  27.8 0.1 collective-permute-start.6
  27.9 0.9 %collective-permute-done.7.refs_0_.refs_1_.refs_2_.refs_5_ = f32[2,4,32,512]{3,2,1,0:T(8,128)S(1)} collective-permute-done((f32[2,4,32,512]{3,2,1,0:T(8,128)S(1)}, f32[2,4,32,512]{3,2,1,0:T(8,128)S(1)}, u32[]{:S(2)}, u32[]{:S(2)}) %collective-permute-start.7) | collective-permute-done | bytes 524320 | tf_op jit(solution)/shard_map/ppermute | solution.py:451
  28.8 0.1 shard_map.45
  28.9 2.9 %collective-permute-start.12 = (f32[2,4,16,512]{3,2,1,0:T(8,128)S(1)}, f32[2,4,16,512]{3,2,1,0:T(8,128)S(1)}, u32[]{:S(2)}, u32[]{:S(2)}) collective-permute-start(f32[2,4,16,512]{3,2,1,0:T(8,128)S(1)} %get-tuple-element.41.refs_3_.refs_5_), channel_id=1, source_target_pairs={{0,28},{4,8},{8,4},{12,16},{16,12},{20,24},{24,20},{28,0},{1,29},{... | collective-permute-start | bytes 786440 | tf_op jit(solution)/shard_map/ppermute | solution.py:438
  31.7 0.1 shard_map.46
  31.8 2.2 %collective-permute-start.10 = (f32[2,2,16,512]{3,2,1,0:T(8,128)S(1)}, f32[2,2,16,512]{3,2,1,0:T(8,128)S(1)}, u32[]{:S(2)}, u32[]{:S(2)}) collective-permute-start(f32[2,2,16,512]{3,2,1,0:T(8,128)S(1)} %get-tuple-element.44), channel_id=1, source_target_pairs={{0,1},{1,0},{2,3},{3,2},{4,5},{5,4},{6,7},{7,6},{8,9},{9,8},{10,11... | collective-permute-start | bytes 393224 | tf_op jit(solution)/shard_map/ppermute | solution.py:430
  34.0 2.9 %collective-permute-done.6.refs_1_ = f32[2,2,32,512]{3,2,1,0:T(8,128)S(1)} collective-permute-done((f32[2,2,32,512]{3,2,1,0:T(8,128)S(1)}, f32[2,2,32,512]{3,2,1,0:T(8,128)S(1)}, u32[]{:S(2)}, u32[]{:S(2)}) %collective-permute-start.6) | collective-permute-done | bytes 262176 | tf_op jit(solution)/shard_map/ppermute | solution.py:430
  36.9 2.5 %collective-permute-start.8 = (f32[2,32,512]{2,1,0:T(8,128)S(1)}, f32[2,32,512]{2,1,0:T(8,128)S(1)}, u32[]{:S(2)}, u32[]{:S(2)}) collective-permute-start(f32[2,32,512]{2,1,0:T(8,128)S(1)} %shard_map.47.refs_7_), channel_id=1, source_target_pairs={{0,3},{1,2},{2,1},{3,0},{4,7},{5,6},{6,5},{7,4},{8,11},{9,10},{10,... | collective-permute-start | bytes 393224 | tf_op jit(solution)/shard_map/ppermute | solution.py:410
  39.5 2.4 %shard_map.48.refs_2_ = f32[2,256,512]{2,1,0:T(8,128)S(1)} custom-call(f32[3]{0:T(128)S(1)} %copy-done.3, f32[4,256,512]{2,1,0:T(8,128)S(1)} %bitcast.13, f32[4,256,512]{2,1,0:T(8,128)S(1)} %copy-done.2, f32[2,256,512]{2,1,0:T(8,128)S(1)} %get-tuple-element.37.refs_2_.refs_3_, f32[2,4,32,512]{3,2,1,0:T(8,128)S(1)} %shard_map.42.refs_4_, ...), custom_call_target="tpu_custom_call" | custom-call | flops 10485760 | bytes 7340044 | tf_op jit(solution)/shard_map/pallas_call | solution.py:364
  41.9 1.4 %collective-permute-start.11 = (f32[2,16,512]{2,1,0:T(8,128)S(1)}, f32[2,16,512]{2,1,0:T(8,128)S(1)}, u32[]{:S(2)}, u32[]{:S(2)}) collective-permute-start(f32[2,16,512]{2,1,0:T(8,128)S(1)} %shard_map.49.refs_3_), channel_id=1, source_target_pairs={{0,3},{1,2},{2,1},{3,0},{4,7},{5,6},{6,5},{7,4},{8,11},{9,10},{10,... | collective-permute-start | bytes 196616 | tf_op jit(solution)/shard_map/ppermute | solution.py:410
  43.3 0.1 shard_map.50
  43.4 1.1 %collective-permute-done.8.refs_2_ = f32[2,32,512]{2,1,0:T(8,128)S(1)} collective-permute-done((f32[2,32,512]{2,1,0:T(8,128)S(1)}, f32[2,32,512]{2,1,0:T(8,128)S(1)}, u32[]{:S(2)}, u32[]{:S(2)}) %collective-permute-start.8) | collective-permute-done | bytes 131104 | tf_op jit(solution)/shard_map/ppermute | solution.py:410
  44.5 1.0 %collective-permute-start.16 = (f32[2,2,32,512]{3,2,1,0:T(8,128)S(1)}, f32[2,2,32,512]{3,2,1,0:T(8,128)S(1)}, u32[]{:S(2)}, u32[]{:S(2)}) collective-permute-start(f32[2,2,32,512]{3,2,1,0:T(8,128)S(1)} %get-tuple-element.53), channel_id=1, source_target_pairs={{0,1},{1,0},{2,3},{3,2},{4,5},{5,4},{6,7},{7,6},{8,9},{9,8},{10,11... | collective-permute-start | bytes 786440 | tf_op jit(solution)/shard_map/ppermute | solution.py:418
  45.5 0.8 %collective-permute-done.12.refs_1_ = f32[2,4,16,512]{3,2,1,0:T(8,128)S(1)} collective-permute-done((f32[2,4,16,512]{3,2,1,0:T(8,128)S(1)}, f32[2,4,16,512]{3,2,1,0:T(8,128)S(1)}, u32[]{:S(2)}, u32[]{:S(2)}) %collective-permute-start.12) | collective-permute-done | bytes 262176 | tf_op jit(solution)/shard_map/ppermute | solution.py:438
  46.3 0.1 shard_map.52
  46.4 2.0 %collective-permute-start.15 = (f32[2,2,16,512]{3,2,1,0:T(8,128)S(1)}, f32[2,2,16,512]{3,2,1,0:T(8,128)S(1)}, u32[]{:S(2)}, u32[]{:S(2)}) collective-permute-start(f32[2,2,16,512]{3,2,1,0:T(8,128)S(1)} %get-tuple-element.52), channel_id=1, source_target_pairs={{0,1},{1,0},{2,3},{3,2},{4,5},{5,4},{6,7},{7,6},{8,9},{9,8},{10,11... | collective-permute-start | bytes 393224 | tf_op jit(solution)/shard_map/ppermute | solution.py:418
  48.3 0.0 collective-permute-done.11.refs_2_
  48.4 0.0 collective-permute-done.14.refs_2_
  48.4 2.5 %shard_map.54 = (f32[4,2,20,512]{3,2,1,0:T(8,128)S(1)}, f32[4,2,16,512]{3,2,1,0:T(8,128)S(1)}, f32[4,2,16,512]{3,2,1,0:T(8,128)S(1)}) custom-call(f32[3]{0:T(128)S(1)} %copy-done.3, f32[4,4,24,512]{3,2,1,0:T(8,128)S(1)} %get-tuple-element.38.refs_3_.refs_1_, f32[4,4,24,512]{3,2,1,0:T(8,128)S(1)} %collective-permute-done.14.refs_2_, ...), custom_call_target="tpu_custom_call" | custom-call | bytes 6619148 | tf_op jit(solution)/shard_map/pallas_call | solution.py:364
  50.9 1.3 %collective-permute-done.13.refs_0_.refs_3_ = f32[120,512]{1,0:T(8,128)S(1)} collective-permute-done((f32[120,512]{1,0:T(8,128)S(1)}, f32[120,512]{1,0:T(8,128)S(1)}, u32[]{:S(2)}, u32[]{:S(2)}) %collective-permute-start.13) | collective-permute-done | bytes 245792 | tf_op jit(solution)/shard_map/ppermute | solution.py:477
  52.2 0.1 shard_map.55
  52.3 0.9 %collective-permute-start.19 = (f32[4,2,16,512]{3,2,1,0:T(8,128)S(1)}, f32[4,2,16,512]{3,2,1,0:T(8,128)S(1)}, u32[]{:S(2)}, u32[]{:S(2)}) collective-permute-start(f32[4,2,16,512]{3,2,1,0:T(8,128)S(1)} %get-tuple-element.55), channel_id=1, source_target_pairs={{0,28},{4,8},{8,4},{12,16},{16,12},{20,24},{24,20},{28,0},{1,29},{... | collective-permute-start | bytes 786440 | tf_op jit(solution)/shard_map/ppermute | solution.py:506
  53.2 0.6 collective-permute-done.16.refs_1_
  53.9 3.0 %collective-permute-start.17 = (f32[2,32,512]{2,1,0:T(8,128)S(1)}, f32[2,32,512]{2,1,0:T(8,128)S(1)}, u32[]{:S(2)}, u32[]{:S(2)}) collective-permute-start(f32[2,32,512]{2,1,0:T(8,128)S(1)} %shard_map.56.refs_2_), channel_id=1, source_target_pairs={{0,3},{1,2},{2,1},{3,0},{4,7},{5,6},{6,5},{7,4},{8,11},{9,10},{10,... | collective-permute-start | bytes 393224 | tf_op jit(solution)/shard_map/ppermute | solution.py:410
  56.9 1.1 %collective-permute-start.18 = (f32[2,16,512]{2,1,0:T(8,128)S(1)}, f32[2,16,512]{2,1,0:T(8,128)S(1)}, u32[]{:S(2)}, u32[]{:S(2)}) collective-permute-start(f32[2,16,512]{2,1,0:T(8,128)S(1)} %shard_map.57.refs_9_), channel_id=1, source_target_pairs={{0,3},{1,2},{2,1},{3,0},{4,7},{5,6},{6,5},{7,4},{8,11},{9,10},{10,... | collective-permute-start | bytes 196616 | tf_op jit(solution)/shard_map/ppermute | solution.py:410
  58.1 1.2 %shard_map.58 = (f32[2,16,512]{2,1,0:T(8,128)S(1)}, f32[4,2,16,512]{3,2,1,0:T(8,128)S(1)}) custom-call(f32[3]{0:T(128)S(1)} %copy-done.3, f32[4,4,24,512]{3,2,1,0:T(8,128)S(1)} %get-tuple-element.38.refs_3_.refs_1_, f32[4,4,64,512]{3,2,1,0:T(8,128)S(1)} %bitcast.15, f32[120,512]{1,0:T(8,128)S(1)} %collective-permute-done.13.refs_0_.refs_3_, ...), custom_call_target="tpu_custom_call" | custom-call | bytes 5357580 | tf_op jit(solution)/shard_map/pallas_call | solution.py:364
  59.2 2.3 %collective-permute-done.17.refs_2_ = f32[2,32,512]{2,1,0:T(8,128)S(1)} collective-permute-done((f32[2,32,512]{2,1,0:T(8,128)S(1)}, f32[2,32,512]{2,1,0:T(8,128)S(1)}, u32[]{:S(2)}, u32[]{:S(2)}) %collective-permute-start.17) | collective-permute-done | bytes 131104 | tf_op jit(solution)/shard_map/ppermute | solution.py:410
  61.5 1.6 %collective-permute-done.18.refs_2_ = f32[2,16,512]{2,1,0:T(8,128)S(1)} collective-permute-done((f32[2,16,512]{2,1,0:T(8,128)S(1)}, f32[2,16,512]{2,1,0:T(8,128)S(1)}, u32[]{:S(2)}, u32[]{:S(2)}) %collective-permute-start.18) | collective-permute-done | bytes 65568 | tf_op jit(solution)/shard_map/ppermute | solution.py:410
  63.2 0.9 %shard_map.61 = f32[4,64,512]{2,1,0:T(8,128)} custom-call(f32[2,32,512]{2,1,0:T(8,128)S(1)} %shard_map.51.refs_3_.refs_0_, f32[2,16,512]{2,1,0:T(8,128)S(1)} %shard_map.53.refs_5_.refs_1_, f32[2,16,512]{2,1,0:T(8,128)S(1)} %get-tuple-element.54.refs_3_.refs_2_, f32[2,32,512]{2,1,0:T(8,128)S(1)} %shard_map.59.refs_3_, ...), custom_call_target="tpu_custom_call" | custom-call | bytes 1523712 | tf_op jit(solution)/shard_map/pallas_call | solution.py:364
  (25 shorter events, 0.2 us)
Async XLA Ops:
  0.0 9.6 %collective-permute-start = (f32[4,256,512]{2,1,0:T(8,128)}, f32[4,256,512]{2,1,0:T(8,128)S(1)}, u32[]{:S(2)}, u32[]{:S(2)}) collective-permute-start(f32[4,256,512]{2,1,0:T(8,128)} %bitcast.7), channel_id=1, source_target_pairs={{0,4},{4,0},{8,12},{12,8},{16,20},{20,16},{24,28},{28,24},{1,5},{5... | collective-permute-start | bytes 6291464 | tf_op jit(solution)/shard_map/ppermute | solution.py:440
  0.5 9.9 %collective-permute-start.1 = (f32[4,256,512]{2,1,0:T(8,128)}, f32[4,256,512]{2,1,0:T(8,128)S(1)}, u32[]{:S(2)}, u32[]{:S(2)}) collective-permute-start(f32[4,256,512]{2,1,0:T(8,128)} %refs_2_.3), channel_id=1, source_target_pairs={{0,4},{4,0},{8,12},{12,8},{16,20},{20,16},{24,28},{28,24},{1,5},{5... | collective-permute-start | bytes 6291464 | tf_op jit(solution)/shard_map/ppermute | solution.py:441
  0.5 1.6 %copy-start = (f32[1,4,256,512]{3,2,1,0:T(8,128)S(1)}, f32[1,4,256,512]{3,2,1,0:T(8,128)}, u32[]{:S(2)}) copy-start(f32[1,4,256,512]{3,2,1,0:T(8,128)} %param.3) | copy-start | bytes 6291460
  2.2 16.1 %collective-permute-start.2 = (f32[2,4,32,512]{3,2,1,0:T(8,128)S(1)}, f32[2,4,32,512]{3,2,1,0:T(8,128)S(1)}, u32[]{:S(2)}, u32[]{:S(2)}) collective-permute-start(f32[2,4,32,512]{3,2,1,0:T(8,128)S(1)} %shard_map.37.refs_1_), channel_id=1, source_target_pairs={{0,28},{4,8},{8,4},{12,16},{16,12},{20,24},{24,20},{28,0},{1,29},{... | collective-permute-start | bytes 1572872 | tf_op jit(solution)/shard_map/ppermute | solution.py:451
  5.8 5.2 %copy-start.2 = (f32[4,256,512]{2,1,0:T(8,128)S(1)}, f32[4,256,512]{2,1,0:T(8,128)}, u32[]{:S(2)}) copy-start(f32[4,256,512]{2,1,0:T(8,128)} %refs_2_.3) | copy-start | bytes 6291460
  5.9 12.5 %collective-permute-start.3 = (f32[4,24,512]{2,1,0:T(8,128)S(1)}, f32[4,24,512]{2,1,0:T(8,128)S(1)}, u32[]{:S(2)}, u32[]{:S(2)}) collective-permute-start(f32[4,24,512]{2,1,0:T(8,128)S(1)} %get-tuple-element.34), channel_id=1, source_target_pairs={{0,3},{1,2},{2,1},{3,0},{4,7},{5,6},{6,5},{7,4},{8,11},{9,10},{10,... | collective-permute-start | bytes 589832 | tf_op jit(solution)/shard_map/ppermute | solution.py:421
  9.6 16.4 %collective-permute-start.4 = (f32[4,24,512]{2,1,0:T(8,128)S(1)}, f32[4,24,512]{2,1,0:T(8,128)S(1)}, u32[]{:S(2)}, u32[]{:S(2)}) collective-permute-start(f32[4,24,512]{2,1,0:T(8,128)S(1)} %get-tuple-element.35), channel_id=1, source_target_pairs={{0,2},{1,3},{2,0},{3,1},{4,6},{5,7},{6,4},{7,5},{8,10},{9,11},{10,... | collective-permute-start | bytes 589832 | tf_op jit(solution)/shard_map/ppermute | solution.py:421
  9.6 16.4 %collective-permute-start.5 = (f32[4,24,512]{2,1,0:T(8,128)S(1)}, f32[4,24,512]{2,1,0:T(8,128)S(1)}, u32[]{:S(2)}, u32[]{:S(2)}) collective-permute-start(f32[4,24,512]{2,1,0:T(8,128)S(1)} %get-tuple-element.36), channel_id=1, source_target_pairs={{0,1},{1,0},{2,3},{3,2},{4,5},{5,4},{6,7},{7,6},{8,9},{9,8},{10,11... | collective-permute-start | bytes 589832 | tf_op jit(solution)/shard_map/ppermute | solution.py:421
  10.3 18.4 %collective-permute-start.7 = (f32[2,4,32,512]{3,2,1,0:T(8,128)S(1)}, f32[2,4,32,512]{3,2,1,0:T(8,128)S(1)}, u32[]{:S(2)}, u32[]{:S(2)}) collective-permute-start(f32[2,4,32,512]{3,2,1,0:T(8,128)S(1)} %shard_map.38.refs_1_), channel_id=1, source_target_pairs={{0,28},{4,8},{8,4},{12,16},{16,12},{20,24},{24,20},{28,0},{1,29},{... | collective-permute-start | bytes 1572872 | tf_op jit(solution)/shard_map/ppermute | solution.py:451
  11.0 1.6 %copy-start.3 = (f32[3]{0:T(128)S(1)}, f32[3]{0:T(128)}, u32[]{:S(2)}) copy-start(f32[3]{0:T(128)} %refs_0_.7) | copy-start | bytes 40
  26.0 22.3 %collective-permute-start.14 = (f32[4,4,24,512]{3,2,1,0:T(8,128)S(1)}, f32[4,4,24,512]{3,2,1,0:T(8,128)S(1)}, u32[]{:S(2)}, u32[]{:S(2)}) collective-permute-start(f32[4,4,24,512]{3,2,1,0:T(8,128)S(1)} %get-tuple-element.38.refs_3_.refs_1_), channel_id=1, source_target_pairs={{0,4},{4,0},{8,12},{12,8},{16,20},{20,16},{24,28},{28,24},{1,5},{5... | collective-permute-start | bytes 2359304 | tf_op jit(solution)/shard_map/ppermute | solution.py:476
  26.1 17.2 %collective-permute-start.9 = (f32[2,4,32,512]{3,2,1,0:T(8,128)S(1)}, f32[2,4,32,512]{3,2,1,0:T(8,128)S(1)}, u32[]{:S(2)}, u32[]{:S(2)}) collective-permute-start(f32[2,4,32,512]{3,2,1,0:T(8,128)S(1)} %shard_map.42.refs_4_), channel_id=1, source_target_pairs={{0,28},{4,8},{8,4},{12,16},{16,12},{20,24},{24,20},{28,0},{1,29},{... | collective-permute-start | bytes 1572872 | tf_op jit(solution)/shard_map/ppermute | solution.py:438
  27.8 9.1 %collective-permute-start.6 = (f32[2,2,32,512]{3,2,1,0:T(8,128)S(1)}, f32[2,2,32,512]{3,2,1,0:T(8,128)S(1)}, u32[]{:S(2)}, u32[]{:S(2)}) collective-permute-start(f32[2,2,32,512]{3,2,1,0:T(8,128)S(1)} %get-tuple-element.40), channel_id=1, source_target_pairs={{0,1},{1,0},{2,3},{3,2},{4,5},{5,4},{6,7},{7,6},{8,9},{9,8},{10,11... | collective-permute-start | bytes 786440 | tf_op jit(solution)/shard_map/ppermute | solution.py:430
  28.8 10.7 %copy-start.1 = (f32[1,4,256,512]{3,2,1,0:T(8,128)S(1)}, f32[1,4,256,512]{3,2,1,0:T(8,128)}, u32[]{:S(2)}) copy-start(f32[1,4,256,512]{3,2,1,0:T(8,128)} %param.3) | copy-start | bytes 6291460
  28.9 17.5 %collective-permute-start.12 = (f32[2,4,16,512]{3,2,1,0:T(8,128)S(1)}, f32[2,4,16,512]{3,2,1,0:T(8,128)S(1)}, u32[]{:S(2)}, u32[]{:S(2)}) collective-permute-start(f32[2,4,16,512]{3,2,1,0:T(8,128)S(1)} %get-tuple-element.41.refs_3_.refs_5_), channel_id=1, source_target_pairs={{0,28},{4,8},{8,4},{12,16},{16,12},{20,24},{24,20},{28,0},{1,29},{... | collective-permute-start | bytes 786440 | tf_op jit(solution)/shard_map/ppermute | solution.py:438
  31.8 10.0 %collective-permute-start.10 = (f32[2,2,16,512]{3,2,1,0:T(8,128)S(1)}, f32[2,2,16,512]{3,2,1,0:T(8,128)S(1)}, u32[]{:S(2)}, u32[]{:S(2)}) collective-permute-start(f32[2,2,16,512]{3,2,1,0:T(8,128)S(1)} %get-tuple-element.44), channel_id=1, source_target_pairs={{0,1},{1,0},{2,3},{3,2},{4,5},{5,4},{6,7},{7,6},{8,9},{9,8},{10,11... | collective-permute-start | bytes 393224 | tf_op jit(solution)/shard_map/ppermute | solution.py:430
  36.9 7.6 %collective-permute-start.8 = (f32[2,32,512]{2,1,0:T(8,128)S(1)}, f32[2,32,512]{2,1,0:T(8,128)S(1)}, u32[]{:S(2)}, u32[]{:S(2)}) collective-permute-start(f32[2,32,512]{2,1,0:T(8,128)S(1)} %shard_map.47.refs_7_), channel_id=1, source_target_pairs={{0,3},{1,2},{2,1},{3,0},{4,7},{5,6},{6,5},{7,4},{8,11},{9,10},{10,... | collective-permute-start | bytes 393224 | tf_op jit(solution)/shard_map/ppermute | solution.py:410
  41.9 6.5 %collective-permute-start.11 = (f32[2,16,512]{2,1,0:T(8,128)S(1)}, f32[2,16,512]{2,1,0:T(8,128)S(1)}, u32[]{:S(2)}, u32[]{:S(2)}) collective-permute-start(f32[2,16,512]{2,1,0:T(8,128)S(1)} %shard_map.49.refs_3_), channel_id=1, source_target_pairs={{0,3},{1,2},{2,1},{3,0},{4,7},{5,6},{6,5},{7,4},{8,11},{9,10},{10,... | collective-permute-start | bytes 196616 | tf_op jit(solution)/shard_map/ppermute | solution.py:410
  43.3 8.9 %collective-permute-start.13 = (f32[120,512]{1,0:T(8,128)S(1)}, f32[120,512]{1,0:T(8,128)S(1)}, u32[]{:S(2)}, u32[]{:S(2)}) collective-permute-start(f32[120,512]{1,0:T(8,128)S(1)} %get-tuple-element.47), channel_id=1, source_target_pairs={{0,28},{4,8},{8,4},{12,16},{16,12},{20,24},{24,20},{28,0},{1,29},{... | collective-permute-start | bytes 737288 | tf_op jit(solution)/shard_map/ppermute | solution.py:477
  44.5 9.4 %collective-permute-start.16 = (f32[2,2,32,512]{3,2,1,0:T(8,128)S(1)}, f32[2,2,32,512]{3,2,1,0:T(8,128)S(1)}, u32[]{:S(2)}, u32[]{:S(2)}) collective-permute-start(f32[2,2,32,512]{3,2,1,0:T(8,128)S(1)} %get-tuple-element.53), channel_id=1, source_target_pairs={{0,1},{1,0},{2,3},{3,2},{4,5},{5,4},{6,7},{7,6},{8,9},{9,8},{10,11... | collective-permute-start | bytes 786440 | tf_op jit(solution)/shard_map/ppermute | solution.py:418
  46.4 10.5 %collective-permute-start.15 = (f32[2,2,16,512]{3,2,1,0:T(8,128)S(1)}, f32[2,2,16,512]{3,2,1,0:T(8,128)S(1)}, u32[]{:S(2)}, u32[]{:S(2)}) collective-permute-start(f32[2,2,16,512]{3,2,1,0:T(8,128)S(1)} %get-tuple-element.52), channel_id=1, source_target_pairs={{0,1},{1,0},{2,3},{3,2},{4,5},{5,4},{6,7},{7,6},{8,9},{9,8},{10,11... | collective-permute-start | bytes 393224 | tf_op jit(solution)/shard_map/ppermute | solution.py:418
  52.3 10.9 %collective-permute-start.19 = (f32[4,2,16,512]{3,2,1,0:T(8,128)S(1)}, f32[4,2,16,512]{3,2,1,0:T(8,128)S(1)}, u32[]{:S(2)}, u32[]{:S(2)}) collective-permute-start(f32[4,2,16,512]{3,2,1,0:T(8,128)S(1)} %get-tuple-element.55), channel_id=1, source_target_pairs={{0,28},{4,8},{8,4},{12,16},{16,12},{20,24},{24,20},{28,0},{1,29},{... | collective-permute-start | bytes 786440 | tf_op jit(solution)/shard_map/ppermute | solution.py:506
  53.9 7.6 %collective-permute-start.17 = (f32[2,32,512]{2,1,0:T(8,128)S(1)}, f32[2,32,512]{2,1,0:T(8,128)S(1)}, u32[]{:S(2)}, u32[]{:S(2)}) collective-permute-start(f32[2,32,512]{2,1,0:T(8,128)S(1)} %shard_map.56.refs_2_), channel_id=1, source_target_pairs={{0,3},{1,2},{2,1},{3,0},{4,7},{5,6},{6,5},{7,4},{8,11},{9,10},{10,... | collective-permute-start | bytes 393224 | tf_op jit(solution)/shard_map/ppermute | solution.py:410
  56.9 6.2 %collective-permute-start.18 = (f32[2,16,512]{2,1,0:T(8,128)S(1)}, f32[2,16,512]{2,1,0:T(8,128)S(1)}, u32[]{:S(2)}, u32[]{:S(2)}) collective-permute-start(f32[2,16,512]{2,1,0:T(8,128)S(1)} %shard_map.57.refs_9_), channel_id=1, source_target_pairs={{0,3},{1,2},{2,1},{3,0},{4,7},{5,6},{6,5},{7,4},{8,11},{9,10},{10,... | collective-permute-start | bytes 196616 | tf_op jit(solution)/shard_map/ppermute | solution.py:410

commit v19 on v17

--- a/solution.py
+++ b/solution.py
@@ -9,7 +9,7 @@
 
 NEAR = -2.0 / 15.0
 FAR = 1.0 / 120.0
-BLOCK = 16
+BLOCK = 32
 
 
 def own(q, odd):
@@ -66,7 +66,7 @@
         body(pl.multiple_of(i * BLOCK, BLOCK))
         return carry
 
-    lax.fori_loop(0, rows // BLOCK, step, 0, unroll=4)
+    lax.fori_loop(0, rows // BLOCK, step, 0, unroll=2)
 
 
 def pack_kernel(chunk, psi, out, sem):

time: 64.2 us -> 64.2 us (level)
  transfers between devices with their start and end apart: 20 -> 20, of which waited for: 6 -> 7; matrix products, arithmetic and copies ran while one was open for 0% -> 0% of each run, Pallas kernels for 22% -> 22%
where the time goes in v19:
time: 64.2 us; the launch traced here: 64.1 us
  starting transfers between devices  30.5 us (48%)
  waiting for transfers between devices  16.6 us (26%)
  Pallas kernels  15.2 us (24%)
  local copies, waits for them, and re-layouts  1.6 us (2%)
    pallas_call x25, Pallas kernels, __call__(): pl.pallas_call(body, out_shape=shapes, in_specs=[smem] * scalars + [pl.Bl...  15.2 us
    ppermute x4, starting transfers between devices, add_far(): return (keep, came, lax.ppermute(total, 'orb', far))  9.06 us
    ppermute x2, starting transfers between devices, faces(): return (fs, lax.ppermute(fs[0], 'slab', face))  5.65 us
    ppermute x3, waiting for transfers between devices, over_orb(): return lax.ppermute(x, 'orb', [(i, i ^ d) for i in range(bands)])  5.15 us
    ppermute x3, starting transfers between devices, over_orb(): return lax.ppermute(x, 'orb', [(i, i ^ d) for i in range(bands)])  4.88 us
    ppermute x2, starting transfers between devices, shards(): halos.append(lax.ppermute(piece, 'slab', face))  3.66 us
    ppermute x4, waiting for transfers between devices, add_far(): return (keep, came, lax.ppermute(total, 'orb', far))  3.6 us
    ppermute x1, waiting for transfers between devices, shards(): x_halo = lax.ppermute(piece, 'slab', face)  3.47 us
  transfers between devices with their start and end apart: 20, of which 7 were waited for; matrix products, arithmetic and copies ran while one was open for 0% of the time, Pallas kernels for 22%

profile of v19, /device:TPU:0, one launch (start us, length us, event | category | flops | bytes accessed | tf_op | source)
XLA Modules:
  0.0 64.1 jit_solution(9423593937016950374)
XLA Ops:
  0.0 0.5 collective-permute-start
  0.5 0.1 collective-permute-start.1
  0.5 1.6 %copy-done = f32[1,4,256,512]{3,2,1,0:T(8,128)S(1)} copy-done((f32[1,4,256,512]{3,2,1,0:T(8,128)S(1)}, f32[1,4,256,512]{3,2,1,0:T(8,128)}, u32[]{:S(2)}) %copy-start) | copy-done | bytes 2097176
  2.2 3.6 %collective-permute-start.2 = (f32[2,4,32,512]{3,2,1,0:T(8,128)S(1)}, f32[2,4,32,512]{3,2,1,0:T(8,128)S(1)}, u32[]{:S(2)}, u32[]{:S(2)}) collective-permute-start(f32[2,4,32,512]{3,2,1,0:T(8,128)S(1)} %shard_map.37.refs_1_), channel_id=1, source_target_pairs={{0,28},{4,8},{8,4},{12,16},{16,12},{20,24},{24,20},{28,0},{1,29},{... | collective-permute-start | bytes 1572872 | tf_op jit(solution)/shard_map/ppermute | solution.py:451
  5.8 0.0 copy-start.2
  5.8 0.1 collective-permute-start.8
  5.9 0.1 shard_map.39
  6.0 4.2 %collective-permute-start.3 = (f32[4,24,512]{2,1,0:T(8,128)S(1)}, f32[4,24,512]{2,1,0:T(8,128)S(1)}, u32[]{:S(2)}, u32[]{:S(2)}) collective-permute-start(f32[4,24,512]{2,1,0:T(8,128)S(1)} %get-tuple-element.34), channel_id=1, source_target_pairs={{0,3},{1,2},{2,1},{3,0},{4,7},{5,6},{6,5},{7,4},{8,11},{9,10},{10,... | collective-permute-start | bytes 589832 | tf_op jit(solution)/shard_map/ppermute | solution.py:421
  10.2 0.6 %collective-permute-start.5 = (f32[4,24,512]{2,1,0:T(8,128)S(1)}, f32[4,24,512]{2,1,0:T(8,128)S(1)}, u32[]{:S(2)}, u32[]{:S(2)}) collective-permute-start(f32[4,24,512]{2,1,0:T(8,128)S(1)} %get-tuple-element.36), channel_id=1, source_target_pairs={{0,1},{1,0},{2,3},{3,2},{4,5},{5,4},{6,7},{7,6},{8,9},{9,8},{10,11... | collective-permute-start | bytes 589832 | tf_op jit(solution)/shard_map/ppermute | solution.py:421
  10.9 1.6 %shard_map.40.refs_5_.refs_6_ = f32[2,256,512]{2,1,0:T(8,128)S(1)} custom-call(f32[4,256,512]{2,1,0:T(8,128)S(1)} %bitcast.11, f32[4,256,512]{2,1,0:T(8,128)S(1)} %copy-done.2, f32[4,24,512]{2,1,0:T(8,128)S(1)} %get-tuple-element.31.refs_2_.refs_0_), custom_call_target="tpu_custom_call" | custom-call | flops 6291456 | bytes 5242880 | tf_op jit(solution)/shard_map/pallas_call | solution.py:364
  12.5 5.6 %shard_map.41 = (f32[2,256,512]{2,1,0:T(8,128)S(1)}, f32[2,256,512]{2,1,0:T(8,128)S(1)}, f32[8,512]{1,0:T(8,128)S(1)}) custom-call(f32[3]{0:T(128)S(1)} %copy-done.3, f32[4,256,512]{2,1,0:T(8,128)S(1)} %bitcast.12, f32[4,256,512]{2,1,0:T(8,128)S(1)} %copy-done.2, f32[4,256,512]{2,1,0:T(8,128)S(1)} %collective-permute-done.refs_3_, ...), custom_call_target="tpu_custom_call" | custom-call | flops 20971520 | bytes 11550732 | tf_op jit(solution)/shard_map/pallas_call | solution.py:364
  18.1 0.0 collective-permute-done.2.refs_0_.refs_1_.refs_4_
  18.1 0.1 shard_map.42.refs_4_
  18.2 2.8 %collective-permute-start.10 = (f32[2,4,32,512]{3,2,1,0:T(8,128)S(1)}, f32[2,4,32,512]{3,2,1,0:T(8,128)S(1)}, u32[]{:S(2)}, u32[]{:S(2)}) collective-permute-start(f32[2,4,32,512]{3,2,1,0:T(8,128)S(1)} %shard_map.42.refs_4_), channel_id=1, source_target_pairs={{0,28},{4,8},{8,4},{12,16},{16,12},{20,24},{24,20},{28,0},{1,29},{... | collective-permute-start | bytes 1572872 | tf_op jit(solution)/shard_map/ppermute | solution.py:438
  21.0 0.0 collective-permute-done.3.refs_1_
  21.0 5.1 %collective-permute-done.4.refs_2_ = f32[4,24,512]{2,1,0:T(8,128)S(1)} collective-permute-done((f32[4,24,512]{2,1,0:T(8,128)S(1)}, f32[4,24,512]{2,1,0:T(8,128)S(1)}, u32[]{:S(2)}, u32[]{:S(2)}) %collective-permute-start.4) | collective-permute-done | bytes 196640 | tf_op jit(solution)/shard_map/ppermute | solution.py:421
  26.2 0.1 shard_map.43
  26.2 0.1 collective-permute-start.7
  26.3 0.2 shard_map.44
  26.5 0.1 collective-permute-start.6
  26.6 2.7 %collective-permute-done.8.refs_0_.refs_1_.refs_2_.refs_5_ = f32[2,4,32,512]{3,2,1,0:T(8,128)S(1)} collective-permute-done((f32[2,4,32,512]{3,2,1,0:T(8,128)S(1)}, f32[2,4,32,512]{3,2,1,0:T(8,128)S(1)}, u32[]{:S(2)}, u32[]{:S(2)}) %collective-permute-start.8) | collective-permute-done | bytes 524320 | tf_op jit(solution)/shard_map/ppermute | solution.py:451
  29.3 0.1 shard_map.45
  29.4 2.9 %collective-permute-start.13 = (f32[2,4,16,512]{3,2,1,0:T(8,128)S(1)}, f32[2,4,16,512]{3,2,1,0:T(8,128)S(1)}, u32[]{:S(2)}, u32[]{:S(2)}) collective-permute-start(f32[2,4,16,512]{3,2,1,0:T(8,128)S(1)} %get-tuple-element.41.refs_3_.refs_5_), channel_id=1, source_target_pairs={{0,28},{4,8},{8,4},{12,16},{16,12},{20,24},{24,20},{28,0},{1,29},{... | collective-permute-start | bytes 786440 | tf_op jit(solution)/shard_map/ppermute | solution.py:438
  32.2 0.1 shard_map.46
  32.3 1.6 %collective-permute-start.11 = (f32[2,2,16,512]{3,2,1,0:T(8,128)S(1)}, f32[2,2,16,512]{3,2,1,0:T(8,128)S(1)}, u32[]{:S(2)}, u32[]{:S(2)}) collective-permute-start(f32[2,2,16,512]{3,2,1,0:T(8,128)S(1)} %get-tuple-element.45), channel_id=1, source_target_pairs={{0,1},{1,0},{2,3},{3,2},{4,5},{5,4},{6,7},{7,6},{8,9},{9,8},{10,11... | collective-permute-start | bytes 393224 | tf_op jit(solution)/shard_map/ppermute | solution.py:430
  34.0 0.0 collective-permute-done.7.refs_2_
  34.0 2.5 %shard_map.47 = (f32[4,2,20,512]{3,2,1,0:T(8,128)S(1)}, f32[4,2,16,512]{3,2,1,0:T(8,128)S(1)}, f32[4,2,16,512]{3,2,1,0:T(8,128)S(1)}) custom-call(f32[3]{0:T(128)S(1)} %copy-done.3, f32[4,4,24,512]{3,2,1,0:T(8,128)S(1)} %get-tuple-element.38.refs_3_.refs_1_, f32[4,4,24,512]{3,2,1,0:T(8,128)S(1)} %collective-permute-done.7.refs_2_, ...), custom_call_target="tpu_custom_call" | custom-call | bytes 6619148 | tf_op jit(solution)/shard_map/pallas_call | solution.py:364
  36.4 0.0 collective-permute-done.6.refs_1_
  36.5 2.5 %collective-permute-start.9 = (f32[2,32,512]{2,1,0:T(8,128)S(1)}, f32[2,32,512]{2,1,0:T(8,128)S(1)}, u32[]{:S(2)}, u32[]{:S(2)}) collective-permute-start(f32[2,32,512]{2,1,0:T(8,128)S(1)} %shard_map.48.refs_7_), channel_id=1, source_target_pairs={{0,3},{1,2},{2,1},{3,0},{4,7},{5,6},{6,5},{7,4},{8,11},{9,10},{10,... | collective-permute-start | bytes 393224 | tf_op jit(solution)/shard_map/ppermute | solution.py:410
  39.0 2.4 %shard_map.49.refs_2_ = f32[2,256,512]{2,1,0:T(8,128)S(1)} custom-call(f32[3]{0:T(128)S(1)} %copy-done.3, f32[4,256,512]{2,1,0:T(8,128)S(1)} %bitcast.13, f32[4,256,512]{2,1,0:T(8,128)S(1)} %copy-done.2, f32[2,256,512]{2,1,0:T(8,128)S(1)} %get-tuple-element.37.refs_2_.refs_3_, f32[2,4,32,512]{3,2,1,0:T(8,128)S(1)} %shard_map.42.refs_4_, ...), custom_call_target="tpu_custom_call" | custom-call | flops 10485760 | bytes 7340044 | tf_op jit(solution)/shard_map/pallas_call | solution.py:364
  41.5 1.4 %collective-permute-start.12 = (f32[2,16,512]{2,1,0:T(8,128)S(1)}, f32[2,16,512]{2,1,0:T(8,128)S(1)}, u32[]{:S(2)}, u32[]{:S(2)}) collective-permute-start(f32[2,16,512]{2,1,0:T(8,128)S(1)} %shard_map.50.refs_3_), channel_id=1, source_target_pairs={{0,3},{1,2},{2,1},{3,0},{4,7},{5,6},{6,5},{7,4},{8,11},{9,10},{10,... | collective-permute-start | bytes 196616 | tf_op jit(solution)/shard_map/ppermute | solution.py:410
  42.9 0.9 %collective-permute-start.14 = (f32[120,512]{1,0:T(8,128)S(1)}, f32[120,512]{1,0:T(8,128)S(1)}, u32[]{:S(2)}, u32[]{:S(2)}) collective-permute-start(f32[120,512]{1,0:T(8,128)S(1)} %get-tuple-element.48), channel_id=1, source_target_pairs={{0,28},{4,8},{8,4},{12,16},{16,12},{20,24},{24,20},{28,0},{1,29},{... | collective-permute-start | bytes 737288 | tf_op jit(solution)/shard_map/ppermute | solution.py:477
  43.7 0.1 shard_map.51
  43.9 0.1 collective-permute-start.16
  43.9 0.0 collective-permute-done.9.refs_2_
  44.0 1.5 %collective-permute-done.13.refs_1_ = f32[2,4,16,512]{3,2,1,0:T(8,128)S(1)} collective-permute-done((f32[2,4,16,512]{3,2,1,0:T(8,128)S(1)}, f32[2,4,16,512]{3,2,1,0:T(8,128)S(1)}, u32[]{:S(2)}, u32[]{:S(2)}) %collective-permute-start.13) | collective-permute-done | bytes 262176 | tf_op jit(solution)/shard_map/ppermute | solution.py:438
  45.5 0.1 shard_map.53
  45.6 2.8 %collective-permute-start.15 = (f32[2,2,16,512]{3,2,1,0:T(8,128)S(1)}, f32[2,2,16,512]{3,2,1,0:T(8,128)S(1)}, u32[]{:S(2)}, u32[]{:S(2)}) collective-permute-start(f32[2,2,16,512]{3,2,1,0:T(8,128)S(1)} %get-tuple-element.52), channel_id=1, source_target_pairs={{0,1},{1,0},{2,3},{3,2},{4,5},{5,4},{6,7},{7,6},{8,9},{9,8},{10,11... | collective-permute-start | bytes 393224 | tf_op jit(solution)/shard_map/ppermute | solution.py:418
  48.4 3.5 %collective-permute-done.14.refs_0_.refs_3_ = f32[120,512]{1,0:T(8,128)S(1)} collective-permute-done((f32[120,512]{1,0:T(8,128)S(1)}, f32[120,512]{1,0:T(8,128)S(1)}, u32[]{:S(2)}, u32[]{:S(2)}) %collective-permute-start.14) | collective-permute-done | bytes 245792 | tf_op jit(solution)/shard_map/ppermute | solution.py:477
  51.8 0.1 shard_map.55
  51.9 1.2 %collective-permute-start.19 = (f32[4,2,16,512]{3,2,1,0:T(8,128)S(1)}, f32[4,2,16,512]{3,2,1,0:T(8,128)S(1)}, u32[]{:S(2)}, u32[]{:S(2)}) collective-permute-start(f32[4,2,16,512]{3,2,1,0:T(8,128)S(1)} %get-tuple-element.55), channel_id=1, source_target_pairs={{0,28},{4,8},{8,4},{12,16},{16,12},{20,24},{24,20},{28,0},{1,29},{... | collective-permute-start | bytes 786440 | tf_op jit(solution)/shard_map/ppermute | solution.py:506
  53.2 0.1 collective-permute-done.16.refs_1_
  53.2 3.7 %collective-permute-start.17 = (f32[2,32,512]{2,1,0:T(8,128)S(1)}, f32[2,32,512]{2,1,0:T(8,128)S(1)}, u32[]{:S(2)}, u32[]{:S(2)}) collective-permute-start(f32[2,32,512]{2,1,0:T(8,128)S(1)} %shard_map.56.refs_2_), channel_id=1, source_target_pairs={{0,3},{1,2},{2,1},{3,0},{4,7},{5,6},{6,5},{7,4},{8,11},{9,10},{10,... | collective-permute-start | bytes 393224 | tf_op jit(solution)/shard_map/ppermute | solution.py:410
  56.9 1.4 %collective-permute-start.18 = (f32[2,16,512]{2,1,0:T(8,128)S(1)}, f32[2,16,512]{2,1,0:T(8,128)S(1)}, u32[]{:S(2)}, u32[]{:S(2)}) collective-permute-start(f32[2,16,512]{2,1,0:T(8,128)S(1)} %shard_map.57.refs_9_), channel_id=1, source_target_pairs={{0,3},{1,2},{2,1},{3,0},{4,7},{5,6},{6,5},{7,4},{8,11},{9,10},{10,... | collective-permute-start | bytes 196616 | tf_op jit(solution)/shard_map/ppermute | solution.py:410
  58.4 1.2 %shard_map.58 = (f32[2,16,512]{2,1,0:T(8,128)S(1)}, f32[4,2,16,512]{3,2,1,0:T(8,128)S(1)}) custom-call(f32[3]{0:T(128)S(1)} %copy-done.3, f32[4,4,24,512]{3,2,1,0:T(8,128)S(1)} %get-tuple-element.38.refs_3_.refs_1_, f32[4,4,64,512]{3,2,1,0:T(8,128)S(1)} %bitcast.15, f32[120,512]{1,0:T(8,128)S(1)} %collective-permute-done.14.refs_0_.refs_3_, ...), custom_call_target="tpu_custom_call" | custom-call | bytes 5357580 | tf_op jit(solution)/shard_map/pallas_call | solution.py:364
  59.5 1.2 %collective-permute-done.17.refs_2_ = f32[2,32,512]{2,1,0:T(8,128)S(1)} collective-permute-done((f32[2,32,512]{2,1,0:T(8,128)S(1)}, f32[2,32,512]{2,1,0:T(8,128)S(1)}, u32[]{:S(2)}, u32[]{:S(2)}) %collective-permute-start.17) | collective-permute-done | bytes 131104 | tf_op jit(solution)/shard_map/ppermute | solution.py:410
  60.7 2.4 %collective-permute-done.18.refs_2_ = f32[2,16,512]{2,1,0:T(8,128)S(1)} collective-permute-done((f32[2,16,512]{2,1,0:T(8,128)S(1)}, f32[2,16,512]{2,1,0:T(8,128)S(1)}, u32[]{:S(2)}, u32[]{:S(2)}) %collective-permute-start.18) | collective-permute-done | bytes 65568 | tf_op jit(solution)/shard_map/ppermute | solution.py:410
  63.2 0.9 %shard_map.61 = f32[4,64,512]{2,1,0:T(8,128)} custom-call(f32[2,32,512]{2,1,0:T(8,128)S(1)} %shard_map.52.refs_3_.refs_0_, f32[2,16,512]{2,1,0:T(8,128)S(1)} %shard_map.54.refs_4_.refs_1_, f32[2,16,512]{2,1,0:T(8,128)S(1)} %get-tuple-element.54.refs_3_.refs_2_, f32[2,32,512]{2,1,0:T(8,128)S(1)} %shard_map.59.refs_3_, ...), custom_call_target="tpu_custom_call" | custom-call | bytes 1523712 | tf_op jit(solution)/shard_map/pallas_call | solution.py:364
  (25 shorter events, 0.2 us)
Async XLA Ops:
  0.0 10.2 %collective-permute-start = (f32[4,256,512]{2,1,0:T(8,128)}, f32[4,256,512]{2,1,0:T(8,128)S(1)}, u32[]{:S(2)}, u32[]{:S(2)}) collective-permute-start(f32[4,256,512]{2,1,0:T(8,128)} %bitcast.7), channel_id=1, source_target_pairs={{0,4},{4,0},{8,12},{12,8},{16,20},{20,16},{24,28},{28,24},{1,5},{5... | collective-permute-start | bytes 6291464 | tf_op jit(solution)/shard_map/ppermute | solution.py:440
  0.5 9.8 %collective-permute-start.1 = (f32[4,256,512]{2,1,0:T(8,128)}, f32[4,256,512]{2,1,0:T(8,128)S(1)}, u32[]{:S(2)}, u32[]{:S(2)}) collective-permute-start(f32[4,256,512]{2,1,0:T(8,128)} %refs_2_.3), channel_id=1, source_target_pairs={{0,4},{4,0},{8,12},{12,8},{16,20},{20,16},{24,28},{28,24},{1,5},{5... | collective-permute-start | bytes 6291464 | tf_op jit(solution)/shard_map/ppermute | solution.py:441
  0.5 1.6 %copy-start = (f32[1,4,256,512]{3,2,1,0:T(8,128)S(1)}, f32[1,4,256,512]{3,2,1,0:T(8,128)}, u32[]{:S(2)}) copy-start(f32[1,4,256,512]{3,2,1,0:T(8,128)} %param.3) | copy-start | bytes 6291460
  2.2 16.0 %collective-permute-start.2 = (f32[2,4,32,512]{3,2,1,0:T(8,128)S(1)}, f32[2,4,32,512]{3,2,1,0:T(8,128)S(1)}, u32[]{:S(2)}, u32[]{:S(2)}) collective-permute-start(f32[2,4,32,512]{3,2,1,0:T(8,128)S(1)} %shard_map.37.refs_1_), channel_id=1, source_target_pairs={{0,28},{4,8},{8,4},{12,16},{16,12},{20,24},{24,20},{28,0},{1,29},{... | collective-permute-start | bytes 1572872 | tf_op jit(solution)/shard_map/ppermute | solution.py:451
  5.8 5.1 %copy-start.2 = (f32[4,256,512]{2,1,0:T(8,128)S(1)}, f32[4,256,512]{2,1,0:T(8,128)}, u32[]{:S(2)}) copy-start(f32[4,256,512]{2,1,0:T(8,128)} %refs_2_.3) | copy-start | bytes 6291460
  5.8 23.5 %collective-permute-start.8 = (f32[2,4,32,512]{3,2,1,0:T(8,128)S(1)}, f32[2,4,32,512]{3,2,1,0:T(8,128)S(1)}, u32[]{:S(2)}, u32[]{:S(2)}) collective-permute-start(f32[2,4,32,512]{3,2,1,0:T(8,128)S(1)} %shard_map.38.refs_1_), channel_id=1, source_target_pairs={{0,28},{4,8},{8,4},{12,16},{16,12},{20,24},{24,20},{28,0},{1,29},{... | collective-permute-start | bytes 1572872 | tf_op jit(solution)/shard_map/ppermute | solution.py:451
  6.0 15.0 %collective-permute-start.3 = (f32[4,24,512]{2,1,0:T(8,128)S(1)}, f32[4,24,512]{2,1,0:T(8,128)S(1)}, u32[]{:S(2)}, u32[]{:S(2)}) collective-permute-start(f32[4,24,512]{2,1,0:T(8,128)S(1)} %get-tuple-element.34), channel_id=1, source_target_pairs={{0,3},{1,2},{2,1},{3,0},{4,7},{5,6},{6,5},{7,4},{8,11},{9,10},{10,... | collective-permute-start | bytes 589832 | tf_op jit(solution)/shard_map/ppermute | solution.py:421
  10.2 16.0 %collective-permute-start.4 = (f32[4,24,512]{2,1,0:T(8,128)S(1)}, f32[4,24,512]{2,1,0:T(8,128)S(1)}, u32[]{:S(2)}, u32[]{:S(2)}) collective-permute-start(f32[4,24,512]{2,1,0:T(8,128)S(1)} %get-tuple-element.35), channel_id=1, source_target_pairs={{0,2},{1,3},{2,0},{3,1},{4,6},{5,7},{6,4},{7,5},{8,10},{9,11},{10,... | collective-permute-start | bytes 589832 | tf_op jit(solution)/shard_map/ppermute | solution.py:421
  10.2 16.0 %collective-permute-start.5 = (f32[4,24,512]{2,1,0:T(8,128)S(1)}, f32[4,24,512]{2,1,0:T(8,128)S(1)}, u32[]{:S(2)}, u32[]{:S(2)}) collective-permute-start(f32[4,24,512]{2,1,0:T(8,128)S(1)} %get-tuple-element.36), channel_id=1, source_target_pairs={{0,1},{1,0},{2,3},{3,2},{4,5},{5,4},{6,7},{7,6},{8,9},{9,8},{10,11... | collective-permute-start | bytes 589832 | tf_op jit(solution)/shard_map/ppermute | solution.py:421
  10.9 1.6 %copy-start.3 = (f32[3]{0:T(128)S(1)}, f32[3]{0:T(128)}, u32[]{:S(2)}) copy-start(f32[3]{0:T(128)} %refs_0_.7) | copy-start | bytes 40
  18.2 25.5 %collective-permute-start.10 = (f32[2,4,32,512]{3,2,1,0:T(8,128)S(1)}, f32[2,4,32,512]{3,2,1,0:T(8,128)S(1)}, u32[]{:S(2)}, u32[]{:S(2)}) collective-permute-start(f32[2,4,32,512]{3,2,1,0:T(8,128)S(1)} %shard_map.42.refs_4_), channel_id=1, source_target_pairs={{0,28},{4,8},{8,4},{12,16},{16,12},{20,24},{24,20},{28,0},{1,29},{... | collective-permute-start | bytes 1572872 | tf_op jit(solution)/shard_map/ppermute | solution.py:438
  26.2 7.7 %collective-permute-start.7 = (f32[4,4,24,512]{3,2,1,0:T(8,128)S(1)}, f32[4,4,24,512]{3,2,1,0:T(8,128)S(1)}, u32[]{:S(2)}, u32[]{:S(2)}) collective-permute-start(f32[4,4,24,512]{3,2,1,0:T(8,128)S(1)} %get-tuple-element.38.refs_3_.refs_1_), channel_id=1, source_target_pairs={{0,4},{4,0},{8,12},{12,8},{16,20},{20,16},{24,28},{28,24},{1,5},{5... | collective-permute-start | bytes 2359304 | tf_op jit(solution)/shard_map/ppermute | solution.py:476
  26.5 10.0 %collective-permute-start.6 = (f32[2,2,32,512]{3,2,1,0:T(8,128)S(1)}, f32[2,2,32,512]{3,2,1,0:T(8,128)S(1)}, u32[]{:S(2)}, u32[]{:S(2)}) collective-permute-start(f32[2,2,32,512]{3,2,1,0:T(8,128)S(1)} %get-tuple-element.40), channel_id=1, source_target_pairs={{0,1},{1,0},{2,3},{3,2},{4,5},{5,4},{6,7},{7,6},{8,9},{9,8},{10,11... | collective-permute-start | bytes 786440 | tf_op jit(solution)/shard_map/ppermute | solution.py:430
  29.4 16.1 %collective-permute-start.13 = (f32[2,4,16,512]{3,2,1,0:T(8,128)S(1)}, f32[2,4,16,512]{3,2,1,0:T(8,128)S(1)}, u32[]{:S(2)}, u32[]{:S(2)}) collective-permute-start(f32[2,4,16,512]{3,2,1,0:T(8,128)S(1)} %get-tuple-element.41.refs_3_.refs_5_), channel_id=1, source_target_pairs={{0,28},{4,8},{8,4},{12,16},{16,12},{20,24},{24,20},{28,0},{1,29},{... | collective-permute-start | bytes 786440 | tf_op jit(solution)/shard_map/ppermute | solution.py:438
  32.3 9.1 %collective-permute-start.11 = (f32[2,2,16,512]{3,2,1,0:T(8,128)S(1)}, f32[2,2,16,512]{3,2,1,0:T(8,128)S(1)}, u32[]{:S(2)}, u32[]{:S(2)}) collective-permute-start(f32[2,2,16,512]{3,2,1,0:T(8,128)S(1)} %get-tuple-element.45), channel_id=1, source_target_pairs={{0,1},{1,0},{2,3},{3,2},{4,5},{5,4},{6,7},{7,6},{8,9},{9,8},{10,11... | collective-permute-start | bytes 393224 | tf_op jit(solution)/shard_map/ppermute | solution.py:430
  34.0 5.1 %copy-start.1 = (f32[1,4,256,512]{3,2,1,0:T(8,128)S(1)}, f32[1,4,256,512]{3,2,1,0:T(8,128)}, u32[]{:S(2)}) copy-start(f32[1,4,256,512]{3,2,1,0:T(8,128)} %param.3) | copy-start | bytes 6291460
  36.5 7.5 %collective-permute-start.9 = (f32[2,32,512]{2,1,0:T(8,128)S(1)}, f32[2,32,512]{2,1,0:T(8,128)S(1)}, u32[]{:S(2)}, u32[]{:S(2)}) collective-permute-start(f32[2,32,512]{2,1,0:T(8,128)S(1)} %shard_map.48.refs_7_), channel_id=1, source_target_pairs={{0,3},{1,2},{2,1},{3,0},{4,7},{5,6},{6,5},{7,4},{8,11},{9,10},{10,... | collective-permute-start | bytes 393224 | tf_op jit(solution)/shard_map/ppermute | solution.py:410
  41.5 6.9 %collective-permute-start.12 = (f32[2,16,512]{2,1,0:T(8,128)S(1)}, f32[2,16,512]{2,1,0:T(8,128)S(1)}, u32[]{:S(2)}, u32[]{:S(2)}) collective-permute-start(f32[2,16,512]{2,1,0:T(8,128)S(1)} %shard_map.50.refs_3_), channel_id=1, source_target_pairs={{0,3},{1,2},{2,1},{3,0},{4,7},{5,6},{6,5},{7,4},{8,11},{9,10},{10,... | collective-permute-start | bytes 196616 | tf_op jit(solution)/shard_map/ppermute | solution.py:410
  42.9 8.9 %collective-permute-start.14 = (f32[120,512]{1,0:T(8,128)S(1)}, f32[120,512]{1,0:T(8,128)S(1)}, u32[]{:S(2)}, u32[]{:S(2)}) collective-permute-start(f32[120,512]{1,0:T(8,128)S(1)} %get-tuple-element.48), channel_id=1, source_target_pairs={{0,28},{4,8},{8,4},{12,16},{16,12},{20,24},{24,20},{28,0},{1,29},{... | collective-permute-start | bytes 737288 | tf_op jit(solution)/shard_map/ppermute | solution.py:477
  43.9 9.4 %collective-permute-start.16 = (f32[2,2,32,512]{3,2,1,0:T(8,128)S(1)}, f32[2,2,32,512]{3,2,1,0:T(8,128)S(1)}, u32[]{:S(2)}, u32[]{:S(2)}) collective-permute-start(f32[2,2,32,512]{3,2,1,0:T(8,128)S(1)} %get-tuple-element.53), channel_id=1, source_target_pairs={{0,1},{1,0},{2,3},{3,2},{4,5},{5,4},{6,7},{7,6},{8,9},{9,8},{10,11... | collective-permute-start | bytes 786440 | tf_op jit(solution)/shard_map/ppermute | solution.py:418
  45.6 11.4 %collective-permute-start.15 = (f32[2,2,16,512]{3,2,1,0:T(8,128)S(1)}, f32[2,2,16,512]{3,2,1,0:T(8,128)S(1)}, u32[]{:S(2)}, u32[]{:S(2)}) collective-permute-start(f32[2,2,16,512]{3,2,1,0:T(8,128)S(1)} %get-tuple-element.52), channel_id=1, source_target_pairs={{0,1},{1,0},{2,3},{3,2},{4,5},{5,4},{6,7},{7,6},{8,9},{9,8},{10,11... | collective-permute-start | bytes 393224 | tf_op jit(solution)/shard_map/ppermute | solution.py:418
  51.9 11.2 %collective-permute-start.19 = (f32[4,2,16,512]{3,2,1,0:T(8,128)S(1)}, f32[4,2,16,512]{3,2,1,0:T(8,128)S(1)}, u32[]{:S(2)}, u32[]{:S(2)}) collective-permute-start(f32[4,2,16,512]{3,2,1,0:T(8,128)S(1)} %get-tuple-element.55), channel_id=1, source_target_pairs={{0,28},{4,8},{8,4},{12,16},{16,12},{20,24},{24,20},{28,0},{1,29},{... | collective-permute-start | bytes 786440 | tf_op jit(solution)/shard_map/ppermute | solution.py:506
  53.2 7.5 %collective-permute-start.17 = (f32[2,32,512]{2,1,0:T(8,128)S(1)}, f32[2,32,512]{2,1,0:T(8,128)S(1)}, u32[]{:S(2)}, u32[]{:S(2)}) collective-permute-start(f32[2,32,512]{2,1,0:T(8,128)S(1)} %shard_map.56.refs_2_), channel_id=1, source_target_pairs={{0,3},{1,2},{2,1},{3,0},{4,7},{5,6},{6,5},{7,4},{8,11},{9,10},{10,... | collective-permute-start | bytes 393224 | tf_op jit(solution)/shard_map/ppermute | solution.py:410
  56.9 6.2 %collective-permute-start.18 = (f32[2,16,512]{2,1,0:T(8,128)S(1)}, f32[2,16,512]{2,1,0:T(8,128)S(1)}, u32[]{:S(2)}, u32[]{:S(2)}) collective-permute-start(f32[2,16,512]{2,1,0:T(8,128)S(1)} %shard_map.57.refs_9_), channel_id=1, source_target_pairs={{0,3},{1,2},{2,1},{3,0},{4,7},{5,6},{6,5},{7,4},{8,11},{9,10},{10,... | collective-permute-start | bytes 196616 | tf_op jit(solution)/shard_map/ppermute | solution.py:410
